TPU v7x, 32 devices: a whole 2x2x4 slice. The times are simulated.
32 devices in a mesh: ctx: 16 (over z, x, core), tp: 2 (over y).
Axes of the slice: x: 2, y: 2, z: 4, core: 2. Of those that a mesh axis runs over, the one named last changes fastest.
Arguments:
- tokens_in: bfloat16 [2048, 8192], P('ctx', 'tp'), may hold values from -6 to 6
- w_query: bfloat16 [2, 4096, 8192], P(None, 'ctx', 'tp'), may hold values from -0.0625 to 0.0625
- w_key: bfloat16 [2, 4096, 8192], P(None, 'ctx', 'tp'), may hold values from -0.0625 to 0.0625
- w_value: bfloat16 [2, 4096, 8192], P(None, 'ctx', 'tp'), may hold values from -0.0625 to 0.0625
- short_taps: float32 [3, 2, 256, 3], P(None, 'tp', 'ctx'), may hold values from -2.5 to 2.5
- long_taps: float32 [2, 256, 128], P('tp', 'ctx'), may hold values from -0.5 to 0.5
- grad_out: bfloat16 [8192, 2048], P('tp', 'ctx'), may hold values from -6 to 6
Outputs:
- mixed_out: bfloat16 [8192, 2048], P('tp', 'ctx')
- grad_tokens: bfloat16 [2048, 8192], P('ctx', 'tp')
- grad_short: float32 [3, 2, 256, 3], P(None, 'tp', 'ctx')
- grad_long: float32 [2, 256, 128], P('tp', 'ctx')
All inputs are finite; a program needn't handle non-finite values.
Results may differ from a plain program's by a relative error of at most 0.019.
Values may be sent and summed in bfloat16 or wider, within the bound.
No kernel may reach another device: no remote copies, remote signals or barrier semaphores. Data moves between devices by JAX's collectives and lax.ppermute only.
A program may use at most 192 MiB of HBM per device.

v0:
```python
import functools

import jax
import jax.numpy as jnp
import numpy as np
from jax import lax
from jax.experimental import pallas as pl
from jax.experimental.pallas import tpu as pltpu
from jax.sharding import PartitionSpec as P

GROUP = 16
SHORT = 3
LONG = 128
F32 = jnp.float32
BF16 = jnp.bfloat16
VMEM = 58 * 1024 * 1024
VMEM_DOT = 24 * 1024 * 1024


def ring_of(mesh):
    chips = mesh.shape["ctx"] // 2
    plain = list(range(chips))
    devices = np.asarray(mesh.devices).reshape(mesh.shape["ctx"], -1)[:, 0]
    places = [getattr(devices[2 * chip], "coords", None) for chip in plain]
    if any(place is None for place in places):
        return plain
    places = np.array([list(place)[:3] for place in places])
    axes = [axis for axis in range(3) if len(set(places[:, axis])) > 1]
    if len(axes) != 2:
        return plain
    rung = min(axes, key=lambda axis: len(set(places[:, axis])))
    along = axes[0] if rung == axes[1] else axes[1]
    sides = sorted(set(places[:, rung]))
    if len(sides) != 2:
        return plain
    there = [c for c in plain if places[c, rung] == sides[0]]
    back = [c for c in plain if places[c, rung] == sides[1]]
    there.sort(key=lambda c: places[c, along])
    back.sort(key=lambda c: -places[c, along])
    return there + back


def dot(a, b, dims):
    return lax.dot_general(a, b, (dims, ((), ())), preferred_element_type=F32)


def mix_body(count, sets, per_step, order, short_ref, long_ref, g_ref, *refs):
    proj_refs = [refs[s * count : (s + 1) * count] for s in range(sets)]
    refs = refs[sets * count :]
    mixed_ref, d_refs, gs_ref, gl_ref = refs[0], refs[1 : 1 + count], refs[1 + count], refs[2 + count]
    p_s, x_s, y_s, d_s, e_s = refs[3 + count :]
    blocks = g_ref.shape[0]
    rows = blocks * GROUP
    step = pl.program_id(0)

    @pl.when(step == 0)
    def _():
        p_s[:, :, 0:GROUP, :] = jnp.zeros((per_step, 3, GROUP, LONG), F32)
        x_s[:, 0:GROUP, :] = jnp.zeros((per_step, GROUP, LONG), BF16)
        y_s[:, rows:, :] = jnp.zeros((per_step, GROUP, LONG), BF16)
        d_s[:, :, rows:, :] = jnp.zeros((per_step, 3, GROUP, LONG), F32)

    halves = [(a, h) for a in range(count) for h in range(proj_refs[0][a].shape[2] // LONG)]
    places = [(a, h, where) for where, (a, h) in enumerate(halves)]
    lane = lax.broadcasted_iota(jnp.int32, (rows, LONG), 1)
    sub8 = lax.broadcasted_iota(jnp.int32, (8, LONG), 0)
    col = lax.broadcasted_iota(jnp.int32, (LONG, LONG), 1)
    row = lax.broadcasted_iota(jnp.int32, (LONG, LONG), 0)

    for j in range(per_step):
        group = step * per_step + j
        mine = slice(j * GROUP, (j + 1) * GROUP)
        for a, h, where in places:
            at = pl.multiple_of((order[where] + 1) * GROUP, GROUP)
            for i in range(3):
                part = proj_refs[0][a][i, mine, h * LONG : (h + 1) * LONG].astype(F32)
                for s in range(1, sets):
                    part = part + proj_refs[s][a][i, mine, h * LONG : (h + 1) * LONG].astype(F32)
                p_s[j, i, pl.ds(at, GROUP), :] = part
        taps = [[short_ref[i, group, k] for k in range(SHORT)] for i in range(3)]
        feats = []
        for i in range(3):
            whole = p_s[j, i]
            one = pltpu.roll(whole, 1, 1)
            two = pltpu.roll(whole, 2, 1)
            one = jnp.where(lane < 1, one[:rows], one[GROUP:])
            two = jnp.where(lane < 2, two[:rows], two[GROUP:])
            feats.append(taps[i][0] * whole[GROUP:] + taps[i][1] * one + taps[i][2] * two)
        fq, fk, fv = feats
        x_s[j, GROUP:, :] = (fk * fv).astype(BF16)

        base = jnp.broadcast_to(long_ref[0, j : j + 1, :], (8, LONG))
        for bit in (1, 2, 4):
            base = jnp.where((sub8 & bit) != 0, pltpu.roll(base, bit, 1), base)
        full = jnp.concatenate([base] + [pltpu.roll(base, 8 * m, 1) for m in range(1, LONG // 8)], axis=0)
        near = jnp.where(col >= row, full, 0.0).astype(BF16)
        far = jnp.where(col < row, full, 0.0).astype(BF16)

        x_two = jnp.concatenate([x_s[j, GROUP:, :], x_s[j, :rows, :]], axis=1)
        inner = dot(x_two, jnp.concatenate([near, far], axis=0), ((1,), (0,)))
        g = g_ref[:, mine, :].reshape(rows, LONG).astype(F32)
        mixed_ref[:, mine, :] = (fq * inner).astype(BF16).reshape(blocks, GROUP, LONG)
        y_s[j, :rows, :] = (g * fq).astype(BF16)
        y_one = y_s[j, :rows, :]
        y_two = jnp.concatenate([y_one, y_s[j, GROUP:, :]], axis=1)
        d_product = dot(y_two, jnp.concatenate([near, far], axis=1), ((1,), (1,)))

        pairs = dot(x_two, y_one, ((0,), (0,)))
        fold = jnp.where(col >= row, pairs[:LONG], pairs[LONG:])
        width = LONG
        while width > 8:
            width //= 2
            fold = fold[:width] + pltpu.roll(fold[width:], LONG - width, 1)
        for bit in (4, 2, 1):
            fold = jnp.where((sub8 & bit) != 0, pltpu.roll(fold, LONG - bit, 1), fold)
        gl_ref[0, j : j + 1, :] = jnp.sum(fold, axis=0, keepdims=True)

        for i, d in enumerate((g * inner, d_product * fv, d_product * fk)):
            d_s[j, i, :rows, :] = d
            whole = d_s[j, i]
            one = pltpu.roll(whole, LONG - 1, 1)
            two = pltpu.roll(whole, LONG - 2, 1)
            one = jnp.where(lane >= LONG - 1, one[GROUP:], one[:rows])
            two = jnp.where(lane >= LONG - 2, two[GROUP:], two[:rows])
            p = p_s[j, i, GROUP:, :]
            for k, moved in enumerate((d, one, two)):
                gs_ref[0, j, 3 * i + k : 3 * i + k + 1, :] = jnp.sum(p * moved, axis=0, keepdims=True)
            e_s[j, i] = (taps[i][0] * d + taps[i][1] * one + taps[i][2] * two).astype(BF16)
        for a, h, where in places:
            at = pl.multiple_of(order[where] * GROUP, GROUP)
            for i in range(3):
                d_refs[a][i, mine, h * LONG : (h + 1) * LONG] = e_s[j, i, pl.ds(at, GROUP), :]


def mix(order, short_kernel, long_kernel, g, proj_sets):
    blocks, channels, _ = g.shape
    count, sets = len(proj_sets[0]), len(proj_sets)
    groups = channels // GROUP
    per_step = 2 if groups % 2 == 0 else 1
    steps = groups // per_step
    rows = blocks * GROUP
    high = per_step * GROUP
    proj_specs = [pl.BlockSpec((3, high, x.shape[2]), lambda i, o: (0, i, 0)) for x in proj_sets[0]]
    token_spec = pl.BlockSpec((blocks, high, LONG), lambda i, o: (0, i, 0))
    outs = pl.pallas_call(
        functools.partial(mix_body, count, sets, per_step),
        grid_spec=pltpu.PrefetchScalarGridSpec(
            num_scalar_prefetch=1,
            grid=(steps,),
            in_specs=[
                pl.BlockSpec(memory_space=pltpu.SMEM),
                pl.BlockSpec((1, per_step, LONG), lambda i, o: (i, 0, 0)),
                token_spec,
            ]
            + proj_specs * sets,
            out_specs=[token_spec]
            + proj_specs
            + [
                pl.BlockSpec((1, per_step, 3 * SHORT, LONG), lambda i, o: (i, 0, 0, 0)),
                pl.BlockSpec((1, per_step, LONG), lambda i, o: (i, 0, 0)),
            ],
            scratch_shapes=[
                pltpu.VMEM((per_step, 3, rows + GROUP, LONG), F32),
                pltpu.VMEM((per_step, rows + GROUP, LONG), BF16),
                pltpu.VMEM((per_step, rows + GROUP, LONG), BF16),
                pltpu.VMEM((per_step, 3, rows + GROUP, LONG), F32),
                pltpu.VMEM((per_step, 3, rows, LONG), BF16),
            ],
        ),
        out_shape=[jax.ShapeDtypeStruct((blocks, channels, LONG), BF16)]
        + [jax.ShapeDtypeStruct(x.shape, BF16) for x in proj_sets[0]]
        + [
            jax.ShapeDtypeStruct((steps, per_step, 3 * SHORT, LONG), F32),
            jax.ShapeDtypeStruct((steps, per_step, LONG), F32),
        ],
        compiler_params=pltpu.CompilerParams(vmem_limit_bytes=VMEM),
        cost_estimate=pl.CostEstimate(
            flops=5 * 2 * channels * blocks * LONG * LONG * 10,
            bytes_accessed=channels * blocks * LONG * 2 * (3 * sets + 5),
            transcendentals=0,
        ),
    )(order, short_kernel, long_kernel.reshape(steps, per_step, LONG), g, *[x for s in proj_sets for x in s])
    mixed, d_proj, gs, gl = outs[0], outs[1 : 1 + count], outs[1 + count], outs[2 + count]
    grad_short = jnp.sum(gs, axis=-1).reshape(groups, 3, SHORT).transpose(1, 0, 2)
    return mixed, d_proj, grad_short, gl.reshape(groups, LONG)


def restack_body(t_ref, *refs):
    w_refs, out_ref, sems = refs[:3], refs[3], refs[4]
    channels = w_refs[0].shape[1]
    copies = []
    for side in range(2):
        block = t_ref[0] if side == 0 else 1 - t_ref[0]
        for i in range(3):
            at = 3 * side + i
            rows = pl.ds(at * channels, channels)
            copies.append(pltpu.make_async_copy(w_refs[i].at[block], out_ref.at[rows], sems.at[at]))
    for copy in copies:
        copy.start()
    for copy in copies:
        copy.wait()


def restack(t, weights):
    _, channels, width = weights[0].shape
    return pl.pallas_call(
        restack_body,
        in_specs=[pl.BlockSpec(memory_space=pltpu.SMEM)] + [pl.BlockSpec(memory_space=pl.ANY)] * 3,
        out_specs=pl.BlockSpec(memory_space=pl.ANY),
        out_shape=jax.ShapeDtypeStruct((6 * channels, width), BF16),
        scratch_shapes=[pltpu.SemaphoreType.DMA((6,))],
        compiler_params=pltpu.CompilerParams(vmem_limit_bytes=VMEM),
        cost_estimate=pl.CostEstimate(flops=0, bytes_accessed=24 * channels * width, transcendentals=0),
    )(t.reshape(1), *weights)


def project_body(pieces, extras, *refs):
    x_refs, w_ref = refs[:pieces], refs[pieces]
    far_ref, near_ref, x_s, sems = refs[pieces + 1 + extras :]
    step, steps = pl.program_id(0), pl.num_programs(0)

    @pl.when(step == 0)
    def _():
        copies, at = [], 0
        for n, x in enumerate(x_refs):
            copies.append(pltpu.make_async_copy(x, x_s.at[pl.ds(at, x.shape[0])], sems.at[n]))
            at += x.shape[0]
        for copy in copies:
            copy.start()
        for copy in copies:
            copy.wait()

    got = dot(w_ref[...], x_s[...], ((1,), (1,))).astype(BF16)

    @pl.when(step < steps // 2)
    def _():
        far_ref[...] = got

    @pl.when(step >= steps // 2)
    def _():
        near_ref[...] = got


def project_kernel(flat, pieces, extras):
    rows, width = flat.shape
    tokens = sum(x.shape[0] for x in pieces)
    tile = rows // 4
    half = jax.ShapeDtypeStruct((rows // 2, tokens), BF16)
    return pl.pallas_call(
        functools.partial(project_body, len(pieces), len(extras)),
        grid=(4,),
        in_specs=[pl.BlockSpec(memory_space=pl.ANY)] * len(pieces)
        + [pl.BlockSpec((tile, width), lambda i: ((i + 2) % 4, 0))]
        + [pl.BlockSpec(memory_space=pl.ANY)] * len(extras),
        out_specs=[
            pl.BlockSpec((tile, tokens), lambda i: (jnp.minimum(i, 1), 0)),
            pl.BlockSpec((tile, tokens), lambda i: (jnp.maximum(i - 2, 0), 0)),
        ],
        out_shape=[half, half],
        scratch_shapes=[pltpu.VMEM((tokens, width), BF16), pltpu.SemaphoreType.DMA((len(pieces),))],
        compiler_params=pltpu.CompilerParams(vmem_limit_bytes=VMEM_DOT),
        cost_estimate=pl.CostEstimate(
            flops=2 * rows * width * tokens,
            bytes_accessed=2 * (rows * width + tokens * width + rows * tokens),
            transcendentals=0,
        ),
    )(*pieces, flat, *extras)


def unproject_body(extras, near_ref, far_ref, w_ref, *refs):
    keep_ref, give_ref, d_s = refs[extras:]
    stay = near_ref.shape[0]

    @pl.when(pl.program_id(0) == 0)
    def _():
        d_s[:, 0:stay] = near_ref[...].T
        d_s[:, stay:] = far_ref[...].T

    got = dot(d_s[...], w_ref[...], ((1,), (0,)))
    half = got.shape[0] // 2
    keep_ref[...] = got[:half].astype(BF16)
    give_ref[...] = got[half:].astype(BF16)


def unproject_kernel(flat, near, far, extras):
    rows, width = flat.shape
    tokens = near.shape[1]
    tile = min(512, width)
    half = jax.ShapeDtypeStruct((tokens // 2, width), BF16)
    return pl.pallas_call(
        functools.partial(unproject_body, len(extras)),
        grid=(width // tile,),
        in_specs=[
            pl.BlockSpec((rows // 2, tokens), lambda i: (0, 0)),
            pl.BlockSpec((rows // 2, tokens), lambda i: (0, 0)),
            pl.BlockSpec((rows, tile), lambda i: (0, i)),
        ]
        + [pl.BlockSpec(memory_space=pl.ANY)] * len(extras),
        out_specs=[pl.BlockSpec((tokens // 2, tile), lambda i: (0, i))] * 2,
        out_shape=[half, half],
        scratch_shapes=[pltpu.VMEM((tokens, rows), BF16)],
        compiler_params=pltpu.CompilerParams(vmem_limit_bytes=VMEM_DOT),
        cost_estimate=pl.CostEstimate(
            flops=2 * rows * width * tokens,
            bytes_accessed=2 * (rows * width + tokens * width + rows * tokens),
            transcendentals=0,
        ),
    )(near, far, flat, *extras)


def on_device(ring, n_tp, tokens_in, w_query, w_key, w_value, short_taps, long_taps, grad_out):
    chips = len(ring)
    half = chips // 2
    n_ctx = 2 * chips
    held, width = tokens_in.shape
    channels = w_query.shape[1]
    weights = (w_query, w_key, w_value)

    def pairs(hop):
        return [(2 * ring[j] + k, 2 * ring[(j + hop) % chips] + k) for j in range(chips) for k in range(2)]

    ahead, behind = pairs(1), pairs(-1)
    mates = [(d, d ^ 1) for d in range(n_ctx)]

    def onward(x):
        return lax.ppermute(x, "ctx", ahead)

    def back(x):
        return lax.ppermute(x, "ctx", behind)

    def swap(x):
        return lax.ppermute(x, "ctx", mates)

    def across(x):
        return lax.ppermute(x, "tp", [(0, 1), (1, 0)])

    me = lax.axis_index("ctx")
    place_of = np.argsort(np.array(ring))
    place = jnp.asarray(place_of, jnp.int32)[me // 2]

    def block_at(hop, other):
        chip = jnp.asarray(ring, jnp.int32)[(place + hop + chips) % chips]
        return 2 * chip + (me % 2 + other) % 2

    lists = [[(0, 0), (0, 1)]]
    lists += [[(-s, 0), (s, 0), (-s, 1), (s, 1)] for s in range(1, half)]
    lists += [[(half, 0), (half, 1)]]
    order = jnp.stack([block_at(*item) for chunk in lists for item in chunk]).astype(jnp.int32)

    stay = 3 * channels
    if n_tp == 2:
        flat = restack(lax.axis_index("tp").astype(jnp.int32), weights)
    else:
        flat = jnp.stack(weights).reshape(-1, width)

    def project(pieces, *extras):
        if n_tp == 2:
            far, near = project_kernel(flat, pieces, extras)
            return [y.reshape(3, channels, -1) for y in (near, across(far))]
        y = dot(flat, jnp.concatenate(pieces, axis=0), ((1,), (1,))).astype(BF16).reshape(3, n_tp, channels, -1)
        return [lax.psum_scatter(y, "tp", scatter_dimension=1, tiled=True).reshape(3, channels, -1)]

    def unproject(d, *extras):
        if n_tp == 2:
            return unproject_kernel(flat, *d, extras)
        y = dot(d[0], flat, ((0,), (0,))).astype(BF16)
        return y[: y.shape[0] // 2], y[y.shape[0] // 2 :]

    def meet(d):
        if n_tp == 2:
            d = d.reshape(stay, -1)
            return [d, across(d)]
        d = lax.all_gather(d.reshape(3, 1, channels, -1), "tp", axis=1, tiled=True)
        return [d.reshape(-1, d.shape[-1])]

    incoming = lax.all_to_all(
        grad_out.reshape(n_ctx, channels, held), "ctx", split_axis=0, concat_axis=0, tiled=True
    )

    cut = held // 2
    projected = []
    right, left = onward(tokens_in), back(tokens_in)
    projected.append(project([tokens_in, swap(tokens_in)]))
    for s in range(1, half + 1):
        late = [projected[-1][-1]] if s < half else [projected[-1][0], projected[-2][-1]]
        if s < half:
            right, left, _ = lax.optimization_barrier((right, left, projected[-1][0]))
        if s < half - 1:
            moving = onward(right), back(left)
        elif s < half:
            moving = onward(right[:cut]), back(left[cut:])
        projected.append(project([right, left, swap(right), swap(left)], *late))
        right, left = moving

    mixed, d_proj, grad_short, grad_long = mix(
        order,
        short_taps.reshape(3, -1, SHORT),
        long_taps.reshape(-1, LONG),
        incoming,
        [list(s) for s in zip(*projected)],
    )

    met = {}
    for s in range(half, -1, -1):
        d = d_proj[s]
        if s + 2 in met:
            d, met[s + 2][-1] = lax.optimization_barrier((d, met[s + 2][-1]))
        met[s] = meet(d)
    mixed_out = lax.all_to_all(mixed, "ctx", split_axis=0, concat_axis=0, tiled=True).reshape(-1, held)
    keep, give = unproject(met[half])
    total = (keep.astype(F32) + swap(give).astype(F32)).astype(BF16)
    from_behind = jnp.pad(onward(total[:cut]), ((0, held - cut), (0, 0)))
    from_ahead = jnp.pad(back(total[cut:]), ((cut, 0), (0, 0)))
    before = [keep]
    for s in range(half - 1, 0, -1):
        keep, give = unproject(met[s], *before)
        give = swap(give)
        fro = (keep[:held].astype(F32) + give[:held].astype(F32) + from_ahead.astype(F32)).astype(BF16)
        to = (keep[held:].astype(F32) + give[held:].astype(F32) + from_behind.astype(F32)).astype(BF16)
        from_behind, from_ahead = onward(to), back(fro)
        before = [keep]
    keep, give = unproject(met[0], *before)
    total = keep.astype(F32) + swap(give).astype(F32)
    grad_tokens = (total + from_behind.astype(F32) + from_ahead.astype(F32)).astype(BF16)
    return (
        mixed_out,
        grad_tokens,
        grad_short.reshape(3, 1, -1, SHORT),
        grad_long.reshape(1, -1, LONG),
    )


def solution(mesh):
    placed = (
        P("ctx", "tp"),
        P(None, "ctx", "tp"),
        P(None, "ctx", "tp"),
        P(None, "ctx", "tp"),
        P(None, "tp", "ctx", None),
        P("tp", "ctx", None),
        P("tp", "ctx"),
    )
    return jax.shard_map(
        functools.partial(on_device, ring_of(mesh), mesh.shape["tp"]),
        mesh=mesh,
        in_specs=placed,
        out_specs=(
            P("tp", "ctx"),
            P("ctx", "tp"),
            P(None, "tp", "ctx", None),
            P("tp", "ctx", None),
        ),
        check_vma=False,
    )
```

profile of v0, /device:TPU:1, one launch (start us, length us, event | category | flops | bytes accessed | tf_op | source)
XLA Modules:
  0.0 718.1 jit_solution(4630561962757465271)
XLA Ops:
  0.8 2.7 collective-permute-start.1
  3.5 382.3 %shard_map.255.refs_2_.refs_4_.w_ref = bf16[1536,4096]{1,0:T(8,128)(2,1)} custom-call(s32[1]{0:T(128)} %bitcast.35.t_ref, bf16[2,256,4096]{2,1,0:T(8,128)(2,1)} %refs_0_.2, bf16[2,256,4096]{2,1,0:T(8,128)(2,1)} %refs_1_.1, bf16[2,256,4096]{2,1,0:T(8,128)(2,1)} %refs_2_.1), custom_call_target="tpu_custom_call" | custom-call | bytes 25165824 | tf_op jit(solution)/shard_map/pallas_call | solution.py:206
  385.9 4.6 copy-done
  390.4 4.3 shard_map.256
  395.4 1.7 collective-permute-start.6
  397.0 1.4 collective-permute-start.5
  398.4 8.5 %collective-permute-done.5 = bf16[768,256]{1,0:T(8,128)(2,1)S(1)} collective-permute-done((bf16[768,256]{1,0:T(8,128)(2,1)S(1)}, bf16[768,256]{1,0:T(8,128)(2,1)S(1)}, u32[]{:S(2)}, u32[]{:S(2)}) %collective-permute-start.5) | collective-permute-done | bytes 393248 | tf_op jit(solution)/shard_map/ppermute | solution.py:335
  407.0 7.8 %shard_map.257 = (bf16[768,512]{1,0:T(8,128)(2,1)S(1)}, bf16[768,512]{1,0:T(8,128)(2,1)S(1)}) custom-call(bf16[128,4096]{1,0:T(8,128)(2,1)S(1)} %collective-permute-done.1.refs_0_, bf16[128,4096]{1,0:T(8,128)(2,1)S(1)} %collective-permute-done.2.refs_1_, bf16[128,4096]{1,0:T(8,128)(2,1)S(1)} %collective-permute-done.3.refs_2_, ...), custom_call_target="tpu_custom_call" | custom-call | flops 6442450944 | bytes 18350080 | tf_op jit(solution)/shard_map/pallas_call | solution.py:249
  415.7 4.3 collective-permute-done.6.refs_0_
  421.0 1.6 collective-permute-start.8
  423.8 1.3 collective-permute-start.11
  425.3 16.0 %collective-permute-done.10 = bf16[768,512]{1,0:T(8,128)(2,1)S(1)} collective-permute-done((bf16[768,512]{1,0:T(8,128)(2,1)S(1)}, bf16[768,512]{1,0:T(8,128)(2,1)S(1)}, u32[]{:S(2)}, u32[]{:S(2)}) %collective-permute-start.10) | collective-permute-done | bytes 786464 | tf_op jit(solution)/shard_map/ppermute | solution.py:335
  441.3 7.8 %shard_map.258 = (bf16[768,512]{1,0:T(8,128)(2,1)S(1)}, bf16[768,512]{1,0:T(8,128)(2,1)S(1)}) custom-call(bf16[128,4096]{1,0:T(8,128)(2,1)S(1)} %collective-permute-done.6.refs_0_, bf16[128,4096]{1,0:T(8,128)(2,1)S(1)} %collective-permute-done.7.refs_1_, bf16[128,4096]{1,0:T(8,128)(2,1)S(1)} %collective-permute-done.8.refs_2_, ...), custom_call_target="tpu_custom_call" | custom-call | flops 6442450944 | bytes 18350080 | tf_op jit(solution)/shard_map/pallas_call | solution.py:249
  450.1 1.3 collective-permute-start.13
  452.6 5.5 all-to-all-start
  458.2 1.4 collective-permute-start.16
  461.0 26.0 %collective-permute-done.16.refs_0_ = bf16[64,4096]{1,0:T(8,128)(2,1)S(1)} collective-permute-done((bf16[64,4096]{1,0:T(8,128)(2,1)S(1)}, bf16[64,4096]{1,0:T(8,128)(2,1)S(1)}, u32[]{:S(2)}, u32[]{:S(2)}) %collective-permute-start.16) | collective-permute-done | bytes 524320 | tf_op jit(solution)/shard_map/ppermute | solution.py:326
  489.5 4.9 copy-done.1
  494.4 9.4 %shard_map.259 = (bf16[768,512]{1,0:T(8,128)(2,1)S(1)}, bf16[768,512]{1,0:T(8,128)(2,1)S(1)}) custom-call(bf16[128,4096]{1,0:T(8,128)(2,1)S(1)} %collective-permute-done.11.refs_0_, bf16[128,4096]{1,0:T(8,128)(2,1)} %collective-permute-done.12.refs_1_, bf16[128,4096]{1,0:T(8,128)(2,1)} %collective-permute-done.13.refs_2_, ...), custom_call_target="tpu_custom_call" | custom-call | flops 6442450944 | bytes 18350080 | tf_op jit(solution)/shard_map/pallas_call | solution.py:249
  504.1 4.4 shard_map.260
  523.5 8.0 %collective-permute-done.21 = bf16[768,256]{1,0:T(8,128)(2,1)S(1)} collective-permute-done((bf16[768,256]{1,0:T(8,128)(2,1)S(1)}, bf16[768,256]{1,0:T(8,128)(2,1)S(1)}, u32[]{:S(2)}, u32[]{:S(2)}) %collective-permute-start.21) | collective-permute-done | bytes 393248 | tf_op jit(solution)/shard_map/ppermute | solution.py:335
  532.2 19.5 %shard_map.261 = (bf16[16,256,128]{2,1,0:T(8,128)(2,1)}, bf16[3,256,256]{2,1,0:T(8,128)(2,1)}, bf16[3,256,512]{2,1,0:T(8,128)(2,1)}, bf16[3,256,512]{2,1,0:T(8,1...) custom-call(s32[16]{0:T(128)} %stack.67.order, ...), custom_call_target="tpu_custom_call" | custom-call | flops 6710886400 | bytes 11534336 | tf_op jit(solution)/shard_map/pallas_call | solution.py:145
  552.0 1.2 collective-permute-start.25
  553.3 8.6 %collective-permute-done.22.far_ref = bf16[768,256]{1,0:T(8,128)(2,1)S(1)} collective-permute-done((bf16[768,256]{1,0:T(8,128)(2,1)}, bf16[768,256]{1,0:T(8,128)(2,1)S(1)}, u32[]{:S(2)}, u32[]{:S(2)}) %collective-permute-start.22) | collective-permute-done | bytes 393248 | tf_op jit(solution)/shard_map/ppermute | solution.py:335
  561.9 4.6 copy-done.2
  567.5 6.0 shard_map.262
  573.5 3.0 collective-permute-start.31
  576.7 2.0 collective-permute-done.25.far_ref
  578.8 9.5 %shard_map.263 = (bf16[256,4096]{1,0:T(8,128)(2,1)S(1)}, bf16[256,4096]{1,0:T(8,128)(2,1)S(1)}) custom-call(bf16[768,512]{1,0:T(8,128)(2,1)S(1)} %bitcast.74, bf16[768,512]{1,0:T(8,128)(2,1)S(1)} %collective-permute-done.25.far_ref, bf16[1536,4096]{1,0:T(8,128)(2,1)S(1)} %copy-done.2, bf16[128,4096]{1,0:T(8,128)(2,1)S(1)} %get-tuple-element.72.refs_0_), custom_call_target="tpu_custom_call" | custom-call | flops 6442450944 | bytes 18350080 | tf_op jit(solution)/shard_map/pallas_call | solution.py:290
  588.3 2.5 collective-permute-start.30
  590.8 5.4 collective-permute-done.23.far_ref
  596.5 6.9 collective-permute-start.32
  603.5 9.5 %shard_map.264 = (bf16[256,4096]{1,0:T(8,128)(2,1)S(1)}, bf16[256,4096]{1,0:T(8,128)(2,1)S(1)}) custom-call(bf16[768,512]{1,0:T(8,128)(2,1)S(1)} %bitcast.72, bf16[768,512]{1,0:T(8,128)(2,1)S(1)} %collective-permute-done.23.far_ref, bf16[1536,4096]{1,0:T(8,128)(2,1)S(1)} %copy-done.2, bf16[256,4096]{1,0:T(8,128)(2,1)S(1)} %get-tuple-element.73.refs_0_), custom_call_target="tpu_custom_call" | custom-call | flops 6442450944 | bytes 18350080 | tf_op jit(solution)/shard_map/pallas_call | solution.py:290
  613.0 1.5 collective-permute-start.29
  617.9 15.7 %collective-permute-done.26.far_ref = bf16[768,512]{1,0:T(8,128)(2,1)S(1)} collective-permute-done((bf16[768,512]{1,0:T(8,128)(2,1)S(1)}, bf16[768,512]{1,0:T(8,128)(2,1)S(1)}, u32[]{:S(2)}, u32[]{:S(2)}) %collective-permute-start.26) | collective-permute-done | bytes 786464 | tf_op jit(solution)/shard_map/ppermute | solution.py:335
  633.6 10.2 %shard_map.265 = (bf16[256,4096]{1,0:T(8,128)(2,1)S(1)}, bf16[256,4096]{1,0:T(8,128)(2,1)}) custom-call(bf16[768,512]{1,0:T(8,128)(2,1)S(1)} %bitcast.70, bf16[768,512]{1,0:T(8,128)(2,1)S(1)} %collective-permute-done.26.far_ref, bf16[1536,4096]{1,0:T(8,128)(2,1)S(1)} %bitcast.57, bf16[256,4096]{1,0:T(8,128)(2,1)S(1)} %get-tuple-element.74.refs_0_), custom_call_target="tpu_custom_call" | custom-call | flops 6442450944 | bytes 18350080 | tf_op jit(solution)/shard_map/pallas_call | solution.py:290
  644.7 2.5 add_convert_fusion.5
  647.2 1.7 collective-permute-start.34
  649.2 4.8 all-to-all-start.1
  654.0 5.4 collective-permute-done.24.far_ref
  660.2 4.6 copy-done.3
  665.8 6.6 shard_map.266
  674.2 4.6 add_convert_fusion.4
  678.7 1.5 collective-permute-start.35
  681.1 11.9 %all-to-all-done.1 = bf16[16,256,128]{2,1,0:T(8,128)(2,1)} async-done(((bf16[16,256,128]{2,1,0:T(8,128)(2,1)}), bf16[16,256,128]{2,1,0:T(8,128)(2,1)}, u32[]{:S(2)}, u32[]{:S(2)}) %all-to-all-start.1) | async-done | bytes 1048608 | tf_op jit(solution)/shard_map/all_to_all | solution.py:409
  693.0 19.9 %collective-permute-done.39 = bf16[128,4096]{1,0:T(8,128)(2,1)S(1)} collective-permute-done((bf16[128,4096]{1,0:T(8,128)(2,1)}, bf16[128,4096]{1,0:T(8,128)(2,1)S(1)}, u32[]{:S(2)}, u32[]{:S(2)}) %collective-permute-start.39) | collective-permute-done | bytes 1048608 | tf_op jit(solution)/shard_map/ppermute | solution.py:329
  712.9 2.9 add_convert_fusion
  715.8 2.3 copy.36
  (122 shorter events, 26.6 us)
Async XLA Ops:
  0.6 385.2 %collective-permute-start = (bf16[128,4096]{1,0:T(8,128)(2,1)}, bf16[128,4096]{1,0:T(8,128)(2,1)S(1)}, u32[]{:S(2)}, u32[]{:S(2)}) collective-permute-start(bf16[128,4096]{1,0:T(8,128)(2,1)} %refs_0_.3), channel_id=1, source_target_pairs={{0,2},{2,0},{4,6},{6,4},{8,10},{10,8},{12,14},{14,12},{16,18},{18,... | collective-permute-start | bytes 3145736 | tf_op jit(solution)/shard_map/ppermute | solution.py:332
  0.8 394.0 %collective-permute-start.1 = (bf16[128,4096]{1,0:T(8,128)(2,1)}, bf16[128,4096]{1,0:T(8,128)(2,1)S(1)}, u32[]{:S(2)}, u32[]{:S(2)}) collective-permute-start(bf16[128,4096]{1,0:T(8,128)(2,1)} %refs_0_.3), channel_id=1, source_target_pairs={{0,8},{2,10},{8,16},{10,18},{16,24},{18,26},{24,28},{26,30},{28,20... | collective-permute-start | bytes 3145736 | tf_op jit(solution)/shard_map/ppermute | solution.py:326
  3.5 391.3 %collective-permute-start.2 = (bf16[128,4096]{1,0:T(8,128)(2,1)}, bf16[128,4096]{1,0:T(8,128)(2,1)S(1)}, u32[]{:S(2)}, u32[]{:S(2)}) collective-permute-start(bf16[128,4096]{1,0:T(8,128)(2,1)} %refs_0_.3), channel_id=1, source_target_pairs={{0,4},{2,6},{8,0},{10,2},{16,8},{18,10},{24,16},{26,18},{28,24},{3... | collective-permute-start | bytes 3145736 | tf_op jit(solution)/shard_map/ppermute | solution.py:329
  3.5 382.3 %copy-start.4 = (bf16[128,4096]{1,0:T(8,128)(2,1)S(1)}, bf16[128,4096]{1,0:T(8,128)(2,1)}, u32[]{:S(2)}) copy-start(bf16[128,4096]{1,0:T(8,128)(2,1)} %refs_0_.3) | copy-start | bytes 3145732
  394.8 20.0 %copy-start.15 = (bf16[768,256]{1,0:T(8,128)(2,1)}, bf16[768,256]{1,0:T(8,128)(2,1)S(1)}, u32[]{:S(2)}) copy-start(bf16[768,256]{1,0:T(8,128)(2,1)S(1)} %get-tuple-element.44) | copy-start | bytes 1179652
  394.8 12.2 %collective-permute-start.3 = (bf16[128,4096]{1,0:T(8,128)(2,1)S(1)}, bf16[128,4096]{1,0:T(8,128)(2,1)S(1)}, u32[]{:S(2)}, u32[]{:S(2)}) collective-permute-start(bf16[128,4096]{1,0:T(8,128)(2,1)S(1)} %collective-permute-done.1.refs_0_), channel_id=1, source_target_pairs={{0,2},{2,0},{4,6},{6,4},{8,10},{10,8},{12,14},{14,12},{16,18},{18,... | collective-permute-start | bytes 3145736 | tf_op jit(solution)/shard_map/ppermute | solution.py:332
  395.2 11.8 %collective-permute-start.4 = (bf16[128,4096]{1,0:T(8,128)(2,1)S(1)}, bf16[128,4096]{1,0:T(8,128)(2,1)S(1)}, u32[]{:S(2)}, u32[]{:S(2)}) collective-permute-start(bf16[128,4096]{1,0:T(8,128)(2,1)S(1)} %collective-permute-done.2.refs_1_), channel_id=1, source_target_pairs={{0,2},{2,0},{4,6},{6,4},{8,10},{10,8},{12,14},{14,12},{16,18},{18,... | collective-permute-start | bytes 3145736 | tf_op jit(solution)/shard_map/ppermute | solution.py:332
  395.4 24.6 %collective-permute-start.6 = (bf16[128,4096]{1,0:T(8,128)(2,1)S(1)}, bf16[128,4096]{1,0:T(8,128)(2,1)S(1)}, u32[]{:S(2)}, u32[]{:S(2)}) collective-permute-start(bf16[128,4096]{1,0:T(8,128)(2,1)S(1)} %collective-permute-done.1.refs_0_), channel_id=1, source_target_pairs={{0,8},{2,10},{8,16},{10,18},{16,24},{18,26},{24,28},{26,30},{28,20... | collective-permute-start | bytes 3145736 | tf_op jit(solution)/shard_map/ppermute | solution.py:326
  397.0 24.0 %collective-permute-start.7 = (bf16[128,4096]{1,0:T(8,128)(2,1)S(1)}, bf16[128,4096]{1,0:T(8,128)(2,1)S(1)}, u32[]{:S(2)}, u32[]{:S(2)}) collective-permute-start(bf16[128,4096]{1,0:T(8,128)(2,1)S(1)} %collective-permute-done.2.refs_1_), channel_id=1, source_target_pairs={{0,4},{2,6},{8,0},{10,2},{16,8},{18,10},{24,16},{26,18},{28,24},{3... | collective-permute-start | bytes 3145736 | tf_op jit(solution)/shard_map/ppermute | solution.py:329
  397.0 9.9 %collective-permute-start.5 = (bf16[768,256]{1,0:T(8,128)(2,1)S(1)}, bf16[768,256]{1,0:T(8,128)(2,1)S(1)}, u32[]{:S(2)}, u32[]{:S(2)}) collective-permute-start(bf16[768,256]{1,0:T(8,128)(2,1)S(1)} %get-tuple-element.47), channel_id=1, source_target_pairs={{0,1},{1,0},{2,3},{3,2},{4,5},{5,4},{6,7},{7,6},{8,9},{9,8},{10,11... | collective-permute-start | bytes 1179656 | tf_op jit(solution)/shard_map/ppermute | solution.py:335
  421.0 20.3 %collective-permute-start.8 = (bf16[128,4096]{1,0:T(8,128)(2,1)S(1)}, bf16[128,4096]{1,0:T(8,128)(2,1)S(1)}, u32[]{:S(2)}, u32[]{:S(2)}) collective-permute-start(bf16[128,4096]{1,0:T(8,128)(2,1)S(1)} %collective-permute-done.6.refs_0_), channel_id=1, source_target_pairs={{0,2},{2,0},{4,6},{6,4},{8,10},{10,8},{12,14},{14,12},{16,18},{18,... | collective-permute-start | bytes 3145736 | tf_op jit(solution)/shard_map/ppermute | solution.py:332
  422.6 18.7 %collective-permute-start.9 = (bf16[128,4096]{1,0:T(8,128)(2,1)S(1)}, bf16[128,4096]{1,0:T(8,128)(2,1)S(1)}, u32[]{:S(2)}, u32[]{:S(2)}) collective-permute-start(bf16[128,4096]{1,0:T(8,128)(2,1)S(1)} %collective-permute-done.7.refs_1_), channel_id=1, source_target_pairs={{0,2},{2,0},{4,6},{6,4},{8,10},{10,8},{12,14},{14,12},{16,18},{18,... | collective-permute-start | bytes 3145736 | tf_op jit(solution)/shard_map/ppermute | solution.py:332
  422.6 18.7 %collective-permute-start.10 = (bf16[768,512]{1,0:T(8,128)(2,1)S(1)}, bf16[768,512]{1,0:T(8,128)(2,1)S(1)}, u32[]{:S(2)}, u32[]{:S(2)}) collective-permute-start(bf16[768,512]{1,0:T(8,128)(2,1)S(1)} %get-tuple-element.51), channel_id=1, source_target_pairs={{0,1},{1,0},{2,3},{3,2},{4,5},{5,4},{6,7},{7,6},{8,9},{9,8},{10,11... | collective-permute-start | bytes 2359304 | tf_op jit(solution)/shard_map/ppermute | solution.py:335
  423.8 26.2 %collective-permute-start.11 = (bf16[128,4096]{1,0:T(8,128)(2,1)S(1)}, bf16[128,4096]{1,0:T(8,128)(2,1)S(1)}, u32[]{:S(2)}, u32[]{:S(2)}) collective-permute-start(bf16[128,4096]{1,0:T(8,128)(2,1)S(1)} %collective-permute-done.6.refs_0_), channel_id=1, source_target_pairs={{0,8},{2,10},{8,16},{10,18},{16,24},{18,26},{24,28},{26,30},{28,20... | collective-permute-start | bytes 3145736 | tf_op jit(solution)/shard_map/ppermute | solution.py:326
  425.1 24.9 %collective-permute-start.12 = (bf16[128,4096]{1,0:T(8,128)(2,1)S(1)}, bf16[128,4096]{1,0:T(8,128)(2,1)}, u32[]{:S(2)}, u32[]{:S(2)}) collective-permute-start(bf16[128,4096]{1,0:T(8,128)(2,1)S(1)} %collective-permute-done.7.refs_1_), channel_id=1, source_target_pairs={{0,4},{2,6},{8,0},{10,2},{16,8},{18,10},{24,16},{26,18},{28,24},{3... | collective-permute-start | bytes 3145736 | tf_op jit(solution)/shard_map/ppermute | solution.py:329
  450.1 39.4 %collective-permute-start.13 = (bf16[128,4096]{1,0:T(8,128)(2,1)S(1)}, bf16[128,4096]{1,0:T(8,128)(2,1)}, u32[]{:S(2)}, u32[]{:S(2)}) collective-permute-start(bf16[128,4096]{1,0:T(8,128)(2,1)S(1)} %collective-permute-done.11.refs_0_), channel_id=1, source_target_pairs={{0,2},{2,0},{4,6},{6,4},{8,10},{10,8},{12,14},{14,12},{16,18},{18,... | collective-permute-start | bytes 3145736 | tf_op jit(solution)/shard_map/ppermute | solution.py:332
  451.3 38.2 %collective-permute-start.14 = (bf16[128,4096]{1,0:T(8,128)(2,1)}, bf16[128,4096]{1,0:T(8,128)(2,1)}, u32[]{:S(2)}, u32[]{:S(2)}) collective-permute-start(bf16[128,4096]{1,0:T(8,128)(2,1)} %collective-permute-done.12.refs_1_), channel_id=1, source_target_pairs={{0,2},{2,0},{4,6},{6,4},{8,10},{10,8},{12,14},{14,12},{16,18},{18,... | collective-permute-start | bytes 3145736 | tf_op jit(solution)/shard_map/ppermute | solution.py:332
  451.4 38.1 %collective-permute-start.15 = (bf16[768,512]{1,0:T(8,128)(2,1)S(1)}, bf16[768,512]{1,0:T(8,128)(2,1)S(1)}, u32[]{:S(2)}, u32[]{:S(2)}) collective-permute-start(bf16[768,512]{1,0:T(8,128)(2,1)S(1)} %get-tuple-element.55), channel_id=1, source_target_pairs={{0,1},{1,0},{2,3},{3,2},{4,5},{5,4},{6,7},{7,6},{8,9},{9,8},{10,11... | collective-permute-start | bytes 2359304 | tf_op jit(solution)/shard_map/ppermute | solution.py:335
  452.6 70.9 %all-to-all-start = ((bf16[16,256,128]{2,1,0:T(8,128)(2,1)}), bf16[16,256,128]{2,1,0:T(8,128)(2,1)}, u32[]{:S(2)}, u32[]{:S(2)}) async-start(bf16[16,256,128]{2,1,0:T(8,128)(2,1)} %bitcast.81), calls=%async_computation | async-start | bytes 2097152 | tf_op jit(solution)/shard_map/all_to_all | solution.py:376
  458.2 28.8 %collective-permute-start.16 = (bf16[64,4096]{1,0:T(8,128)(2,1)S(1)}, bf16[64,4096]{1,0:T(8,128)(2,1)S(1)}, u32[]{:S(2)}, u32[]{:S(2)}) collective-permute-start(bf16[64,4096]{1,0:T(8,128)(2,1)S(1)} %slice.48), channel_id=1, source_target_pairs={{0,8},{2,10},{8,16},{10,18},{16,24},{18,26},{24,28},{26,30},{28,20... | collective-permute-start | bytes 1572872 | tf_op jit(solution)/shard_map/ppermute | solution.py:326
  460.7 27.9 %collective-permute-start.17 = (bf16[64,4096]{1,0:T(8,128)(2,1)S(1)}, bf16[64,4096]{1,0:T(8,128)(2,1)S(1)}, u32[]{:S(2)}, u32[]{:S(2)}) collective-permute-start(bf16[64,4096]{1,0:T(8,128)(2,1)S(1)} %slice.49), channel_id=1, source_target_pairs={{0,4},{2,6},{8,0},{10,2},{16,8},{18,10},{24,16},{26,18},{28,24},{3... | collective-permute-start | bytes 1572872 | tf_op jit(solution)/shard_map/ppermute | solution.py:329
  487.0 17.1 %collective-permute-start.18 = (bf16[64,4096]{1,0:T(8,128)(2,1)S(1)}, bf16[64,4096]{1,0:T(8,128)(2,1)S(1)}, u32[]{:S(2)}, u32[]{:S(2)}) collective-permute-start(bf16[64,4096]{1,0:T(8,128)(2,1)S(1)} %collective-permute-done.16.refs_0_), channel_id=1, source_target_pairs={{0,2},{2,0},{4,6},{6,4},{8,10},{10,8},{12,14},{14,12},{16,18},{18,... | collective-permute-start | bytes 1572872 | tf_op jit(solution)/shard_map/ppermute | solution.py:332
  488.6 15.5 %collective-permute-start.19 = (bf16[64,4096]{1,0:T(8,128)(2,1)S(1)}, bf16[64,4096]{1,0:T(8,128)(2,1)S(1)}, u32[]{:S(2)}, u32[]{:S(2)}) collective-permute-start(bf16[64,4096]{1,0:T(8,128)(2,1)S(1)} %collective-permute-done.17.refs_1_), channel_id=1, source_target_pairs={{0,2},{2,0},{4,6},{6,4},{8,10},{10,8},{12,14},{14,12},{16,18},{18,... | collective-permute-start | bytes 1572872 | tf_op jit(solution)/shard_map/ppermute | solution.py:332
  503.8 27.7 %collective-permute-start.20 = (bf16[768,512]{1,0:T(8,128)(2,1)S(1)}, bf16[768,512]{1,0:T(8,128)(2,1)}, u32[]{:S(2)}, u32[]{:S(2)}) collective-permute-start(bf16[768,512]{1,0:T(8,128)(2,1)S(1)} %get-tuple-element.58), channel_id=1, source_target_pairs={{0,1},{1,0},{2,3},{3,2},{4,5},{5,4},{6,7},{7,6},{8,9},{9,8},{10,11... | collective-permute-start | bytes 2359304 | tf_op jit(solution)/shard_map/ppermute | solution.py:335
  504.1 18.1 %copy-start.22 = (f32[3,1,16,3]{2,1,3,0:T(1,128)S(1)}, f32[3,1,16,3]{2,1,3,0:T(1,128)}, u32[]{:S(2)}) copy-start(f32[3,1,16,3]{2,1,3,0:T(1,128)} %param.28) | copy-start | bytes 1732
  509.3 22.2 %collective-permute-start.21 = (bf16[768,256]{1,0:T(8,128)(2,1)S(1)}, bf16[768,256]{1,0:T(8,128)(2,1)S(1)}, u32[]{:S(2)}, u32[]{:S(2)}) collective-permute-start(bf16[768,256]{1,0:T(8,128)(2,1)S(1)} %get-tuple-element.59), channel_id=1, source_target_pairs={{0,1},{1,0},{2,3},{3,2},{4,5},{5,4},{6,7},{7,6},{8,9},{9,8},{10,11... | collective-permute-start | bytes 1179656 | tf_op jit(solution)/shard_map/ppermute | solution.py:335
  551.8 10.1 %collective-permute-start.22 = (bf16[768,256]{1,0:T(8,128)(2,1)}, bf16[768,256]{1,0:T(8,128)(2,1)S(1)}, u32[]{:S(2)}, u32[]{:S(2)}) collective-permute-start(bf16[768,256]{1,0:T(8,128)(2,1)} %bitcast.63), channel_id=1, source_target_pairs={{0,1},{1,0},{2,3},{3,2},{4,5},{5,4},{6,7},{7,6},{8,9},{9,8},{10,11... | collective-permute-start | bytes 1179656 | tf_op jit(solution)/shard_map/ppermute | solution.py:335
  552.0 26.7 %collective-permute-start.25 = (bf16[768,512]{1,0:T(8,128)(2,1)}, bf16[768,512]{1,0:T(8,128)(2,1)S(1)}, u32[]{:S(2)}, u32[]{:S(2)}) collective-permute-start(bf16[768,512]{1,0:T(8,128)(2,1)} %bitcast.73), channel_id=1, source_target_pairs={{0,1},{1,0},{2,3},{3,2},{4,5},{5,4},{6,7},{7,6},{8,9},{9,8},{10,11... | collective-permute-start | bytes 2359304 | tf_op jit(solution)/shard_map/ppermute | solution.py:335
  573.5 22.7 %collective-permute-start.31 = (bf16[128,4096]{1,0:T(8,128)(2,1)S(1)}, bf16[128,4096]{1,0:T(8,128)(2,1)S(1)}, u32[]{:S(2)}, u32[]{:S(2)}) collective-permute-start(bf16[128,4096]{1,0:T(8,128)(2,1)S(1)} %get-tuple-element.81), channel_id=1, source_target_pairs={{0,2},{2,0},{4,6},{6,4},{8,10},{10,8},{12,14},{14,12},{16,18},{18,... | collective-permute-start | bytes 3145736 | tf_op jit(solution)/shard_map/ppermute | solution.py:332
  576.5 19.6 %collective-permute-start.23 = (bf16[768,512]{1,0:T(8,128)(2,1)S(1)}, bf16[768,512]{1,0:T(8,128)(2,1)S(1)}, u32[]{:S(2)}, u32[]{:S(2)}) collective-permute-start(bf16[768,512]{1,0:T(8,128)(2,1)S(1)} %bitcast.71), channel_id=1, source_target_pairs={{0,1},{1,0},{2,3},{3,2},{4,5},{5,4},{6,7},{7,6},{8,9},{9,8},{10,11... | collective-permute-start | bytes 2359304 | tf_op jit(solution)/shard_map/ppermute | solution.py:335
  588.3 27.1 %collective-permute-start.30 = (bf16[256,4096]{1,0:T(8,128)(2,1)S(1)}, bf16[256,4096]{1,0:T(8,128)(2,1)S(1)}, u32[]{:S(2)}, u32[]{:S(2)}) collective-permute-start(bf16[256,4096]{1,0:T(8,128)(2,1)S(1)} %get-tuple-element.80), channel_id=1, source_target_pairs={{0,2},{2,0},{4,6},{6,4},{8,10},{10,8},{12,14},{14,12},{16,18},{18,... | collective-permute-start | bytes 6291464 | tf_op jit(solution)/shard_map/ppermute | solution.py:332
  596.4 37.2 %slice-start = ((s8[12582912]{0:T(1024)(128)(4,1)}), s8[4194304]{0:T(1024)(128)(4,1)S(1)}, s32[]{:S(2)}) async-start(s8[12582912]{0:T(1024)(128)(4,1)} %bitcast.56), calls=%async_computation.2 | async-start | bytes 8388608
  596.5 18.3 %collective-permute-start.32 = (bf16[64,4096]{1,0:T(8,128)(2,1)S(1)}, bf16[64,4096]{1,0:T(8,128)(2,1)S(1)}, u32[]{:S(2)}, u32[]{:S(2)}) collective-permute-start(bf16[64,4096]{1,0:T(8,128)(2,1)S(1)} %get-tuple-element.98), channel_id=1, source_target_pairs={{0,8},{2,10},{8,16},{10,18},{16,24},{18,26},{24,28},{26,30},{28,20... | collective-permute-start | bytes 1572872 | tf_op jit(solution)/shard_map/ppermute | solution.py:326
  603.4 12.0 %collective-permute-start.36 = (bf16[64,4096]{1,0:T(8,128)(2,1)S(1)}, bf16[64,4096]{1,0:T(8,128)(2,1)S(1)}, u32[]{:S(2)}, u32[]{:S(2)}) collective-permute-start(bf16[64,4096]{1,0:T(8,128)(2,1)S(1)} %get-tuple-element.99), channel_id=1, source_target_pairs={{0,4},{2,6},{8,0},{10,2},{16,8},{18,10},{24,16},{26,18},{28,24},{3... | collective-permute-start | bytes 1572872 | tf_op jit(solution)/shard_map/ppermute | solution.py:329
  603.5 30.2 %slice-start.1 = ((s8[12582912]{0:T(1024)(128)(4,1)}), s8[4194304]{0:T(1024)(128)(4,1)S(1)}, s32[]{:S(2)}) async-start(s8[12582912]{0:T(1024)(128)(4,1)} %bitcast.56), calls=%async_computation.3 | async-start | bytes 8388608
  603.5 30.2 %slice-start.2 = ((s8[12582912]{0:T(1024)(128)(4,1)}), s8[4194304]{0:T(1024)(128)(4,1)S(1)}, s32[]{:S(2)}) async-start(s8[12582912]{0:T(1024)(128)(4,1)} %bitcast.56), calls=%async_computation.4 | async-start | bytes 8388608
  613.0 31.7 %collective-permute-start.29 = (bf16[256,4096]{1,0:T(8,128)(2,1)S(1)}, bf16[256,4096]{1,0:T(8,128)(2,1)S(1)}, u32[]{:S(2)}, u32[]{:S(2)}) collective-permute-start(bf16[256,4096]{1,0:T(8,128)(2,1)S(1)} %get-tuple-element.79), channel_id=1, source_target_pairs={{0,2},{2,0},{4,6},{6,4},{8,10},{10,8},{12,14},{14,12},{16,18},{18,... | collective-permute-start | bytes 6291464 | tf_op jit(solution)/shard_map/ppermute | solution.py:332
  614.5 19.1 %collective-permute-start.26 = (bf16[768,512]{1,0:T(8,128)(2,1)S(1)}, bf16[768,512]{1,0:T(8,128)(2,1)S(1)}, u32[]{:S(2)}, u32[]{:S(2)}) collective-permute-start(bf16[768,512]{1,0:T(8,128)(2,1)S(1)} %bitcast.69), channel_id=1, source_target_pairs={{0,1},{1,0},{2,3},{3,2},{4,5},{5,4},{6,7},{7,6},{8,9},{9,8},{10,11... | collective-permute-start | bytes 2359304 | tf_op jit(solution)/shard_map/ppermute | solution.py:335
  616.4 28.3 %collective-permute-start.33 = (bf16[128,4096]{1,0:T(8,128)(2,1)S(1)}, bf16[128,4096]{1,0:T(8,128)(2,1)S(1)}, u32[]{:S(2)}, u32[]{:S(2)}) collective-permute-start(bf16[128,4096]{1,0:T(8,128)(2,1)S(1)} %get-tuple-element.96), channel_id=1, source_target_pairs={{0,8},{2,10},{8,16},{10,18},{16,24},{18,26},{24,28},{26,30},{28,20... | collective-permute-start | bytes 3145736 | tf_op jit(solution)/shard_map/ppermute | solution.py:326
  617.5 27.2 %collective-permute-start.37 = (bf16[128,4096]{1,0:T(8,128)(2,1)S(1)}, bf16[128,4096]{1,0:T(8,128)(2,1)S(1)}, u32[]{:S(2)}, u32[]{:S(2)}) collective-permute-start(bf16[128,4096]{1,0:T(8,128)(2,1)S(1)} %get-tuple-element.97), channel_id=1, source_target_pairs={{0,4},{2,6},{8,0},{10,2},{16,8},{18,10},{24,16},{26,18},{28,24},{3... | collective-permute-start | bytes 3145736 | tf_op jit(solution)/shard_map/ppermute | solution.py:329
  643.8 29.6 %collective-permute-start.28 = (bf16[256,4096]{1,0:T(8,128)(2,1)}, bf16[256,4096]{1,0:T(8,128)(2,1)}, u32[]{:S(2)}, u32[]{:S(2)}) collective-permute-start(bf16[256,4096]{1,0:T(8,128)(2,1)} %get-tuple-element.78), channel_id=1, source_target_pairs={{0,2},{2,0},{4,6},{6,4},{8,10},{10,8},{12,14},{14,12},{16,18},{18,... | collective-permute-start | bytes 6291464 | tf_op jit(solution)/shard_map/ppermute | solution.py:332
  647.2 26.2 %collective-permute-start.34 = (bf16[128,4096]{1,0:T(8,128)(2,1)}, bf16[128,4096]{1,0:T(8,128)(2,1)}, u32[]{:S(2)}, u32[]{:S(2)}) collective-permute-start(bf16[128,4096]{1,0:T(8,128)(2,1)} %get-tuple-element.94), channel_id=1, source_target_pairs={{0,8},{2,10},{8,16},{10,18},{16,24},{18,26},{24,28},{26,30},{28,20... | collective-permute-start | bytes 3145736 | tf_op jit(solution)/shard_map/ppermute | solution.py:326
  648.9 25.2 %collective-permute-start.38 = (bf16[128,4096]{1,0:T(8,128)(2,1)}, bf16[128,4096]{1,0:T(8,128)(2,1)}, u32[]{:S(2)}, u32[]{:S(2)}) collective-permute-start(bf16[128,4096]{1,0:T(8,128)(2,1)} %get-tuple-element.95), channel_id=1, source_target_pairs={{0,4},{2,6},{8,0},{10,2},{16,8},{18,10},{24,16},{26,18},{28,24},{3... | collective-permute-start | bytes 3145736 | tf_op jit(solution)/shard_map/ppermute | solution.py:329
  649.0 10.5 %collective-permute-start.24 = (bf16[768,256]{1,0:T(8,128)(2,1)S(1)}, bf16[768,256]{1,0:T(8,128)(2,1)S(1)}, u32[]{:S(2)}, u32[]{:S(2)}) collective-permute-start(bf16[768,256]{1,0:T(8,128)(2,1)S(1)} %bitcast.65), channel_id=1, source_target_pairs={{0,1},{1,0},{2,3},{3,2},{4,5},{5,4},{6,7},{7,6},{8,9},{9,8},{10,11... | collective-permute-start | bytes 1179656 | tf_op jit(solution)/shard_map/ppermute | solution.py:335
  649.2 43.8 %all-to-all-start.1 = ((bf16[16,256,128]{2,1,0:T(8,128)(2,1)}), bf16[16,256,128]{2,1,0:T(8,128)(2,1)}, u32[]{:S(2)}, u32[]{:S(2)}) async-start(bf16[16,256,128]{2,1,0:T(8,128)(2,1)} %get-tuple-element.60), calls=%async_computation.1 | async-start | bytes 2097152 | tf_op jit(solution)/shard_map/all_to_all | solution.py:409
  672.4 20.6 %collective-permute-start.27 = (bf16[128,4096]{1,0:T(8,128)(2,1)}, bf16[128,4096]{1,0:T(8,128)(2,1)}, u32[]{:S(2)}, u32[]{:S(2)}) collective-permute-start(bf16[128,4096]{1,0:T(8,128)(2,1)} %get-tuple-element.77), channel_id=1, source_target_pairs={{0,2},{2,0},{4,6},{6,4},{8,10},{10,8},{12,14},{14,12},{16,18},{18,... | collective-permute-start | bytes 3145736 | tf_op jit(solution)/shard_map/ppermute | solution.py:332
  678.7 34.2 %collective-permute-start.39 = (bf16[128,4096]{1,0:T(8,128)(2,1)}, bf16[128,4096]{1,0:T(8,128)(2,1)S(1)}, u32[]{:S(2)}, u32[]{:S(2)}) collective-permute-start(bf16[128,4096]{1,0:T(8,128)(2,1)} %get-tuple-element.93), channel_id=1, source_target_pairs={{0,4},{2,6},{8,0},{10,2},{16,8},{18,10},{24,16},{26,18},{28,24},{3... | collective-permute-start | bytes 3145736 | tf_op jit(solution)/shard_map/ppermute | solution.py:329
  678.7 34.2 %collective-permute-start.35 = (bf16[128,4096]{1,0:T(8,128)(2,1)}, bf16[128,4096]{1,0:T(8,128)(2,1)S(1)}, u32[]{:S(2)}, u32[]{:S(2)}) collective-permute-start(bf16[128,4096]{1,0:T(8,128)(2,1)} %get-tuple-element.92), channel_id=1, source_target_pairs={{0,8},{2,10},{8,16},{10,18},{16,24},{18,26},{24,28},{26,30},{28,20... | collective-permute-start | bytes 3145736 | tf_op jit(solution)/shard_map/ppermute | solution.py:326
  (22 other events, 122.8 us)
where the time goes:
time: 723 us; the launch traced here: 718 us
  Pallas kernels  477 us (66%)
  waiting for transfers between devices  135 us (19%)
  starting transfers between devices  51.2 us (7%)
  local copies, waits for them, and re-layouts  31.5 us (4%)
  between operations  11.4 us (2%)
  other arithmetic  11.2 us (2%)
    pallas_call x1, Pallas kernels, restack(): pl.pallas_call(restack_body, in_specs=[pl.BlockSpec(memory_space=pltpu.SM...  382 us
    ppermute x10, waiting for transfers between devices, across(): return lax.ppermute(x, 'tp', [(0, 1), (1, 0)])  69.6 us
    pallas_call x5, Pallas kernels, unproject_kernel(): pl.pallas_call(functools.partial(unproject_body, len(extras)), grid=(widt...  41.9 us
    pallas_call x5, Pallas kernels, project_kernel(): pl.pallas_call(functools.partial(project_body, len(pieces), len(extras)),...  33.7 us
    ppermute x8, waiting for transfers between devices, onward(): return lax.ppermute(x, 'ctx', ahead)  30.3 us
    unnamed x59, local copies, waits for them, and re-layouts  28.3 us
    ppermute x8, waiting for transfers between devices, back(): return lax.ppermute(x, 'ctx', behind)  23.4 us
    pallas_call x1, Pallas kernels, mix(): pl.pallas_call(functools.partial(mix_body, count, sets, per_step), grid_s...  19.5 us
  transfers between devices with their start and end apart: 42, of which 16 were waited for; matrix products, arithmetic and copies ran while one was open for 2% of the time, Pallas kernels for 64%

commit v1 on v0

--- a/solution.py
+++ b/solution.py
@@ -14,7 +14,8 @@
 F32 = jnp.float32
 BF16 = jnp.bfloat16
 VMEM = 58 * 1024 * 1024
-VMEM_DOT = 24 * 1024 * 1024
+VMEM_DOT = 54 * 1024 * 1024
+SMALL = pl.CostEstimate(flops=1, bytes_accessed=1, transcendentals=0)
 
 
 def ring_of(mesh):
@@ -44,11 +45,12 @@
     return lax.dot_general(a, b, (dims, ((), ())), preferred_element_type=F32)
 
 
-def mix_body(count, sets, per_step, order, short_ref, long_ref, g_ref, *refs):
+def mix_body(count, sets, per_step, grouped, order, short_ref, long_ref, g_ref, *refs):
     proj_refs = [refs[s * count : (s + 1) * count] for s in range(sets)]
     refs = refs[sets * count :]
-    mixed_ref, d_refs, gs_ref, gl_ref = refs[0], refs[1 : 1 + count], refs[1 + count], refs[2 + count]
-    p_s, x_s, y_s, d_s, e_s = refs[3 + count :]
+    d_count = len(grouped)
+    mixed_ref, d_refs, gs_ref, gl_ref = refs[0], refs[1 : 1 + d_count], refs[1 + d_count], refs[2 + d_count]
+    p_s, x_s, y_s, d_s, e_s = refs[3 + d_count :]
     blocks = g_ref.shape[0]
     rows = blocks * GROUP
     step = pl.program_id(0)
@@ -62,6 +64,10 @@
 
     halves = [(a, h) for a in range(count) for h in range(proj_refs[0][a].shape[2] // LONG)]
     places = [(a, h, where) for where, (a, h) in enumerate(halves)]
+    d_places = []
+    for b, arrays in enumerate(grouped):
+        inside = [where for array in arrays for a, _, where in places if a == array]
+        d_places += [(b, h, where) for h, where in enumerate(inside)]
     lane = lax.broadcasted_iota(jnp.int32, (rows, LONG), 1)
     sub8 = lax.broadcasted_iota(jnp.int32, (8, LONG), 0)
     col = lax.broadcasted_iota(jnp.int32, (LONG, LONG), 1)
@@ -126,13 +132,13 @@
             for k, moved in enumerate((d, one, two)):
                 gs_ref[0, j, 3 * i + k : 3 * i + k + 1, :] = jnp.sum(p * moved, axis=0, keepdims=True)
             e_s[j, i] = (taps[i][0] * d + taps[i][1] * one + taps[i][2] * two).astype(BF16)
-        for a, h, where in places:
+        for a, h, where in d_places:
             at = pl.multiple_of(order[where] * GROUP, GROUP)
             for i in range(3):
                 d_refs[a][i, mine, h * LONG : (h + 1) * LONG] = e_s[j, i, pl.ds(at, GROUP), :]
 
 
-def mix(order, short_kernel, long_kernel, g, proj_sets):
+def mix(order, short_kernel, long_kernel, g, proj_sets, grouped):
     blocks, channels, _ = g.shape
     count, sets = len(proj_sets[0]), len(proj_sets)
     groups = channels // GROUP
@@ -141,9 +147,11 @@
     rows = blocks * GROUP
     high = per_step * GROUP
     proj_specs = [pl.BlockSpec((3, high, x.shape[2]), lambda i, o: (0, i, 0)) for x in proj_sets[0]]
+    d_widths = [sum(proj_sets[0][a].shape[2] for a in arrays) for arrays in grouped]
+    d_specs = [pl.BlockSpec((3, high, w), lambda i, o: (0, i, 0)) for w in d_widths]
     token_spec = pl.BlockSpec((blocks, high, LONG), lambda i, o: (0, i, 0))
     outs = pl.pallas_call(
-        functools.partial(mix_body, count, sets, per_step),
+        functools.partial(mix_body, count, sets, per_step, grouped),
         grid_spec=pltpu.PrefetchScalarGridSpec(
             num_scalar_prefetch=1,
             grid=(steps,),
@@ -154,7 +162,7 @@
             ]
             + proj_specs * sets,
             out_specs=[token_spec]
-            + proj_specs
+            + d_specs
             + [
                 pl.BlockSpec((1, per_step, 3 * SHORT, LONG), lambda i, o: (i, 0, 0, 0)),
                 pl.BlockSpec((1, per_step, LONG), lambda i, o: (i, 0, 0)),
@@ -168,55 +176,49 @@
             ],
         ),
         out_shape=[jax.ShapeDtypeStruct((blocks, channels, LONG), BF16)]
-        + [jax.ShapeDtypeStruct(x.shape, BF16) for x in proj_sets[0]]
+        + [jax.ShapeDtypeStruct((3, channels, w), BF16) for w in d_widths]
         + [
             jax.ShapeDtypeStruct((steps, per_step, 3 * SHORT, LONG), F32),
             jax.ShapeDtypeStruct((steps, per_step, LONG), F32),
         ],
         compiler_params=pltpu.CompilerParams(vmem_limit_bytes=VMEM),
-        cost_estimate=pl.CostEstimate(
-            flops=5 * 2 * channels * blocks * LONG * LONG * 10,
-            bytes_accessed=channels * blocks * LONG * 2 * (3 * sets + 5),
-            transcendentals=0,
-        ),
+        cost_estimate=SMALL,
     )(order, short_kernel, long_kernel.reshape(steps, per_step, LONG), g, *[x for s in proj_sets for x in s])
-    mixed, d_proj, gs, gl = outs[0], outs[1 : 1 + count], outs[1 + count], outs[2 + count]
+    mixed, d_proj, (gs, gl) = outs[0], outs[1:-2], outs[-2:]
     grad_short = jnp.sum(gs, axis=-1).reshape(groups, 3, SHORT).transpose(1, 0, 2)
     return mixed, d_proj, grad_short, gl.reshape(groups, LONG)
 
 
 def restack_body(t_ref, *refs):
-    w_refs, out_ref, sems = refs[:3], refs[3], refs[4]
-    channels = w_refs[0].shape[1]
-    copies = []
-    for side in range(2):
-        block = t_ref[0] if side == 0 else 1 - t_ref[0]
-        for i in range(3):
-            at = 3 * side + i
-            rows = pl.ds(at * channels, channels)
-            copies.append(pltpu.make_async_copy(w_refs[i].at[block], out_ref.at[rows], sems.at[at]))
-    for copy in copies:
-        copy.start()
-    for copy in copies:
-        copy.wait()
+    out_ref = refs[3]
+    for i in range(3):
+        out_ref[0, i] = refs[i][0]
 
 
 def restack(t, weights):
     _, channels, width = weights[0].shape
+    tile = min(128, channels)
+
+    def source(side, part, t):
+        return (jnp.where(side == 0, t[0], 1 - t[0]), part, 0)
+
     return pl.pallas_call(
         restack_body,
-        in_specs=[pl.BlockSpec(memory_space=pltpu.SMEM)] + [pl.BlockSpec(memory_space=pl.ANY)] * 3,
-        out_specs=pl.BlockSpec(memory_space=pl.ANY),
-        out_shape=jax.ShapeDtypeStruct((6 * channels, width), BF16),
-        scratch_shapes=[pltpu.SemaphoreType.DMA((6,))],
-        compiler_params=pltpu.CompilerParams(vmem_limit_bytes=VMEM),
-        cost_estimate=pl.CostEstimate(flops=0, bytes_accessed=24 * channels * width, transcendentals=0),
-    )(t.reshape(1), *weights)
-
-
-def project_body(pieces, extras, *refs):
+        grid_spec=pltpu.PrefetchScalarGridSpec(
+            num_scalar_prefetch=1,
+            grid=(2, channels // tile),
+            in_specs=[pl.BlockSpec((1, tile, width), source)] * 3,
+            out_specs=pl.BlockSpec((1, 3, tile, width), lambda side, part, t: (side, 0, part, 0)),
+        ),
+        out_shape=jax.ShapeDtypeStruct((2, 3, channels, width), BF16),
+        compiler_params=pltpu.CompilerParams(vmem_limit_bytes=VMEM_DOT),
+        cost_estimate=SMALL,
+    )(t.reshape(1), *weights).reshape(6 * channels, width)
+
+
+def project_body(pieces, *refs):
     x_refs, w_ref = refs[:pieces], refs[pieces]
-    far_ref, near_ref, x_s, sems = refs[pieces + 1 + extras :]
+    far_ref, near_ref, x_s, sems = refs[pieces + 1 :]
     step, steps = pl.program_id(0), pl.num_programs(0)
 
     @pl.when(step == 0)
@@ -241,17 +243,16 @@
         near_ref[...] = got
 
 
-def project_kernel(flat, pieces, extras):
+def project_kernel(flat, pieces):
     rows, width = flat.shape
     tokens = sum(x.shape[0] for x in pieces)
     tile = rows // 4
     half = jax.ShapeDtypeStruct((rows // 2, tokens), BF16)
-    return pl.pallas_call(
-        functools.partial(project_body, len(pieces), len(extras)),
+    far, near = pl.pallas_call(
+        functools.partial(project_body, len(pieces)),
         grid=(4,),
         in_specs=[pl.BlockSpec(memory_space=pl.ANY)] * len(pieces)
-        + [pl.BlockSpec((tile, width), lambda i: ((i + 2) % 4, 0))]
-        + [pl.BlockSpec(memory_space=pl.ANY)] * len(extras),
+        + [pl.BlockSpec((tile, width), lambda i: ((i + 2) % 4, 0))],
         out_specs=[
             pl.BlockSpec((tile, tokens), lambda i: (jnp.minimum(i, 1), 0)),
             pl.BlockSpec((tile, tokens), lambda i: (jnp.maximum(i - 2, 0), 0)),
@@ -259,16 +260,12 @@
         out_shape=[half, half],
         scratch_shapes=[pltpu.VMEM((tokens, width), BF16), pltpu.SemaphoreType.DMA((len(pieces),))],
         compiler_params=pltpu.CompilerParams(vmem_limit_bytes=VMEM_DOT),
-        cost_estimate=pl.CostEstimate(
-            flops=2 * rows * width * tokens,
-            bytes_accessed=2 * (rows * width + tokens * width + rows * tokens),
-            transcendentals=0,
-        ),
-    )(*pieces, flat, *extras)
-
-
-def unproject_body(extras, near_ref, far_ref, w_ref, *refs):
-    keep_ref, give_ref, d_s = refs[extras:]
+        cost_estimate=SMALL,
+    )(*pieces, flat)
+    return near, far
+
+
+def unproject_body(near_ref, far_ref, w_ref, keep_ref, give_ref, d_s):
     stay = near_ref.shape[0]
 
     @pl.when(pl.program_id(0) == 0)
@@ -282,30 +279,25 @@
     give_ref[...] = got[half:].astype(BF16)
 
 
-def unproject_kernel(flat, near, far, extras):
+def unproject_kernel(flat, near, far):
     rows, width = flat.shape
     tokens = near.shape[1]
     tile = min(512, width)
     half = jax.ShapeDtypeStruct((tokens // 2, width), BF16)
     return pl.pallas_call(
-        functools.partial(unproject_body, len(extras)),
+        unproject_body,
         grid=(width // tile,),
         in_specs=[
             pl.BlockSpec((rows // 2, tokens), lambda i: (0, 0)),
             pl.BlockSpec((rows // 2, tokens), lambda i: (0, 0)),
             pl.BlockSpec((rows, tile), lambda i: (0, i)),
-        ]
-        + [pl.BlockSpec(memory_space=pl.ANY)] * len(extras),
+        ],
         out_specs=[pl.BlockSpec((tokens // 2, tile), lambda i: (0, i))] * 2,
         out_shape=[half, half],
         scratch_shapes=[pltpu.VMEM((tokens, rows), BF16)],
         compiler_params=pltpu.CompilerParams(vmem_limit_bytes=VMEM_DOT),
-        cost_estimate=pl.CostEstimate(
-            flops=2 * rows * width * tokens,
-            bytes_accessed=2 * (rows * width + tokens * width + rows * tokens),
-            transcendentals=0,
-        ),
-    )(near, far, flat, *extras)
+        cost_estimate=SMALL,
+    )(near, far, flat)
 
 
 def on_device(ring, n_tp, tokens_in, w_query, w_key, w_value, short_taps, long_taps, grad_out):
@@ -331,9 +323,6 @@
     def swap(x):
         return lax.ppermute(x, "ctx", mates)
 
-    def across(x):
-        return lax.ppermute(x, "tp", [(0, 1), (1, 0)])
-
     me = lax.axis_index("ctx")
     place_of = np.argsort(np.array(ring))
     place = jnp.asarray(place_of, jnp.int32)[me // 2]
@@ -353,75 +342,79 @@
     else:
         flat = jnp.stack(weights).reshape(-1, width)
 
-    def project(pieces, *extras):
+    def project(pieces):
         if n_tp == 2:
-            far, near = project_kernel(flat, pieces, extras)
-            return [y.reshape(3, channels, -1) for y in (near, across(far))]
+            return project_kernel(flat, pieces)
         y = dot(flat, jnp.concatenate(pieces, axis=0), ((1,), (1,))).astype(BF16).reshape(3, n_tp, channels, -1)
-        return [lax.psum_scatter(y, "tp", scatter_dimension=1, tiled=True).reshape(3, channels, -1)]
-
-    def unproject(d, *extras):
+        return lax.psum_scatter(y, "tp", scatter_dimension=1, tiled=True).reshape(stay, -1), None
+
+    def across(x):
+        return None if x is None else lax.ppermute(x, "tp", [(0, 1), (1, 0)])
+
+    def meet(d):
         if n_tp == 2:
-            return unproject_kernel(flat, *d, extras)
+            return d.reshape(stay, -1), across(d.reshape(stay, -1))
+        d = lax.all_gather(d.reshape(3, 1, channels, -1), "tp", axis=1, tiled=True)
+        return (d.reshape(-1, d.shape[-1]),)
+
+    def unproject(d):
+        if n_tp == 2:
+            return unproject_kernel(flat, *d)
         y = dot(d[0], flat, ((0,), (0,))).astype(BF16)
         return y[: y.shape[0] // 2], y[y.shape[0] // 2 :]
 
-    def meet(d):
-        if n_tp == 2:
-            d = d.reshape(stay, -1)
-            return [d, across(d)]
-        d = lax.all_gather(d.reshape(3, 1, channels, -1), "tp", axis=1, tiled=True)
-        return [d.reshape(-1, d.shape[-1])]
-
-    incoming = lax.all_to_all(
-        grad_out.reshape(n_ctx, channels, held), "ctx", split_axis=0, concat_axis=0, tiled=True
-    )
+    stage = lax.optimization_barrier
 
     cut = held // 2
+    right, left = onward(tokens_in), back(tokens_in)
+    near, far = project([tokens_in, swap(tokens_in)])
+    right, left, near, far = stage((right, left, near, far))
     projected = []
-    right, left = onward(tokens_in), back(tokens_in)
-    projected.append(project([tokens_in, swap(tokens_in)]))
-    for s in range(1, half + 1):
-        late = [projected[-1][-1]] if s < half else [projected[-1][0], projected[-2][-1]]
-        if s < half:
-            right, left, _ = lax.optimization_barrier((right, left, projected[-1][0]))
-        if s < half - 1:
-            moving = onward(right), back(left)
-        elif s < half:
-            moving = onward(right[:cut]), back(left[cut:])
-        projected.append(project([right, left, swap(right), swap(left)], *late))
-        right, left = moving
+    for s in range(1, half):
+        if s == half - 1:
+            ahead_x, behind_x = onward(right[:cut]), back(left[cut:])
+            right, left, grad_out = stage((right, left, grad_out))
+            incoming = lax.all_to_all(
+                grad_out.reshape(n_ctx, channels, held), "ctx", split_axis=0, concat_axis=0, tiled=True
+            )
+        else:
+            ahead_x, behind_x = onward(right), back(left)
+        projected.append((near, across(far)))
+        near, far = project([right, left, swap(right), swap(left)])
+        right, left, near, far, projected[-1] = stage((ahead_x, behind_x, near, far, projected[-1]))
+    projected.append((near, across(far)))
+    near, far = project([right, left, swap(right), swap(left)])
+    near, far, projected[-1], incoming = stage((near, far, projected[-1], incoming))
+    projected.append((near, across(far)))
 
     mixed, d_proj, grad_short, grad_long = mix(
         order,
         short_taps.reshape(3, -1, SHORT),
         long_taps.reshape(-1, LONG),
         incoming,
-        [list(s) for s in zip(*projected)],
+        [[y.reshape(3, channels, -1) for y in side] for side in zip(*projected) if side[0] is not None],
+        [[s] for s in range(half + 1)],
     )
 
-    met = {}
-    for s in range(half, -1, -1):
-        d = d_proj[s]
-        if s + 2 in met:
-            d, met[s + 2][-1] = lax.optimization_barrier((d, met[s + 2][-1]))
-        met[s] = meet(d)
+    def add(*parts):
+        return functools.reduce(lambda a, b: a + b, [part.astype(F32) for part in parts]).astype(BF16)
+
     mixed_out = lax.all_to_all(mixed, "ctx", split_axis=0, concat_axis=0, tiled=True).reshape(-1, held)
-    keep, give = unproject(met[half])
-    total = (keep.astype(F32) + swap(give).astype(F32)).astype(BF16)
+    met, rest = stage((meet(d_proj[half]), d_proj[:half]))
+    keep, give = unproject(met)
+    total = add(keep, swap(give))
+    total, met, rest = stage((total, meet(rest[-1]), rest[:-1]))
     from_behind = jnp.pad(onward(total[:cut]), ((0, held - cut), (0, 0)))
     from_ahead = jnp.pad(back(total[cut:]), ((cut, 0), (0, 0)))
-    before = [keep]
     for s in range(half - 1, 0, -1):
-        keep, give = unproject(met[s], *before)
+        later = meet(rest[-1])
+        keep, give = unproject(met)
         give = swap(give)
-        fro = (keep[:held].astype(F32) + give[:held].astype(F32) + from_ahead.astype(F32)).astype(BF16)
-        to = (keep[held:].astype(F32) + give[held:].astype(F32) + from_behind.astype(F32)).astype(BF16)
+        fro, to = add(keep[:held], give[:held], from_ahead), add(keep[held:], give[held:], from_behind)
+        fro, to, met, rest, mixed_out = stage((fro, to, later, rest[:-1], mixed_out))
         from_behind, from_ahead = onward(to), back(fro)
-        before = [keep]
-    keep, give = unproject(met[0], *before)
-    total = keep.astype(F32) + swap(give).astype(F32)
-    grad_tokens = (total + from_behind.astype(F32) + from_ahead.astype(F32)).astype(BF16)
+    keep, give = unproject(met)
+    grad_tokens = add(keep, swap(give), from_behind, from_ahead)
     return (
         mixed_out,
         grad_tokens,

time: 723 us -> 406 us (0.56)
  Pallas kernels: 477 us -> 146 us
  waiting for transfers between devices: 135 us -> 165 us
  local copies, waits for them, and re-layouts: 31.5 us -> 13.9 us
    pallas_call x12, Pallas kernels: 477 us -> 146 us  [the longest x5 59.7 us: unproject_kernel(): pl.pallas_call(unproject_body, grid=(width // tile,), in_specs=[pl.BlockS...]
    ppermute x8, waiting for transfers between devices: 23.4 us -> 79 us  [back(): return lax.ppermute(x, 'ctx', behind)]
    ppermute x10, waiting for transfers between devices: 69.6 us -> 28.6 us  [across(): return None if x is None else lax.ppermute(x, 'tp', [(0, 1), (1, 0)])]
    ppermute x8, waiting for transfers between devices: 30.3 us -> 49.8 us  [onward(): return lax.ppermute(x, 'ctx', ahead)]
    unnamed x59 -> x73, local copies, waits for them, and re-layouts: 28.3 us -> 11.6 us
    all_to_all x1, waiting for transfers between devices: 11.9 us -> 0.01 us  [on_device(): lax.all_to_all(mixed, 'ctx', split_axis=0, concat_axis=0, tiled=True)]
  transfers between devices with their start and end apart: 42 -> 42, of which waited for: 16 -> 25; matrix products, arithmetic and copies ran while one was open for 2% -> 4% of each run, Pallas kernels for 64% -> 17%
where the time goes in v1:
time: 406 us; the launch traced here: 403 us
  waiting for transfers between devices  165 us (41%)
  Pallas kernels  146 us (36%)
  starting transfers between devices  53.4 us (13%)
  local copies, waits for them, and re-layouts  13.9 us (3%)
  other arithmetic  13.7 us (3%)
  between operations  11.4 us (3%)
    ppermute x8, waiting for transfers between devices, back(): return lax.ppermute(x, 'ctx', behind)  79 us
    pallas_call x5, Pallas kernels, unproject_kernel(): pl.pallas_call(unproject_body, grid=(width // tile,), in_specs=[pl.BlockS...  59.7 us
    pallas_call x5, Pallas kernels, project_kernel(): pl.pallas_call(functools.partial(project_body, len(pieces)), grid=(4,), i...  58 us
    ppermute x8, waiting for transfers between devices, onward(): return lax.ppermute(x, 'ctx', ahead)  49.8 us
    ppermute x10, waiting for transfers between devices, across(): return None if x is None else lax.ppermute(x, 'tp', [(0, 1), (1, 0)])  28.6 us
    pallas_call x1, Pallas kernels, mix(): pl.pallas_call(functools.partial(mix_body, count, sets, per_step, grouped...  19.5 us
    convert_element_type x5, other arithmetic, add(): functools.reduce(lambda a, b: a + b, [part.astype(F32) for part in parts])  13.6 us
    ppermute x8, starting transfers between devices, onward(): return lax.ppermute(x, 'ctx', ahead)  12.6 us
  transfers between devices with their start and end apart: 42, of which 25 were waited for; matrix products, arithmetic and copies ran while one was open for 4% of the time, Pallas kernels for 17%

profile of v1, /device:TPU:1, one launch (start us, length us, event | category | flops | bytes accessed | tf_op | source)
XLA Modules:
  0.0 403.3 jit_solution(10891206059098219560)
XLA Ops:
  0.8 2.7 collective-permute-start
  3.5 9.2 %shard_map.255 = bf16[2,3,256,4096]{3,2,1,0:T(8,128)(2,1)} custom-call(s32[1]{0:T(128)} %bitcast.34.t_ref, bf16[2,256,4096]{2,1,0:T(8,128)(2,1)} %refs_0_.2, bf16[2,256,4096]{2,1,0:T(8,128)(2,1)} %refs_1_.1, bf16[2,256,4096]{2,1,0:T(8,128)(2,1)} %refs_2_.1), custom_call_target="tpu_custom_call" | custom-call | flops 1 | bytes 1 | tf_op jit(solution)/shard_map/pallas_call | solution.py:205
  13.7 9.7 %shard_map.256 = (bf16[768,256]{1,0:T(8,128)(2,1)}, bf16[768,256]{1,0:T(8,128)(2,1)}) custom-call(bf16[128,4096]{1,0:T(8,128)(2,1)} %refs_0_.3, bf16[128,4096]{1,0:T(8,128)(2,1)} %copy-done.4, bf16[1536,4096]{1,0:T(8,128)(2,1)} %bitcast.57), custom_call_target="tpu_custom_call" | custom-call | flops 1 | bytes 1 | tf_op jit(solution)/shard_map/pallas_call | solution.py:251
  23.4 3.7 collective-permute-done.refs_0_
  29.3 1.3 collective-permute-start.3
  30.8 1.2 collective-permute-start.7
  34.1 12.9 %shard_map.257 = (bf16[768,512]{1,0:T(8,128)(2,1)}, bf16[768,512]{1,0:T(8,128)(2,1)}) custom-call(bf16[128,4096]{1,0:T(8,128)(2,1)} %copy-done.7, bf16[128,4096]{1,0:T(8,128)(2,1)} %copy-done.8, bf16[128,4096]{1,0:T(8,128)(2,1)} %copy-done.11, bf16[128,4096]{1,0:T(8,128)(2,1)} %copy-done.13, bf16[1536,4096]{1,0:T(8,128)(2,1)} %bitcast.58), custom_call_target="tpu_custom_call" | custom-call | flops 1 | bytes 1 | tf_op jit(solution)/shard_map/pallas_call | solution.py:251
  47.0 6.5 %collective-permute-done.3.refs_0_ = bf16[128,4096]{1,0:T(8,128)(2,1)S(1)} collective-permute-done((bf16[128,4096]{1,0:T(8,128)(2,1)S(1)}, bf16[128,4096]{1,0:T(8,128)(2,1)S(1)}, u32[]{:S(2)}, u32[]{:S(2)}) %collective-permute-start.3) | collective-permute-done | bytes 1048608 | tf_op jit(solution)/shard_map/ppermute | solution.py:318
  54.5 1.7 collective-permute-start.10
  56.2 1.3 collective-permute-start.8
  61.0 12.8 %shard_map.258 = (bf16[768,512]{1,0:T(8,128)(2,1)}, bf16[768,512]{1,0:T(8,128)(2,1)}) custom-call(bf16[128,4096]{1,0:T(8,128)(2,1)} %copy-done.5, bf16[128,4096]{1,0:T(8,128)(2,1)} %copy-done.6, bf16[128,4096]{1,0:T(8,128)(2,1)} %copy-done.12, bf16[128,4096]{1,0:T(8,128)(2,1)} %copy-done.14, bf16[1536,4096]{1,0:T(8,128)(2,1)} %bitcast.59), custom_call_target="tpu_custom_call" | custom-call | flops 1 | bytes 1 | tf_op jit(solution)/shard_map/pallas_call | solution.py:251
  73.8 2.0 collective-permute-done.12
  75.8 4.6 %collective-permute-done.8.refs_0_ = bf16[128,4096]{1,0:T(8,128)(2,1)S(1)} collective-permute-done((bf16[128,4096]{1,0:T(8,128)(2,1)S(1)}, bf16[128,4096]{1,0:T(8,128)(2,1)S(1)}, u32[]{:S(2)}, u32[]{:S(2)}) %collective-permute-start.8) | collective-permute-done | bytes 1048608 | tf_op jit(solution)/shard_map/ppermute | solution.py:318
  81.4 5.1 %all-to-all-start = ((bf16[16,256,128]{2,1,0:T(8,128)(2,1)}), bf16[16,256,128]{2,1,0:T(8,128)(2,1)S(1)}, u32[]{:S(2)}, u32[]{:S(2)}) async-start(bf16[16,256,128]{2,1,0:T(8,128)(2,1)} %bitcast.68), calls=%async_computation | async-start | bytes 2097152 | tf_op jit(solution)/shard_map/all_to_all | solution.py:377
  87.0 1.2 collective-permute-start.17
  88.3 1.5 collective-permute-start.13
  92.0 12.9 %shard_map.259 = (bf16[768,512]{1,0:T(8,128)(2,1)}, bf16[768,512]{1,0:T(8,128)(2,1)}) custom-call(bf16[128,4096]{1,0:T(8,128)(2,1)} %copy-done.1, bf16[128,4096]{1,0:T(8,128)(2,1)} %copy-done.2, bf16[128,4096]{1,0:T(8,128)(2,1)} %copy-done.9, bf16[128,4096]{1,0:T(8,128)(2,1)} %copy-done.10, bf16[1536,4096]{1,0:T(8,128)(2,1)} %bitcast.60), custom_call_target="tpu_custom_call" | custom-call | flops 1 | bytes 1 | tf_op jit(solution)/shard_map/pallas_call | solution.py:251
  104.9 10.3 %collective-permute-done.13.refs_0_ = bf16[64,4096]{1,0:T(8,128)(2,1)S(1)} collective-permute-done((bf16[64,4096]{1,0:T(8,128)(2,1)S(1)}, bf16[64,4096]{1,0:T(8,128)(2,1)S(1)}, u32[]{:S(2)}, u32[]{:S(2)}) %collective-permute-start.13) | collective-permute-done | bytes 524320 | tf_op jit(solution)/shard_map/ppermute | solution.py:318
  115.2 1.8 collective-permute-done.14.refs_1_
  117.0 1.3 collective-permute-start.20
  119.5 1.5 collective-permute-done.18.refs_2_
  122.6 9.7 %shard_map.260 = (bf16[768,256]{1,0:T(8,128)(2,1)}, bf16[768,256]{1,0:T(8,128)(2,1)}) custom-call(bf16[64,4096]{1,0:T(8,128)(2,1)} %copy-done.22, bf16[64,4096]{1,0:T(8,128)(2,1)} %copy-done.23, bf16[64,4096]{1,0:T(8,128)(2,1)} %copy-done.24, bf16[64,4096]{1,0:T(8,128)(2,1)} %copy-done.25, bf16[1536,4096]{1,0:T(8,128)(2,1)} %bitcast.61), custom_call_target="tpu_custom_call" | custom-call | flops 1 | bytes 1 | tf_op jit(solution)/shard_map/pallas_call | solution.py:251
  132.3 3.2 collective-permute-done.20
  135.5 1.3 collective-permute-start.21
  150.7 19.5 %shard_map.261 = (bf16[16,256,128]{2,1,0:T(8,128)(2,1)}, bf16[3,256,256]{2,1,0:T(8,128)(2,1)}, bf16[3,256,512]{2,1,0:T(8,128)(2,1)}, bf16[3,256,512]{2,1,0:T(8,1...) custom-call(s32[16]{0:T(128)} %stack.67.order, ...), custom_call_target="tpu_custom_call" | custom-call | flops 1 | bytes 1 | tf_op jit(solution)/shard_map/pallas_call | solution.py:153
  170.7 8.3 %collective-permute-done.22.far_ref = bf16[768,256]{1,0:T(8,128)(2,1)S(1)} collective-permute-done((bf16[768,256]{1,0:T(8,128)(2,1)}, bf16[768,256]{1,0:T(8,128)(2,1)S(1)}, u32[]{:S(2)}, u32[]{:S(2)}) %collective-permute-start.22) | collective-permute-done | bytes 393248 | tf_op jit(solution)/shard_map/ppermute | solution.py:352
  179.8 10.4 %shard_map.262 = (bf16[128,4096]{1,0:T(8,128)(2,1)}, bf16[128,4096]{1,0:T(8,128)(2,1)}) custom-call(bf16[768,256]{1,0:T(8,128)(2,1)} %bitcast.82, bf16[768,256]{1,0:T(8,128)(2,1)} %copy-done.28, bf16[1536,4096]{1,0:T(8,128)(2,1)} %bitcast.62), custom_call_target="tpu_custom_call" | custom-call | flops 1 | bytes 1 | tf_op jit(solution)/shard_map/pallas_call | solution.py:287
  190.1 3.0 collective-permute-start.23
  193.6 2.0 collective-permute-done.23
  195.6 1.5 add_convert_fusion.7
  197.1 15.1 %collective-permute-done.24.far_ref = bf16[768,512]{1,0:T(8,128)(2,1)S(1)} collective-permute-done((bf16[768,512]{1,0:T(8,128)(2,1)S(1)}, bf16[768,512]{1,0:T(8,128)(2,1)S(1)}, u32[]{:S(2)}, u32[]{:S(2)}) %collective-permute-start.24) | collective-permute-done | bytes 786464 | tf_op jit(solution)/shard_map/ppermute | solution.py:352
  213.1 13.0 %shard_map.263 = (bf16[256,4096]{1,0:T(8,128)(2,1)}, bf16[256,4096]{1,0:T(8,128)(2,1)}) custom-call(bf16[768,512]{1,0:T(8,128)(2,1)} %bitcast.71, bf16[768,512]{1,0:T(8,128)(2,1)} %copy-done.18, bf16[1536,4096]{1,0:T(8,128)(2,1)} %bitcast.63), custom_call_target="tpu_custom_call" | custom-call | flops 1 | bytes 1 | tf_op jit(solution)/shard_map/pallas_call | solution.py:287
  226.9 9.5 %all-to-all-start.1 = ((bf16[16,256,128]{2,1,0:T(8,128)(2,1)}), bf16[16,256,128]{2,1,0:T(8,128)(2,1)S(1)}, u32[]{:S(2)}, u32[]{:S(2)}) async-start(bf16[16,256,128]{2,1,0:T(8,128)(2,1)} %get-tuple-element.153), calls=%async_computation.1 | async-start | bytes 2097152 | tf_op jit(solution)/shard_map/all_to_all | solution.py:402
  236.5 1.4 collective-permute-start.26
  238.6 28.4 %collective-permute-done.26 = bf16[64,4096]{1,0:T(8,128)(2,1)S(1)} collective-permute-done((bf16[64,4096]{1,0:T(8,128)(2,1)S(1)}, bf16[64,4096]{1,0:T(8,128)(2,1)S(1)}, u32[]{:S(2)}, u32[]{:S(2)}) %collective-permute-start.26) | collective-permute-done | bytes 524320 | tf_op jit(solution)/shard_map/ppermute | solution.py:321
  266.9 2.4 add_convert_fusion.5
  269.4 13.0 %shard_map.264 = (bf16[256,4096]{1,0:T(8,128)(2,1)}, bf16[256,4096]{1,0:T(8,128)(2,1)}) custom-call(bf16[768,512]{1,0:T(8,128)(2,1)} %bitcast.49.near_ref, bf16[768,512]{1,0:T(8,128)(2,1)} %collective-permute-done.28.far_ref, bf16[1536,4096]{1,0:T(8,128)(2,1)} %bitcast.64), custom_call_target="tpu_custom_call" | custom-call | flops 1 | bytes 1 | tf_op jit(solution)/shard_map/pallas_call | solution.py:287
  284.5 5.7 %collective-permute-start.31 = (bf16[128,4096]{1,0:T(8,128)(2,1)S(1)}, bf16[128,4096]{1,0:T(8,128)(2,1)S(1)}, u32[]{:S(2)}, u32[]{:S(2)}) collective-permute-start(bf16[128,4096]{1,0:T(8,128)(2,1)S(1)} %get-tuple-element.159), channel_id=1, source_target_pairs={{0,8},{2,10},{8,16},{10,18},{16,24},{18,26},{24,28},{26,30},{28,20... | collective-permute-start | bytes 3145736 | tf_op jit(solution)/shard_map/ppermute | solution.py:318
  290.7 23.1 %collective-permute-done.30 = bf16[128,4096]{1,0:T(8,128)(2,1)S(1)} collective-permute-done((bf16[128,4096]{1,0:T(8,128)(2,1)S(1)}, bf16[128,4096]{1,0:T(8,128)(2,1)S(1)}, u32[]{:S(2)}, u32[]{:S(2)}) %collective-permute-start.30) | collective-permute-done | bytes 1048608 | tf_op jit(solution)/shard_map/ppermute | solution.py:321
  314.7 2.6 add_convert_fusion.3
  318.2 13.0 %shard_map.265 = (bf16[256,4096]{1,0:T(8,128)(2,1)}, bf16[256,4096]{1,0:T(8,128)(2,1)}) custom-call(bf16[768,512]{1,0:T(8,128)(2,1)} %bitcast.69, bf16[768,512]{1,0:T(8,128)(2,1)} %copy-done.17, bf16[1536,4096]{1,0:T(8,128)(2,1)} %bitcast.65), custom_call_target="tpu_custom_call" | custom-call | flops 1 | bytes 1 | tf_op jit(solution)/shard_map/pallas_call | solution.py:287
  332.0 1.5 collective-permute-start.34
  333.9 22.9 %collective-permute-done.34 = bf16[128,4096]{1,0:T(8,128)(2,1)S(1)} collective-permute-done((bf16[128,4096]{1,0:T(8,128)(2,1)S(1)}, bf16[128,4096]{1,0:T(8,128)(2,1)S(1)}, u32[]{:S(2)}, u32[]{:S(2)}) %collective-permute-start.34) | collective-permute-done | bytes 1048608 | tf_op jit(solution)/shard_map/ppermute | solution.py:321
  358.0 4.0 add_convert_fusion.1
  362.7 10.3 %shard_map.266 = (bf16[128,4096]{1,0:T(8,128)(2,1)}, bf16[128,4096]{1,0:T(8,128)(2,1)}) custom-call(bf16[768,256]{1,0:T(8,128)(2,1)} %bitcast.79, bf16[768,256]{1,0:T(8,128)(2,1)} %copy-done.27, bf16[1536,4096]{1,0:T(8,128)(2,1)} %bitcast.66), custom_call_target="tpu_custom_call" | custom-call | flops 1 | bytes 1 | tf_op jit(solution)/shard_map/pallas_call | solution.py:287
  374.1 1.5 collective-permute-start.39
  376.6 22.6 %collective-permute-done.38 = bf16[128,4096]{1,0:T(8,128)(2,1)S(1)} collective-permute-done((bf16[128,4096]{1,0:T(8,128)(2,1)}, bf16[128,4096]{1,0:T(8,128)(2,1)S(1)}, u32[]{:S(2)}, u32[]{:S(2)}) %collective-permute-start.38) | collective-permute-done | bytes 1048608 | tf_op jit(solution)/shard_map/ppermute | solution.py:318
  399.2 3.1 add_convert_fusion
  (135 shorter events, 34.8 us)
Async XLA Ops:
  0.6 12.1 %collective-permute-start.2 = (bf16[128,4096]{1,0:T(8,128)(2,1)}, bf16[128,4096]{1,0:T(8,128)(2,1)S(1)}, u32[]{:S(2)}, u32[]{:S(2)}) collective-permute-start(bf16[128,4096]{1,0:T(8,128)(2,1)} %refs_0_.3), channel_id=1, source_target_pairs={{0,2},{2,0},{4,6},{6,4},{8,10},{10,8},{12,14},{14,12},{16,18},{18,... | collective-permute-start | bytes 3145736 | tf_op jit(solution)/shard_map/ppermute | solution.py:324
  0.8 26.3 %collective-permute-start = (bf16[128,4096]{1,0:T(8,128)(2,1)}, bf16[128,4096]{1,0:T(8,128)(2,1)S(1)}, u32[]{:S(2)}, u32[]{:S(2)}) collective-permute-start(bf16[128,4096]{1,0:T(8,128)(2,1)} %refs_0_.3), channel_id=1, source_target_pairs={{0,8},{2,10},{8,16},{10,18},{16,24},{18,26},{24,28},{26,30},{28,20... | collective-permute-start | bytes 3145736 | tf_op jit(solution)/shard_map/ppermute | solution.py:318
  3.5 24.6 %collective-permute-start.1 = (bf16[128,4096]{1,0:T(8,128)(2,1)}, bf16[128,4096]{1,0:T(8,128)(2,1)S(1)}, u32[]{:S(2)}, u32[]{:S(2)}) collective-permute-start(bf16[128,4096]{1,0:T(8,128)(2,1)} %refs_0_.3), channel_id=1, source_target_pairs={{0,4},{2,6},{8,0},{10,2},{16,8},{18,10},{24,16},{26,18},{28,24},{3... | collective-permute-start | bytes 3145736 | tf_op jit(solution)/shard_map/ppermute | solution.py:321
  28.1 3.9 collective-permute-start.5
  29.3 3.8 collective-permute-start.6
  29.3 24.2 %collective-permute-start.3 = (bf16[128,4096]{1,0:T(8,128)(2,1)S(1)}, bf16[128,4096]{1,0:T(8,128)(2,1)S(1)}, u32[]{:S(2)}, u32[]{:S(2)}) collective-permute-start(bf16[128,4096]{1,0:T(8,128)(2,1)S(1)} %collective-permute-done.refs_0_), channel_id=1, source_target_pairs={{0,8},{2,10},{8,16},{10,18},{16,24},{18,26},{24,28},{26,30},{28,20... | collective-permute-start | bytes 3145736 | tf_op jit(solution)/shard_map/ppermute | solution.py:318
  30.6 23.9 %collective-permute-start.4 = (bf16[128,4096]{1,0:T(8,128)(2,1)S(1)}, bf16[128,4096]{1,0:T(8,128)(2,1)S(1)}, u32[]{:S(2)}, u32[]{:S(2)}) collective-permute-start(bf16[128,4096]{1,0:T(8,128)(2,1)S(1)} %collective-permute-done.1.refs_1_), channel_id=1, source_target_pairs={{0,4},{2,6},{8,0},{10,2},{16,8},{18,10},{24,16},{26,18},{28,24},{3... | collective-permute-start | bytes 3145736 | tf_op jit(solution)/shard_map/ppermute | solution.py:321
  30.8 16.2 %collective-permute-start.7 = (bf16[768,256]{1,0:T(8,128)(2,1)}, bf16[768,256]{1,0:T(8,128)(2,1)S(1)}, u32[]{:S(2)}, u32[]{:S(2)}) collective-permute-start(bf16[768,256]{1,0:T(8,128)(2,1)} %get-tuple-element.99), channel_id=1, source_target_pairs={{0,1},{1,0},{2,3},{3,2},{4,5},{5,4},{6,7},{7,6},{8,9},{9,8},{10,11... | collective-permute-start | bytes 1179656 | tf_op jit(solution)/shard_map/ppermute | solution.py:352
  47.0 26.8 %copy-start.29 = (bf16[768,256]{1,0:T(8,128)(2,1)}, bf16[768,256]{1,0:T(8,128)(2,1)S(1)}, u32[]{:S(2)}) copy-start(bf16[768,256]{1,0:T(8,128)(2,1)S(1)} %collective-permute-done.7) | copy-start | bytes 1179652
  54.5 4.4 %collective-permute-start.10 = (bf16[128,4096]{1,0:T(8,128)(2,1)S(1)}, bf16[128,4096]{1,0:T(8,128)(2,1)S(1)}, u32[]{:S(2)}, u32[]{:S(2)}) collective-permute-start(bf16[128,4096]{1,0:T(8,128)(2,1)S(1)} %collective-permute-done.3.refs_0_), channel_id=1, source_target_pairs={{0,2},{2,0},{4,6},{6,4},{8,10},{10,8},{12,14},{14,12},{16,18},{18,... | collective-permute-start | bytes 3145736 | tf_op jit(solution)/shard_map/ppermute | solution.py:324
  56.2 3.8 collective-permute-start.11
  56.2 24.2 %collective-permute-start.8 = (bf16[128,4096]{1,0:T(8,128)(2,1)S(1)}, bf16[128,4096]{1,0:T(8,128)(2,1)S(1)}, u32[]{:S(2)}, u32[]{:S(2)}) collective-permute-start(bf16[128,4096]{1,0:T(8,128)(2,1)S(1)} %collective-permute-done.3.refs_0_), channel_id=1, source_target_pairs={{0,8},{2,10},{8,16},{10,18},{16,24},{18,26},{24,28},{26,30},{28,20... | collective-permute-start | bytes 3145736 | tf_op jit(solution)/shard_map/ppermute | solution.py:318
  57.5 23.9 %collective-permute-start.9 = (bf16[128,4096]{1,0:T(8,128)(2,1)S(1)}, bf16[128,4096]{1,0:T(8,128)(2,1)S(1)}, u32[]{:S(2)}, u32[]{:S(2)}) collective-permute-start(bf16[128,4096]{1,0:T(8,128)(2,1)S(1)} %collective-permute-done.4.refs_1_), channel_id=1, source_target_pairs={{0,4},{2,6},{8,0},{10,2},{16,8},{18,10},{24,16},{26,18},{28,24},{3... | collective-permute-start | bytes 3145736 | tf_op jit(solution)/shard_map/ppermute | solution.py:321
  57.6 18.2 %collective-permute-start.12 = (bf16[768,512]{1,0:T(8,128)(2,1)}, bf16[768,512]{1,0:T(8,128)(2,1)S(1)}, u32[]{:S(2)}, u32[]{:S(2)}) collective-permute-start(bf16[768,512]{1,0:T(8,128)(2,1)} %get-tuple-element.105), channel_id=1, source_target_pairs={{0,1},{1,0},{2,3},{3,2},{4,5},{5,4},{6,7},{7,6},{8,9},{9,8},{10,11... | collective-permute-start | bytes 2359304 | tf_op jit(solution)/shard_map/ppermute | solution.py:352
  81.4 54.1 %all-to-all-start = ((bf16[16,256,128]{2,1,0:T(8,128)(2,1)}), bf16[16,256,128]{2,1,0:T(8,128)(2,1)S(1)}, u32[]{:S(2)}, u32[]{:S(2)}) async-start(bf16[16,256,128]{2,1,0:T(8,128)(2,1)} %bitcast.68), calls=%async_computation | async-start | bytes 2097152 | tf_op jit(solution)/shard_map/all_to_all | solution.py:377
  86.5 3.5 collective-permute-start.15
  86.8 3.9 collective-permute-start.16
  87.0 30.0 %collective-permute-start.17 = (bf16[768,512]{1,0:T(8,128)(2,1)}, bf16[768,512]{1,0:T(8,128)(2,1)S(1)}, u32[]{:S(2)}, u32[]{:S(2)}) collective-permute-start(bf16[768,512]{1,0:T(8,128)(2,1)} %get-tuple-element.113), channel_id=1, source_target_pairs={{0,1},{1,0},{2,3},{3,2},{4,5},{5,4},{6,7},{7,6},{8,9},{9,8},{10,11... | collective-permute-start | bytes 2359304 | tf_op jit(solution)/shard_map/ppermute | solution.py:352
  88.3 26.8 %collective-permute-start.13 = (bf16[64,4096]{1,0:T(8,128)(2,1)S(1)}, bf16[64,4096]{1,0:T(8,128)(2,1)S(1)}, u32[]{:S(2)}, u32[]{:S(2)}) collective-permute-start(bf16[64,4096]{1,0:T(8,128)(2,1)S(1)} %slice.48), channel_id=1, source_target_pairs={{0,8},{2,10},{8,16},{10,18},{16,24},{18,26},{24,28},{26,30},{28,20... | collective-permute-start | bytes 1572872 | tf_op jit(solution)/shard_map/ppermute | solution.py:318
  89.8 27.2 %collective-permute-start.14 = (bf16[64,4096]{1,0:T(8,128)(2,1)S(1)}, bf16[64,4096]{1,0:T(8,128)(2,1)S(1)}, u32[]{:S(2)}, u32[]{:S(2)}) collective-permute-start(bf16[64,4096]{1,0:T(8,128)(2,1)S(1)} %slice.49), channel_id=1, source_target_pairs={{0,4},{2,6},{8,0},{10,2},{16,8},{18,10},{24,16},{26,18},{28,24},{3... | collective-permute-start | bytes 1572872 | tf_op jit(solution)/shard_map/ppermute | solution.py:321
  117.0 19.8 %copy-start.34 = (s32[8]{0:T(128)S(1)}, s32[8]{0:T(128)}, u32[]{:S(2)}) copy-start(s32[8]{0:T(128)} %constant.207.clone) | copy-start | bytes 100
  117.0 25.7 %copy-start.32 = (s32[8]{0:T(128)S(1)}, s32[8]{0:T(128)}, u32[]{:S(2)}) copy-start(s32[8]{0:T(128)} %constant.208.clone) | copy-start | bytes 100
  117.0 31.6 %copy-start.33 = (f32[3,1,16,3]{2,1,3,0:T(1,128)S(1)}, f32[3,1,16,3]{2,1,3,0:T(1,128)}, u32[]{:S(2)}) copy-start(f32[3,1,16,3]{2,1,3,0:T(1,128)} %param.28) | copy-start | bytes 1732
  117.0 18.5 %collective-permute-start.20 = (bf16[768,512]{1,0:T(8,128)(2,1)}, bf16[768,512]{1,0:T(8,128)(2,1)S(1)}, u32[]{:S(2)}, u32[]{:S(2)}) collective-permute-start(bf16[768,512]{1,0:T(8,128)(2,1)} %get-tuple-element.119), channel_id=1, source_target_pairs={{0,1},{1,0},{2,3},{3,2},{4,5},{5,4},{6,7},{7,6},{8,9},{9,8},{10,11... | collective-permute-start | bytes 2359304 | tf_op jit(solution)/shard_map/ppermute | solution.py:352
  118.3 2.7 collective-permute-start.18
  119.5 2.3 collective-permute-start.19
  135.5 14.5 %collective-permute-start.21 = (bf16[768,256]{1,0:T(8,128)(2,1)}, bf16[768,256]{1,0:T(8,128)(2,1)S(1)}, u32[]{:S(2)}, u32[]{:S(2)}) collective-permute-start(bf16[768,256]{1,0:T(8,128)(2,1)} %get-tuple-element.131), channel_id=1, source_target_pairs={{0,1},{1,0},{2,3},{3,2},{4,5},{5,4},{6,7},{7,6},{8,9},{9,8},{10,11... | collective-permute-start | bytes 1179656 | tf_op jit(solution)/shard_map/ppermute | solution.py:352
  170.2 8.8 %collective-permute-start.22 = (bf16[768,256]{1,0:T(8,128)(2,1)}, bf16[768,256]{1,0:T(8,128)(2,1)S(1)}, u32[]{:S(2)}, u32[]{:S(2)}) collective-permute-start(bf16[768,256]{1,0:T(8,128)(2,1)} %bitcast.81), channel_id=1, source_target_pairs={{0,1},{1,0},{2,3},{3,2},{4,5},{5,4},{6,7},{7,6},{8,9},{9,8},{10,11... | collective-permute-start | bytes 1179656 | tf_op jit(solution)/shard_map/ppermute | solution.py:352
  190.1 5.5 %collective-permute-start.23 = (bf16[128,4096]{1,0:T(8,128)(2,1)}, bf16[128,4096]{1,0:T(8,128)(2,1)S(1)}, u32[]{:S(2)}, u32[]{:S(2)}) collective-permute-start(bf16[128,4096]{1,0:T(8,128)(2,1)} %get-tuple-element.140), channel_id=1, source_target_pairs={{0,2},{2,0},{4,6},{6,4},{8,10},{10,8},{12,14},{14,12},{16,18},{18,... | collective-permute-start | bytes 3145736 | tf_op jit(solution)/shard_map/ppermute | solution.py:324
  193.1 19.1 %collective-permute-start.24 = (bf16[768,512]{1,0:T(8,128)(2,1)S(1)}, bf16[768,512]{1,0:T(8,128)(2,1)S(1)}, u32[]{:S(2)}, u32[]{:S(2)}) collective-permute-start(bf16[768,512]{1,0:T(8,128)(2,1)S(1)} %bitcast.72), channel_id=1, source_target_pairs={{0,1},{1,0},{2,3},{3,2},{4,5},{5,4},{6,7},{7,6},{8,9},{9,8},{10,11... | collective-permute-start | bytes 2359304 | tf_op jit(solution)/shard_map/ppermute | solution.py:352
  226.1 40.9 %collective-permute-start.25 = (bf16[256,4096]{1,0:T(8,128)(2,1)}, bf16[256,4096]{1,0:T(8,128)(2,1)}, u32[]{:S(2)}, u32[]{:S(2)}) collective-permute-start(bf16[256,4096]{1,0:T(8,128)(2,1)} %get-tuple-element.148), channel_id=1, source_target_pairs={{0,2},{2,0},{4,6},{6,4},{8,10},{10,8},{12,14},{14,12},{16,18},{18,... | collective-permute-start | bytes 6291464 | tf_op jit(solution)/shard_map/ppermute | solution.py:324
  226.9 42.5 %all-to-all-start.1 = ((bf16[16,256,128]{2,1,0:T(8,128)(2,1)}), bf16[16,256,128]{2,1,0:T(8,128)(2,1)S(1)}, u32[]{:S(2)}, u32[]{:S(2)}) async-start(bf16[16,256,128]{2,1,0:T(8,128)(2,1)} %get-tuple-element.153), calls=%async_computation.1 | async-start | bytes 2097152 | tf_op jit(solution)/shard_map/all_to_all | solution.py:402
  236.5 30.5 %copy-start.3 = (bf16[256,4096]{1,0:T(8,128)(2,1)S(1)}, bf16[256,4096]{1,0:T(8,128)(2,1)}, u32[]{:S(2)}) copy-start(bf16[256,4096]{1,0:T(8,128)(2,1)} %get-tuple-element.147) | copy-start | bytes 6291460
  236.5 30.4 %collective-permute-start.26 = (bf16[64,4096]{1,0:T(8,128)(2,1)S(1)}, bf16[64,4096]{1,0:T(8,128)(2,1)S(1)}, u32[]{:S(2)}, u32[]{:S(2)}) collective-permute-start(bf16[64,4096]{1,0:T(8,128)(2,1)S(1)} %get-tuple-element.195), channel_id=1, source_target_pairs={{0,4},{2,6},{8,0},{10,2},{16,8},{18,10},{24,16},{26,18},{28,24},{3... | collective-permute-start | bytes 1572872 | tf_op jit(solution)/shard_map/ppermute | solution.py:321
  238.0 28.9 %collective-permute-start.27 = (bf16[64,4096]{1,0:T(8,128)(2,1)S(1)}, bf16[64,4096]{1,0:T(8,128)(2,1)S(1)}, u32[]{:S(2)}, u32[]{:S(2)}) collective-permute-start(bf16[64,4096]{1,0:T(8,128)(2,1)S(1)} %get-tuple-element.194), channel_id=1, source_target_pairs={{0,8},{2,10},{8,16},{10,18},{16,24},{18,26},{24,28},{26,30},{28,20... | collective-permute-start | bytes 1572872 | tf_op jit(solution)/shard_map/ppermute | solution.py:318
  238.1 31.3 %collective-permute-start.28 = (bf16[768,512]{1,0:T(8,128)(2,1)}, bf16[768,512]{1,0:T(8,128)(2,1)}, u32[]{:S(2)}, u32[]{:S(2)}) collective-permute-start(bf16[768,512]{1,0:T(8,128)(2,1)} %bitcast.49.near_ref), channel_id=1, source_target_pairs={{0,1},{1,0},{2,3},{3,2},{4,5},{5,4},{6,7},{7,6},{8,9},{9,8},{10,11... | collective-permute-start | bytes 2359304 | tf_op jit(solution)/shard_map/ppermute | solution.py:352
  269.4 20.8 %copy-start.15 = (bf16[3,256,512]{2,1,0:T(8,128)(2,1)S(1)}, bf16[3,256,512]{2,1,0:T(8,128)(2,1)}, u32[]{:S(2)}) copy-start(bf16[3,256,512]{2,1,0:T(8,128)(2,1)} %get-tuple-element.160) | copy-start | bytes 2359300
  282.4 32.3 %collective-permute-start.29 = (bf16[256,4096]{1,0:T(8,128)(2,1)}, bf16[256,4096]{1,0:T(8,128)(2,1)S(1)}, u32[]{:S(2)}, u32[]{:S(2)}) collective-permute-start(bf16[256,4096]{1,0:T(8,128)(2,1)} %get-tuple-element.157), channel_id=1, source_target_pairs={{0,2},{2,0},{4,6},{6,4},{8,10},{10,8},{12,14},{14,12},{16,18},{18,... | collective-permute-start | bytes 6291464 | tf_op jit(solution)/shard_map/ppermute | solution.py:324
  283.3 30.4 %collective-permute-start.30 = (bf16[128,4096]{1,0:T(8,128)(2,1)S(1)}, bf16[128,4096]{1,0:T(8,128)(2,1)S(1)}, u32[]{:S(2)}, u32[]{:S(2)}) collective-permute-start(bf16[128,4096]{1,0:T(8,128)(2,1)S(1)} %get-tuple-element.158), channel_id=1, source_target_pairs={{0,4},{2,6},{8,0},{10,2},{16,8},{18,10},{24,16},{26,18},{28,24},{3... | collective-permute-start | bytes 3145736 | tf_op jit(solution)/shard_map/ppermute | solution.py:321
  284.5 30.2 %collective-permute-start.31 = (bf16[128,4096]{1,0:T(8,128)(2,1)S(1)}, bf16[128,4096]{1,0:T(8,128)(2,1)S(1)}, u32[]{:S(2)}, u32[]{:S(2)}) collective-permute-start(bf16[128,4096]{1,0:T(8,128)(2,1)S(1)} %get-tuple-element.159), channel_id=1, source_target_pairs={{0,8},{2,10},{8,16},{10,18},{16,24},{18,26},{24,28},{26,30},{28,20... | collective-permute-start | bytes 3145736 | tf_op jit(solution)/shard_map/ppermute | solution.py:318
  290.2 27.1 %collective-permute-start.32 = (bf16[768,512]{1,0:T(8,128)(2,1)S(1)}, bf16[768,512]{1,0:T(8,128)(2,1)S(1)}, u32[]{:S(2)}, u32[]{:S(2)}) collective-permute-start(bf16[768,512]{1,0:T(8,128)(2,1)S(1)} %bitcast.70), channel_id=1, source_target_pairs={{0,1},{1,0},{2,3},{3,2},{4,5},{5,4},{6,7},{7,6},{8,9},{9,8},{10,11... | collective-permute-start | bytes 2359304 | tf_op jit(solution)/shard_map/ppermute | solution.py:352
  331.2 26.7 %collective-permute-start.33 = (bf16[256,4096]{1,0:T(8,128)(2,1)}, bf16[256,4096]{1,0:T(8,128)(2,1)S(1)}, u32[]{:S(2)}, u32[]{:S(2)}) collective-permute-start(bf16[256,4096]{1,0:T(8,128)(2,1)} %get-tuple-element.166), channel_id=1, source_target_pairs={{0,2},{2,0},{4,6},{6,4},{8,10},{10,8},{12,14},{14,12},{16,18},{18,... | collective-permute-start | bytes 6291464 | tf_op jit(solution)/shard_map/ppermute | solution.py:324
  332.0 24.8 %collective-permute-start.34 = (bf16[128,4096]{1,0:T(8,128)(2,1)S(1)}, bf16[128,4096]{1,0:T(8,128)(2,1)S(1)}, u32[]{:S(2)}, u32[]{:S(2)}) collective-permute-start(bf16[128,4096]{1,0:T(8,128)(2,1)S(1)} %get-tuple-element.167), channel_id=1, source_target_pairs={{0,4},{2,6},{8,0},{10,2},{16,8},{18,10},{24,16},{26,18},{28,24},{3... | collective-permute-start | bytes 3145736 | tf_op jit(solution)/shard_map/ppermute | solution.py:321
  333.5 24.5 %collective-permute-start.35 = (bf16[128,4096]{1,0:T(8,128)(2,1)S(1)}, bf16[128,4096]{1,0:T(8,128)(2,1)S(1)}, u32[]{:S(2)}, u32[]{:S(2)}) collective-permute-start(bf16[128,4096]{1,0:T(8,128)(2,1)S(1)} %get-tuple-element.168), channel_id=1, source_target_pairs={{0,8},{2,10},{8,16},{10,18},{16,24},{18,26},{24,28},{26,30},{28,20... | collective-permute-start | bytes 3145736 | tf_op jit(solution)/shard_map/ppermute | solution.py:318
  333.5 28.4 %collective-permute-start.36 = (bf16[768,256]{1,0:T(8,128)(2,1)S(1)}, bf16[768,256]{1,0:T(8,128)(2,1)S(1)}, u32[]{:S(2)}, u32[]{:S(2)}) collective-permute-start(bf16[768,256]{1,0:T(8,128)(2,1)S(1)} %bitcast.80), channel_id=1, source_target_pairs={{0,1},{1,0},{2,3},{3,2},{4,5},{5,4},{6,7},{7,6},{8,9},{9,8},{10,11... | collective-permute-start | bytes 1179656 | tf_op jit(solution)/shard_map/ppermute | solution.py:352
  373.0 3.6 collective-permute-start.37
  374.1 25.1 %collective-permute-start.38 = (bf16[128,4096]{1,0:T(8,128)(2,1)}, bf16[128,4096]{1,0:T(8,128)(2,1)S(1)}, u32[]{:S(2)}, u32[]{:S(2)}) collective-permute-start(bf16[128,4096]{1,0:T(8,128)(2,1)} %get-tuple-element.176), channel_id=1, source_target_pairs={{0,8},{2,10},{8,16},{10,18},{16,24},{18,26},{24,28},{26,30},{28,20... | collective-permute-start | bytes 3145736 | tf_op jit(solution)/shard_map/ppermute | solution.py:318
  374.1 25.1 %collective-permute-start.39 = (bf16[128,4096]{1,0:T(8,128)(2,1)}, bf16[128,4096]{1,0:T(8,128)(2,1)}, u32[]{:S(2)}, u32[]{:S(2)}) collective-permute-start(bf16[128,4096]{1,0:T(8,128)(2,1)} %get-tuple-element.177), channel_id=1, source_target_pairs={{0,4},{2,6},{8,0},{10,2},{16,8},{18,10},{24,16},{26,18},{28,24},{3... | collective-permute-start | bytes 3145736 | tf_op jit(solution)/shard_map/ppermute | solution.py:321
  (29 other events, 153.2 us)

commit v2 on v1

--- a/solution.py
+++ b/solution.py
@@ -13,8 +13,8 @@
 LONG = 128
 F32 = jnp.float32
 BF16 = jnp.bfloat16
-VMEM = 58 * 1024 * 1024
-VMEM_DOT = 54 * 1024 * 1024
+VMEM = 44 * 1024 * 1024
+VMEM_DOT = 20 * 1024 * 1024
 SMALL = pl.CostEstimate(flops=1, bytes_accessed=1, transcendentals=0)
 
 
@@ -265,7 +265,8 @@
     return near, far
 
 
-def unproject_body(near_ref, far_ref, w_ref, keep_ref, give_ref, d_s):
+def unproject_body(near_ref, far_ref, w_ref, *refs):
+    out_refs, d_s = refs[:-1], refs[-1]
     stay = near_ref.shape[0]
 
     @pl.when(pl.program_id(0) == 0)
@@ -274,16 +275,16 @@
         d_s[:, stay:] = far_ref[...].T
 
     got = dot(d_s[...], w_ref[...], ((1,), (0,)))
-    half = got.shape[0] // 2
-    keep_ref[...] = got[:half].astype(BF16)
-    give_ref[...] = got[half:].astype(BF16)
-
-
-def unproject_kernel(flat, near, far):
+    at = 0
+    for out_ref in out_refs:
+        out_ref[...] = got[at : at + out_ref.shape[0]].astype(BF16)
+        at += out_ref.shape[0]
+
+
+def unproject_kernel(flat, near, far, cuts):
     rows, width = flat.shape
     tokens = near.shape[1]
     tile = min(512, width)
-    half = jax.ShapeDtypeStruct((tokens // 2, width), BF16)
     return pl.pallas_call(
         unproject_body,
         grid=(width // tile,),
@@ -292,12 +293,45 @@
             pl.BlockSpec((rows // 2, tokens), lambda i: (0, 0)),
             pl.BlockSpec((rows, tile), lambda i: (0, i)),
         ],
-        out_specs=[pl.BlockSpec((tokens // 2, tile), lambda i: (0, i))] * 2,
-        out_shape=[half, half],
+        out_specs=[pl.BlockSpec((cut, tile), lambda i: (0, i)) for cut in cuts],
+        out_shape=[jax.ShapeDtypeStruct((cut, width), BF16) for cut in cuts],
         scratch_shapes=[pltpu.VMEM((tokens, rows), BF16)],
         compiler_params=pltpu.CompilerParams(vmem_limit_bytes=VMEM_DOT),
         cost_estimate=SMALL,
     )(near, far, flat)
+
+
+def add_body(heights, *refs):
+    out_ref = refs[-1]
+    groups, at = [], 0
+    for height in heights:
+        groups.append(refs[at : at + height])
+        at += height
+    tops = [[sum(r.shape[0] for r in group[:n]) for n in range(len(group) + 1)] for group in groups]
+    edges = sorted({edge for top in tops for edge in top} | {out_ref.shape[0]})
+    for low, high in zip(edges[:-1], edges[1:]):
+        total = None
+        for group, top in zip(groups, tops):
+            for n, ref in enumerate(group):
+                if top[n] <= low and high <= top[n + 1]:
+                    part = ref[low - top[n] : high - top[n], :].astype(F32)
+                    total = part if total is None else total + part
+        out_ref[low:high, :] = total.astype(BF16)
+
+
+def add_kernel(*groups):
+    rows, width = sum(x.shape[0] for x in groups[0]), groups[0][0].shape[1]
+    tile = min(1024, width)
+    arrays = [x for group in groups for x in group]
+    return pl.pallas_call(
+        functools.partial(add_body, [len(group) for group in groups]),
+        grid=(width // tile,),
+        in_specs=[pl.BlockSpec((x.shape[0], tile), lambda i: (0, i)) for x in arrays],
+        out_specs=pl.BlockSpec((rows, tile), lambda i: (0, i)),
+        out_shape=jax.ShapeDtypeStruct((rows, width), BF16),
+        compiler_params=pltpu.CompilerParams(vmem_limit_bytes=VMEM_DOT),
+        cost_estimate=SMALL,
+    )(*arrays)
 
 
 def on_device(ring, n_tp, tokens_in, w_query, w_key, w_value, short_taps, long_taps, grad_out):
@@ -308,33 +342,28 @@
     channels = w_query.shape[1]
     weights = (w_query, w_key, w_value)
 
-    def pairs(hop):
-        return [(2 * ring[j] + k, 2 * ring[(j + hop) % chips] + k) for j in range(chips) for k in range(2)]
-
-    ahead, behind = pairs(1), pairs(-1)
-    mates = [(d, d ^ 1) for d in range(n_ctx)]
-
-    def onward(x):
-        return lax.ppermute(x, "ctx", ahead)
-
-    def back(x):
-        return lax.ppermute(x, "ctx", behind)
+    def one_way(x, turned=False, to_mate=False):
+        hops = []
+        for j in range(chips):
+            for core in range(2):
+                chip = ring[(j + (1 if (core == 0) != turned else -1)) % chips]
+                hops.append((2 * ring[j] + core, 2 * chip + (core ^ int(to_mate))))
+        return lax.ppermute(x, "ctx", hops)
 
     def swap(x):
-        return lax.ppermute(x, "ctx", mates)
-
-    me = lax.axis_index("ctx")
-    place_of = np.argsort(np.array(ring))
-    place = jnp.asarray(place_of, jnp.int32)[me // 2]
-
-    def block_at(hop, other):
-        chip = jnp.asarray(ring, jnp.int32)[(place + hop + chips) % chips]
-        return 2 * chip + (me % 2 + other) % 2
-
-    lists = [[(0, 0), (0, 1)]]
-    lists += [[(-s, 0), (s, 0), (-s, 1), (s, 1)] for s in range(1, half)]
-    lists += [[(half, 0), (half, 1)]]
-    order = jnp.stack([block_at(*item) for chunk in lists for item in chunk]).astype(jnp.int32)
+        return lax.ppermute(x, "ctx", [(d, d ^ 1) for d in range(n_ctx)])
+
+    table = np.zeros((n_ctx, n_ctx), np.int32)
+    for device in range(n_ctx):
+        place, core = ring.index(device // 2), device % 2
+        way = -1 if core == 0 else 1
+        items = [(0, 0), (0, 1)]
+        for s in range(1, half):
+            items += [(way * s, 0), (way * s, 1), (-way * s, 1), (-way * s, 0)]
+        items += [(half, 0), (half, 1)]
+        table[device] = [2 * ring[(place + hop) % chips] + (core ^ other) for hop, other in items]
+    order = lax.dynamic_index_in_dim(jnp.asarray(table), lax.axis_index("ctx"), 0, keepdims=False)
+    short_kernel, long_kernel = short_taps.reshape(3, -1, SHORT), long_taps.reshape(-1, LONG)
 
     stay = 3 * channels
     if n_tp == 2:
@@ -357,64 +386,55 @@
         d = lax.all_gather(d.reshape(3, 1, channels, -1), "tp", axis=1, tiled=True)
         return (d.reshape(-1, d.shape[-1]),)
 
-    def unproject(d):
+    def unproject(d, *cuts):
         if n_tp == 2:
-            return unproject_kernel(flat, *d)
+            return unproject_kernel(flat, *d, cuts)
         y = dot(d[0], flat, ((0,), (0,))).astype(BF16)
-        return y[: y.shape[0] // 2], y[y.shape[0] // 2 :]
+        return jnp.split(y, np.cumsum(cuts)[:-1], axis=0)
 
     stage = lax.optimization_barrier
 
-    cut = held // 2
-    right, left = onward(tokens_in), back(tokens_in)
+    arrived = [one_way(tokens_in), one_way(tokens_in, to_mate=True, turned=True)]
     near, far = project([tokens_in, swap(tokens_in)])
-    right, left, near, far = stage((right, left, near, far))
+    arrived, near, far, order, short_kernel, long_kernel = stage((arrived, near, far, order, short_kernel, long_kernel))
+    arrived = jnp.concatenate(arrived, axis=0)
     projected = []
     for s in range(1, half):
-        if s == half - 1:
-            ahead_x, behind_x = onward(right[:cut]), back(left[cut:])
-            right, left, grad_out = stage((right, left, grad_out))
-            incoming = lax.all_to_all(
-                grad_out.reshape(n_ctx, channels, held), "ctx", split_axis=0, concat_axis=0, tiled=True
-            )
-        else:
-            ahead_x, behind_x = onward(right), back(left)
+        coming = one_way(arrived if s < half - 1 else arrived[:held])
         projected.append((near, across(far)))
-        near, far = project([right, left, swap(right), swap(left)])
-        right, left, near, far, projected[-1] = stage((ahead_x, behind_x, near, far, projected[-1]))
+        near, far = project([arrived, swap(arrived)])
+        arrived, near, far, projected[-1], grad_out = stage((coming, near, far, projected[-1], grad_out))
     projected.append((near, across(far)))
-    near, far = project([right, left, swap(right), swap(left)])
-    near, far, projected[-1], incoming = stage((near, far, projected[-1], incoming))
+    incoming = lax.all_to_all(
+        grad_out.reshape(n_ctx, channels, held), "ctx", split_axis=0, concat_axis=0, tiled=True
+    )
+    near, far = project([arrived, swap(arrived)])
     projected.append((near, across(far)))
 
     mixed, d_proj, grad_short, grad_long = mix(
         order,
-        short_taps.reshape(3, -1, SHORT),
-        long_taps.reshape(-1, LONG),
+        short_kernel,
+        long_kernel,
         incoming,
         [[y.reshape(3, channels, -1) for y in side] for side in zip(*projected) if side[0] is not None],
         [[s] for s in range(half + 1)],
     )
 
-    def add(*parts):
-        return functools.reduce(lambda a, b: a + b, [part.astype(F32) for part in parts]).astype(BF16)
-
     mixed_out = lax.all_to_all(mixed, "ctx", split_axis=0, concat_axis=0, tiled=True).reshape(-1, held)
-    met, rest = stage((meet(d_proj[half]), d_proj[:half]))
-    keep, give = unproject(met)
-    total = add(keep, swap(give))
-    total, met, rest = stage((total, meet(rest[-1]), rest[:-1]))
-    from_behind = jnp.pad(onward(total[:cut]), ((0, held - cut), (0, 0)))
-    from_ahead = jnp.pad(back(total[cut:]), ((cut, 0), (0, 0)))
+    met = meet(d_proj[half - 1])
+    keep, *give = unproject(meet(d_proj[half]), held, held // 2, held // 2)
+    total = add_kernel([keep], [swap(x) for x in give])
+    total, met, rest, mixed_out = stage((total, met, d_proj[: half - 1], mixed_out))
     for s in range(half - 1, 0, -1):
+        coming = one_way(total, turned=True)
         later = meet(rest[-1])
-        keep, give = unproject(met)
-        give = swap(give)
-        fro, to = add(keep[:held], give[:held], from_ahead), add(keep[held:], give[held:], from_behind)
-        fro, to, met, rest, mixed_out = stage((fro, to, later, rest[:-1], mixed_out))
-        from_behind, from_ahead = onward(to), back(fro)
-    keep, give = unproject(met)
-    grad_tokens = add(keep, swap(give), from_behind, from_ahead)
+        cuts = (96, 80, 80) if s == half - 1 and held == 128 else (held, held)
+        keep, *give = unproject(met, 2 * held, *cuts)
+        total = add_kernel([keep], [swap(x) for x in give], [coming])
+        total, met, rest = stage((total, later, rest[:-1]))
+    coming = [one_way(total[:held], turned=True), one_way(total[held:], turned=True, to_mate=True)]
+    keep, *give = unproject(met, held, held // 2, held // 2)
+    grad_tokens = add_kernel([keep], [swap(x) for x in give], coming[:1], coming[1:])
     return (
         mixed_out,
         grad_tokens,

time: 406 us -> 338 us (0.83)
  local copies, waits for them, and re-layouts: 13.9 us -> 59.4 us
  Pallas kernels: 146 us -> 102 us
  waiting for transfers between devices: 165 us -> 125 us
  other arithmetic: 13.7 us -> 0.12 us
  between operations: 11.4 us -> 0.96 us
  starting transfers between devices: 53.4 us -> 48.3 us
    ppermute x30 -> x26, waiting for transfers between devices: 136 us -> 63.3 us  [the longest x10 47.4 us: one_way(): return lax.ppermute(x, 'ctx', hops)]
    unnamed x73 -> x76, local copies, waits for them, and re-layouts: 11.6 us -> 55.6 us
    ppermute x10, waiting for transfers between devices: 28.6 us -> 61.8 us  [across(): return None if x is None else lax.ppermute(x, 'tp', [(0, 1), (1, 0)])]
    pallas_call x5, Pallas kernels: 58 us -> 31.9 us  [project_kernel(): pl.pallas_call(functools.partial(project_body, len(pieces)), grid=(4,), i...]
    pallas_call x5, Pallas kernels: 59.7 us -> 41.3 us  [unproject_kernel(): pl.pallas_call(unproject_body, grid=(width // tile,), in_specs=[pl.BlockS...]
    convert_element_type x5 -> x0, other arithmetic: 13.6 us -> none  [add(): functools.reduce(lambda a, b: a + b, [part.astype(F32) for part in parts])]
    pallas_call x0 -> x5, Pallas kernels: none -> 8.16 us  [add_kernel(): pl.pallas_call(functools.partial(add_body, [len(group) for group in group...]
    pallas_call x1, Pallas kernels: 9.2 us -> 1.7 us  [restack(): pl.pallas_call(restack_body, grid_spec=pltpu.PrefetchScalarGridSpec(num_s...]
  transfers between devices with their start and end apart: 42 -> 38, of which waited for: 25 -> 29; matrix products, arithmetic and copies ran while one was open for 4% -> 1% of each run, Pallas kernels for 17% -> 24%
where the time goes in v2:
time: 338 us; the launch traced here: 336 us
  waiting for transfers between devices  125 us (37%)
  Pallas kernels  102 us (30%)
  local copies, waits for them, and re-layouts  59.4 us (18%)
  starting transfers between devices  48.3 us (14%)
    ppermute x10, waiting for transfers between devices, across(): return None if x is None else lax.ppermute(x, 'tp', [(0, 1), (1, 0)])  61.8 us
    unnamed x76, local copies, waits for them, and re-layouts  55.6 us
    ppermute x10, waiting for transfers between devices, one_way(): return lax.ppermute(x, 'ctx', hops)  47.4 us
    pallas_call x5, Pallas kernels, unproject_kernel(): pl.pallas_call(unproject_body, grid=(width // tile,), in_specs=[pl.BlockS...  41.3 us
    pallas_call x5, Pallas kernels, project_kernel(): pl.pallas_call(functools.partial(project_body, len(pieces)), grid=(4,), i...  31.9 us
    pallas_call x1, Pallas kernels, mix(): pl.pallas_call(functools.partial(mix_body, count, sets, per_step, grouped...  19.2 us
    ppermute x16, waiting for transfers between devices, swap(): return lax.ppermute(x, 'ctx', [(d, d ^ 1) for d in range(n_ctx)])  15.9 us
    ppermute x16, starting transfers between devices, swap(): return lax.ppermute(x, 'ctx', [(d, d ^ 1) for d in range(n_ctx)])  11.9 us
  transfers between devices with their start and end apart: 38, of which 29 were waited for; matrix products, arithmetic and copies ran while one was open for 1% of the time, Pallas kernels for 24%

profile of v2, /device:TPU:1, one launch (start us, length us, event | category | flops | bytes accessed | tf_op | source)
XLA Modules:
  0.0 336.3 jit_solution(3347618286197120286)
XLA Ops:
  0.8 2.7 collective-permute-start.1
  3.5 2.2 copy-done.7
  5.7 2.2 copy-done.8
  7.8 2.2 copy-done.9
  10.0 1.7 shard_map.111
  11.8 4.6 %copy-done = bf16[2,3,256,4096]{3,2,1,0:T(8,128)(2,1)} copy-done((bf16[2,3,256,4096]{3,2,1,0:T(8,128)(2,1)}, bf16[2,3,256,4096]{3,2,1,0:T(8,128)(2,1)S(1)}, u32[]{:S(2)}) %copy-start) | copy-done | bytes 12582936
  17.8 4.6 %copy-done.1 = bf16[2,3,256,4096]{3,2,1,0:T(8,128)(2,1)S(1)} copy-done((bf16[2,3,256,4096]{3,2,1,0:T(8,128)(2,1)S(1)}, bf16[2,3,256,4096]{3,2,1,0:T(8,128)(2,1)}, u32[]{:S(2)}) %copy-start.1) | copy-done | bytes 12582936
  22.3 4.3 %shard_map.112 = (bf16[768,256]{1,0:T(8,128)(2,1)S(1)}, bf16[768,256]{1,0:T(8,128)(2,1)S(1)}) custom-call(bf16[128,4096]{1,0:T(8,128)(2,1)S(1)} %copy-done.10, bf16[128,4096]{1,0:T(8,128)(2,1)S(1)} %collective-permute-done.2.refs_1_, bf16[1536,4096]{1,0:T(8,128)(2,1)S(1)} %bitcast.28), custom_call_target="tpu_custom_call" | custom-call | flops 1 | bytes 1 | tf_op jit(solution)/shard_map/pallas_call | solution.py:251
  34.4 7.8 %shard_map.113 = (bf16[768,512]{1,0:T(8,128)(2,1)S(1)}, bf16[768,512]{1,0:T(8,128)(2,1)S(1)}) custom-call(bf16[256,4096]{1,0:T(8,128)(2,1)S(1)} %constant_dynamic-update-slice_fusion.refs_0_, bf16[256,4096]{1,0:T(8,128)(2,1)S(1)} %collective-permute-done.4.refs_1_, bf16[1536,4096]{1,0:T(8,128)(2,1)S(1)} %bitcast.29), custom_call_target="tpu_custom_call" | custom-call | flops 1 | bytes 1 | tf_op jit(solution)/shard_map/pallas_call | solution.py:251
  43.0 12.7 %collective-permute-done.3.refs_0_ = bf16[256,4096]{1,0:T(8,128)(2,1)S(1)} collective-permute-done((bf16[256,4096]{1,0:T(8,128)(2,1)S(1)}, bf16[256,4096]{1,0:T(8,128)(2,1)S(1)}, u32[]{:S(2)}, u32[]{:S(2)}) %collective-permute-start.3) | collective-permute-done | bytes 2097184 | tf_op jit(solution)/shard_map/ppermute | solution.py:351
  60.5 7.8 %shard_map.114 = (bf16[768,512]{1,0:T(8,128)(2,1)S(1)}, bf16[768,512]{1,0:T(8,128)(2,1)S(1)}) custom-call(bf16[256,4096]{1,0:T(8,128)(2,1)S(1)} %collective-permute-done.3.refs_0_, bf16[256,4096]{1,0:T(8,128)(2,1)S(1)} %collective-permute-done.7.refs_1_, bf16[1536,4096]{1,0:T(8,128)(2,1)S(1)} %bitcast.30), custom_call_target="tpu_custom_call" | custom-call | flops 1 | bytes 1 | tf_op jit(solution)/shard_map/pallas_call | solution.py:251
  68.3 8.2 %collective-permute-done.8 = bf16[768,512]{1,0:T(8,128)(2,1)S(1)} collective-permute-done((bf16[768,512]{1,0:T(8,128)(2,1)S(1)}, bf16[768,512]{1,0:T(8,128)(2,1)S(1)}, u32[]{:S(2)}, u32[]{:S(2)}) %collective-permute-start.8) | collective-permute-done | bytes 786464 | tf_op jit(solution)/shard_map/ppermute | solution.py:381
  76.5 5.7 %collective-permute-done.6.refs_0_ = bf16[256,4096]{1,0:T(8,128)(2,1)S(1)} collective-permute-done((bf16[256,4096]{1,0:T(8,128)(2,1)S(1)}, bf16[256,4096]{1,0:T(8,128)(2,1)S(1)}, u32[]{:S(2)}, u32[]{:S(2)}) %collective-permute-start.6) | collective-permute-done | bytes 2097184 | tf_op jit(solution)/shard_map/ppermute | solution.py:351
  86.6 7.8 %shard_map.115 = (bf16[768,512]{1,0:T(8,128)(2,1)S(1)}, bf16[768,512]{1,0:T(8,128)(2,1)S(1)}) custom-call(bf16[256,4096]{1,0:T(8,128)(2,1)S(1)} %collective-permute-done.6.refs_0_, bf16[256,4096]{1,0:T(8,128)(2,1)S(1)} %collective-permute-done.10.refs_1_, bf16[1536,4096]{1,0:T(8,128)(2,1)S(1)} %bitcast.31), custom_call_target="tpu_custom_call" | custom-call | flops 1 | bytes 1 | tf_op jit(solution)/shard_map/pallas_call | solution.py:251
  95.3 7.4 %collective-permute-done.11 = bf16[768,512]{1,0:T(8,128)(2,1)S(1)} collective-permute-done((bf16[768,512]{1,0:T(8,128)(2,1)S(1)}, bf16[768,512]{1,0:T(8,128)(2,1)S(1)}, u32[]{:S(2)}, u32[]{:S(2)}) %collective-permute-start.11) | collective-permute-done | bytes 786464 | tf_op jit(solution)/shard_map/ppermute | solution.py:381
  102.7 6.9 %all-to-all-start = ((bf16[16,256,128]{2,1,0:T(8,128)(2,1)}), bf16[16,256,128]{2,1,0:T(8,128)(2,1)}, u32[]{:S(2)}, u32[]{:S(2)}) async-start(bf16[16,256,128]{2,1,0:T(8,128)(2,1)} %bitcast.60), calls=%async_computation | async-start | bytes 2097152 | tf_op jit(solution)/shard_map/all_to_all | solution.py:408
  112.3 4.6 %copy-done.2 = bf16[2,3,256,4096]{3,2,1,0:T(8,128)(2,1)S(1)} copy-done((bf16[2,3,256,4096]{3,2,1,0:T(8,128)(2,1)S(1)}, bf16[2,3,256,4096]{3,2,1,0:T(8,128)(2,1)}, u32[]{:S(2)}) %copy-start.2) | copy-done | bytes 12582936
  116.8 4.3 %shard_map.116 = (bf16[768,256]{1,0:T(8,128)(2,1)S(1)}, bf16[768,256]{1,0:T(8,128)(2,1)S(1)}) custom-call(bf16[128,4096]{1,0:T(8,128)(2,1)S(1)} %collective-permute-done.9.refs_0_, bf16[128,4096]{1,0:T(8,128)(2,1)S(1)} %collective-permute-done.12.refs_1_, bf16[1536,4096]{1,0:T(8,128)(2,1)S(1)} %bitcast.32), custom_call_target="tpu_custom_call" | custom-call | flops 1 | bytes 1 | tf_op jit(solution)/shard_map/pallas_call | solution.py:251
  123.2 5.5 %collective-permute-done.13 = bf16[768,512]{1,0:T(8,128)(2,1)S(1)} collective-permute-done((bf16[768,512]{1,0:T(8,128)(2,1)S(1)}, bf16[768,512]{1,0:T(8,128)(2,1)S(1)}, u32[]{:S(2)}, u32[]{:S(2)}) %collective-permute-start.13) | collective-permute-done | bytes 786464 | tf_op jit(solution)/shard_map/ppermute | solution.py:381
  129.5 7.5 %collective-permute-done.14 = bf16[768,256]{1,0:T(8,128)(2,1)S(1)} collective-permute-done((bf16[768,256]{1,0:T(8,128)(2,1)S(1)}, bf16[768,256]{1,0:T(8,128)(2,1)S(1)}, u32[]{:S(2)}, u32[]{:S(2)}) %collective-permute-start.14) | collective-permute-done | bytes 393248 | tf_op jit(solution)/shard_map/ppermute | solution.py:381
  147.6 19.2 %shard_map.117 = (bf16[16,256,128]{2,1,0:T(8,128)(2,1)}, bf16[3,256,256]{2,1,0:T(8,128)(2,1)S(1)}, bf16[3,256,512]{2,1,0:T(8,128)(2,1)S(1)}, bf16[3,256,512]{2,1...) custom-call(s32[16]{0:T(128)S(1)} %dynamic-slice_bitcast_fusion.orde, ...), custom_call_target="tpu_custom_call" | custom-call | flops 1 | bytes 1 | tf_op jit(solution)/shard_map/pallas_call | solution.py:153
  167.6 6.9 %all-to-all-start.1 = ((bf16[16,256,128]{2,1,0:T(8,128)(2,1)}), bf16[16,256,128]{2,1,0:T(8,128)(2,1)}, u32[]{:S(2)}, u32[]{:S(2)}) async-start(bf16[16,256,128]{2,1,0:T(8,128)(2,1)} %get-tuple-element.125), calls=%async_computation.1 | async-start | bytes 2097152 | tf_op jit(solution)/shard_map/all_to_all | solution.py:423
  176.0 9.1 %collective-permute-done.15.far_ref = bf16[768,256]{1,0:T(8,128)(2,1)S(1)} collective-permute-done((bf16[768,256]{1,0:T(8,128)(2,1)S(1)}, bf16[768,256]{1,0:T(8,128)(2,1)S(1)}, u32[]{:S(2)}, u32[]{:S(2)}) %collective-permute-start.15) | collective-permute-done | bytes 393248 | tf_op jit(solution)/shard_map/ppermute | solution.py:381
  185.1 4.6 %copy-done.3 = bf16[2,3,256,4096]{3,2,1,0:T(8,128)(2,1)S(1)} copy-done((bf16[2,3,256,4096]{3,2,1,0:T(8,128)(2,1)S(1)}, bf16[2,3,256,4096]{3,2,1,0:T(8,128)(2,1)}, u32[]{:S(2)}) %copy-start.3) | copy-done | bytes 12582936
  189.7 6.0 %shard_map.118 = (bf16[128,4096]{1,0:T(8,128)(2,1)S(1)}, bf16[64,4096]{1,0:T(8,128)(2,1)S(1)}, bf16[64,4096]{1,0:T(8,128)(2,1)S(1)}) custom-call(bf16[768,256]{1,0:T(8,128)(2,1)S(1)} %bitcast.53, bf16[768,256]{1,0:T(8,128)(2,1)S(1)} %collective-permute-done.15.far_ref, bf16[1536,4096]{1,0:T(8,128)(2,1)S(1)} %bitcast.33), custom_call_target="tpu_custom_call" | custom-call | flops 1 | bytes 1 | tf_op jit(solution)/shard_map/pallas_call | solution.py:288
  195.7 1.6 collective-permute-start.16
  200.2 1.7 collective-permute-done.18.far_ref
  204.0 4.6 %copy-done.4 = bf16[2,3,256,4096]{3,2,1,0:T(8,128)(2,1)S(1)} copy-done((bf16[2,3,256,4096]{3,2,1,0:T(8,128)(2,1)S(1)}, bf16[2,3,256,4096]{3,2,1,0:T(8,128)(2,1)}, u32[]{:S(2)}) %copy-start.4) | copy-done | bytes 12582936
  209.7 9.6 %shard_map.120 = (bf16[256,4096]{1,0:T(8,128)(2,1)S(1)}, bf16[96,4096]{1,0:T(8,128)(2,1)S(1)}, bf16[80,4096]{1,0:T(8,128)(2,1)S(1)}, bf16[80,4096]{1,0:T(8,128)(2,1)S(1)}) custom-call(bf16[768,512]{1,0:T(8,128)(2,1)S(1)} %bitcast.43, bf16[768,512]{1,0:T(8,128)(2,1)S(1)} %copy-done.12, bf16[1536,4096]{1,0:T(8,128)(2,1)S(1)} %bitcast.34), custom_call_target="tpu_custom_call" | custom-call | flops 1 | bytes 1 | tf_op jit(solution)/shard_map/pallas_call | solution.py:288
  219.3 1.5 collective-permute-start.19
  222.6 1.6 collective-permute-done.20.refs_2_
  226.3 13.6 %collective-permute-done.23.far_ref = bf16[768,512]{1,0:T(8,128)(2,1)S(1)} collective-permute-done((bf16[768,512]{1,0:T(8,128)(2,1)S(1)}, bf16[768,512]{1,0:T(8,128)(2,1)S(1)}, u32[]{:S(2)}, u32[]{:S(2)}) %collective-permute-start.23) | collective-permute-done | bytes 786464 | tf_op jit(solution)/shard_map/ppermute | solution.py:381
  239.9 4.6 %copy-done.5 = bf16[2,3,256,4096]{3,2,1,0:T(8,128)(2,1)S(1)} copy-done((bf16[2,3,256,4096]{3,2,1,0:T(8,128)(2,1)S(1)}, bf16[2,3,256,4096]{3,2,1,0:T(8,128)(2,1)}, u32[]{:S(2)}) %copy-start.5) | copy-done | bytes 12582936
  244.5 9.5 %shard_map.122 = (bf16[256,4096]{1,0:T(8,128)(2,1)S(1)}, bf16[128,4096]{1,0:T(8,128)(2,1)S(1)}, bf16[128,4096]{1,0:T(8,128)(2,1)S(1)}) custom-call(bf16[768,512]{1,0:T(8,128)(2,1)S(1)} %bitcast.41, bf16[768,512]{1,0:T(8,128)(2,1)S(1)} %collective-permute-done.23.far_ref, bf16[1536,4096]{1,0:T(8,128)(2,1)S(1)} %bitcast.35), custom_call_target="tpu_custom_call" | custom-call | flops 1 | bytes 1 | tf_op jit(solution)/shard_map/pallas_call | solution.py:288
  254.1 2.4 collective-permute-start.24
  258.7 1.5 collective-permute-done.25.refs_2_
  260.2 4.9 %collective-permute-done.26.refs_3_ = bf16[256,4096]{1,0:T(8,128)(2,1)S(1)} collective-permute-done((bf16[256,4096]{1,0:T(8,128)(2,1)S(1)}, bf16[256,4096]{1,0:T(8,128)(2,1)S(1)}, u32[]{:S(2)}, u32[]{:S(2)}) %collective-permute-start.26) | collective-permute-done | bytes 2097184 | tf_op jit(solution)/shard_map/ppermute | solution.py:351
  266.5 8.7 %collective-permute-done.27.far_ref = bf16[768,512]{1,0:T(8,128)(2,1)S(1)} collective-permute-done((bf16[768,512]{1,0:T(8,128)(2,1)S(1)}, bf16[768,512]{1,0:T(8,128)(2,1)S(1)}, u32[]{:S(2)}, u32[]{:S(2)}) %collective-permute-start.27) | collective-permute-done | bytes 786464 | tf_op jit(solution)/shard_map/ppermute | solution.py:381
  275.5 9.5 %shard_map.124 = (bf16[256,4096]{1,0:T(8,128)(2,1)S(1)}, bf16[128,4096]{1,0:T(8,128)(2,1)S(1)}, bf16[128,4096]{1,0:T(8,128)(2,1)S(1)}) custom-call(bf16[768,512]{1,0:T(8,128)(2,1)S(1)} %bitcast.39, bf16[768,512]{1,0:T(8,128)(2,1)S(1)} %collective-permute-done.27.far_ref, bf16[1536,4096]{1,0:T(8,128)(2,1)S(1)} %bitcast.36), custom_call_target="tpu_custom_call" | custom-call | flops 1 | bytes 1 | tf_op jit(solution)/shard_map/pallas_call | solution.py:288
  285.0 2.5 collective-permute-start.28
  291.3 9.0 %collective-permute-done.30.refs_3_ = bf16[256,4096]{1,0:T(8,128)(2,1)S(1)} collective-permute-done((bf16[256,4096]{1,0:T(8,128)(2,1)S(1)}, bf16[256,4096]{1,0:T(8,128)(2,1)S(1)}, u32[]{:S(2)}, u32[]{:S(2)}) %collective-permute-start.30) | collective-permute-done | bytes 2097184 | tf_op jit(solution)/shard_map/ppermute | solution.py:351
  301.8 1.5 fusion
  303.3 2.3 collective-permute-start.35
  306.1 6.7 %shard_map.126 = (bf16[128,4096]{1,0:T(8,128)(2,1)S(1)}, bf16[64,4096]{1,0:T(8,128)(2,1)}, bf16[64,4096]{1,0:T(8,128)(2,1)}) custom-call(bf16[768,256]{1,0:T(8,128)(2,1)S(1)} %bitcast.51, bf16[768,256]{1,0:T(8,128)(2,1)S(1)} %collective-permute-done.31.far_ref, bf16[1536,4096]{1,0:T(8,128)(2,1)S(1)} %bitcast.37), custom_call_target="tpu_custom_call" | custom-call | flops 1 | bytes 1 | tf_op jit(solution)/shard_map/pallas_call | solution.py:288
  316.2 2.4 collective-permute-done.35.refs_4_
  318.6 11.8 %collective-permute-done.34.refs_3_ = bf16[128,4096]{1,0:T(8,128)(2,1)S(1)} collective-permute-done((bf16[128,4096]{1,0:T(8,128)(2,1)}, bf16[128,4096]{1,0:T(8,128)(2,1)S(1)}, u32[]{:S(2)}, u32[]{:S(2)}) %collective-permute-start.34) | collective-permute-done | bytes 1048608 | tf_op jit(solution)/shard_map/ppermute | solution.py:351
  330.4 3.7 %shard_map.127 = bf16[128,4096]{1,0:T(8,128)(2,1)} custom-call(bf16[128,4096]{1,0:T(8,128)(2,1)S(1)} %get-tuple-element.154.refs_0_, bf16[64,4096]{1,0:T(8,128)(2,1)} %collective-permute-done.32.refs_1_, bf16[64,4096]{1,0:T(8,128)(2,1)} %collective-permute-done.33.refs_2_, bf16[128,4096]{1,0:T(8,128)(2,1)S(1)} %collective-permute-done.34.refs_3_, ...), custom_call_target="tpu_custom_call" | custom-call | flops 1 | bytes 1 | tf_op jit(solution)/shard_map/pallas_call | solution.py:326
  334.1 2.3 copy.21
  (128 shorter events, 61.4 us)
Async XLA Ops:
  0.6 17.1 %collective-permute-start.2 = (bf16[128,4096]{1,0:T(8,128)(2,1)}, bf16[128,4096]{1,0:T(8,128)(2,1)S(1)}, u32[]{:S(2)}, u32[]{:S(2)}) collective-permute-start(bf16[128,4096]{1,0:T(8,128)(2,1)} %refs_0_.3), channel_id=1, source_target_pairs={{0,2},{2,0},{4,6},{6,4},{8,10},{10,8},{12,14},{14,12},{16,18},{18,... | collective-permute-start | bytes 3145736 | tf_op jit(solution)/shard_map/ppermute | solution.py:354
  0.8 25.9 %collective-permute-start.1 = (bf16[128,4096]{1,0:T(8,128)(2,1)}, bf16[128,4096]{1,0:T(8,128)(2,1)}, u32[]{:S(2)}, u32[]{:S(2)}) collective-permute-start(bf16[128,4096]{1,0:T(8,128)(2,1)} %refs_0_.3), channel_id=1, source_target_pairs={{0,6},{2,8},{8,2},{10,16},{16,10},{18,24},{24,18},{26,28},{28,26},... | collective-permute-start | bytes 3145736 | tf_op jit(solution)/shard_map/ppermute | solution.py:351
  3.5 24.0 %collective-permute-start = (bf16[128,4096]{1,0:T(8,128)(2,1)}, bf16[128,4096]{1,0:T(8,128)(2,1)}, u32[]{:S(2)}, u32[]{:S(2)}) collective-permute-start(bf16[128,4096]{1,0:T(8,128)(2,1)} %refs_0_.3), channel_id=1, source_target_pairs={{0,8},{2,6},{8,16},{10,2},{16,24},{18,10},{24,28},{26,18},{28,20},... | collective-permute-start | bytes 3145736 | tf_op jit(solution)/shard_map/ppermute | solution.py:351
  10.0 6.3 %copy-start.35 = (f32[3,1,16,3]{2,1,3,0:T(1,128)S(1)}, f32[3,1,16,3]{2,1,3,0:T(1,128)}, u32[]{:S(2)}) copy-start(f32[3,1,16,3]{2,1,3,0:T(1,128)} %param.12) | copy-start | bytes 1732
  10.0 7.7 %copy-start.10 = (bf16[128,4096]{1,0:T(8,128)(2,1)S(1)}, bf16[128,4096]{1,0:T(8,128)(2,1)}, u32[]{:S(2)}) copy-start(bf16[128,4096]{1,0:T(8,128)(2,1)} %refs_0_.3) | copy-start | bytes 3145732
  11.7 4.6 %copy-start = (bf16[2,3,256,4096]{3,2,1,0:T(8,128)(2,1)}, bf16[2,3,256,4096]{3,2,1,0:T(8,128)(2,1)S(1)}, u32[]{:S(2)}) copy-start(bf16[2,3,256,4096]{3,2,1,0:T(8,128)(2,1)S(1)} %shard_map.111) | copy-start | bytes 37748740
  30.1 4.2 %collective-permute-start.4 = (bf16[256,4096]{1,0:T(8,128)(2,1)S(1)}, bf16[256,4096]{1,0:T(8,128)(2,1)S(1)}, u32[]{:S(2)}, u32[]{:S(2)}) collective-permute-start(bf16[256,4096]{1,0:T(8,128)(2,1)S(1)} %constant_dynamic-update-slice_fusion.refs_0_), channel_id=1, source_target_pairs={{0,2},{2,0},{4,6},{6,4},{8,10},{10,8},{12,14},{14,12},{16,18},{18,... | collective-permute-start | bytes 6291464 | tf_op jit(solution)/shard_map/ppermute | solution.py:354
  30.6 25.2 %collective-permute-start.3 = (bf16[256,4096]{1,0:T(8,128)(2,1)S(1)}, bf16[256,4096]{1,0:T(8,128)(2,1)S(1)}, u32[]{:S(2)}, u32[]{:S(2)}) collective-permute-start(bf16[256,4096]{1,0:T(8,128)(2,1)S(1)} %constant_dynamic-update-slice_fusion.refs_0_), channel_id=1, source_target_pairs={{0,8},{2,6},{8,16},{10,2},{16,24},{18,10},{24,28},{26,18},{28,20},... | collective-permute-start | bytes 6291464 | tf_op jit(solution)/shard_map/ppermute | solution.py:351
  32.0 11.1 %collective-permute-start.5 = (bf16[768,256]{1,0:T(8,128)(2,1)S(1)}, bf16[768,256]{1,0:T(8,128)(2,1)S(1)}, u32[]{:S(2)}, u32[]{:S(2)}) collective-permute-start(bf16[768,256]{1,0:T(8,128)(2,1)S(1)} %get-tuple-element.92), channel_id=1, source_target_pairs={{0,1},{1,0},{2,3},{3,2},{4,5},{5,4},{6,7},{7,6},{8,9},{9,8},{10,11... | collective-permute-start | bytes 1179656 | tf_op jit(solution)/shard_map/ppermute | solution.py:381
  43.0 25.3 %copy-start.29 = (bf16[768,256]{1,0:T(8,128)(2,1)}, bf16[768,256]{1,0:T(8,128)(2,1)S(1)}, u32[]{:S(2)}) copy-start(bf16[768,256]{1,0:T(8,128)(2,1)S(1)} %collective-permute-done.5) | copy-start | bytes 1179652
  55.8 4.8 %collective-permute-start.7 = (bf16[256,4096]{1,0:T(8,128)(2,1)S(1)}, bf16[256,4096]{1,0:T(8,128)(2,1)S(1)}, u32[]{:S(2)}, u32[]{:S(2)}) collective-permute-start(bf16[256,4096]{1,0:T(8,128)(2,1)S(1)} %collective-permute-done.3.refs_0_), channel_id=1, source_target_pairs={{0,2},{2,0},{4,6},{6,4},{8,10},{10,8},{12,14},{14,12},{16,18},{18,... | collective-permute-start | bytes 6291464 | tf_op jit(solution)/shard_map/ppermute | solution.py:354
  56.8 25.5 %collective-permute-start.6 = (bf16[256,4096]{1,0:T(8,128)(2,1)S(1)}, bf16[256,4096]{1,0:T(8,128)(2,1)S(1)}, u32[]{:S(2)}, u32[]{:S(2)}) collective-permute-start(bf16[256,4096]{1,0:T(8,128)(2,1)S(1)} %collective-permute-done.3.refs_0_), channel_id=1, source_target_pairs={{0,8},{2,6},{8,16},{10,2},{16,24},{18,10},{24,28},{26,18},{28,20},... | collective-permute-start | bytes 6291464 | tf_op jit(solution)/shard_map/ppermute | solution.py:351
  58.1 18.4 %collective-permute-start.8 = (bf16[768,512]{1,0:T(8,128)(2,1)S(1)}, bf16[768,512]{1,0:T(8,128)(2,1)S(1)}, u32[]{:S(2)}, u32[]{:S(2)}) collective-permute-start(bf16[768,512]{1,0:T(8,128)(2,1)S(1)} %get-tuple-element.97), channel_id=1, source_target_pairs={{0,1},{1,0},{2,3},{3,2},{4,5},{5,4},{6,7},{7,6},{8,9},{9,8},{10,11... | collective-permute-start | bytes 2359304 | tf_op jit(solution)/shard_map/ppermute | solution.py:381
  68.3 16.0 %copy-start.17 = (bf16[768,512]{1,0:T(8,128)(2,1)}, bf16[768,512]{1,0:T(8,128)(2,1)S(1)}, u32[]{:S(2)}) copy-start(bf16[768,512]{1,0:T(8,128)(2,1)S(1)} %get-tuple-element.108) | copy-start | bytes 2359300
  76.5 17.8 %copy-start.15 = (bf16[768,512]{1,0:T(8,128)(2,1)}, bf16[768,512]{1,0:T(8,128)(2,1)S(1)}, u32[]{:S(2)}) copy-start(bf16[768,512]{1,0:T(8,128)(2,1)S(1)} %collective-permute-done.8) | copy-start | bytes 2359300
  82.2 4.3 %collective-permute-start.10 = (bf16[256,4096]{1,0:T(8,128)(2,1)S(1)}, bf16[256,4096]{1,0:T(8,128)(2,1)S(1)}, u32[]{:S(2)}, u32[]{:S(2)}) collective-permute-start(bf16[256,4096]{1,0:T(8,128)(2,1)S(1)} %collective-permute-done.6.refs_0_), channel_id=1, source_target_pairs={{0,2},{2,0},{4,6},{6,4},{8,10},{10,8},{12,14},{14,12},{16,18},{18,... | collective-permute-start | bytes 6291464 | tf_op jit(solution)/shard_map/ppermute | solution.py:354
  82.9 19.8 %collective-permute-start.9 = (bf16[128,4096]{1,0:T(8,128)(2,1)S(1)}, bf16[128,4096]{1,0:T(8,128)(2,1)S(1)}, u32[]{:S(2)}, u32[]{:S(2)}) collective-permute-start(bf16[128,4096]{1,0:T(8,128)(2,1)S(1)} %slice.9), channel_id=1, source_target_pairs={{0,8},{2,6},{8,16},{10,2},{16,24},{18,10},{24,28},{26,18},{28,20},... | collective-permute-start | bytes 3145736 | tf_op jit(solution)/shard_map/ppermute | solution.py:351
  84.3 18.4 %collective-permute-start.11 = (bf16[768,512]{1,0:T(8,128)(2,1)S(1)}, bf16[768,512]{1,0:T(8,128)(2,1)S(1)}, u32[]{:S(2)}, u32[]{:S(2)}) collective-permute-start(bf16[768,512]{1,0:T(8,128)(2,1)S(1)} %get-tuple-element.103), channel_id=1, source_target_pairs={{0,1},{1,0},{2,3},{3,2},{4,5},{5,4},{6,7},{7,6},{8,9},{9,8},{10,11... | collective-permute-start | bytes 2359304 | tf_op jit(solution)/shard_map/ppermute | solution.py:381
  102.7 18.4 %copy-start.19 = (bf16[768,512]{1,0:T(8,128)(2,1)}, bf16[768,512]{1,0:T(8,128)(2,1)S(1)}, u32[]{:S(2)}) copy-start(bf16[768,512]{1,0:T(8,128)(2,1)S(1)} %collective-permute-done.11) | copy-start | bytes 2359300
  102.7 34.4 %copy-start.34 = (f32[1,16,128]{2,1,0:T(8,128)S(1)}, f32[1,16,128]{2,1,0:T(8,128)}, u32[]{:S(2)}) copy-start(f32[1,16,128]{2,1,0:T(8,128)} %param.13) | copy-start | bytes 24580
  102.7 34.4 %all-to-all-start = ((bf16[16,256,128]{2,1,0:T(8,128)(2,1)}), bf16[16,256,128]{2,1,0:T(8,128)(2,1)}, u32[]{:S(2)}, u32[]{:S(2)}) async-start(bf16[16,256,128]{2,1,0:T(8,128)(2,1)} %bitcast.60), calls=%async_computation | async-start | bytes 2097152 | tf_op jit(solution)/shard_map/all_to_all | solution.py:408
  109.6 2.7 collective-permute-start.12
  109.8 18.8 %collective-permute-start.13 = (bf16[768,512]{1,0:T(8,128)(2,1)S(1)}, bf16[768,512]{1,0:T(8,128)(2,1)S(1)}, u32[]{:S(2)}, u32[]{:S(2)}) collective-permute-start(bf16[768,512]{1,0:T(8,128)(2,1)S(1)} %get-tuple-element.115), channel_id=1, source_target_pairs={{0,1},{1,0},{2,3},{3,2},{4,5},{5,4},{6,7},{7,6},{8,9},{9,8},{10,11... | collective-permute-start | bytes 2359304 | tf_op jit(solution)/shard_map/ppermute | solution.py:381
  121.9 15.2 %collective-permute-start.14 = (bf16[768,256]{1,0:T(8,128)(2,1)S(1)}, bf16[768,256]{1,0:T(8,128)(2,1)S(1)}, u32[]{:S(2)}, u32[]{:S(2)}) collective-permute-start(bf16[768,256]{1,0:T(8,128)(2,1)S(1)} %get-tuple-element.116), channel_id=1, source_target_pairs={{0,1},{1,0},{2,3},{3,2},{4,5},{5,4},{6,7},{7,6},{8,9},{9,8},{10,11... | collective-permute-start | bytes 1179656 | tf_op jit(solution)/shard_map/ppermute | solution.py:381
  167.6 35.2 %all-to-all-start.1 = ((bf16[16,256,128]{2,1,0:T(8,128)(2,1)}), bf16[16,256,128]{2,1,0:T(8,128)(2,1)}, u32[]{:S(2)}, u32[]{:S(2)}) async-start(bf16[16,256,128]{2,1,0:T(8,128)(2,1)} %get-tuple-element.125), calls=%async_computation.1 | async-start | bytes 2097152 | tf_op jit(solution)/shard_map/all_to_all | solution.py:423
  174.5 10.6 %collective-permute-start.15 = (bf16[768,256]{1,0:T(8,128)(2,1)S(1)}, bf16[768,256]{1,0:T(8,128)(2,1)S(1)}, u32[]{:S(2)}, u32[]{:S(2)}) collective-permute-start(bf16[768,256]{1,0:T(8,128)(2,1)S(1)} %bitcast.52), channel_id=1, source_target_pairs={{0,1},{1,0},{2,3},{3,2},{4,5},{5,4},{6,7},{7,6},{8,9},{9,8},{10,11... | collective-permute-start | bytes 1179656 | tf_op jit(solution)/shard_map/ppermute | solution.py:381
  175.8 26.1 %collective-permute-start.18 = (bf16[768,512]{1,0:T(8,128)(2,1)S(1)}, bf16[768,512]{1,0:T(8,128)(2,1)S(1)}, u32[]{:S(2)}, u32[]{:S(2)}) collective-permute-start(bf16[768,512]{1,0:T(8,128)(2,1)S(1)} %bitcast.42), channel_id=1, source_target_pairs={{0,1},{1,0},{2,3},{3,2},{4,5},{5,4},{6,7},{7,6},{8,9},{9,8},{10,11... | collective-permute-start | bytes 2359304 | tf_op jit(solution)/shard_map/ppermute | solution.py:381
  195.7 3.2 collective-permute-start.16
  197.3 2.3 collective-permute-start.17
  202.8 22.3 %collective-permute-start.22 = (bf16[128,4096]{1,0:T(8,128)(2,1)S(1)}, bf16[128,4096]{1,0:T(8,128)(2,1)S(1)}, u32[]{:S(2)}, u32[]{:S(2)}) collective-permute-start(bf16[128,4096]{1,0:T(8,128)(2,1)S(1)} %shard_map.119), channel_id=1, source_target_pairs={{0,4},{2,10},{8,0},{10,18},{16,8},{18,26},{24,16},{26,30},{28,24},... | collective-permute-start | bytes 3145736 | tf_op jit(solution)/shard_map/ppermute | solution.py:351
  219.3 5.8 %collective-permute-start.19 = (bf16[96,4096]{1,0:T(8,128)(2,1)S(1)}, bf16[96,4096]{1,0:T(8,128)(2,1)S(1)}, u32[]{:S(2)}, u32[]{:S(2)}) collective-permute-start(bf16[96,4096]{1,0:T(8,128)(2,1)S(1)} %get-tuple-element.130), channel_id=1, source_target_pairs={{0,2},{2,0},{4,6},{6,4},{8,10},{10,8},{12,14},{14,12},{16,18},{18,... | collective-permute-start | bytes 2359304 | tf_op jit(solution)/shard_map/ppermute | solution.py:354
  220.8 19.1 %collective-permute-start.23 = (bf16[768,512]{1,0:T(8,128)(2,1)S(1)}, bf16[768,512]{1,0:T(8,128)(2,1)S(1)}, u32[]{:S(2)}, u32[]{:S(2)}) collective-permute-start(bf16[768,512]{1,0:T(8,128)(2,1)S(1)} %bitcast.40), channel_id=1, source_target_pairs={{0,1},{1,0},{2,3},{3,2},{4,5},{5,4},{6,7},{7,6},{8,9},{9,8},{10,11... | collective-permute-start | bytes 2359304 | tf_op jit(solution)/shard_map/ppermute | solution.py:381
  222.1 2.1 collective-permute-start.20
  222.4 2.7 collective-permute-start.21
  239.9 25.2 %collective-permute-start.26 = (bf16[256,4096]{1,0:T(8,128)(2,1)S(1)}, bf16[256,4096]{1,0:T(8,128)(2,1)S(1)}, u32[]{:S(2)}, u32[]{:S(2)}) collective-permute-start(bf16[256,4096]{1,0:T(8,128)(2,1)S(1)} %shard_map.121), channel_id=1, source_target_pairs={{0,4},{2,10},{8,0},{10,18},{16,8},{18,26},{24,16},{26,30},{28,24},... | collective-permute-start | bytes 6291464 | tf_op jit(solution)/shard_map/ppermute | solution.py:351
  244.5 31.0 %copy-start.6 = (bf16[2,3,256,4096]{3,2,1,0:T(8,128)(2,1)S(1)}, bf16[2,3,256,4096]{3,2,1,0:T(8,128)(2,1)}, u32[]{:S(2)}) copy-start(bf16[2,3,256,4096]{3,2,1,0:T(8,128)(2,1)} %copy-done) | copy-start | bytes 37748740
  254.1 4.7 %collective-permute-start.24 = (bf16[128,4096]{1,0:T(8,128)(2,1)S(1)}, bf16[128,4096]{1,0:T(8,128)(2,1)S(1)}, u32[]{:S(2)}, u32[]{:S(2)}) collective-permute-start(bf16[128,4096]{1,0:T(8,128)(2,1)S(1)} %get-tuple-element.140), channel_id=1, source_target_pairs={{0,2},{2,0},{4,6},{6,4},{8,10},{10,8},{12,14},{14,12},{16,18},{18,... | collective-permute-start | bytes 3145736 | tf_op jit(solution)/shard_map/ppermute | solution.py:354
  256.4 3.8 %collective-permute-start.25 = (bf16[128,4096]{1,0:T(8,128)(2,1)S(1)}, bf16[128,4096]{1,0:T(8,128)(2,1)S(1)}, u32[]{:S(2)}, u32[]{:S(2)}) collective-permute-start(bf16[128,4096]{1,0:T(8,128)(2,1)S(1)} %get-tuple-element.141), channel_id=1, source_target_pairs={{0,2},{2,0},{4,6},{6,4},{8,10},{10,8},{12,14},{14,12},{16,18},{18,... | collective-permute-start | bytes 3145736 | tf_op jit(solution)/shard_map/ppermute | solution.py:354
  256.5 18.7 %collective-permute-start.27 = (bf16[768,512]{1,0:T(8,128)(2,1)S(1)}, bf16[768,512]{1,0:T(8,128)(2,1)S(1)}, u32[]{:S(2)}, u32[]{:S(2)}) collective-permute-start(bf16[768,512]{1,0:T(8,128)(2,1)S(1)} %bitcast.38), channel_id=1, source_target_pairs={{0,1},{1,0},{2,3},{3,2},{4,5},{5,4},{6,7},{7,6},{8,9},{9,8},{10,11... | collective-permute-start | bytes 2359304 | tf_op jit(solution)/shard_map/ppermute | solution.py:381
  266.5 21.2 %copy-start.26 = (bf16[3,256,256]{2,1,0:T(8,128)(2,1)S(1)}, bf16[3,256,256]{2,1,0:T(8,128)(2,1)}, u32[]{:S(2)}) copy-start(bf16[3,256,256]{2,1,0:T(8,128)(2,1)} %copy-done.25) | copy-start | bytes 1179652
  275.2 25.2 %collective-permute-start.30 = (bf16[256,4096]{1,0:T(8,128)(2,1)S(1)}, bf16[256,4096]{1,0:T(8,128)(2,1)S(1)}, u32[]{:S(2)}, u32[]{:S(2)}) collective-permute-start(bf16[256,4096]{1,0:T(8,128)(2,1)S(1)} %shard_map.123), channel_id=1, source_target_pairs={{0,4},{2,10},{8,0},{10,18},{16,8},{18,26},{24,16},{26,30},{28,24},... | collective-permute-start | bytes 6291464 | tf_op jit(solution)/shard_map/ppermute | solution.py:351
  285.0 4.8 %collective-permute-start.28 = (bf16[128,4096]{1,0:T(8,128)(2,1)S(1)}, bf16[128,4096]{1,0:T(8,128)(2,1)S(1)}, u32[]{:S(2)}, u32[]{:S(2)}) collective-permute-start(bf16[128,4096]{1,0:T(8,128)(2,1)S(1)} %get-tuple-element.148), channel_id=1, source_target_pairs={{0,2},{2,0},{4,6},{6,4},{8,10},{10,8},{12,14},{14,12},{16,18},{18,... | collective-permute-start | bytes 3145736 | tf_op jit(solution)/shard_map/ppermute | solution.py:354
  287.6 3.8 %collective-permute-start.29 = (bf16[128,4096]{1,0:T(8,128)(2,1)S(1)}, bf16[128,4096]{1,0:T(8,128)(2,1)S(1)}, u32[]{:S(2)}, u32[]{:S(2)}) collective-permute-start(bf16[128,4096]{1,0:T(8,128)(2,1)S(1)} %get-tuple-element.149), channel_id=1, source_target_pairs={{0,2},{2,0},{4,6},{6,4},{8,10},{10,8},{12,14},{14,12},{16,18},{18,... | collective-permute-start | bytes 3145736 | tf_op jit(solution)/shard_map/ppermute | solution.py:354
  287.6 14.1 %collective-permute-start.31 = (bf16[768,256]{1,0:T(8,128)(2,1)S(1)}, bf16[768,256]{1,0:T(8,128)(2,1)S(1)}, u32[]{:S(2)}, u32[]{:S(2)}) collective-permute-start(bf16[768,256]{1,0:T(8,128)(2,1)S(1)} %bitcast.50), channel_id=1, source_target_pairs={{0,1},{1,0},{2,3},{3,2},{4,5},{5,4},{6,7},{7,6},{8,9},{9,8},{10,11... | collective-permute-start | bytes 1179656 | tf_op jit(solution)/shard_map/ppermute | solution.py:381
  303.3 15.3 %collective-permute-start.35 = (bf16[128,4096]{1,0:T(8,128)(2,1)}, bf16[128,4096]{1,0:T(8,128)(2,1)S(1)}, u32[]{:S(2)}, u32[]{:S(2)}) collective-permute-start(bf16[128,4096]{1,0:T(8,128)(2,1)} %get-tuple-element.168), channel_id=1, source_target_pairs={{0,6},{2,8},{8,2},{10,16},{16,10},{18,24},{24,18},{26,28},{28,26},... | collective-permute-start | bytes 3145736 | tf_op jit(solution)/shard_map/ppermute | solution.py:351
  305.6 24.8 %collective-permute-start.34 = (bf16[128,4096]{1,0:T(8,128)(2,1)}, bf16[128,4096]{1,0:T(8,128)(2,1)S(1)}, u32[]{:S(2)}, u32[]{:S(2)}) collective-permute-start(bf16[128,4096]{1,0:T(8,128)(2,1)} %get-tuple-element.169), channel_id=1, source_target_pairs={{0,4},{2,10},{8,0},{10,18},{16,8},{18,26},{24,16},{26,30},{28,24},... | collective-permute-start | bytes 3145736 | tf_op jit(solution)/shard_map/ppermute | solution.py:351
  312.8 2.7 collective-permute-start.32
  313.6 2.6 collective-permute-start.33
  (26 other events, 48.3 us)

commit v3 on v2

--- a/solution.py
+++ b/solution.py
@@ -13,8 +13,7 @@
 LONG = 128
 F32 = jnp.float32
 BF16 = jnp.bfloat16
-VMEM = 44 * 1024 * 1024
-VMEM_DOT = 20 * 1024 * 1024
+MIB = 1024 * 1024
 SMALL = pl.CostEstimate(flops=1, bytes_accessed=1, transcendentals=0)
 
 
@@ -181,7 +180,7 @@
             jax.ShapeDtypeStruct((steps, per_step, 3 * SHORT, LONG), F32),
             jax.ShapeDtypeStruct((steps, per_step, LONG), F32),
         ],
-        compiler_params=pltpu.CompilerParams(vmem_limit_bytes=VMEM),
+        compiler_params=pltpu.CompilerParams(vmem_limit_bytes=20 * MIB),
         cost_estimate=SMALL,
     )(order, short_kernel, long_kernel.reshape(steps, per_step, LONG), g, *[x for s in proj_sets for x in s])
     mixed, d_proj, (gs, gl) = outs[0], outs[1:-2], outs[-2:]
@@ -211,7 +210,7 @@
             out_specs=pl.BlockSpec((1, 3, tile, width), lambda side, part, t: (side, 0, part, 0)),
         ),
         out_shape=jax.ShapeDtypeStruct((2, 3, channels, width), BF16),
-        compiler_params=pltpu.CompilerParams(vmem_limit_bytes=VMEM_DOT),
+        compiler_params=pltpu.CompilerParams(vmem_limit_bytes=16 * MIB),
         cost_estimate=SMALL,
     )(t.reshape(1), *weights).reshape(6 * channels, width)
 
@@ -259,7 +258,7 @@
         ],
         out_shape=[half, half],
         scratch_shapes=[pltpu.VMEM((tokens, width), BF16), pltpu.SemaphoreType.DMA((len(pieces),))],
-        compiler_params=pltpu.CompilerParams(vmem_limit_bytes=VMEM_DOT),
+        compiler_params=pltpu.CompilerParams(vmem_limit_bytes=16 * MIB),
         cost_estimate=SMALL,
     )(*pieces, flat)
     return near, far
@@ -296,19 +295,21 @@
         out_specs=[pl.BlockSpec((cut, tile), lambda i: (0, i)) for cut in cuts],
         out_shape=[jax.ShapeDtypeStruct((cut, width), BF16) for cut in cuts],
         scratch_shapes=[pltpu.VMEM((tokens, rows), BF16)],
-        compiler_params=pltpu.CompilerParams(vmem_limit_bytes=VMEM_DOT),
+        compiler_params=pltpu.CompilerParams(vmem_limit_bytes=14 * MIB),
         cost_estimate=SMALL,
     )(near, far, flat)
 
 
 def add_body(heights, *refs):
-    out_ref = refs[-1]
+    out_refs = refs[sum(heights) :]
     groups, at = [], 0
     for height in heights:
         groups.append(refs[at : at + height])
         at += height
     tops = [[sum(r.shape[0] for r in group[:n]) for n in range(len(group) + 1)] for group in groups]
-    edges = sorted({edge for top in tops for edge in top} | {out_ref.shape[0]})
+    height = out_refs[0].shape[0]
+    edges = {edge for top in tops for edge in top} | {n * height for n in range(len(out_refs) + 1)}
+    edges = sorted(edges)
     for low, high in zip(edges[:-1], edges[1:]):
         total = None
         for group, top in zip(groups, tops):
@@ -316,20 +317,20 @@
                 if top[n] <= low and high <= top[n + 1]:
                     part = ref[low - top[n] : high - top[n], :].astype(F32)
                     total = part if total is None else total + part
-        out_ref[low:high, :] = total.astype(BF16)
-
-
-def add_kernel(*groups):
-    rows, width = sum(x.shape[0] for x in groups[0]), groups[0][0].shape[1]
+        out_refs[low // height][low % height : low % height + high - low, :] = total.astype(BF16)
+
+
+def add_kernel(*groups, cut=1):
+    rows, width = sum(x.shape[0] for x in groups[0]) // cut, groups[0][0].shape[1]
     tile = min(1024, width)
     arrays = [x for group in groups for x in group]
     return pl.pallas_call(
         functools.partial(add_body, [len(group) for group in groups]),
         grid=(width // tile,),
         in_specs=[pl.BlockSpec((x.shape[0], tile), lambda i: (0, i)) for x in arrays],
-        out_specs=pl.BlockSpec((rows, tile), lambda i: (0, i)),
-        out_shape=jax.ShapeDtypeStruct((rows, width), BF16),
-        compiler_params=pltpu.CompilerParams(vmem_limit_bytes=VMEM_DOT),
+        out_specs=[pl.BlockSpec((rows, tile), lambda i: (0, i))] * cut,
+        out_shape=[jax.ShapeDtypeStruct((rows, width), BF16)] * cut,
+        compiler_params=pltpu.CompilerParams(vmem_limit_bytes=8 * MIB),
         cost_estimate=SMALL,
     )(*arrays)
 
@@ -403,13 +404,17 @@
         coming = one_way(arrived if s < half - 1 else arrived[:held])
         projected.append((near, across(far)))
         near, far = project([arrived, swap(arrived)])
-        arrived, near, far, projected[-1], grad_out = stage((coming, near, far, projected[-1], grad_out))
-    projected.append((near, across(far)))
+        if s < half - 1:
+            arrived, near, far, projected[-1] = stage((coming, near, far, projected[-1]))
+    crossed = across(far)
+    arrived, near, grad_out = stage((coming, near, grad_out))
     incoming = lax.all_to_all(
         grad_out.reshape(n_ctx, channels, held), "ctx", split_axis=0, concat_axis=0, tiled=True
     )
-    near, far = project([arrived, swap(arrived)])
-    projected.append((near, across(far)))
+    shared, projected[-1] = stage((arrived, projected[-1]))
+    last, far = project([arrived, swap(shared[: held // 2]), swap(shared[held // 2 :])])
+    far, crossed = stage((far, crossed))
+    projected += [(near, crossed), (last, across(far))]
 
     mixed, d_proj, grad_short, grad_long = mix(
         order,
@@ -420,21 +425,24 @@
         [[s] for s in range(half + 1)],
     )
 
+    first, met, later = [meet(d_proj[s]) for s in (half, half - 1, half - 2)]
     mixed_out = lax.all_to_all(mixed, "ctx", split_axis=0, concat_axis=0, tiled=True).reshape(-1, held)
-    met = meet(d_proj[half - 1])
-    keep, *give = unproject(meet(d_proj[half]), held, held // 2, held // 2)
+    keep, *give = unproject(first, held, held // 2, held // 2)
     total = add_kernel([keep], [swap(x) for x in give])
-    total, met, rest, mixed_out = stage((total, met, d_proj[: half - 1], mixed_out))
+    total, met, rest, mixed_out = stage((total, met, d_proj[: half - 2], mixed_out))
     for s in range(half - 1, 0, -1):
-        coming = one_way(total, turned=True)
-        later = meet(rest[-1])
+        coming = one_way(total[0], turned=True)
+        if s < half - 1:
+            later = meet(rest[-1])
+            rest = rest[:-1]
         cuts = (96, 80, 80) if s == half - 1 and held == 128 else (held, held)
         keep, *give = unproject(met, 2 * held, *cuts)
-        total = add_kernel([keep], [swap(x) for x in give], [coming])
-        total, met, rest = stage((total, later, rest[:-1]))
-    coming = [one_way(total[:held], turned=True), one_way(total[held:], turned=True, to_mate=True)]
+        give, later = stage((give, later))
+        total = add_kernel([keep], [swap(x) for x in give], [coming], cut=2 if s == 1 else 1)
+        total, met, rest = stage((total, later, rest))
+    coming = [one_way(total[0], turned=True), one_way(total[1], turned=True, to_mate=True)]
     keep, *give = unproject(met, held, held // 2, held // 2)
-    grad_tokens = add_kernel([keep], [swap(x) for x in give], coming[:1], coming[1:])
+    (grad_tokens,) = add_kernel([keep], [swap(x) for x in give], coming[:1], coming[1:])
     return (
         mixed_out,
         grad_tokens,

time: 338 us -> 310 us (0.917)
  waiting for transfers between devices: 125 us -> 93.4 us
  local copies, waits for them, and re-layouts: 59.4 us -> 54.1 us
  starting transfers between devices: 48.3 us -> 52.7 us
  Pallas kernels: 102 us -> 106 us
    ppermute x10, waiting for transfers between devices: 61.8 us -> 30.9 us  [across(): return None if x is None else lax.ppermute(x, 'tp', [(0, 1), (1, 0)])]
    unnamed x76 -> x72, local copies, waits for them, and re-layouts: 55.6 us -> 53 us
    ppermute x16 -> x17, starting transfers between devices: 11.9 us -> 13.9 us  [swap(): return lax.ppermute(x, 'ctx', [(d, d ^ 1) for d in range(n_ctx)])]
    ppermute x16 -> x17, waiting for transfers between devices: 15.9 us -> 17.9 us  [swap(): return lax.ppermute(x, 'ctx', [(d, d ^ 1) for d in range(n_ctx)])]
  transfers between devices with their start and end apart: 38 -> 39, of which waited for: 29 -> 28; matrix products, arithmetic and copies ran while one was open for 1% -> 1% of each run, Pallas kernels for 24% -> 25%
where the time goes in v3:
time: 310 us; the launch traced here: 309 us
  Pallas kernels  106 us (34%)
  waiting for transfers between devices  93.4 us (30%)
  local copies, waits for them, and re-layouts  54.1 us (17%)
  starting transfers between devices  52.7 us (17%)
    unnamed x72, local copies, waits for them, and re-layouts  53 us
    ppermute x10, waiting for transfers between devices, one_way(): return lax.ppermute(x, 'ctx', hops)  44.5 us
    pallas_call x5, Pallas kernels, unproject_kernel(): pl.pallas_call(unproject_body, grid=(width // tile,), in_specs=[pl.BlockS...  43.5 us
    pallas_call x5, Pallas kernels, project_kernel(): pl.pallas_call(functools.partial(project_body, len(pieces)), grid=(4,), i...  32.7 us
    ppermute x10, waiting for transfers between devices, across(): return None if x is None else lax.ppermute(x, 'tp', [(0, 1), (1, 0)])  30.9 us
    pallas_call x1, Pallas kernels, mix(): pl.pallas_call(functools.partial(mix_body, count, sets, per_step, grouped...  19.3 us
    ppermute x17, waiting for transfers between devices, swap(): return lax.ppermute(x, 'ctx', [(d, d ^ 1) for d in range(n_ctx)])  17.9 us
    ppermute x17, starting transfers between devices, swap(): return lax.ppermute(x, 'ctx', [(d, d ^ 1) for d in range(n_ctx)])  13.9 us
  transfers between devices with their start and end apart: 39, of which 28 were waited for; matrix products, arithmetic and copies ran while one was open for 1% of the time, Pallas kernels for 25%

profile of v3, /device:TPU:1, one launch (start us, length us, event | category | flops | bytes accessed | tf_op | source)
XLA Modules:
  0.0 308.6 jit_solution(16131405225685642118)
XLA Ops:
  0.8 2.7 collective-permute-start.1
  3.5 2.2 copy-done.7
  5.7 2.2 copy-done.8
  7.8 2.2 copy-done.9
  10.0 1.7 shard_map.111
  11.8 4.6 %copy-done = bf16[2,3,256,4096]{3,2,1,0:T(8,128)(2,1)} copy-done((bf16[2,3,256,4096]{3,2,1,0:T(8,128)(2,1)}, bf16[2,3,256,4096]{3,2,1,0:T(8,128)(2,1)S(1)}, u32[]{:S(2)}) %copy-start) | copy-done | bytes 12582936
  17.8 4.6 %copy-done.1 = bf16[2,3,256,4096]{3,2,1,0:T(8,128)(2,1)S(1)} copy-done((bf16[2,3,256,4096]{3,2,1,0:T(8,128)(2,1)S(1)}, bf16[2,3,256,4096]{3,2,1,0:T(8,128)(2,1)}, u32[]{:S(2)}) %copy-start.1) | copy-done | bytes 12582936
  22.3 4.3 %shard_map.112 = (bf16[768,256]{1,0:T(8,128)(2,1)S(1)}, bf16[768,256]{1,0:T(8,128)(2,1)S(1)}) custom-call(bf16[128,4096]{1,0:T(8,128)(2,1)S(1)} %copy-done.10, bf16[128,4096]{1,0:T(8,128)(2,1)S(1)} %collective-permute-done.2.refs_1_, bf16[1536,4096]{1,0:T(8,128)(2,1)S(1)} %bitcast.28), custom_call_target="tpu_custom_call" | custom-call | flops 1 | bytes 1 | tf_op jit(solution)/shard_map/pallas_call | solution.py:250
  33.1 7.8 %shard_map.113 = (bf16[768,512]{1,0:T(8,128)(2,1)S(1)}, bf16[768,512]{1,0:T(8,128)(2,1)S(1)}) custom-call(bf16[256,4096]{1,0:T(8,128)(2,1)S(1)} %constant_dynamic-update-slice_fusion.refs_0_, bf16[256,4096]{1,0:T(8,128)(2,1)S(1)} %collective-permute-done.4.refs_1_, bf16[1536,4096]{1,0:T(8,128)(2,1)S(1)} %bitcast.29), custom_call_target="tpu_custom_call" | custom-call | flops 1 | bytes 1 | tf_op jit(solution)/shard_map/pallas_call | solution.py:250
  41.8 12.7 %collective-permute-done.3.refs_0_ = bf16[256,4096]{1,0:T(8,128)(2,1)S(1)} collective-permute-done((bf16[256,4096]{1,0:T(8,128)(2,1)S(1)}, bf16[256,4096]{1,0:T(8,128)(2,1)S(1)}, u32[]{:S(2)}, u32[]{:S(2)}) %collective-permute-start.3) | collective-permute-done | bytes 2097184 | tf_op jit(solution)/shard_map/ppermute | solution.py:352
  59.3 8.5 %shard_map.114 = (bf16[768,512]{1,0:T(8,128)(2,1)}, bf16[768,512]{1,0:T(8,128)(2,1)S(1)}) custom-call(bf16[256,4096]{1,0:T(8,128)(2,1)S(1)} %collective-permute-done.3.refs_0_, bf16[256,4096]{1,0:T(8,128)(2,1)S(1)} %collective-permute-done.7.refs_1_, bf16[1536,4096]{1,0:T(8,128)(2,1)S(1)} %bitcast.30), custom_call_target="tpu_custom_call" | custom-call | flops 1 | bytes 1 | tf_op jit(solution)/shard_map/pallas_call | solution.py:250
  67.9 7.4 %collective-permute-done.8 = bf16[768,512]{1,0:T(8,128)(2,1)S(1)} collective-permute-done((bf16[768,512]{1,0:T(8,128)(2,1)S(1)}, bf16[768,512]{1,0:T(8,128)(2,1)S(1)}, u32[]{:S(2)}, u32[]{:S(2)}) %collective-permute-start.8) | collective-permute-done | bytes 786464 | tf_op jit(solution)/shard_map/ppermute | solution.py:382
  75.3 5.7 %collective-permute-done.6.refs_0_ = bf16[256,4096]{1,0:T(8,128)(2,1)S(1)} collective-permute-done((bf16[256,4096]{1,0:T(8,128)(2,1)S(1)}, bf16[256,4096]{1,0:T(8,128)(2,1)S(1)}, u32[]{:S(2)}, u32[]{:S(2)}) %collective-permute-start.6) | collective-permute-done | bytes 2097184 | tf_op jit(solution)/shard_map/ppermute | solution.py:352
  85.3 7.8 %shard_map.115 = (bf16[768,512]{1,0:T(8,128)(2,1)S(1)}, bf16[768,512]{1,0:T(8,128)(2,1)S(1)}) custom-call(bf16[256,4096]{1,0:T(8,128)(2,1)S(1)} %collective-permute-done.6.refs_0_, bf16[256,4096]{1,0:T(8,128)(2,1)S(1)} %collective-permute-done.10.refs_1_, bf16[1536,4096]{1,0:T(8,128)(2,1)S(1)} %bitcast.31), custom_call_target="tpu_custom_call" | custom-call | flops 1 | bytes 1 | tf_op jit(solution)/shard_map/pallas_call | solution.py:250
  94.0 2.1 collective-permute-done.9.refs_0_
  96.1 6.4 %all-to-all-start = ((bf16[16,256,128]{2,1,0:T(8,128)(2,1)}), bf16[16,256,128]{2,1,0:T(8,128)(2,1)S(1)}, u32[]{:S(2)}, u32[]{:S(2)}) async-start(bf16[16,256,128]{2,1,0:T(8,128)(2,1)} %bitcast.55), calls=%async_computation | async-start | bytes 2097152 | tf_op jit(solution)/shard_map/all_to_all | solution.py:411
  105.1 1.5 collective-permute-done.13.refs_2_
  107.3 4.6 %copy-done.2 = bf16[2,3,256,4096]{3,2,1,0:T(8,128)(2,1)S(1)} copy-done((bf16[2,3,256,4096]{3,2,1,0:T(8,128)(2,1)S(1)}, bf16[2,3,256,4096]{3,2,1,0:T(8,128)(2,1)}, u32[]{:S(2)}) %copy-start.2) | copy-done | bytes 12582936
  111.9 4.3 %shard_map.116 = (bf16[768,256]{1,0:T(8,128)(2,1)S(1)}, bf16[768,256]{1,0:T(8,128)(2,1)S(1)}) custom-call(bf16[128,4096]{1,0:T(8,128)(2,1)S(1)} %collective-permute-done.9.refs_0_, bf16[64,4096]{1,0:T(8,128)(2,1)S(1)} %collective-permute-done.12.refs_1_, bf16[64,4096]{1,0:T(8,128)(2,1)S(1)} %collective-permute-done.13.refs_2_, bf16[1536,4096]{1,0:T(8,128)(2,1)S(1)} %bitcast.32), custom_call_target="tpu_custom_call" | custom-call | flops 1 | bytes 1 | tf_op jit(solution)/shard_map/pallas_call | solution.py:250
  117.0 4.1 %collective-permute-done.14 = bf16[768,512]{1,0:T(8,128)(2,1)S(1)} collective-permute-done((bf16[768,512]{1,0:T(8,128)(2,1)}, bf16[768,512]{1,0:T(8,128)(2,1)S(1)}, u32[]{:S(2)}, u32[]{:S(2)}) %collective-permute-start.14) | collective-permute-done | bytes 786464 | tf_op jit(solution)/shard_map/ppermute | solution.py:382
  123.2 7.7 %collective-permute-done.15 = bf16[768,256]{1,0:T(8,128)(2,1)S(1)} collective-permute-done((bf16[768,256]{1,0:T(8,128)(2,1)S(1)}, bf16[768,256]{1,0:T(8,128)(2,1)S(1)}, u32[]{:S(2)}, u32[]{:S(2)}) %collective-permute-start.15) | collective-permute-done | bytes 393248 | tf_op jit(solution)/shard_map/ppermute | solution.py:382
  139.5 19.3 %shard_map.117 = (bf16[16,256,128]{2,1,0:T(8,128)(2,1)}, bf16[3,256,256]{2,1,0:T(8,128)(2,1)S(1)}, bf16[3,256,512]{2,1,0:T(8,128)(2,1)S(1)}, bf16[3,256,512]{2,1...) custom-call(s32[16]{0:T(128)S(1)} %dynamic-slice_bitcast_fusion.orde, ...), custom_call_target="tpu_custom_call" | custom-call | flops 1 | bytes 1 | tf_op jit(solution)/shard_map/pallas_call | solution.py:152
  158.8 8.8 %all-to-all-start.1 = ((bf16[16,256,128]{2,1,0:T(8,128)(2,1)}), bf16[16,256,128]{2,1,0:T(8,128)(2,1)}, u32[]{:S(2)}, u32[]{:S(2)}) async-start(bf16[16,256,128]{2,1,0:T(8,128)(2,1)} %get-tuple-element.139), calls=%async_computation.1 | async-start | bytes 2097152 | tf_op jit(solution)/shard_map/all_to_all | solution.py:429
  169.1 9.2 %collective-permute-done.16.far_ref = bf16[768,256]{1,0:T(8,128)(2,1)S(1)} collective-permute-done((bf16[768,256]{1,0:T(8,128)(2,1)S(1)}, bf16[768,256]{1,0:T(8,128)(2,1)S(1)}, u32[]{:S(2)}, u32[]{:S(2)}) %collective-permute-start.16) | collective-permute-done | bytes 393248 | tf_op jit(solution)/shard_map/ppermute | solution.py:382
  178.3 4.6 %copy-done.3 = bf16[2,3,256,4096]{3,2,1,0:T(8,128)(2,1)S(1)} copy-done((bf16[2,3,256,4096]{3,2,1,0:T(8,128)(2,1)S(1)}, bf16[2,3,256,4096]{3,2,1,0:T(8,128)(2,1)}, u32[]{:S(2)}) %copy-start.3) | copy-done | bytes 12582936
  182.9 6.0 %shard_map.118 = (bf16[128,4096]{1,0:T(8,128)(2,1)S(1)}, bf16[64,4096]{1,0:T(8,128)(2,1)S(1)}, bf16[64,4096]{1,0:T(8,128)(2,1)S(1)}) custom-call(bf16[768,256]{1,0:T(8,128)(2,1)S(1)} %bitcast.48, bf16[768,256]{1,0:T(8,128)(2,1)S(1)} %collective-permute-done.16.far_ref, bf16[1536,4096]{1,0:T(8,128)(2,1)S(1)} %bitcast.33), custom_call_target="tpu_custom_call" | custom-call | flops 1 | bytes 1 | tf_op jit(solution)/shard_map/pallas_call | solution.py:287
  188.9 1.5 collective-permute-start.17
  193.3 1.8 collective-permute-done.19.far_ref
  197.2 4.6 %copy-done.4 = bf16[2,3,256,4096]{3,2,1,0:T(8,128)(2,1)S(1)} copy-done((bf16[2,3,256,4096]{3,2,1,0:T(8,128)(2,1)S(1)}, bf16[2,3,256,4096]{3,2,1,0:T(8,128)(2,1)}, u32[]{:S(2)}) %copy-start.4) | copy-done | bytes 12582936
  202.9 10.6 %shard_map.120 = (bf16[256,4096]{1,0:T(8,128)(2,1)S(1)}, bf16[96,4096]{1,0:T(8,128)(2,1)S(1)}, bf16[80,4096]{1,0:T(8,128)(2,1)S(1)}, bf16[80,4096]{1,0:T(8,128)(2,1)S(1)}) custom-call(bf16[768,512]{1,0:T(8,128)(2,1)} %bitcast.18.near_ref, bf16[768,512]{1,0:T(8,128)(2,1)S(1)} %copy-done.12, bf16[1536,4096]{1,0:T(8,128)(2,1)S(1)} %bitcast.34), custom_call_target="tpu_custom_call" | custom-call | flops 1 | bytes 1 | tf_op jit(solution)/shard_map/pallas_call | solution.py:287
  213.4 2.3 collective-permute-start.21
  216.3 2.3 collective-permute-done.22.refs_2_
  222.2 4.6 %copy-done.5 = bf16[2,3,256,4096]{3,2,1,0:T(8,128)(2,1)S(1)} copy-done((bf16[2,3,256,4096]{3,2,1,0:T(8,128)(2,1)S(1)}, bf16[2,3,256,4096]{3,2,1,0:T(8,128)(2,1)}, u32[]{:S(2)}) %copy-start.5) | copy-done | bytes 12582936
  226.7 10.7 %shard_map.122 = (bf16[256,4096]{1,0:T(8,128)(2,1)S(1)}, bf16[128,4096]{1,0:T(8,128)(2,1)S(1)}, bf16[128,4096]{1,0:T(8,128)(2,1)S(1)}) custom-call(bf16[768,512]{1,0:T(8,128)(2,1)} %bitcast.20.near_ref, bf16[768,512]{1,0:T(8,128)(2,1)S(1)} %collective-permute-done.20.far_ref, bf16[1536,4096]{1,0:T(8,128)(2,1)S(1)} %bitcast.35), custom_call_target="tpu_custom_call" | custom-call | flops 1 | bytes 1 | tf_op jit(solution)/shard_map/pallas_call | solution.py:287
  238.2 2.7 collective-permute-start.26
  240.9 2.3 collective-permute-done.26.refs_1_
  243.2 1.5 collective-permute-done.27.refs_2_
  248.8 9.5 %shard_map.124 = (bf16[256,4096]{1,0:T(8,128)(2,1)S(1)}, bf16[128,4096]{1,0:T(8,128)(2,1)S(1)}, bf16[128,4096]{1,0:T(8,128)(2,1)S(1)}) custom-call(bf16[768,512]{1,0:T(8,128)(2,1)S(1)} %bitcast.39, bf16[768,512]{1,0:T(8,128)(2,1)S(1)} %collective-permute-done.25.far_ref, bf16[1536,4096]{1,0:T(8,128)(2,1)S(1)} %bitcast.36), custom_call_target="tpu_custom_call" | custom-call | flops 1 | bytes 1 | tf_op jit(solution)/shard_map/pallas_call | solution.py:287
  258.4 3.0 collective-permute-start.30
  261.4 2.2 collective-permute-done.30.refs_1_
  263.6 1.5 collective-permute-done.31.refs_2_
  265.1 7.5 %collective-permute-done.32.refs_3_ = bf16[256,4096]{1,0:T(8,128)(2,1)S(1)} collective-permute-done((bf16[256,4096]{1,0:T(8,128)(2,1)S(1)}, bf16[256,4096]{1,0:T(8,128)(2,1)S(1)}, u32[]{:S(2)}, u32[]{:S(2)}) %collective-permute-start.32) | collective-permute-done | bytes 2097184 | tf_op jit(solution)/shard_map/ppermute | solution.py:352
  272.6 2.4 shard_map.125
  275.0 3.7 %collective-permute-start.36 = (bf16[128,4096]{1,0:T(8,128)(2,1)}, bf16[128,4096]{1,0:T(8,128)(2,1)S(1)}, u32[]{:S(2)}, u32[]{:S(2)}) collective-permute-start(bf16[128,4096]{1,0:T(8,128)(2,1)} %get-tuple-element.187), channel_id=1, source_target_pairs={{0,6},{2,8},{8,2},{10,16},{16,10},{18,24},{24,18},{26,28},{28,26},... | collective-permute-start | bytes 3145736 | tf_op jit(solution)/shard_map/ppermute | solution.py:352
  278.7 6.7 %shard_map.126 = (bf16[128,4096]{1,0:T(8,128)(2,1)S(1)}, bf16[64,4096]{1,0:T(8,128)(2,1)}, bf16[64,4096]{1,0:T(8,128)(2,1)}) custom-call(bf16[768,256]{1,0:T(8,128)(2,1)S(1)} %bitcast.46, bf16[768,256]{1,0:T(8,128)(2,1)S(1)} %collective-permute-done.29.far_ref, bf16[1536,4096]{1,0:T(8,128)(2,1)S(1)} %bitcast.37), custom_call_target="tpu_custom_call" | custom-call | flops 1 | bytes 1 | tf_op jit(solution)/shard_map/pallas_call | solution.py:287
  289.1 13.5 %collective-permute-done.36.refs_4_ = bf16[128,4096]{1,0:T(8,128)(2,1)S(1)} collective-permute-done((bf16[128,4096]{1,0:T(8,128)(2,1)}, bf16[128,4096]{1,0:T(8,128)(2,1)S(1)}, u32[]{:S(2)}, u32[]{:S(2)}) %collective-permute-start.36) | collective-permute-done | bytes 1048608 | tf_op jit(solution)/shard_map/ppermute | solution.py:352
  302.6 3.7 %shard_map.127 = bf16[128,4096]{1,0:T(8,128)(2,1)} custom-call(bf16[128,4096]{1,0:T(8,128)(2,1)S(1)} %get-tuple-element.183.refs_0_, bf16[64,4096]{1,0:T(8,128)(2,1)} %collective-permute-done.33.refs_1_, bf16[64,4096]{1,0:T(8,128)(2,1)} %collective-permute-done.34.refs_2_, bf16[128,4096]{1,0:T(8,128)(2,1)S(1)} %collective-permute-done.35.refs_3_, ...), custom_call_target="tpu_custom_call" | custom-call | flops 1 | bytes 1 | tf_op jit(solution)/shard_map/pallas_call | solution.py:327
  306.3 2.3 copy.21
  (126 shorter events, 54.0 us)
Async XLA Ops:
  0.6 17.1 %collective-permute-start.2 = (bf16[128,4096]{1,0:T(8,128)(2,1)}, bf16[128,4096]{1,0:T(8,128)(2,1)S(1)}, u32[]{:S(2)}, u32[]{:S(2)}) collective-permute-start(bf16[128,4096]{1,0:T(8,128)(2,1)} %refs_0_.3), channel_id=1, source_target_pairs={{0,2},{2,0},{4,6},{6,4},{8,10},{10,8},{12,14},{14,12},{16,18},{18,... | collective-permute-start | bytes 3145736 | tf_op jit(solution)/shard_map/ppermute | solution.py:355
  0.8 25.9 %collective-permute-start.1 = (bf16[128,4096]{1,0:T(8,128)(2,1)}, bf16[128,4096]{1,0:T(8,128)(2,1)S(1)}, u32[]{:S(2)}, u32[]{:S(2)}) collective-permute-start(bf16[128,4096]{1,0:T(8,128)(2,1)} %refs_0_.3), channel_id=1, source_target_pairs={{0,6},{2,8},{8,2},{10,16},{16,10},{18,24},{24,18},{26,28},{28,26},... | collective-permute-start | bytes 3145736 | tf_op jit(solution)/shard_map/ppermute | solution.py:352
  3.5 24.0 %collective-permute-start = (bf16[128,4096]{1,0:T(8,128)(2,1)}, bf16[128,4096]{1,0:T(8,128)(2,1)}, u32[]{:S(2)}, u32[]{:S(2)}) collective-permute-start(bf16[128,4096]{1,0:T(8,128)(2,1)} %refs_0_.3), channel_id=1, source_target_pairs={{0,8},{2,6},{8,16},{10,2},{16,24},{18,10},{24,28},{26,18},{28,20},... | collective-permute-start | bytes 3145736 | tf_op jit(solution)/shard_map/ppermute | solution.py:352
  10.0 6.3 %copy-start.33 = (f32[3,1,16,3]{2,1,3,0:T(1,128)S(1)}, f32[3,1,16,3]{2,1,3,0:T(1,128)}, u32[]{:S(2)}) copy-start(f32[3,1,16,3]{2,1,3,0:T(1,128)} %param.12) | copy-start | bytes 1732
  10.0 7.7 %copy-start.10 = (bf16[128,4096]{1,0:T(8,128)(2,1)S(1)}, bf16[128,4096]{1,0:T(8,128)(2,1)}, u32[]{:S(2)}) copy-start(bf16[128,4096]{1,0:T(8,128)(2,1)} %refs_0_.3) | copy-start | bytes 3145732
  28.9 4.2 %collective-permute-start.4 = (bf16[256,4096]{1,0:T(8,128)(2,1)S(1)}, bf16[256,4096]{1,0:T(8,128)(2,1)S(1)}, u32[]{:S(2)}, u32[]{:S(2)}) collective-permute-start(bf16[256,4096]{1,0:T(8,128)(2,1)S(1)} %constant_dynamic-update-slice_fusion.refs_0_), channel_id=1, source_target_pairs={{0,2},{2,0},{4,6},{6,4},{8,10},{10,8},{12,14},{14,12},{16,18},{18,... | collective-permute-start | bytes 6291464 | tf_op jit(solution)/shard_map/ppermute | solution.py:355
  29.3 25.2 %collective-permute-start.3 = (bf16[256,4096]{1,0:T(8,128)(2,1)S(1)}, bf16[256,4096]{1,0:T(8,128)(2,1)S(1)}, u32[]{:S(2)}, u32[]{:S(2)}) collective-permute-start(bf16[256,4096]{1,0:T(8,128)(2,1)S(1)} %constant_dynamic-update-slice_fusion.refs_0_), channel_id=1, source_target_pairs={{0,8},{2,6},{8,16},{10,2},{16,24},{18,10},{24,28},{26,18},{28,20},... | collective-permute-start | bytes 6291464 | tf_op jit(solution)/shard_map/ppermute | solution.py:352
  30.7 11.0 %collective-permute-start.5 = (bf16[768,256]{1,0:T(8,128)(2,1)S(1)}, bf16[768,256]{1,0:T(8,128)(2,1)S(1)}, u32[]{:S(2)}, u32[]{:S(2)}) collective-permute-start(bf16[768,256]{1,0:T(8,128)(2,1)S(1)} %get-tuple-element.107), channel_id=1, source_target_pairs={{0,1},{1,0},{2,3},{3,2},{4,5},{5,4},{6,7},{7,6},{8,9},{9,8},{10,11... | collective-permute-start | bytes 1179656 | tf_op jit(solution)/shard_map/ppermute | solution.py:382
  41.8 26.1 %copy-start.25 = (bf16[768,256]{1,0:T(8,128)(2,1)}, bf16[768,256]{1,0:T(8,128)(2,1)S(1)}, u32[]{:S(2)}) copy-start(bf16[768,256]{1,0:T(8,128)(2,1)S(1)} %collective-permute-done.5) | copy-start | bytes 1179652
  54.5 4.8 %collective-permute-start.7 = (bf16[256,4096]{1,0:T(8,128)(2,1)S(1)}, bf16[256,4096]{1,0:T(8,128)(2,1)S(1)}, u32[]{:S(2)}, u32[]{:S(2)}) collective-permute-start(bf16[256,4096]{1,0:T(8,128)(2,1)S(1)} %collective-permute-done.3.refs_0_), channel_id=1, source_target_pairs={{0,2},{2,0},{4,6},{6,4},{8,10},{10,8},{12,14},{14,12},{16,18},{18,... | collective-permute-start | bytes 6291464 | tf_op jit(solution)/shard_map/ppermute | solution.py:355
  55.5 25.5 %collective-permute-start.6 = (bf16[256,4096]{1,0:T(8,128)(2,1)S(1)}, bf16[256,4096]{1,0:T(8,128)(2,1)S(1)}, u32[]{:S(2)}, u32[]{:S(2)}) collective-permute-start(bf16[256,4096]{1,0:T(8,128)(2,1)S(1)} %collective-permute-done.3.refs_0_), channel_id=1, source_target_pairs={{0,8},{2,6},{8,16},{10,2},{16,24},{18,10},{24,28},{26,18},{28,20},... | collective-permute-start | bytes 6291464 | tf_op jit(solution)/shard_map/ppermute | solution.py:352
  56.9 18.4 %collective-permute-start.8 = (bf16[768,512]{1,0:T(8,128)(2,1)S(1)}, bf16[768,512]{1,0:T(8,128)(2,1)S(1)}, u32[]{:S(2)}, u32[]{:S(2)}) collective-permute-start(bf16[768,512]{1,0:T(8,128)(2,1)S(1)} %get-tuple-element.112), channel_id=1, source_target_pairs={{0,1},{1,0},{2,3},{3,2},{4,5},{5,4},{6,7},{7,6},{8,9},{9,8},{10,11... | collective-permute-start | bytes 2359304 | tf_op jit(solution)/shard_map/ppermute | solution.py:382
  67.8 15.2 %copy-start.17 = (bf16[768,512]{1,0:T(8,128)(2,1)}, bf16[768,512]{1,0:T(8,128)(2,1)S(1)}, u32[]{:S(2)}) copy-start(bf16[768,512]{1,0:T(8,128)(2,1)S(1)} %get-tuple-element.121) | copy-start | bytes 2359300
  75.3 17.8 %copy-start.15 = (bf16[768,512]{1,0:T(8,128)(2,1)}, bf16[768,512]{1,0:T(8,128)(2,1)S(1)}, u32[]{:S(2)}) copy-start(bf16[768,512]{1,0:T(8,128)(2,1)S(1)} %collective-permute-done.8) | copy-start | bytes 2359300
  81.0 4.3 %collective-permute-start.10 = (bf16[256,4096]{1,0:T(8,128)(2,1)S(1)}, bf16[256,4096]{1,0:T(8,128)(2,1)S(1)}, u32[]{:S(2)}, u32[]{:S(2)}) collective-permute-start(bf16[256,4096]{1,0:T(8,128)(2,1)S(1)} %collective-permute-done.6.refs_0_), channel_id=1, source_target_pairs={{0,2},{2,0},{4,6},{6,4},{8,10},{10,8},{12,14},{14,12},{16,18},{18,... | collective-permute-start | bytes 6291464 | tf_op jit(solution)/shard_map/ppermute | solution.py:355
  81.6 14.4 %collective-permute-start.9 = (bf16[128,4096]{1,0:T(8,128)(2,1)S(1)}, bf16[128,4096]{1,0:T(8,128)(2,1)S(1)}, u32[]{:S(2)}, u32[]{:S(2)}) collective-permute-start(bf16[128,4096]{1,0:T(8,128)(2,1)S(1)} %slice.9), channel_id=1, source_target_pairs={{0,8},{2,6},{8,16},{10,2},{16,24},{18,10},{24,28},{26,18},{28,20},... | collective-permute-start | bytes 3145736 | tf_op jit(solution)/shard_map/ppermute | solution.py:352
  83.1 19.4 %collective-permute-start.11 = (bf16[768,512]{1,0:T(8,128)(2,1)}, bf16[768,512]{1,0:T(8,128)(2,1)}, u32[]{:S(2)}, u32[]{:S(2)}) collective-permute-start(bf16[768,512]{1,0:T(8,128)(2,1)} %get-tuple-element.120), channel_id=1, source_target_pairs={{0,1},{1,0},{2,3},{3,2},{4,5},{5,4},{6,7},{7,6},{8,9},{9,8},{10,11... | collective-permute-start | bytes 2359304 | tf_op jit(solution)/shard_map/ppermute | solution.py:382
  96.1 34.8 %all-to-all-start = ((bf16[16,256,128]{2,1,0:T(8,128)(2,1)}), bf16[16,256,128]{2,1,0:T(8,128)(2,1)S(1)}, u32[]{:S(2)}, u32[]{:S(2)}) async-start(bf16[16,256,128]{2,1,0:T(8,128)(2,1)} %bitcast.55), calls=%async_computation | async-start | bytes 2097152 | tf_op jit(solution)/shard_map/all_to_all | solution.py:411
  102.5 18.6 %collective-permute-start.14 = (bf16[768,512]{1,0:T(8,128)(2,1)}, bf16[768,512]{1,0:T(8,128)(2,1)S(1)}, u32[]{:S(2)}, u32[]{:S(2)}) collective-permute-start(bf16[768,512]{1,0:T(8,128)(2,1)} %copy-done.32), channel_id=1, source_target_pairs={{0,1},{1,0},{2,3},{3,2},{4,5},{5,4},{6,7},{7,6},{8,9},{9,8},{10,11... | collective-permute-start | bytes 2359304 | tf_op jit(solution)/shard_map/ppermute | solution.py:382
  103.9 2.7 collective-permute-start.13
  105.0 2.3 collective-permute-start.12
  111.9 19.0 %copy-start.30 = (f32[3,1,16,3]{3,2,0,1:T(8,128)S(1)}, f32[3,1,16,3]{3,2,0,1:T(8,128)}, u32[]{:S(2)}) copy-start(f32[3,1,16,3]{3,2,0,1:T(8,128)} %copy.15) | copy-start | bytes 1732
  111.9 19.0 %copy-start.31 = (f32[1,16,128]{2,1,0:T(8,128)S(1)}, f32[1,16,128]{2,1,0:T(8,128)}, u32[]{:S(2)}) copy-start(f32[1,16,128]{2,1,0:T(8,128)} %param.13) | copy-start | bytes 24580
  121.9 8.9 %collective-permute-start.15 = (bf16[768,256]{1,0:T(8,128)(2,1)S(1)}, bf16[768,256]{1,0:T(8,128)(2,1)S(1)}, u32[]{:S(2)}, u32[]{:S(2)}) collective-permute-start(bf16[768,256]{1,0:T(8,128)(2,1)S(1)} %get-tuple-element.131), channel_id=1, source_target_pairs={{0,1},{1,0},{2,3},{3,2},{4,5},{5,4},{6,7},{7,6},{8,9},{9,8},{10,11... | collective-permute-start | bytes 1179656 | tf_op jit(solution)/shard_map/ppermute | solution.py:382
  158.8 30.1 %copy-start.29 = (f32[8,2,9,128]{3,2,1,0:T(8,128)}, f32[8,2,9,128]{3,2,1,0:T(8,128)S(1)}, u32[]{:S(2)}) copy-start(f32[8,2,9,128]{3,2,1,0:T(8,128)S(1)} %get-tuple-element.188) | copy-start | bytes 221188
  158.8 37.1 %all-to-all-start.1 = ((bf16[16,256,128]{2,1,0:T(8,128)(2,1)}), bf16[16,256,128]{2,1,0:T(8,128)(2,1)}, u32[]{:S(2)}, u32[]{:S(2)}) async-start(bf16[16,256,128]{2,1,0:T(8,128)(2,1)} %get-tuple-element.139), calls=%async_computation.1 | async-start | bytes 2097152 | tf_op jit(solution)/shard_map/all_to_all | solution.py:429
  167.6 10.7 %collective-permute-start.16 = (bf16[768,256]{1,0:T(8,128)(2,1)S(1)}, bf16[768,256]{1,0:T(8,128)(2,1)S(1)}, u32[]{:S(2)}, u32[]{:S(2)}) collective-permute-start(bf16[768,256]{1,0:T(8,128)(2,1)S(1)} %bitcast.47), channel_id=1, source_target_pairs={{0,1},{1,0},{2,3},{3,2},{4,5},{5,4},{6,7},{7,6},{8,9},{9,8},{10,11... | collective-permute-start | bytes 1179656 | tf_op jit(solution)/shard_map/ppermute | solution.py:382
  168.9 26.2 %collective-permute-start.19 = (bf16[768,512]{1,0:T(8,128)(2,1)}, bf16[768,512]{1,0:T(8,128)(2,1)S(1)}, u32[]{:S(2)}, u32[]{:S(2)}) collective-permute-start(bf16[768,512]{1,0:T(8,128)(2,1)} %bitcast.18.near_ref), channel_id=1, source_target_pairs={{0,1},{1,0},{2,3},{3,2},{4,5},{5,4},{6,7},{7,6},{8,9},{9,8},{10,11... | collective-permute-start | bytes 2359304 | tf_op jit(solution)/shard_map/ppermute | solution.py:382
  188.9 3.0 collective-permute-start.17
  190.4 2.3 collective-permute-start.18
  190.5 22.9 %collective-permute-start.20 = (bf16[768,512]{1,0:T(8,128)(2,1)}, bf16[768,512]{1,0:T(8,128)(2,1)S(1)}, u32[]{:S(2)}, u32[]{:S(2)}) collective-permute-start(bf16[768,512]{1,0:T(8,128)(2,1)} %bitcast.20.near_ref), channel_id=1, source_target_pairs={{0,1},{1,0},{2,3},{3,2},{4,5},{5,4},{6,7},{7,6},{8,9},{9,8},{10,11... | collective-permute-start | bytes 2359304 | tf_op jit(solution)/shard_map/ppermute | solution.py:382
  196.0 23.6 %collective-permute-start.24 = (bf16[128,4096]{1,0:T(8,128)(2,1)S(1)}, bf16[128,4096]{1,0:T(8,128)(2,1)S(1)}, u32[]{:S(2)}, u32[]{:S(2)}) collective-permute-start(bf16[128,4096]{1,0:T(8,128)(2,1)S(1)} %shard_map.119), channel_id=1, source_target_pairs={{0,4},{2,10},{8,0},{10,18},{16,8},{18,26},{24,16},{26,30},{28,24},... | collective-permute-start | bytes 3145736 | tf_op jit(solution)/shard_map/ppermute | solution.py:352
  213.4 6.1 %collective-permute-start.21 = (bf16[96,4096]{1,0:T(8,128)(2,1)S(1)}, bf16[96,4096]{1,0:T(8,128)(2,1)S(1)}, u32[]{:S(2)}, u32[]{:S(2)}) collective-permute-start(bf16[96,4096]{1,0:T(8,128)(2,1)S(1)} %get-tuple-element.148), channel_id=1, source_target_pairs={{0,2},{2,0},{4,6},{6,4},{8,10},{10,8},{12,14},{14,12},{16,18},{18,... | collective-permute-start | bytes 2359304 | tf_op jit(solution)/shard_map/ppermute | solution.py:355
  215.8 2.8 collective-permute-start.22
  215.9 3.7 %collective-permute-start.23 = (bf16[80,4096]{1,0:T(8,128)(2,1)S(1)}, bf16[80,4096]{1,0:T(8,128)(2,1)S(1)}, u32[]{:S(2)}, u32[]{:S(2)}) collective-permute-start(bf16[80,4096]{1,0:T(8,128)(2,1)S(1)} %get-tuple-element.150), channel_id=1, source_target_pairs={{0,2},{2,0},{4,6},{6,4},{8,10},{10,8},{12,14},{14,12},{16,18},{18,... | collective-permute-start | bytes 1966088 | tf_op jit(solution)/shard_map/ppermute | solution.py:355
  220.8 25.2 %collective-permute-start.28 = (bf16[256,4096]{1,0:T(8,128)(2,1)S(1)}, bf16[256,4096]{1,0:T(8,128)(2,1)S(1)}, u32[]{:S(2)}, u32[]{:S(2)}) collective-permute-start(bf16[256,4096]{1,0:T(8,128)(2,1)S(1)} %shard_map.121), channel_id=1, source_target_pairs={{0,4},{2,10},{8,0},{10,18},{16,8},{18,26},{24,16},{26,30},{28,24},... | collective-permute-start | bytes 6291464 | tf_op jit(solution)/shard_map/ppermute | solution.py:352
  220.8 17.3 %collective-permute-start.25 = (bf16[768,512]{1,0:T(8,128)(2,1)S(1)}, bf16[768,512]{1,0:T(8,128)(2,1)S(1)}, u32[]{:S(2)}, u32[]{:S(2)}) collective-permute-start(bf16[768,512]{1,0:T(8,128)(2,1)S(1)} %bitcast.38), channel_id=1, source_target_pairs={{0,1},{1,0},{2,3},{3,2},{4,5},{5,4},{6,7},{7,6},{8,9},{9,8},{10,11... | collective-permute-start | bytes 2359304 | tf_op jit(solution)/shard_map/ppermute | solution.py:382
  226.7 22.0 %copy-start.6 = (bf16[2,3,256,4096]{3,2,1,0:T(8,128)(2,1)S(1)}, bf16[2,3,256,4096]{3,2,1,0:T(8,128)(2,1)}, u32[]{:S(2)}) copy-start(bf16[2,3,256,4096]{3,2,1,0:T(8,128)(2,1)} %copy-done) | copy-start | bytes 37748740
  238.2 5.0 %collective-permute-start.26 = (bf16[128,4096]{1,0:T(8,128)(2,1)S(1)}, bf16[128,4096]{1,0:T(8,128)(2,1)S(1)}, u32[]{:S(2)}, u32[]{:S(2)}) collective-permute-start(bf16[128,4096]{1,0:T(8,128)(2,1)S(1)} %get-tuple-element.162), channel_id=1, source_target_pairs={{0,2},{2,0},{4,6},{6,4},{8,10},{10,8},{12,14},{14,12},{16,18},{18,... | collective-permute-start | bytes 3145736 | tf_op jit(solution)/shard_map/ppermute | solution.py:355
  240.9 3.8 %collective-permute-start.27 = (bf16[128,4096]{1,0:T(8,128)(2,1)S(1)}, bf16[128,4096]{1,0:T(8,128)(2,1)S(1)}, u32[]{:S(2)}, u32[]{:S(2)}) collective-permute-start(bf16[128,4096]{1,0:T(8,128)(2,1)S(1)} %get-tuple-element.163), channel_id=1, source_target_pairs={{0,2},{2,0},{4,6},{6,4},{8,10},{10,8},{12,14},{14,12},{16,18},{18,... | collective-permute-start | bytes 3145736 | tf_op jit(solution)/shard_map/ppermute | solution.py:355
  247.4 25.2 %collective-permute-start.32 = (bf16[256,4096]{1,0:T(8,128)(2,1)S(1)}, bf16[256,4096]{1,0:T(8,128)(2,1)S(1)}, u32[]{:S(2)}, u32[]{:S(2)}) collective-permute-start(bf16[256,4096]{1,0:T(8,128)(2,1)S(1)} %shard_map.123), channel_id=1, source_target_pairs={{0,4},{2,10},{8,0},{10,18},{16,8},{18,26},{24,16},{26,30},{28,24},... | collective-permute-start | bytes 6291464 | tf_op jit(solution)/shard_map/ppermute | solution.py:352
  247.5 10.9 %collective-permute-start.29 = (bf16[768,256]{1,0:T(8,128)(2,1)S(1)}, bf16[768,256]{1,0:T(8,128)(2,1)S(1)}, u32[]{:S(2)}, u32[]{:S(2)}) collective-permute-start(bf16[768,256]{1,0:T(8,128)(2,1)S(1)} %bitcast.45), channel_id=1, source_target_pairs={{0,1},{1,0},{2,3},{3,2},{4,5},{5,4},{6,7},{7,6},{8,9},{9,8},{10,11... | collective-permute-start | bytes 1179656 | tf_op jit(solution)/shard_map/ppermute | solution.py:382
  258.4 5.2 %collective-permute-start.30 = (bf16[128,4096]{1,0:T(8,128)(2,1)S(1)}, bf16[128,4096]{1,0:T(8,128)(2,1)S(1)}, u32[]{:S(2)}, u32[]{:S(2)}) collective-permute-start(bf16[128,4096]{1,0:T(8,128)(2,1)S(1)} %get-tuple-element.174), channel_id=1, source_target_pairs={{0,2},{2,0},{4,6},{6,4},{8,10},{10,8},{12,14},{14,12},{16,18},{18,... | collective-permute-start | bytes 3145736 | tf_op jit(solution)/shard_map/ppermute | solution.py:355
  261.3 3.8 %collective-permute-start.31 = (bf16[128,4096]{1,0:T(8,128)(2,1)S(1)}, bf16[128,4096]{1,0:T(8,128)(2,1)S(1)}, u32[]{:S(2)}, u32[]{:S(2)}) collective-permute-start(bf16[128,4096]{1,0:T(8,128)(2,1)S(1)} %get-tuple-element.175), channel_id=1, source_target_pairs={{0,2},{2,0},{4,6},{6,4},{8,10},{10,8},{12,14},{14,12},{16,18},{18,... | collective-permute-start | bytes 3145736 | tf_op jit(solution)/shard_map/ppermute | solution.py:355
  275.0 14.2 %collective-permute-start.35 = (bf16[128,4096]{1,0:T(8,128)(2,1)}, bf16[128,4096]{1,0:T(8,128)(2,1)S(1)}, u32[]{:S(2)}, u32[]{:S(2)}) collective-permute-start(bf16[128,4096]{1,0:T(8,128)(2,1)} %get-tuple-element.186), channel_id=1, source_target_pairs={{0,4},{2,10},{8,0},{10,18},{16,8},{18,26},{24,16},{26,30},{28,24},... | collective-permute-start | bytes 3145736 | tf_op jit(solution)/shard_map/ppermute | solution.py:352
  275.0 27.6 %collective-permute-start.36 = (bf16[128,4096]{1,0:T(8,128)(2,1)}, bf16[128,4096]{1,0:T(8,128)(2,1)S(1)}, u32[]{:S(2)}, u32[]{:S(2)}) collective-permute-start(bf16[128,4096]{1,0:T(8,128)(2,1)} %get-tuple-element.187), channel_id=1, source_target_pairs={{0,6},{2,8},{8,2},{10,16},{16,10},{18,24},{24,18},{26,28},{28,26},... | collective-permute-start | bytes 3145736 | tf_op jit(solution)/shard_map/ppermute | solution.py:352
  285.4 2.3 collective-permute-start.33
  285.4 3.0 collective-permute-start.34
  (25 other events, 52.4 us)

commit v4 on v3

--- a/solution.py
+++ b/solution.py
@@ -72,46 +72,58 @@
     col = lax.broadcasted_iota(jnp.int32, (LONG, LONG), 1)
     row = lax.broadcasted_iota(jnp.int32, (LONG, LONG), 0)
 
-    for j in range(per_step):
-        group = step * per_step + j
-        mine = slice(j * GROUP, (j + 1) * GROUP)
-        for a, h, where in places:
-            at = pl.multiple_of((order[where] + 1) * GROUP, GROUP)
+    every = range(per_step)
+    mine = [slice(j * GROUP, (j + 1) * GROUP) for j in every]
+    taps = [
+        [[short_ref[i, step * per_step + j, k] for k in range(SHORT)] for i in range(3)] for j in every
+    ]
+    for a, h, where in places:
+        at = pl.multiple_of((order[where] + 1) * GROUP, GROUP)
+        for j in every:
             for i in range(3):
-                part = proj_refs[0][a][i, mine, h * LONG : (h + 1) * LONG].astype(F32)
+                part = proj_refs[0][a][i, mine[j], h * LONG : (h + 1) * LONG].astype(F32)
                 for s in range(1, sets):
-                    part = part + proj_refs[s][a][i, mine, h * LONG : (h + 1) * LONG].astype(F32)
+                    part = part + proj_refs[s][a][i, mine[j], h * LONG : (h + 1) * LONG].astype(F32)
                 p_s[j, i, pl.ds(at, GROUP), :] = part
-        taps = [[short_ref[i, group, k] for k in range(SHORT)] for i in range(3)]
-        feats = []
+
+    feats = []
+    for j in every:
+        feat = []
         for i in range(3):
             whole = p_s[j, i]
             one = pltpu.roll(whole, 1, 1)
             two = pltpu.roll(whole, 2, 1)
             one = jnp.where(lane < 1, one[:rows], one[GROUP:])
             two = jnp.where(lane < 2, two[:rows], two[GROUP:])
-            feats.append(taps[i][0] * whole[GROUP:] + taps[i][1] * one + taps[i][2] * two)
-        fq, fk, fv = feats
-        x_s[j, GROUP:, :] = (fk * fv).astype(BF16)
-
+            feat.append(taps[j][i][0] * whole[GROUP:] + taps[j][i][1] * one + taps[j][i][2] * two)
+        feats.append(feat)
+        x_s[j, GROUP:, :] = (feat[1] * feat[2]).astype(BF16)
+
+    filters = []
+    for j in every:
         base = jnp.broadcast_to(long_ref[0, j : j + 1, :], (8, LONG))
         for bit in (1, 2, 4):
             base = jnp.where((sub8 & bit) != 0, pltpu.roll(base, bit, 1), base)
         full = jnp.concatenate([base] + [pltpu.roll(base, 8 * m, 1) for m in range(1, LONG // 8)], axis=0)
         near = jnp.where(col >= row, full, 0.0).astype(BF16)
         far = jnp.where(col < row, full, 0.0).astype(BF16)
-
-        x_two = jnp.concatenate([x_s[j, GROUP:, :], x_s[j, :rows, :]], axis=1)
-        inner = dot(x_two, jnp.concatenate([near, far], axis=0), ((1,), (0,)))
-        g = g_ref[:, mine, :].reshape(rows, LONG).astype(F32)
-        mixed_ref[:, mine, :] = (fq * inner).astype(BF16).reshape(blocks, GROUP, LONG)
-        y_s[j, :rows, :] = (g * fq).astype(BF16)
-        y_one = y_s[j, :rows, :]
-        y_two = jnp.concatenate([y_one, y_s[j, GROUP:, :]], axis=1)
-        d_product = dot(y_two, jnp.concatenate([near, far], axis=1), ((1,), (1,)))
-
-        pairs = dot(x_two, y_one, ((0,), (0,)))
-        fold = jnp.where(col >= row, pairs[:LONG], pairs[LONG:])
+        filters.append((near, far))
+
+    x_twos = [jnp.concatenate([x_s[j, GROUP:, :], x_s[j, :rows, :]], axis=1) for j in every]
+    inners = [dot(x_twos[j], jnp.concatenate(filters[j], axis=0), ((1,), (0,))) for j in every]
+    d_queries = []
+    for j in every:
+        g = g_ref[:, mine[j], :].reshape(rows, LONG).astype(F32)
+        mixed_ref[:, mine[j], :] = (feats[j][0] * inners[j]).astype(BF16).reshape(blocks, GROUP, LONG)
+        y_s[j, :rows, :] = (g * feats[j][0]).astype(BF16)
+        d_queries.append(g * inners[j])
+    d_products = []
+    for j in every:
+        y_two = jnp.concatenate([y_s[j, :rows, :], y_s[j, GROUP:, :]], axis=1)
+        d_products.append(dot(y_two, jnp.concatenate(filters[j], axis=1), ((1,), (1,))))
+    folds = [dot(x_twos[j], y_s[j, :rows, :], ((0,), (0,))) for j in every]
+    for j in every:
+        fold = jnp.where(col >= row, folds[j][:LONG], folds[j][LONG:])
         width = LONG
         while width > 8:
             width //= 2
@@ -120,7 +132,8 @@
             fold = jnp.where((sub8 & bit) != 0, pltpu.roll(fold, LONG - bit, 1), fold)
         gl_ref[0, j : j + 1, :] = jnp.sum(fold, axis=0, keepdims=True)
 
-        for i, d in enumerate((g * inner, d_product * fv, d_product * fk)):
+    for j in every:
+        for i, d in enumerate((d_queries[j], d_products[j] * feats[j][2], d_products[j] * feats[j][1])):
             d_s[j, i, :rows, :] = d
             whole = d_s[j, i]
             one = pltpu.roll(whole, LONG - 1, 1)
@@ -130,18 +143,19 @@
             p = p_s[j, i, GROUP:, :]
             for k, moved in enumerate((d, one, two)):
                 gs_ref[0, j, 3 * i + k : 3 * i + k + 1, :] = jnp.sum(p * moved, axis=0, keepdims=True)
-            e_s[j, i] = (taps[i][0] * d + taps[i][1] * one + taps[i][2] * two).astype(BF16)
-        for a, h, where in d_places:
-            at = pl.multiple_of(order[where] * GROUP, GROUP)
+            e_s[j, i] = (taps[j][i][0] * d + taps[j][i][1] * one + taps[j][i][2] * two).astype(BF16)
+    for a, h, where in d_places:
+        at = pl.multiple_of(order[where] * GROUP, GROUP)
+        for j in every:
             for i in range(3):
-                d_refs[a][i, mine, h * LONG : (h + 1) * LONG] = e_s[j, i, pl.ds(at, GROUP), :]
+                d_refs[a][i, mine[j], h * LONG : (h + 1) * LONG] = e_s[j, i, pl.ds(at, GROUP), :]
 
 
 def mix(order, short_kernel, long_kernel, g, proj_sets, grouped):
     blocks, channels, _ = g.shape
     count, sets = len(proj_sets[0]), len(proj_sets)
     groups = channels // GROUP
-    per_step = 2 if groups % 2 == 0 else 1
+    per_step = next(n for n in (4, 2, 1) if groups % n == 0)
     steps = groups // per_step
     rows = blocks * GROUP
     high = per_step * GROUP
@@ -180,7 +194,7 @@
             jax.ShapeDtypeStruct((steps, per_step, 3 * SHORT, LONG), F32),
             jax.ShapeDtypeStruct((steps, per_step, LONG), F32),
         ],
-        compiler_params=pltpu.CompilerParams(vmem_limit_bytes=20 * MIB),
+        compiler_params=pltpu.CompilerParams(vmem_limit_bytes=58 * MIB),
         cost_estimate=SMALL,
     )(order, short_kernel, long_kernel.reshape(steps, per_step, LONG), g, *[x for s in proj_sets for x in s])
     mixed, d_proj, (gs, gl) = outs[0], outs[1:-2], outs[-2:]
@@ -335,6 +349,24 @@
     )(*arrays)
 
 
+def copy_body(in_ref, out_ref):
+    out_ref[...] = in_ref[...]
+
+
+def copy_kernel(x):
+    rows, width = x.shape
+    tile = rows // 4
+    return pl.pallas_call(
+        copy_body,
+        grid=(4,),
+        in_specs=[pl.BlockSpec((tile, width), lambda i: (i, 0))],
+        out_specs=pl.BlockSpec((tile, width), lambda i: (i, 0)),
+        out_shape=jax.ShapeDtypeStruct(x.shape, x.dtype),
+        compiler_params=pltpu.CompilerParams(vmem_limit_bytes=8 * MIB),
+        cost_estimate=SMALL,
+    )(x)
+
+
 def on_device(ring, n_tp, tokens_in, w_query, w_key, w_value, short_taps, long_taps, grad_out):
     chips = len(ring)
     half = chips // 2
@@ -368,7 +400,9 @@
 
     stay = 3 * channels
     if n_tp == 2:
-        flat = restack(lax.axis_index("tp").astype(jnp.int32), weights)
+        t = lax.axis_index("tp").astype(jnp.int32)
+        t, order, short_kernel, long_kernel = lax.optimization_barrier((t, order, short_kernel, long_kernel))
+        flat = restack(t, weights)
     else:
         flat = jnp.stack(weights).reshape(-1, width)
 
@@ -397,7 +431,7 @@
 
     arrived = [one_way(tokens_in), one_way(tokens_in, to_mate=True, turned=True)]
     near, far = project([tokens_in, swap(tokens_in)])
-    arrived, near, far, order, short_kernel, long_kernel = stage((arrived, near, far, order, short_kernel, long_kernel))
+    arrived, near, far = stage((arrived, near, far))
     arrived = jnp.concatenate(arrived, axis=0)
     projected = []
     for s in range(1, half):
@@ -407,12 +441,14 @@
         if s < half - 1:
             arrived, near, far, projected[-1] = stage((coming, near, far, projected[-1]))
     crossed = across(far)
-    arrived, near, grad_out = stage((coming, near, grad_out))
+    arrived, near = stage((coming, near))
+    shared, projected[-1] = stage((arrived, projected[-1]))
+    mates = [swap(shared[: held // 2]), swap(shared[held // 2 :])]
+    grad_out, mates = stage((grad_out, mates))
     incoming = lax.all_to_all(
         grad_out.reshape(n_ctx, channels, held), "ctx", split_axis=0, concat_axis=0, tiled=True
     )
-    shared, projected[-1] = stage((arrived, projected[-1]))
-    last, far = project([arrived, swap(shared[: held // 2]), swap(shared[held // 2 :])])
+    last, far = project([arrived, *mates])
     far, crossed = stage((far, crossed))
     projected += [(near, crossed), (last, across(far))]
 
@@ -426,10 +462,11 @@
     )
 
     first, met, later = [meet(d_proj[s]) for s in (half, half - 1, half - 2)]
+    mixed, first = stage((mixed, first))
     mixed_out = lax.all_to_all(mixed, "ctx", split_axis=0, concat_axis=0, tiled=True).reshape(-1, held)
     keep, *give = unproject(first, held, held // 2, held // 2)
     total = add_kernel([keep], [swap(x) for x in give])
-    total, met, rest, mixed_out = stage((total, met, d_proj[: half - 2], mixed_out))
+    total, met, rest = stage((total, met, d_proj[: half - 2]))
     for s in range(half - 1, 0, -1):
         coming = one_way(total[0], turned=True)
         if s < half - 1:
@@ -439,7 +476,9 @@
         keep, *give = unproject(met, 2 * held, *cuts)
         give, later = stage((give, later))
         total = add_kernel([keep], [swap(x) for x in give], [coming], cut=2 if s == 1 else 1)
-        total, met, rest = stage((total, later, rest))
+        if s == half - 2:
+            mixed_out = copy_kernel(mixed_out)
+        total, met, rest, mixed_out = stage((total, later, rest, mixed_out))
     coming = [one_way(total[0], turned=True), one_way(total[1], turned=True, to_mate=True)]
     keep, *give = unproject(met, held, held // 2, held // 2)
     (grad_tokens,) = add_kernel([keep], [swap(x) for x in give], coming[:1], coming[1:])

time: 310 us -> 306 us (0.987)
  waiting for transfers between devices: 93.4 us -> 118 us
  local copies, waits for them, and re-layouts: 54.1 us -> 30.5 us
  starting transfers between devices: 52.7 us -> 49.3 us
    unnamed x72 -> x63, local copies, waits for them, and re-layouts: 53 us -> 28.8 us
    ppermute x10, waiting for transfers between devices: 30.9 us -> 49.1 us  [across(): return None if x is None else lax.ppermute(x, 'tp', [(0, 1), (1, 0)])]
    ppermute x10, waiting for transfers between devices: 44.5 us -> 50.8 us  [one_way(): return lax.ppermute(x, 'ctx', hops)]
    ppermute x17, starting transfers between devices: 13.9 us -> 9.66 us  [swap(): return lax.ppermute(x, 'ctx', [(d, d ^ 1) for d in range(n_ctx)])]
  transfers between devices with their start and end apart: 39 -> 39, of which waited for: 28 -> 31; matrix products, arithmetic and copies ran while one was open for 1% -> 1% of each run, Pallas kernels for 25% -> 26%
where the time goes in v4:
time: 306 us; the launch traced here: 305 us
  waiting for transfers between devices  118 us (39%)
  Pallas kernels  106 us (35%)
  starting transfers between devices  49.3 us (16%)
  local copies, waits for them, and re-layouts  30.5 us (10%)
    ppermute x10, waiting for transfers between devices, one_way(): return lax.ppermute(x, 'ctx', hops)  50.8 us
    ppermute x10, waiting for transfers between devices, across(): return None if x is None else lax.ppermute(x, 'tp', [(0, 1), (1, 0)])  49.1 us
    pallas_call x5, Pallas kernels, unproject_kernel(): pl.pallas_call(unproject_body, grid=(width // tile,), in_specs=[pl.BlockS...  41.3 us
    pallas_call x5, Pallas kernels, project_kernel(): pl.pallas_call(functools.partial(project_body, len(pieces)), grid=(4,), i...  32 us
    unnamed x63, local copies, waits for them, and re-layouts  28.8 us
    pallas_call x1, Pallas kernels, mix(): pl.pallas_call(functools.partial(mix_body, count, sets, per_step, grouped...  20.7 us
    ppermute x17, waiting for transfers between devices, swap(): return lax.ppermute(x, 'ctx', [(d, d ^ 1) for d in range(n_ctx)])  18.3 us
    ppermute x10, starting transfers between devices, one_way(): return lax.ppermute(x, 'ctx', hops)  14.2 us
  transfers between devices with their start and end apart: 39, of which 31 were waited for; matrix products, arithmetic and copies ran while one was open for 1% of the time, Pallas kernels for 26%

profile of v4, /device:TPU:1, one launch (start us, length us, event | category | flops | bytes accessed | tf_op | source)
XLA Modules:
  0.0 305.4 jit_solution(7592589164823548186)
XLA Ops:
  0.8 2.7 collective-permute-start.1
  6.0 2.2 copy-done.4
  8.2 2.2 copy-done.5
  10.4 2.2 copy-done.6
  12.6 1.7 shard_map.111
  14.4 4.3 %shard_map.112 = (bf16[768,256]{1,0:T(8,128)(2,1)S(1)}, bf16[768,256]{1,0:T(8,128)(2,1)S(1)}) custom-call(bf16[128,4096]{1,0:T(8,128)(2,1)S(1)} %copy-done.7, bf16[128,4096]{1,0:T(8,128)(2,1)S(1)} %collective-permute-done.2.refs_1_, bf16[1536,4096]{1,0:T(8,128)(2,1)S(1)} %bitcast.30), custom_call_target="tpu_custom_call" | custom-call | flops 1 | bytes 1 | tf_op jit(solution)/shard_map/pallas_call | solution.py:264
  18.7 7.8 %collective-permute-done.1 = bf16[128,4096]{1,0:T(8,128)(2,1)S(1)} collective-permute-done((bf16[128,4096]{1,0:T(8,128)(2,1)}, bf16[128,4096]{1,0:T(8,128)(2,1)S(1)}, u32[]{:S(2)}, u32[]{:S(2)}) %collective-permute-start.1) | collective-permute-done | bytes 1048608 | tf_op jit(solution)/shard_map/ppermute | solution.py:384
  28.0 1.4 collective-permute-start.3
  31.8 7.8 %shard_map.113 = (bf16[768,512]{1,0:T(8,128)(2,1)S(1)}, bf16[768,512]{1,0:T(8,128)(2,1)S(1)}) custom-call(bf16[256,4096]{1,0:T(8,128)(2,1)S(1)} %constant_dynamic-update-slice_fusion.refs_0_, bf16[256,4096]{1,0:T(8,128)(2,1)S(1)} %collective-permute-done.4.refs_1_, bf16[1536,4096]{1,0:T(8,128)(2,1)S(1)} %bitcast.31), custom_call_target="tpu_custom_call" | custom-call | flops 1 | bytes 1 | tf_op jit(solution)/shard_map/pallas_call | solution.py:264
  40.4 12.7 %collective-permute-done.3.refs_0_ = bf16[256,4096]{1,0:T(8,128)(2,1)S(1)} collective-permute-done((bf16[256,4096]{1,0:T(8,128)(2,1)S(1)}, bf16[256,4096]{1,0:T(8,128)(2,1)S(1)}, u32[]{:S(2)}, u32[]{:S(2)}) %collective-permute-start.3) | collective-permute-done | bytes 2097184 | tf_op jit(solution)/shard_map/ppermute | solution.py:384
  58.0 7.8 %shard_map.114 = (bf16[768,512]{1,0:T(8,128)(2,1)S(1)}, bf16[768,512]{1,0:T(8,128)(2,1)S(1)}) custom-call(bf16[256,4096]{1,0:T(8,128)(2,1)S(1)} %collective-permute-done.3.refs_0_, bf16[256,4096]{1,0:T(8,128)(2,1)S(1)} %collective-permute-done.7.refs_1_, bf16[1536,4096]{1,0:T(8,128)(2,1)S(1)} %bitcast.32), custom_call_target="tpu_custom_call" | custom-call | flops 1 | bytes 1 | tf_op jit(solution)/shard_map/pallas_call | solution.py:264
  65.8 8.2 %collective-permute-done.8 = bf16[768,512]{1,0:T(8,128)(2,1)S(1)} collective-permute-done((bf16[768,512]{1,0:T(8,128)(2,1)S(1)}, bf16[768,512]{1,0:T(8,128)(2,1)S(1)}, u32[]{:S(2)}, u32[]{:S(2)}) %collective-permute-start.8) | collective-permute-done | bytes 786464 | tf_op jit(solution)/shard_map/ppermute | solution.py:416
  74.0 5.7 %collective-permute-done.6.refs_0_ = bf16[256,4096]{1,0:T(8,128)(2,1)S(1)} collective-permute-done((bf16[256,4096]{1,0:T(8,128)(2,1)S(1)}, bf16[256,4096]{1,0:T(8,128)(2,1)S(1)}, u32[]{:S(2)}, u32[]{:S(2)}) %collective-permute-start.6) | collective-permute-done | bytes 2097184 | tf_op jit(solution)/shard_map/ppermute | solution.py:384
  80.3 1.4 collective-permute-start.9
  84.0 7.8 %shard_map.115 = (bf16[768,512]{1,0:T(8,128)(2,1)S(1)}, bf16[768,512]{1,0:T(8,128)(2,1)S(1)}) custom-call(bf16[256,4096]{1,0:T(8,128)(2,1)S(1)} %collective-permute-done.6.refs_0_, bf16[256,4096]{1,0:T(8,128)(2,1)S(1)} %collective-permute-done.10.refs_1_, bf16[1536,4096]{1,0:T(8,128)(2,1)S(1)} %bitcast.33), custom_call_target="tpu_custom_call" | custom-call | flops 1 | bytes 1 | tf_op jit(solution)/shard_map/pallas_call | solution.py:264
  92.7 1.9 collective-permute-done.9.refs_0_
  94.6 5.5 %collective-permute-done.11 = bf16[768,512]{1,0:T(8,128)(2,1)S(1)} collective-permute-done((bf16[768,512]{1,0:T(8,128)(2,1)S(1)}, bf16[768,512]{1,0:T(8,128)(2,1)S(1)}, u32[]{:S(2)}, u32[]{:S(2)}) %collective-permute-start.11) | collective-permute-done | bytes 786464 | tf_op jit(solution)/shard_map/ppermute | solution.py:416
  100.2 1.6 collective-permute-start.13
  101.9 1.5 collective-permute-done.13.refs_2_
  104.1 5.5 %all-to-all-start = ((bf16[16,256,128]{2,1,0:T(8,128)(2,1)}), bf16[16,256,128]{2,1,0:T(8,128)(2,1)}, u32[]{:S(2)}, u32[]{:S(2)}) async-start(bf16[16,256,128]{2,1,0:T(8,128)(2,1)} %bitcast.58), calls=%async_computation | async-start | bytes 2097152 | tf_op jit(solution)/shard_map/all_to_all | solution.py:448
  111.0 4.6 %copy-done.1 = bf16[2,3,256,4096]{3,2,1,0:T(8,128)(2,1)S(1)} copy-done((bf16[2,3,256,4096]{3,2,1,0:T(8,128)(2,1)S(1)}, bf16[2,3,256,4096]{3,2,1,0:T(8,128)(2,1)}, u32[]{:S(2)}) %copy-start.1) | copy-done | bytes 12582936
  115.6 4.3 %shard_map.116 = (bf16[768,256]{1,0:T(8,128)(2,1)S(1)}, bf16[768,256]{1,0:T(8,128)(2,1)S(1)}) custom-call(bf16[128,4096]{1,0:T(8,128)(2,1)S(1)} %collective-permute-done.9.refs_0_, bf16[64,4096]{1,0:T(8,128)(2,1)S(1)} %collective-permute-done.12.refs_1_, bf16[64,4096]{1,0:T(8,128)(2,1)S(1)} %collective-permute-done.13.refs_2_, bf16[1536,4096]{1,0:T(8,128)(2,1)S(1)} %bitcast.34), custom_call_target="tpu_custom_call" | custom-call | flops 1 | bytes 1 | tf_op jit(solution)/shard_map/pallas_call | solution.py:264
  120.7 8.1 %collective-permute-done.14 = bf16[768,512]{1,0:T(8,128)(2,1)S(1)} collective-permute-done((bf16[768,512]{1,0:T(8,128)(2,1)S(1)}, bf16[768,512]{1,0:T(8,128)(2,1)S(1)}, u32[]{:S(2)}, u32[]{:S(2)}) %collective-permute-start.14) | collective-permute-done | bytes 786464 | tf_op jit(solution)/shard_map/ppermute | solution.py:416
  130.0 8.4 %collective-permute-done.15 = bf16[768,256]{1,0:T(8,128)(2,1)S(1)} collective-permute-done((bf16[768,256]{1,0:T(8,128)(2,1)S(1)}, bf16[768,256]{1,0:T(8,128)(2,1)S(1)}, u32[]{:S(2)}, u32[]{:S(2)}) %collective-permute-start.15) | collective-permute-done | bytes 393248 | tf_op jit(solution)/shard_map/ppermute | solution.py:416
  139.1 20.7 %shard_map.117 = (bf16[16,256,128]{2,1,0:T(8,128)(2,1)}, bf16[3,256,256]{2,1,0:T(8,128)(2,1)}, bf16[3,256,512]{2,1,0:T(8,128)(2,1)}, bf16[3,256,512]{2,1,0:T(8,1...) custom-call(s32[16]{0:T(128)} %dynamic-slice_bitcast_fusion.order, ...), custom_call_target="tpu_custom_call" | custom-call | flops 1 | bytes 1 | tf_op jit(solution)/shard_map/pallas_call | solution.py:166
  161.1 7.7 %collective-permute-done.16.far_ref = bf16[768,256]{1,0:T(8,128)(2,1)S(1)} collective-permute-done((bf16[768,256]{1,0:T(8,128)(2,1)}, bf16[768,256]{1,0:T(8,128)(2,1)S(1)}, u32[]{:S(2)}, u32[]{:S(2)}) %collective-permute-start.16) | collective-permute-done | bytes 393248 | tf_op jit(solution)/shard_map/ppermute | solution.py:416
  168.8 8.2 %all-to-all-start.1 = ((bf16[16,256,128]{2,1,0:T(8,128)(2,1)}), bf16[16,256,128]{2,1,0:T(8,128)(2,1)S(1)}, u32[]{:S(2)}, u32[]{:S(2)}) async-start(bf16[16,256,128]{2,1,0:T(8,128)(2,1)} %get-tuple-element.168), calls=%async_computation.1 | async-start | bytes 2097152 | tf_op jit(solution)/shard_map/all_to_all | solution.py:466
  178.4 4.6 %copy-done.2 = bf16[2,3,256,4096]{3,2,1,0:T(8,128)(2,1)S(1)} copy-done((bf16[2,3,256,4096]{3,2,1,0:T(8,128)(2,1)S(1)}, bf16[2,3,256,4096]{3,2,1,0:T(8,128)(2,1)}, u32[]{:S(2)}) %copy-start.2) | copy-done | bytes 12582936
  183.0 6.0 %shard_map.118 = (bf16[128,4096]{1,0:T(8,128)(2,1)S(1)}, bf16[64,4096]{1,0:T(8,128)(2,1)S(1)}, bf16[64,4096]{1,0:T(8,128)(2,1)S(1)}) custom-call(bf16[768,256]{1,0:T(8,128)(2,1)S(1)} %bitcast.55, bf16[768,256]{1,0:T(8,128)(2,1)S(1)} %collective-permute-done.16.far_ref, bf16[1536,4096]{1,0:T(8,128)(2,1)S(1)} %bitcast.35), custom_call_target="tpu_custom_call" | custom-call | flops 1 | bytes 1 | tf_op jit(solution)/shard_map/pallas_call | solution.py:301
  192.3 4.0 %collective-permute-done.19.far_ref = bf16[768,512]{1,0:T(8,128)(2,1)S(1)} collective-permute-done((bf16[768,512]{1,0:T(8,128)(2,1)S(1)}, bf16[768,512]{1,0:T(8,128)(2,1)S(1)}, u32[]{:S(2)}, u32[]{:S(2)}) %collective-permute-start.19) | collective-permute-done | bytes 786464 | tf_op jit(solution)/shard_map/ppermute | solution.py:416
  197.3 9.6 %shard_map.120 = (bf16[256,4096]{1,0:T(8,128)(2,1)S(1)}, bf16[96,4096]{1,0:T(8,128)(2,1)S(1)}, bf16[80,4096]{1,0:T(8,128)(2,1)S(1)}, bf16[80,4096]{1,0:T(8,128)(2,1)S(1)}) custom-call(bf16[768,512]{1,0:T(8,128)(2,1)S(1)} %bitcast.48, bf16[768,512]{1,0:T(8,128)(2,1)S(1)} %collective-permute-done.19.far_ref, bf16[1536,4096]{1,0:T(8,128)(2,1)S(1)} %bitcast.36), custom_call_target="tpu_custom_call" | custom-call | flops 1 | bytes 1 | tf_op jit(solution)/shard_map/pallas_call | solution.py:301
  206.9 6.2 %collective-permute-done.20.far_ref = bf16[768,512]{1,0:T(8,128)(2,1)S(1)} collective-permute-done((bf16[768,512]{1,0:T(8,128)(2,1)S(1)}, bf16[768,512]{1,0:T(8,128)(2,1)S(1)}, u32[]{:S(2)}, u32[]{:S(2)}) %collective-permute-start.20) | collective-permute-done | bytes 786464 | tf_op jit(solution)/shard_map/ppermute | solution.py:416
  215.4 2.3 collective-permute-done.22.refs_2_
  222.5 4.6 %copy-done.3 = bf16[2,3,256,4096]{3,2,1,0:T(8,128)(2,1)S(1)} copy-done((bf16[2,3,256,4096]{3,2,1,0:T(8,128)(2,1)S(1)}, bf16[2,3,256,4096]{3,2,1,0:T(8,128)(2,1)}, u32[]{:S(2)}) %copy-start.3) | copy-done | bytes 12582936
  229.4 9.5 %shard_map.122 = (bf16[256,4096]{1,0:T(8,128)(2,1)S(1)}, bf16[128,4096]{1,0:T(8,128)(2,1)S(1)}, bf16[128,4096]{1,0:T(8,128)(2,1)S(1)}) custom-call(bf16[768,512]{1,0:T(8,128)(2,1)S(1)} %bitcast.46, bf16[768,512]{1,0:T(8,128)(2,1)S(1)} %copy-done.12, bf16[1536,4096]{1,0:T(8,128)(2,1)S(1)} %bitcast.37), custom_call_target="tpu_custom_call" | custom-call | flops 1 | bytes 1 | tf_op jit(solution)/shard_map/pallas_call | solution.py:301
  239.9 1.5 collective-permute-start.26
  241.4 1.5 shard_map.124
  243.7 1.5 collective-permute-done.27.refs_2_
  249.2 9.6 %shard_map.125 = (bf16[256,4096]{1,0:T(8,128)(2,1)S(1)}, bf16[128,4096]{1,0:T(8,128)(2,1)S(1)}, bf16[128,4096]{1,0:T(8,128)(2,1)S(1)}) custom-call(bf16[768,512]{1,0:T(8,128)(2,1)S(1)} %bitcast.44, bf16[768,512]{1,0:T(8,128)(2,1)S(1)} %collective-permute-done.25.far_ref, bf16[1536,4096]{1,0:T(8,128)(2,1)S(1)} %bitcast.40), custom_call_target="tpu_custom_call" | custom-call | flops 1 | bytes 1 | tf_op jit(solution)/shard_map/pallas_call | solution.py:301
  258.7 1.9 collective-permute-start.30
  260.7 2.2 collective-permute-done.30.refs_1_
  262.9 1.5 collective-permute-done.31.refs_2_
  264.4 7.5 %collective-permute-done.32.refs_3_ = bf16[256,4096]{1,0:T(8,128)(2,1)S(1)} collective-permute-done((bf16[256,4096]{1,0:T(8,128)(2,1)S(1)}, bf16[256,4096]{1,0:T(8,128)(2,1)S(1)}, u32[]{:S(2)}, u32[]{:S(2)}) %collective-permute-start.32) | collective-permute-done | bytes 2097184 | tf_op jit(solution)/shard_map/ppermute | solution.py:384
  271.9 2.4 shard_map.126
  275.5 2.4 collective-permute-start.36
  277.8 6.6 %shard_map.127 = (bf16[128,4096]{1,0:T(8,128)(2,1)S(1)}, bf16[64,4096]{1,0:T(8,128)(2,1)}, bf16[64,4096]{1,0:T(8,128)(2,1)}) custom-call(bf16[768,256]{1,0:T(8,128)(2,1)S(1)} %bitcast.53, bf16[768,256]{1,0:T(8,128)(2,1)S(1)} %collective-permute-done.29.far_ref, bf16[1536,4096]{1,0:T(8,128)(2,1)S(1)} %bitcast.41), custom_call_target="tpu_custom_call" | custom-call | flops 1 | bytes 1 | tf_op jit(solution)/shard_map/pallas_call | solution.py:301
  288.4 13.3 %collective-permute-done.36.refs_4_ = bf16[128,4096]{1,0:T(8,128)(2,1)S(1)} collective-permute-done((bf16[128,4096]{1,0:T(8,128)(2,1)}, bf16[128,4096]{1,0:T(8,128)(2,1)S(1)}, u32[]{:S(2)}, u32[]{:S(2)}) %collective-permute-start.36) | collective-permute-done | bytes 1048608 | tf_op jit(solution)/shard_map/ppermute | solution.py:384
  301.8 3.7 %shard_map.128 = bf16[128,4096]{1,0:T(8,128)(2,1)} custom-call(bf16[128,4096]{1,0:T(8,128)(2,1)S(1)} %get-tuple-element.199.refs_0_, bf16[64,4096]{1,0:T(8,128)(2,1)} %collective-permute-done.33.refs_1_, bf16[64,4096]{1,0:T(8,128)(2,1)} %collective-permute-done.34.refs_2_, bf16[128,4096]{1,0:T(8,128)(2,1)S(1)} %collective-permute-done.35.refs_3_, ...), custom_call_target="tpu_custom_call" | custom-call | flops 1 | bytes 1 | tf_op jit(solution)/shard_map/pallas_call | solution.py:341
  (119 shorter events, 48.2 us)
Async XLA Ops:
  0.6 13.7 %collective-permute-start.2 = (bf16[128,4096]{1,0:T(8,128)(2,1)}, bf16[128,4096]{1,0:T(8,128)(2,1)S(1)}, u32[]{:S(2)}, u32[]{:S(2)}) collective-permute-start(bf16[128,4096]{1,0:T(8,128)(2,1)} %refs_0_.3), channel_id=1, source_target_pairs={{0,2},{2,0},{4,6},{6,4},{8,10},{10,8},{12,14},{14,12},{16,18},{18,... | collective-permute-start | bytes 3145736 | tf_op jit(solution)/shard_map/ppermute | solution.py:387
  0.8 25.7 %collective-permute-start.1 = (bf16[128,4096]{1,0:T(8,128)(2,1)}, bf16[128,4096]{1,0:T(8,128)(2,1)S(1)}, u32[]{:S(2)}, u32[]{:S(2)}) collective-permute-start(bf16[128,4096]{1,0:T(8,128)(2,1)} %refs_0_.3), channel_id=1, source_target_pairs={{0,6},{2,8},{8,2},{10,16},{16,10},{18,24},{24,18},{26,28},{28,26},... | collective-permute-start | bytes 3145736 | tf_op jit(solution)/shard_map/ppermute | solution.py:384
  3.5 23.9 %collective-permute-start = (bf16[128,4096]{1,0:T(8,128)(2,1)}, bf16[128,4096]{1,0:T(8,128)(2,1)S(1)}, u32[]{:S(2)}, u32[]{:S(2)}) collective-permute-start(bf16[128,4096]{1,0:T(8,128)(2,1)} %refs_0_.3), channel_id=1, source_target_pairs={{0,8},{2,6},{8,16},{10,2},{16,24},{18,10},{24,28},{26,18},{28,20},... | collective-permute-start | bytes 3145736 | tf_op jit(solution)/shard_map/ppermute | solution.py:384
  14.3 69.7 %copy-start = (bf16[2,3,256,4096]{3,2,1,0:T(8,128)(2,1)}, bf16[2,3,256,4096]{3,2,1,0:T(8,128)(2,1)S(1)}, u32[]{:S(2)}) copy-start(bf16[2,3,256,4096]{3,2,1,0:T(8,128)(2,1)S(1)} %shard_map.111) | copy-start | bytes 37748740
  27.6 4.2 %collective-permute-start.4 = (bf16[256,4096]{1,0:T(8,128)(2,1)S(1)}, bf16[256,4096]{1,0:T(8,128)(2,1)S(1)}, u32[]{:S(2)}, u32[]{:S(2)}) collective-permute-start(bf16[256,4096]{1,0:T(8,128)(2,1)S(1)} %constant_dynamic-update-slice_fusion.refs_0_), channel_id=1, source_target_pairs={{0,2},{2,0},{4,6},{6,4},{8,10},{10,8},{12,14},{14,12},{16,18},{18,... | collective-permute-start | bytes 6291464 | tf_op jit(solution)/shard_map/ppermute | solution.py:387
  28.0 25.2 %collective-permute-start.3 = (bf16[256,4096]{1,0:T(8,128)(2,1)S(1)}, bf16[256,4096]{1,0:T(8,128)(2,1)S(1)}, u32[]{:S(2)}, u32[]{:S(2)}) collective-permute-start(bf16[256,4096]{1,0:T(8,128)(2,1)S(1)} %constant_dynamic-update-slice_fusion.refs_0_), channel_id=1, source_target_pairs={{0,8},{2,6},{8,16},{10,2},{16,24},{18,10},{24,28},{26,18},{28,20},... | collective-permute-start | bytes 6291464 | tf_op jit(solution)/shard_map/ppermute | solution.py:384
  29.4 11.0 %collective-permute-start.5 = (bf16[768,256]{1,0:T(8,128)(2,1)S(1)}, bf16[768,256]{1,0:T(8,128)(2,1)S(1)}, u32[]{:S(2)}, u32[]{:S(2)}) collective-permute-start(bf16[768,256]{1,0:T(8,128)(2,1)S(1)} %get-tuple-element.116), channel_id=1, source_target_pairs={{0,1},{1,0},{2,3},{3,2},{4,5},{5,4},{6,7},{7,6},{8,9},{9,8},{10,11... | collective-permute-start | bytes 1179656 | tf_op jit(solution)/shard_map/ppermute | solution.py:416
  40.4 25.3 %copy-start.24 = (bf16[768,256]{1,0:T(8,128)(2,1)}, bf16[768,256]{1,0:T(8,128)(2,1)S(1)}, u32[]{:S(2)}) copy-start(bf16[768,256]{1,0:T(8,128)(2,1)S(1)} %collective-permute-done.5) | copy-start | bytes 1179652
  53.2 4.8 %collective-permute-start.7 = (bf16[256,4096]{1,0:T(8,128)(2,1)S(1)}, bf16[256,4096]{1,0:T(8,128)(2,1)S(1)}, u32[]{:S(2)}, u32[]{:S(2)}) collective-permute-start(bf16[256,4096]{1,0:T(8,128)(2,1)S(1)} %collective-permute-done.3.refs_0_), channel_id=1, source_target_pairs={{0,2},{2,0},{4,6},{6,4},{8,10},{10,8},{12,14},{14,12},{16,18},{18,... | collective-permute-start | bytes 6291464 | tf_op jit(solution)/shard_map/ppermute | solution.py:387
  54.2 25.5 %collective-permute-start.6 = (bf16[256,4096]{1,0:T(8,128)(2,1)S(1)}, bf16[256,4096]{1,0:T(8,128)(2,1)S(1)}, u32[]{:S(2)}, u32[]{:S(2)}) collective-permute-start(bf16[256,4096]{1,0:T(8,128)(2,1)S(1)} %collective-permute-done.3.refs_0_), channel_id=1, source_target_pairs={{0,8},{2,6},{8,16},{10,2},{16,24},{18,10},{24,28},{26,18},{28,20},... | collective-permute-start | bytes 6291464 | tf_op jit(solution)/shard_map/ppermute | solution.py:384
  55.5 18.4 %collective-permute-start.8 = (bf16[768,512]{1,0:T(8,128)(2,1)S(1)}, bf16[768,512]{1,0:T(8,128)(2,1)S(1)}, u32[]{:S(2)}, u32[]{:S(2)}) collective-permute-start(bf16[768,512]{1,0:T(8,128)(2,1)S(1)} %get-tuple-element.121), channel_id=1, source_target_pairs={{0,1},{1,0},{2,3},{3,2},{4,5},{5,4},{6,7},{7,6},{8,9},{9,8},{10,11... | collective-permute-start | bytes 2359304 | tf_op jit(solution)/shard_map/ppermute | solution.py:416
  65.7 26.0 %copy-start.15 = (bf16[768,512]{1,0:T(8,128)(2,1)}, bf16[768,512]{1,0:T(8,128)(2,1)S(1)}, u32[]{:S(2)}) copy-start(bf16[768,512]{1,0:T(8,128)(2,1)S(1)} %get-tuple-element.131) | copy-start | bytes 2359300
  74.0 17.8 %copy-start.21 = (bf16[768,512]{1,0:T(8,128)(2,1)}, bf16[768,512]{1,0:T(8,128)(2,1)S(1)}, u32[]{:S(2)}) copy-start(bf16[768,512]{1,0:T(8,128)(2,1)S(1)} %collective-permute-done.8) | copy-start | bytes 2359300
  79.7 4.3 %collective-permute-start.10 = (bf16[256,4096]{1,0:T(8,128)(2,1)S(1)}, bf16[256,4096]{1,0:T(8,128)(2,1)S(1)}, u32[]{:S(2)}, u32[]{:S(2)}) collective-permute-start(bf16[256,4096]{1,0:T(8,128)(2,1)S(1)} %collective-permute-done.6.refs_0_), channel_id=1, source_target_pairs={{0,2},{2,0},{4,6},{6,4},{8,10},{10,8},{12,14},{14,12},{16,18},{18,... | collective-permute-start | bytes 6291464 | tf_op jit(solution)/shard_map/ppermute | solution.py:387
  80.3 14.3 %collective-permute-start.9 = (bf16[128,4096]{1,0:T(8,128)(2,1)S(1)}, bf16[128,4096]{1,0:T(8,128)(2,1)S(1)}, u32[]{:S(2)}, u32[]{:S(2)}) collective-permute-start(bf16[128,4096]{1,0:T(8,128)(2,1)S(1)} %slice.9), channel_id=1, source_target_pairs={{0,8},{2,6},{8,16},{10,2},{16,24},{18,10},{24,28},{26,18},{28,20},... | collective-permute-start | bytes 3145736 | tf_op jit(solution)/shard_map/ppermute | solution.py:384
  81.7 18.4 %collective-permute-start.11 = (bf16[768,512]{1,0:T(8,128)(2,1)S(1)}, bf16[768,512]{1,0:T(8,128)(2,1)S(1)}, u32[]{:S(2)}, u32[]{:S(2)}) collective-permute-start(bf16[768,512]{1,0:T(8,128)(2,1)S(1)} %get-tuple-element.126), channel_id=1, source_target_pairs={{0,1},{1,0},{2,3},{3,2},{4,5},{5,4},{6,7},{7,6},{8,9},{9,8},{10,11... | collective-permute-start | bytes 2359304 | tf_op jit(solution)/shard_map/ppermute | solution.py:416
  100.2 3.2 %collective-permute-start.13 = (bf16[64,4096]{1,0:T(8,128)(2,1)S(1)}, bf16[64,4096]{1,0:T(8,128)(2,1)S(1)}, u32[]{:S(2)}, u32[]{:S(2)}) collective-permute-start(bf16[64,4096]{1,0:T(8,128)(2,1)S(1)} %get-tuple-element.214), channel_id=1, source_target_pairs={{0,2},{2,0},{4,6},{6,4},{8,10},{10,8},{12,14},{14,12},{16,18},{18,... | collective-permute-start | bytes 1572872 | tf_op jit(solution)/shard_map/ppermute | solution.py:387
  101.9 2.3 collective-permute-start.12
  104.1 34.2 %all-to-all-start = ((bf16[16,256,128]{2,1,0:T(8,128)(2,1)}), bf16[16,256,128]{2,1,0:T(8,128)(2,1)}, u32[]{:S(2)}, u32[]{:S(2)}) async-start(bf16[16,256,128]{2,1,0:T(8,128)(2,1)} %bitcast.58), calls=%async_computation | async-start | bytes 2097152 | tf_op jit(solution)/shard_map/all_to_all | solution.py:448
  109.7 19.0 %collective-permute-start.14 = (bf16[768,512]{1,0:T(8,128)(2,1)S(1)}, bf16[768,512]{1,0:T(8,128)(2,1)S(1)}, u32[]{:S(2)}, u32[]{:S(2)}) collective-permute-start(bf16[768,512]{1,0:T(8,128)(2,1)S(1)} %get-tuple-element.140), channel_id=1, source_target_pairs={{0,1},{1,0},{2,3},{3,2},{4,5},{5,4},{6,7},{7,6},{8,9},{9,8},{10,11... | collective-permute-start | bytes 2359304 | tf_op jit(solution)/shard_map/ppermute | solution.py:416
  128.7 9.6 %collective-permute-start.15 = (bf16[768,256]{1,0:T(8,128)(2,1)S(1)}, bf16[768,256]{1,0:T(8,128)(2,1)S(1)}, u32[]{:S(2)}, u32[]{:S(2)}) collective-permute-start(bf16[768,256]{1,0:T(8,128)(2,1)S(1)} %get-tuple-element.142), channel_id=1, source_target_pairs={{0,1},{1,0},{2,3},{3,2},{4,5},{5,4},{6,7},{7,6},{8,9},{9,8},{10,11... | collective-permute-start | bytes 1179656 | tf_op jit(solution)/shard_map/ppermute | solution.py:416
  159.8 17.2 %copy-start.13 = (bf16[3,256,512]{2,1,0:T(8,128)(2,1)S(1)}, bf16[3,256,512]{2,1,0:T(8,128)(2,1)}, u32[]{:S(2)}) copy-start(bf16[3,256,512]{2,1,0:T(8,128)(2,1)} %get-tuple-element.150) | copy-start | bytes 2359300
  159.8 18.6 %copy-start.18 = (bf16[3,256,256]{2,1,0:T(8,128)(2,1)S(1)}, bf16[3,256,256]{2,1,0:T(8,128)(2,1)}, u32[]{:S(2)}) copy-start(bf16[3,256,256]{2,1,0:T(8,128)(2,1)} %get-tuple-element.144) | copy-start | bytes 1179652
  159.8 9.0 %collective-permute-start.16 = (bf16[768,256]{1,0:T(8,128)(2,1)}, bf16[768,256]{1,0:T(8,128)(2,1)S(1)}, u32[]{:S(2)}, u32[]{:S(2)}) collective-permute-start(bf16[768,256]{1,0:T(8,128)(2,1)} %bitcast.54), channel_id=1, source_target_pairs={{0,1},{1,0},{2,3},{3,2},{4,5},{5,4},{6,7},{7,6},{8,9},{9,8},{10,11... | collective-permute-start | bytes 1179656 | tf_op jit(solution)/shard_map/ppermute | solution.py:416
  168.8 51.0 %all-to-all-start.1 = ((bf16[16,256,128]{2,1,0:T(8,128)(2,1)}), bf16[16,256,128]{2,1,0:T(8,128)(2,1)S(1)}, u32[]{:S(2)}, u32[]{:S(2)}) async-start(bf16[16,256,128]{2,1,0:T(8,128)(2,1)} %get-tuple-element.168), calls=%async_computation.1 | async-start | bytes 2097152 | tf_op jit(solution)/shard_map/all_to_all | solution.py:466
  177.1 19.2 %collective-permute-start.19 = (bf16[768,512]{1,0:T(8,128)(2,1)S(1)}, bf16[768,512]{1,0:T(8,128)(2,1)S(1)}, u32[]{:S(2)}, u32[]{:S(2)}) collective-permute-start(bf16[768,512]{1,0:T(8,128)(2,1)S(1)} %bitcast.47), channel_id=1, source_target_pairs={{0,1},{1,0},{2,3},{3,2},{4,5},{5,4},{6,7},{7,6},{8,9},{9,8},{10,11... | collective-permute-start | bytes 2359304 | tf_op jit(solution)/shard_map/ppermute | solution.py:416
  189.0 2.0 collective-permute-start.17
  189.4 2.3 collective-permute-start.18
  189.6 23.5 %collective-permute-start.20 = (bf16[768,512]{1,0:T(8,128)(2,1)S(1)}, bf16[768,512]{1,0:T(8,128)(2,1)S(1)}, u32[]{:S(2)}, u32[]{:S(2)}) collective-permute-start(bf16[768,512]{1,0:T(8,128)(2,1)S(1)} %bitcast.45), channel_id=1, source_target_pairs={{0,1},{1,0},{2,3},{3,2},{4,5},{5,4},{6,7},{7,6},{8,9},{9,8},{10,11... | collective-permute-start | bytes 2359304 | tf_op jit(solution)/shard_map/ppermute | solution.py:416
  196.2 22.4 %collective-permute-start.24 = (bf16[128,4096]{1,0:T(8,128)(2,1)S(1)}, bf16[128,4096]{1,0:T(8,128)(2,1)S(1)}, u32[]{:S(2)}, u32[]{:S(2)}) collective-permute-start(bf16[128,4096]{1,0:T(8,128)(2,1)S(1)} %shard_map.119), channel_id=1, source_target_pairs={{0,4},{2,10},{8,0},{10,18},{16,8},{18,26},{24,16},{26,30},{28,24},... | collective-permute-start | bytes 3145736 | tf_op jit(solution)/shard_map/ppermute | solution.py:384
  214.0 4.7 %collective-permute-start.21 = (bf16[96,4096]{1,0:T(8,128)(2,1)S(1)}, bf16[96,4096]{1,0:T(8,128)(2,1)S(1)}, u32[]{:S(2)}, u32[]{:S(2)}) collective-permute-start(bf16[96,4096]{1,0:T(8,128)(2,1)S(1)} %get-tuple-element.160), channel_id=1, source_target_pairs={{0,2},{2,0},{4,6},{6,4},{8,10},{10,8},{12,14},{14,12},{16,18},{18,... | collective-permute-start | bytes 2359304 | tf_op jit(solution)/shard_map/ppermute | solution.py:387
  214.8 2.8 collective-permute-start.22
  214.8 3.8 %collective-permute-start.23 = (bf16[80,4096]{1,0:T(8,128)(2,1)S(1)}, bf16[80,4096]{1,0:T(8,128)(2,1)S(1)}, u32[]{:S(2)}, u32[]{:S(2)}) collective-permute-start(bf16[80,4096]{1,0:T(8,128)(2,1)S(1)} %get-tuple-element.162), channel_id=1, source_target_pairs={{0,2},{2,0},{4,6},{6,4},{8,10},{10,8},{12,14},{14,12},{16,18},{18,... | collective-permute-start | bytes 1966088 | tf_op jit(solution)/shard_map/ppermute | solution.py:387
  219.9 25.4 %collective-permute-start.28 = (bf16[256,4096]{1,0:T(8,128)(2,1)S(1)}, bf16[256,4096]{1,0:T(8,128)(2,1)S(1)}, u32[]{:S(2)}, u32[]{:S(2)}) collective-permute-start(bf16[256,4096]{1,0:T(8,128)(2,1)S(1)} %shard_map.121), channel_id=1, source_target_pairs={{0,4},{2,10},{8,0},{10,18},{16,8},{18,26},{24,16},{26,30},{28,24},... | collective-permute-start | bytes 6291464 | tf_op jit(solution)/shard_map/ppermute | solution.py:384
  221.3 18.6 %collective-permute-start.25 = (bf16[768,512]{1,0:T(8,128)(2,1)}, bf16[768,512]{1,0:T(8,128)(2,1)S(1)}, u32[]{:S(2)}, u32[]{:S(2)}) collective-permute-start(bf16[768,512]{1,0:T(8,128)(2,1)} %bitcast.43), channel_id=1, source_target_pairs={{0,1},{1,0},{2,3},{3,2},{4,5},{5,4},{6,7},{7,6},{8,9},{9,8},{10,11... | collective-permute-start | bytes 2359304 | tf_op jit(solution)/shard_map/ppermute | solution.py:416
  229.4 19.8 %slice-start = ((s8[12582912]{0:T(1024)(128)(4,1)}), s8[4194304]{0:T(1024)(128)(4,1)S(1)}, s32[]{:S(2)}) async-start(s8[12582912]{0:T(1024)(128)(4,1)} %bitcast.38), calls=%async_computation.2 | async-start | bytes 8388608
  229.4 19.8 %slice-start.1 = ((s8[12582912]{0:T(1024)(128)(4,1)}), s8[4194304]{0:T(1024)(128)(4,1)S(1)}, s32[]{:S(2)}) async-start(s8[12582912]{0:T(1024)(128)(4,1)} %bitcast.38), calls=%async_computation.3 | async-start | bytes 8388608
  239.9 3.8 %collective-permute-start.26 = (bf16[128,4096]{1,0:T(8,128)(2,1)S(1)}, bf16[128,4096]{1,0:T(8,128)(2,1)S(1)}, u32[]{:S(2)}, u32[]{:S(2)}) collective-permute-start(bf16[128,4096]{1,0:T(8,128)(2,1)S(1)} %get-tuple-element.175), channel_id=1, source_target_pairs={{0,2},{2,0},{4,6},{6,4},{8,10},{10,8},{12,14},{14,12},{16,18},{18,... | collective-permute-start | bytes 3145736 | tf_op jit(solution)/shard_map/ppermute | solution.py:387
  241.4 3.8 %collective-permute-start.27 = (bf16[128,4096]{1,0:T(8,128)(2,1)S(1)}, bf16[128,4096]{1,0:T(8,128)(2,1)S(1)}, u32[]{:S(2)}, u32[]{:S(2)}) collective-permute-start(bf16[128,4096]{1,0:T(8,128)(2,1)S(1)} %get-tuple-element.176), channel_id=1, source_target_pairs={{0,2},{2,0},{4,6},{6,4},{8,10},{10,8},{12,14},{14,12},{16,18},{18,... | collective-permute-start | bytes 3145736 | tf_op jit(solution)/shard_map/ppermute | solution.py:387
  246.6 25.2 %collective-permute-start.32 = (bf16[256,4096]{1,0:T(8,128)(2,1)S(1)}, bf16[256,4096]{1,0:T(8,128)(2,1)S(1)}, u32[]{:S(2)}, u32[]{:S(2)}) collective-permute-start(bf16[256,4096]{1,0:T(8,128)(2,1)S(1)} %shard_map.123), channel_id=1, source_target_pairs={{0,4},{2,10},{8,0},{10,18},{16,8},{18,26},{24,16},{26,30},{28,24},... | collective-permute-start | bytes 6291464 | tf_op jit(solution)/shard_map/ppermute | solution.py:384
  247.9 10.8 %collective-permute-start.29 = (bf16[768,256]{1,0:T(8,128)(2,1)S(1)}, bf16[768,256]{1,0:T(8,128)(2,1)S(1)}, u32[]{:S(2)}, u32[]{:S(2)}) collective-permute-start(bf16[768,256]{1,0:T(8,128)(2,1)S(1)} %bitcast.52), channel_id=1, source_target_pairs={{0,1},{1,0},{2,3},{3,2},{4,5},{5,4},{6,7},{7,6},{8,9},{9,8},{10,11... | collective-permute-start | bytes 1179656 | tf_op jit(solution)/shard_map/ppermute | solution.py:416
  258.7 4.1 %collective-permute-start.30 = (bf16[128,4096]{1,0:T(8,128)(2,1)S(1)}, bf16[128,4096]{1,0:T(8,128)(2,1)S(1)}, u32[]{:S(2)}, u32[]{:S(2)}) collective-permute-start(bf16[128,4096]{1,0:T(8,128)(2,1)S(1)} %get-tuple-element.188), channel_id=1, source_target_pairs={{0,2},{2,0},{4,6},{6,4},{8,10},{10,8},{12,14},{14,12},{16,18},{18,... | collective-permute-start | bytes 3145736 | tf_op jit(solution)/shard_map/ppermute | solution.py:387
  260.6 3.8 %collective-permute-start.31 = (bf16[128,4096]{1,0:T(8,128)(2,1)S(1)}, bf16[128,4096]{1,0:T(8,128)(2,1)S(1)}, u32[]{:S(2)}, u32[]{:S(2)}) collective-permute-start(bf16[128,4096]{1,0:T(8,128)(2,1)S(1)} %get-tuple-element.189), channel_id=1, source_target_pairs={{0,2},{2,0},{4,6},{6,4},{8,10},{10,8},{12,14},{14,12},{16,18},{18,... | collective-permute-start | bytes 3145736 | tf_op jit(solution)/shard_map/ppermute | solution.py:387
  274.3 10.7 %copy-start.26 = (f32[4,4,9,128]{3,2,1,0:T(8,128)S(1)}, f32[4,4,9,128]{3,2,1,0:T(8,128)}, u32[]{:S(2)}) copy-start(f32[4,4,9,128]{3,2,1,0:T(8,128)} %get-tuple-element.204) | copy-start | bytes 221188
  274.3 14.2 %collective-permute-start.35 = (bf16[128,4096]{1,0:T(8,128)(2,1)}, bf16[128,4096]{1,0:T(8,128)(2,1)S(1)}, u32[]{:S(2)}, u32[]{:S(2)}) collective-permute-start(bf16[128,4096]{1,0:T(8,128)(2,1)} %get-tuple-element.202), channel_id=1, source_target_pairs={{0,4},{2,10},{8,0},{10,18},{16,8},{18,26},{24,16},{26,30},{28,24},... | collective-permute-start | bytes 3145736 | tf_op jit(solution)/shard_map/ppermute | solution.py:384
  275.5 26.3 %collective-permute-start.36 = (bf16[128,4096]{1,0:T(8,128)(2,1)}, bf16[128,4096]{1,0:T(8,128)(2,1)S(1)}, u32[]{:S(2)}, u32[]{:S(2)}) collective-permute-start(bf16[128,4096]{1,0:T(8,128)(2,1)} %get-tuple-element.203), channel_id=1, source_target_pairs={{0,6},{2,8},{8,2},{10,16},{16,10},{18,24},{24,18},{26,28},{28,26},... | collective-permute-start | bytes 3145736 | tf_op jit(solution)/shard_map/ppermute | solution.py:384
  284.5 2.3 collective-permute-start.33
  284.5 3.0 collective-permute-start.34
  (21 other events, 59.7 us)

commit v5 on v4

--- a/solution.py
+++ b/solution.py
@@ -121,9 +121,9 @@
     for j in every:
         y_two = jnp.concatenate([y_s[j, :rows, :], y_s[j, GROUP:, :]], axis=1)
         d_products.append(dot(y_two, jnp.concatenate(filters[j], axis=1), ((1,), (1,))))
-    folds = [dot(x_twos[j], y_s[j, :rows, :], ((0,), (0,))) for j in every]
+    folds = [dot(y_s[j, :rows, :], x_twos[j], ((0,), (0,))) for j in every]
     for j in every:
-        fold = jnp.where(col >= row, folds[j][:LONG], folds[j][LONG:])
+        fold = jnp.where(col <= row, folds[j][:, :LONG], folds[j][:, LONG:])
         width = LONG
         while width > 8:
             width //= 2
@@ -155,7 +155,7 @@
     blocks, channels, _ = g.shape
     count, sets = len(proj_sets[0]), len(proj_sets)
     groups = channels // GROUP
-    per_step = next(n for n in (4, 2, 1) if groups % n == 0)
+    per_step = next(n for n in (2, 1) if groups % n == 0)
     steps = groups // per_step
     rows = blocks * GROUP
     high = per_step * GROUP
@@ -199,7 +199,8 @@
     )(order, short_kernel, long_kernel.reshape(steps, per_step, LONG), g, *[x for s in proj_sets for x in s])
     mixed, d_proj, (gs, gl) = outs[0], outs[1:-2], outs[-2:]
     grad_short = jnp.sum(gs, axis=-1).reshape(groups, 3, SHORT).transpose(1, 0, 2)
-    return mixed, d_proj, grad_short, gl.reshape(groups, LONG)
+    grad_long = jnp.roll(jnp.flip(gl.reshape(groups, LONG), axis=1), 1, axis=1)
+    return mixed, d_proj, grad_short, grad_long
 
 
 def restack_body(t_ref, *refs):
@@ -441,14 +442,12 @@
         if s < half - 1:
             arrived, near, far, projected[-1] = stage((coming, near, far, projected[-1]))
     crossed = across(far)
-    arrived, near = stage((coming, near))
-    shared, projected[-1] = stage((arrived, projected[-1]))
-    mates = [swap(shared[: held // 2]), swap(shared[held // 2 :])]
-    grad_out, mates = stage((grad_out, mates))
+    arrived, near, grad_out = stage((coming, near, grad_out))
     incoming = lax.all_to_all(
         grad_out.reshape(n_ctx, channels, held), "ctx", split_axis=0, concat_axis=0, tiled=True
     )
-    last, far = project([arrived, *mates])
+    shared, projected[-1] = stage((arrived, projected[-1]))
+    last, far = project([arrived, swap(shared[: held // 2]), swap(shared[held // 2 :])])
     far, crossed = stage((far, crossed))
     projected += [(near, crossed), (last, across(far))]
 
@@ -462,9 +461,8 @@
     )
 
     first, met, later = [meet(d_proj[s]) for s in (half, half - 1, half - 2)]
-    mixed, first = stage((mixed, first))
     mixed_out = lax.all_to_all(mixed, "ctx", split_axis=0, concat_axis=0, tiled=True).reshape(-1, held)
-    keep, *give = unproject(first, held, held // 2, held // 2)
+    keep, *give = unproject(first, held, *((80, 48) if held == 128 else (held // 2, held // 2)))
     total = add_kernel([keep], [swap(x) for x in give])
     total, met, rest = stage((total, met, d_proj[: half - 2]))
     for s in range(half - 1, 0, -1):

time: 306 us -> 285 us (0.931)
  waiting for transfers between devices: 118 us -> 100 us
  Pallas kernels: 106 us -> 102 us
    ppermute x10, waiting for transfers between devices: 49.1 us -> 31.4 us  [across(): return None if x is None else lax.ppermute(x, 'tp', [(0, 1), (1, 0)])]
    pallas_call x1, Pallas kernels: 20.7 us -> 16.6 us  [mix(): pl.pallas_call(functools.partial(mix_body, count, sets, per_step, grouped...]
  transfers between devices with their start and end apart: 39 -> 39, of which waited for: 31 -> 27; matrix products, arithmetic and copies ran while one was open for 1% -> 2% of each run, Pallas kernels for 26% -> 27%
where the time goes in v5:
time: 285 us
  Pallas kernels  102 us (36%)
  waiting for transfers between devices  100 us (35%)
  starting transfers between devices  49.8 us (17%)
  local copies, waits for them, and re-layouts  30.6 us (11%)
    ppermute x10, waiting for transfers between devices, one_way(): return lax.ppermute(x, 'ctx', hops)  51.8 us
    pallas_call x5, Pallas kernels, unproject_kernel(): pl.pallas_call(unproject_body, grid=(width // tile,), in_specs=[pl.BlockS...  41.3 us
    pallas_call x5, Pallas kernels, project_kernel(): pl.pallas_call(functools.partial(project_body, len(pieces)), grid=(4,), i...  32 us
    ppermute x10, waiting for transfers between devices, across(): return None if x is None else lax.ppermute(x, 'tp', [(0, 1), (1, 0)])  31.4 us
    unnamed x63, local copies, waits for them, and re-layouts  28.8 us
    ppermute x17, waiting for transfers between devices, swap(): return lax.ppermute(x, 'ctx', [(d, d ^ 1) for d in range(n_ctx)])  16.9 us
    pallas_call x1, Pallas kernels, mix(): pl.pallas_call(functools.partial(mix_body, count, sets, per_step, grouped...  16.6 us
    ppermute x10, starting transfers between devices, one_way(): return lax.ppermute(x, 'ctx', hops)  14.2 us
  transfers between devices with their start and end apart: 39, of which 27 were waited for; matrix products, arithmetic and copies ran while one was open for 2% of the time, Pallas kernels for 27%

profile of v5, /device:TPU:1, one launch (start us, length us, event | category | flops | bytes accessed | tf_op | source)
XLA Modules:
  0.0 284.6 jit_solution(9503064756858401305)
XLA Ops:
  0.8 2.7 collective-permute-start.1
  6.0 2.2 copy-done.4
  8.2 2.2 copy-done.5
  10.4 2.2 copy-done.6
  12.6 1.7 shard_map.111
  14.4 4.3 %shard_map.112 = (bf16[768,256]{1,0:T(8,128)(2,1)S(1)}, bf16[768,256]{1,0:T(8,128)(2,1)S(1)}) custom-call(bf16[128,4096]{1,0:T(8,128)(2,1)S(1)} %copy-done.7, bf16[128,4096]{1,0:T(8,128)(2,1)S(1)} %collective-permute-done.2.refs_1_, bf16[1536,4096]{1,0:T(8,128)(2,1)S(1)} %bitcast.31), custom_call_target="tpu_custom_call" | custom-call | flops 1 | bytes 1 | tf_op jit(solution)/shard_map/pallas_call | solution.py:265
  18.7 7.8 %collective-permute-done.1 = bf16[128,4096]{1,0:T(8,128)(2,1)S(1)} collective-permute-done((bf16[128,4096]{1,0:T(8,128)(2,1)}, bf16[128,4096]{1,0:T(8,128)(2,1)S(1)}, u32[]{:S(2)}, u32[]{:S(2)}) %collective-permute-start.1) | collective-permute-done | bytes 1048608 | tf_op jit(solution)/shard_map/ppermute | solution.py:385
  28.0 1.4 collective-permute-start.3
  31.8 7.8 %shard_map.113 = (bf16[768,512]{1,0:T(8,128)(2,1)S(1)}, bf16[768,512]{1,0:T(8,128)(2,1)S(1)}) custom-call(bf16[256,4096]{1,0:T(8,128)(2,1)S(1)} %constant_dynamic-update-slice_fusion.refs_0_, bf16[256,4096]{1,0:T(8,128)(2,1)S(1)} %collective-permute-done.4.refs_1_, bf16[1536,4096]{1,0:T(8,128)(2,1)S(1)} %bitcast.32), custom_call_target="tpu_custom_call" | custom-call | flops 1 | bytes 1 | tf_op jit(solution)/shard_map/pallas_call | solution.py:265
  40.4 12.7 %collective-permute-done.3.refs_0_ = bf16[256,4096]{1,0:T(8,128)(2,1)S(1)} collective-permute-done((bf16[256,4096]{1,0:T(8,128)(2,1)S(1)}, bf16[256,4096]{1,0:T(8,128)(2,1)S(1)}, u32[]{:S(2)}, u32[]{:S(2)}) %collective-permute-start.3) | collective-permute-done | bytes 2097184 | tf_op jit(solution)/shard_map/ppermute | solution.py:385
  58.0 7.8 %shard_map.114 = (bf16[768,512]{1,0:T(8,128)(2,1)S(1)}, bf16[768,512]{1,0:T(8,128)(2,1)S(1)}) custom-call(bf16[256,4096]{1,0:T(8,128)(2,1)S(1)} %collective-permute-done.3.refs_0_, bf16[256,4096]{1,0:T(8,128)(2,1)S(1)} %collective-permute-done.7.refs_1_, bf16[1536,4096]{1,0:T(8,128)(2,1)S(1)} %bitcast.33), custom_call_target="tpu_custom_call" | custom-call | flops 1 | bytes 1 | tf_op jit(solution)/shard_map/pallas_call | solution.py:265
  65.7 8.2 %collective-permute-done.8 = bf16[768,512]{1,0:T(8,128)(2,1)S(1)} collective-permute-done((bf16[768,512]{1,0:T(8,128)(2,1)S(1)}, bf16[768,512]{1,0:T(8,128)(2,1)S(1)}, u32[]{:S(2)}, u32[]{:S(2)}) %collective-permute-start.8) | collective-permute-done | bytes 786464 | tf_op jit(solution)/shard_map/ppermute | solution.py:417
  74.0 5.7 %collective-permute-done.6.refs_0_ = bf16[256,4096]{1,0:T(8,128)(2,1)S(1)} collective-permute-done((bf16[256,4096]{1,0:T(8,128)(2,1)S(1)}, bf16[256,4096]{1,0:T(8,128)(2,1)S(1)}, u32[]{:S(2)}, u32[]{:S(2)}) %collective-permute-start.6) | collective-permute-done | bytes 2097184 | tf_op jit(solution)/shard_map/ppermute | solution.py:385
  80.3 1.4 collective-permute-start.9
  84.0 7.8 %shard_map.115 = (bf16[768,512]{1,0:T(8,128)(2,1)S(1)}, bf16[768,512]{1,0:T(8,128)(2,1)S(1)}) custom-call(bf16[256,4096]{1,0:T(8,128)(2,1)S(1)} %collective-permute-done.6.refs_0_, bf16[256,4096]{1,0:T(8,128)(2,1)S(1)} %collective-permute-done.10.refs_1_, bf16[1536,4096]{1,0:T(8,128)(2,1)S(1)} %bitcast.34), custom_call_target="tpu_custom_call" | custom-call | flops 1 | bytes 1 | tf_op jit(solution)/shard_map/pallas_call | solution.py:265
  92.7 2.0 collective-permute-done.9.refs_0_
  94.7 6.4 %all-to-all-start = ((bf16[16,256,128]{2,1,0:T(8,128)(2,1)}), bf16[16,256,128]{2,1,0:T(8,128)(2,1)}, u32[]{:S(2)}, u32[]{:S(2)}) async-start(bf16[16,256,128]{2,1,0:T(8,128)(2,1)} %bitcast.59), calls=%async_computation | async-start | bytes 2097152 | tf_op jit(solution)/shard_map/all_to_all | solution.py:446
  103.5 1.5 collective-permute-done.13.refs_2_
  105.8 4.6 %copy-done.1 = bf16[2,3,256,4096]{3,2,1,0:T(8,128)(2,1)S(1)} copy-done((bf16[2,3,256,4096]{3,2,1,0:T(8,128)(2,1)S(1)}, bf16[2,3,256,4096]{3,2,1,0:T(8,128)(2,1)}, u32[]{:S(2)}) %copy-start.1) | copy-done | bytes 12582936
  110.3 4.3 %shard_map.116 = (bf16[768,256]{1,0:T(8,128)(2,1)S(1)}, bf16[768,256]{1,0:T(8,128)(2,1)S(1)}) custom-call(bf16[128,4096]{1,0:T(8,128)(2,1)S(1)} %collective-permute-done.9.refs_0_, bf16[64,4096]{1,0:T(8,128)(2,1)S(1)} %collective-permute-done.12.refs_1_, bf16[64,4096]{1,0:T(8,128)(2,1)S(1)} %collective-permute-done.13.refs_2_, bf16[1536,4096]{1,0:T(8,128)(2,1)S(1)} %bitcast.35), custom_call_target="tpu_custom_call" | custom-call | flops 1 | bytes 1 | tf_op jit(solution)/shard_map/pallas_call | solution.py:265
  115.4 4.3 %collective-permute-done.14 = bf16[768,512]{1,0:T(8,128)(2,1)S(1)} collective-permute-done((bf16[768,512]{1,0:T(8,128)(2,1)S(1)}, bf16[768,512]{1,0:T(8,128)(2,1)S(1)}, u32[]{:S(2)}, u32[]{:S(2)}) %collective-permute-start.14) | collective-permute-done | bytes 786464 | tf_op jit(solution)/shard_map/ppermute | solution.py:417
  121.0 7.9 %collective-permute-done.15 = bf16[768,256]{1,0:T(8,128)(2,1)S(1)} collective-permute-done((bf16[768,256]{1,0:T(8,128)(2,1)S(1)}, bf16[768,256]{1,0:T(8,128)(2,1)S(1)}, u32[]{:S(2)}, u32[]{:S(2)}) %collective-permute-start.15) | collective-permute-done | bytes 393248 | tf_op jit(solution)/shard_map/ppermute | solution.py:417
  129.7 16.6 %shard_map.117 = (bf16[16,256,128]{2,1,0:T(8,128)(2,1)}, bf16[3,256,256]{2,1,0:T(8,128)(2,1)}, bf16[3,256,512]{2,1,0:T(8,128)(2,1)}, bf16[3,256,512]{2,1,0:T(8,1...) custom-call(s32[16]{0:T(128)} %dynamic-slice_bitcast_fusion.order, ...), custom_call_target="tpu_custom_call" | custom-call | flops 1 | bytes 1 | tf_op jit(solution)/shard_map/pallas_call | solution.py:166
  147.6 8.7 %all-to-all-start.1 = ((bf16[16,256,128]{2,1,0:T(8,128)(2,1)}), bf16[16,256,128]{2,1,0:T(8,128)(2,1)S(1)}, u32[]{:S(2)}, u32[]{:S(2)}) async-start(bf16[16,256,128]{2,1,0:T(8,128)(2,1)} %get-tuple-element.158), calls=%async_computation.1 | async-start | bytes 2097152 | tf_op jit(solution)/shard_map/all_to_all | solution.py:464
  156.6 4.6 %copy-done.2 = bf16[2,3,256,4096]{3,2,1,0:T(8,128)(2,1)S(1)} copy-done((bf16[2,3,256,4096]{3,2,1,0:T(8,128)(2,1)S(1)}, bf16[2,3,256,4096]{3,2,1,0:T(8,128)(2,1)}, u32[]{:S(2)}) %copy-start.2) | copy-done | bytes 12582936
  161.2 6.0 %shard_map.118 = (bf16[128,4096]{1,0:T(8,128)(2,1)S(1)}, bf16[80,4096]{1,0:T(8,128)(2,1)S(1)}, bf16[48,4096]{1,0:T(8,128)(2,1)S(1)}) custom-call(bf16[768,256]{1,0:T(8,128)(2,1)S(1)} %bitcast.56, bf16[768,256]{1,0:T(8,128)(2,1)S(1)} %collective-permute-done.16.far_ref, bf16[1536,4096]{1,0:T(8,128)(2,1)S(1)} %bitcast.36), custom_call_target="tpu_custom_call" | custom-call | flops 1 | bytes 1 | tf_op jit(solution)/shard_map/pallas_call | solution.py:302
  167.2 1.6 collective-permute-start.17
  172.3 3.1 %collective-permute-done.19.far_ref = bf16[768,512]{1,0:T(8,128)(2,1)S(1)} collective-permute-done((bf16[768,512]{1,0:T(8,128)(2,1)S(1)}, bf16[768,512]{1,0:T(8,128)(2,1)S(1)}, u32[]{:S(2)}, u32[]{:S(2)}) %collective-permute-start.19) | collective-permute-done | bytes 786464 | tf_op jit(solution)/shard_map/ppermute | solution.py:417
  176.5 9.6 %shard_map.120 = (bf16[256,4096]{1,0:T(8,128)(2,1)S(1)}, bf16[96,4096]{1,0:T(8,128)(2,1)S(1)}, bf16[80,4096]{1,0:T(8,128)(2,1)S(1)}, bf16[80,4096]{1,0:T(8,128)(2,1)S(1)}) custom-call(bf16[768,512]{1,0:T(8,128)(2,1)S(1)} %bitcast.49, bf16[768,512]{1,0:T(8,128)(2,1)S(1)} %collective-permute-done.19.far_ref, bf16[1536,4096]{1,0:T(8,128)(2,1)S(1)} %bitcast.37), custom_call_target="tpu_custom_call" | custom-call | flops 1 | bytes 1 | tf_op jit(solution)/shard_map/pallas_call | solution.py:302
  186.1 6.2 %collective-permute-done.20.far_ref = bf16[768,512]{1,0:T(8,128)(2,1)S(1)} collective-permute-done((bf16[768,512]{1,0:T(8,128)(2,1)S(1)}, bf16[768,512]{1,0:T(8,128)(2,1)S(1)}, u32[]{:S(2)}, u32[]{:S(2)}) %collective-permute-start.20) | collective-permute-done | bytes 786464 | tf_op jit(solution)/shard_map/ppermute | solution.py:417
  194.6 2.3 collective-permute-done.22.refs_2_
  199.1 1.4 collective-permute-start.28
  201.1 4.6 %copy-done.3 = bf16[2,3,256,4096]{3,2,1,0:T(8,128)(2,1)S(1)} copy-done((bf16[2,3,256,4096]{3,2,1,0:T(8,128)(2,1)S(1)}, bf16[2,3,256,4096]{3,2,1,0:T(8,128)(2,1)}, u32[]{:S(2)}) %copy-start.3) | copy-done | bytes 12582936
  208.0 9.5 %shard_map.122 = (bf16[256,4096]{1,0:T(8,128)(2,1)S(1)}, bf16[128,4096]{1,0:T(8,128)(2,1)S(1)}, bf16[128,4096]{1,0:T(8,128)(2,1)S(1)}) custom-call(bf16[768,512]{1,0:T(8,128)(2,1)S(1)} %bitcast.47, bf16[768,512]{1,0:T(8,128)(2,1)S(1)} %copy-done.12, bf16[1536,4096]{1,0:T(8,128)(2,1)S(1)} %bitcast.38), custom_call_target="tpu_custom_call" | custom-call | flops 1 | bytes 1 | tf_op jit(solution)/shard_map/pallas_call | solution.py:302
  217.5 1.6 collective-permute-done.25.far_ref
  219.1 1.5 collective-permute-start.26
  220.7 1.5 shard_map.124
  222.9 1.5 collective-permute-done.27.refs_2_
  227.8 9.6 %shard_map.125 = (bf16[256,4096]{1,0:T(8,128)(2,1)S(1)}, bf16[128,4096]{1,0:T(8,128)(2,1)S(1)}, bf16[128,4096]{1,0:T(8,128)(2,1)S(1)}) custom-call(bf16[768,512]{1,0:T(8,128)(2,1)S(1)} %bitcast.45, bf16[768,512]{1,0:T(8,128)(2,1)S(1)} %collective-permute-done.25.far_ref, bf16[1536,4096]{1,0:T(8,128)(2,1)S(1)} %bitcast.41), custom_call_target="tpu_custom_call" | custom-call | flops 1 | bytes 1 | tf_op jit(solution)/shard_map/pallas_call | solution.py:302
  237.3 1.6 collective-permute-start.30
  239.0 2.2 collective-permute-done.30.refs_1_
  241.2 1.5 collective-permute-done.31.refs_2_
  242.7 8.4 %collective-permute-done.32.refs_3_ = bf16[256,4096]{1,0:T(8,128)(2,1)S(1)} collective-permute-done((bf16[256,4096]{1,0:T(8,128)(2,1)S(1)}, bf16[256,4096]{1,0:T(8,128)(2,1)S(1)}, u32[]{:S(2)}, u32[]{:S(2)}) %collective-permute-start.32) | collective-permute-done | bytes 2097184 | tf_op jit(solution)/shard_map/ppermute | solution.py:385
  251.1 2.4 shard_map.126
  254.7 2.4 collective-permute-start.36
  257.1 6.6 %shard_map.127 = (bf16[128,4096]{1,0:T(8,128)(2,1)S(1)}, bf16[64,4096]{1,0:T(8,128)(2,1)}, bf16[64,4096]{1,0:T(8,128)(2,1)}) custom-call(bf16[768,256]{1,0:T(8,128)(2,1)S(1)} %bitcast.54, bf16[768,256]{1,0:T(8,128)(2,1)S(1)} %collective-permute-done.29.far_ref, bf16[1536,4096]{1,0:T(8,128)(2,1)S(1)} %bitcast.42), custom_call_target="tpu_custom_call" | custom-call | flops 1 | bytes 1 | tf_op jit(solution)/shard_map/pallas_call | solution.py:302
  267.7 13.3 %collective-permute-done.36.refs_4_ = bf16[128,4096]{1,0:T(8,128)(2,1)S(1)} collective-permute-done((bf16[128,4096]{1,0:T(8,128)(2,1)}, bf16[128,4096]{1,0:T(8,128)(2,1)S(1)}, u32[]{:S(2)}, u32[]{:S(2)}) %collective-permute-start.36) | collective-permute-done | bytes 1048608 | tf_op jit(solution)/shard_map/ppermute | solution.py:385
  281.0 3.7 %shard_map.128 = bf16[128,4096]{1,0:T(8,128)(2,1)} custom-call(bf16[128,4096]{1,0:T(8,128)(2,1)S(1)} %get-tuple-element.189.refs_0_, bf16[64,4096]{1,0:T(8,128)(2,1)} %collective-permute-done.33.refs_1_, bf16[64,4096]{1,0:T(8,128)(2,1)} %collective-permute-done.34.refs_2_, bf16[128,4096]{1,0:T(8,128)(2,1)S(1)} %collective-permute-done.35.refs_3_, ...), custom_call_target="tpu_custom_call" | custom-call | flops 1 | bytes 1 | tf_op jit(solution)/shard_map/pallas_call | solution.py:342
  (122 shorter events, 44.7 us)
Async XLA Ops:
  0.6 13.7 %collective-permute-start.2 = (bf16[128,4096]{1,0:T(8,128)(2,1)}, bf16[128,4096]{1,0:T(8,128)(2,1)S(1)}, u32[]{:S(2)}, u32[]{:S(2)}) collective-permute-start(bf16[128,4096]{1,0:T(8,128)(2,1)} %refs_0_.3), channel_id=1, source_target_pairs={{0,2},{2,0},{4,6},{6,4},{8,10},{10,8},{12,14},{14,12},{16,18},{18,... | collective-permute-start | bytes 3145736 | tf_op jit(solution)/shard_map/ppermute | solution.py:388
  0.8 25.7 %collective-permute-start.1 = (bf16[128,4096]{1,0:T(8,128)(2,1)}, bf16[128,4096]{1,0:T(8,128)(2,1)S(1)}, u32[]{:S(2)}, u32[]{:S(2)}) collective-permute-start(bf16[128,4096]{1,0:T(8,128)(2,1)} %refs_0_.3), channel_id=1, source_target_pairs={{0,6},{2,8},{8,2},{10,16},{16,10},{18,24},{24,18},{26,28},{28,26},... | collective-permute-start | bytes 3145736 | tf_op jit(solution)/shard_map/ppermute | solution.py:385
  3.5 23.9 %collective-permute-start = (bf16[128,4096]{1,0:T(8,128)(2,1)}, bf16[128,4096]{1,0:T(8,128)(2,1)S(1)}, u32[]{:S(2)}, u32[]{:S(2)}) collective-permute-start(bf16[128,4096]{1,0:T(8,128)(2,1)} %refs_0_.3), channel_id=1, source_target_pairs={{0,8},{2,6},{8,16},{10,2},{16,24},{18,10},{24,28},{26,18},{28,20},... | collective-permute-start | bytes 3145736 | tf_op jit(solution)/shard_map/ppermute | solution.py:385
  14.3 69.7 %copy-start = (bf16[2,3,256,4096]{3,2,1,0:T(8,128)(2,1)}, bf16[2,3,256,4096]{3,2,1,0:T(8,128)(2,1)S(1)}, u32[]{:S(2)}) copy-start(bf16[2,3,256,4096]{3,2,1,0:T(8,128)(2,1)S(1)} %shard_map.111) | copy-start | bytes 37748740
  27.6 4.2 %collective-permute-start.4 = (bf16[256,4096]{1,0:T(8,128)(2,1)S(1)}, bf16[256,4096]{1,0:T(8,128)(2,1)S(1)}, u32[]{:S(2)}, u32[]{:S(2)}) collective-permute-start(bf16[256,4096]{1,0:T(8,128)(2,1)S(1)} %constant_dynamic-update-slice_fusion.refs_0_), channel_id=1, source_target_pairs={{0,2},{2,0},{4,6},{6,4},{8,10},{10,8},{12,14},{14,12},{16,18},{18,... | collective-permute-start | bytes 6291464 | tf_op jit(solution)/shard_map/ppermute | solution.py:388
  28.0 25.2 %collective-permute-start.3 = (bf16[256,4096]{1,0:T(8,128)(2,1)S(1)}, bf16[256,4096]{1,0:T(8,128)(2,1)S(1)}, u32[]{:S(2)}, u32[]{:S(2)}) collective-permute-start(bf16[256,4096]{1,0:T(8,128)(2,1)S(1)} %constant_dynamic-update-slice_fusion.refs_0_), channel_id=1, source_target_pairs={{0,8},{2,6},{8,16},{10,2},{16,24},{18,10},{24,28},{26,18},{28,20},... | collective-permute-start | bytes 6291464 | tf_op jit(solution)/shard_map/ppermute | solution.py:385
  29.4 11.0 %collective-permute-start.5 = (bf16[768,256]{1,0:T(8,128)(2,1)S(1)}, bf16[768,256]{1,0:T(8,128)(2,1)S(1)}, u32[]{:S(2)}, u32[]{:S(2)}) collective-permute-start(bf16[768,256]{1,0:T(8,128)(2,1)S(1)} %get-tuple-element.111), channel_id=1, source_target_pairs={{0,1},{1,0},{2,3},{3,2},{4,5},{5,4},{6,7},{7,6},{8,9},{9,8},{10,11... | collective-permute-start | bytes 1179656 | tf_op jit(solution)/shard_map/ppermute | solution.py:417
  40.4 16.3 %copy-start.23 = (bf16[768,256]{1,0:T(8,128)(2,1)}, bf16[768,256]{1,0:T(8,128)(2,1)S(1)}, u32[]{:S(2)}) copy-start(bf16[768,256]{1,0:T(8,128)(2,1)S(1)} %collective-permute-done.5) | copy-start | bytes 1179652
  53.2 4.8 %collective-permute-start.7 = (bf16[256,4096]{1,0:T(8,128)(2,1)S(1)}, bf16[256,4096]{1,0:T(8,128)(2,1)S(1)}, u32[]{:S(2)}, u32[]{:S(2)}) collective-permute-start(bf16[256,4096]{1,0:T(8,128)(2,1)S(1)} %collective-permute-done.3.refs_0_), channel_id=1, source_target_pairs={{0,2},{2,0},{4,6},{6,4},{8,10},{10,8},{12,14},{14,12},{16,18},{18,... | collective-permute-start | bytes 6291464 | tf_op jit(solution)/shard_map/ppermute | solution.py:388
  54.2 25.5 %collective-permute-start.6 = (bf16[256,4096]{1,0:T(8,128)(2,1)S(1)}, bf16[256,4096]{1,0:T(8,128)(2,1)S(1)}, u32[]{:S(2)}, u32[]{:S(2)}) collective-permute-start(bf16[256,4096]{1,0:T(8,128)(2,1)S(1)} %collective-permute-done.3.refs_0_), channel_id=1, source_target_pairs={{0,8},{2,6},{8,16},{10,2},{16,24},{18,10},{24,28},{26,18},{28,20},... | collective-permute-start | bytes 6291464 | tf_op jit(solution)/shard_map/ppermute | solution.py:385
  55.5 18.4 %collective-permute-start.8 = (bf16[768,512]{1,0:T(8,128)(2,1)S(1)}, bf16[768,512]{1,0:T(8,128)(2,1)S(1)}, u32[]{:S(2)}, u32[]{:S(2)}) collective-permute-start(bf16[768,512]{1,0:T(8,128)(2,1)S(1)} %get-tuple-element.116), channel_id=1, source_target_pairs={{0,1},{1,0},{2,3},{3,2},{4,5},{5,4},{6,7},{7,6},{8,9},{9,8},{10,11... | collective-permute-start | bytes 2359304 | tf_op jit(solution)/shard_map/ppermute | solution.py:417
  65.7 26.0 %copy-start.15 = (bf16[768,512]{1,0:T(8,128)(2,1)}, bf16[768,512]{1,0:T(8,128)(2,1)S(1)}, u32[]{:S(2)}) copy-start(bf16[768,512]{1,0:T(8,128)(2,1)S(1)} %get-tuple-element.125) | copy-start | bytes 2359300
  74.0 17.8 %copy-start.21 = (bf16[768,512]{1,0:T(8,128)(2,1)}, bf16[768,512]{1,0:T(8,128)(2,1)S(1)}, u32[]{:S(2)}) copy-start(bf16[768,512]{1,0:T(8,128)(2,1)S(1)} %collective-permute-done.8) | copy-start | bytes 2359300
  79.7 4.3 %collective-permute-start.10 = (bf16[256,4096]{1,0:T(8,128)(2,1)S(1)}, bf16[256,4096]{1,0:T(8,128)(2,1)S(1)}, u32[]{:S(2)}, u32[]{:S(2)}) collective-permute-start(bf16[256,4096]{1,0:T(8,128)(2,1)S(1)} %collective-permute-done.6.refs_0_), channel_id=1, source_target_pairs={{0,2},{2,0},{4,6},{6,4},{8,10},{10,8},{12,14},{14,12},{16,18},{18,... | collective-permute-start | bytes 6291464 | tf_op jit(solution)/shard_map/ppermute | solution.py:388
  80.3 14.4 %collective-permute-start.9 = (bf16[128,4096]{1,0:T(8,128)(2,1)S(1)}, bf16[128,4096]{1,0:T(8,128)(2,1)S(1)}, u32[]{:S(2)}, u32[]{:S(2)}) collective-permute-start(bf16[128,4096]{1,0:T(8,128)(2,1)S(1)} %slice.21), channel_id=1, source_target_pairs={{0,8},{2,6},{8,16},{10,2},{16,24},{18,10},{24,28},{26,18},{28,20},... | collective-permute-start | bytes 3145736 | tf_op jit(solution)/shard_map/ppermute | solution.py:385
  81.7 19.4 %collective-permute-start.11 = (bf16[768,512]{1,0:T(8,128)(2,1)S(1)}, bf16[768,512]{1,0:T(8,128)(2,1)}, u32[]{:S(2)}, u32[]{:S(2)}) collective-permute-start(bf16[768,512]{1,0:T(8,128)(2,1)S(1)} %get-tuple-element.124), channel_id=1, source_target_pairs={{0,1},{1,0},{2,3},{3,2},{4,5},{5,4},{6,7},{7,6},{8,9},{9,8},{10,11... | collective-permute-start | bytes 2359304 | tf_op jit(solution)/shard_map/ppermute | solution.py:417
  94.7 34.2 %all-to-all-start = ((bf16[16,256,128]{2,1,0:T(8,128)(2,1)}), bf16[16,256,128]{2,1,0:T(8,128)(2,1)}, u32[]{:S(2)}, u32[]{:S(2)}) async-start(bf16[16,256,128]{2,1,0:T(8,128)(2,1)} %bitcast.59), calls=%async_computation | async-start | bytes 2097152 | tf_op jit(solution)/shard_map/all_to_all | solution.py:446
  101.1 18.6 %collective-permute-start.14 = (bf16[768,512]{1,0:T(8,128)(2,1)S(1)}, bf16[768,512]{1,0:T(8,128)(2,1)S(1)}, u32[]{:S(2)}, u32[]{:S(2)}) collective-permute-start(bf16[768,512]{1,0:T(8,128)(2,1)S(1)} %get-tuple-element.133), channel_id=1, source_target_pairs={{0,1},{1,0},{2,3},{3,2},{4,5},{5,4},{6,7},{7,6},{8,9},{9,8},{10,11... | collective-permute-start | bytes 2359304 | tf_op jit(solution)/shard_map/ppermute | solution.py:417
  102.5 2.5 collective-permute-start.13
  103.5 2.3 collective-permute-start.12
  119.7 9.2 %collective-permute-start.15 = (bf16[768,256]{1,0:T(8,128)(2,1)S(1)}, bf16[768,256]{1,0:T(8,128)(2,1)S(1)}, u32[]{:S(2)}, u32[]{:S(2)}) collective-permute-start(bf16[768,256]{1,0:T(8,128)(2,1)S(1)} %get-tuple-element.135), channel_id=1, source_target_pairs={{0,1},{1,0},{2,3},{3,2},{4,5},{5,4},{6,7},{7,6},{8,9},{9,8},{10,11... | collective-permute-start | bytes 1179656 | tf_op jit(solution)/shard_map/ppermute | solution.py:417
  146.3 10.3 %copy-start.18 = (bf16[3,256,256]{2,1,0:T(8,128)(2,1)S(1)}, bf16[3,256,256]{2,1,0:T(8,128)(2,1)}, u32[]{:S(2)}) copy-start(bf16[3,256,256]{2,1,0:T(8,128)(2,1)} %get-tuple-element.136) | copy-start | bytes 1179652
  146.3 10.3 %collective-permute-start.16 = (bf16[768,256]{1,0:T(8,128)(2,1)}, bf16[768,256]{1,0:T(8,128)(2,1)S(1)}, u32[]{:S(2)}, u32[]{:S(2)}) collective-permute-start(bf16[768,256]{1,0:T(8,128)(2,1)} %bitcast.55), channel_id=1, source_target_pairs={{0,1},{1,0},{2,3},{3,2},{4,5},{5,4},{6,7},{7,6},{8,9},{9,8},{10,11... | collective-permute-start | bytes 1179656 | tf_op jit(solution)/shard_map/ppermute | solution.py:417
  147.6 51.4 %all-to-all-start.1 = ((bf16[16,256,128]{2,1,0:T(8,128)(2,1)}), bf16[16,256,128]{2,1,0:T(8,128)(2,1)S(1)}, u32[]{:S(2)}, u32[]{:S(2)}) async-start(bf16[16,256,128]{2,1,0:T(8,128)(2,1)} %get-tuple-element.158), calls=%async_computation.1 | async-start | bytes 2097152 | tf_op jit(solution)/shard_map/all_to_all | solution.py:464
  156.3 19.2 %collective-permute-start.19 = (bf16[768,512]{1,0:T(8,128)(2,1)S(1)}, bf16[768,512]{1,0:T(8,128)(2,1)S(1)}, u32[]{:S(2)}, u32[]{:S(2)}) collective-permute-start(bf16[768,512]{1,0:T(8,128)(2,1)S(1)} %bitcast.48), channel_id=1, source_target_pairs={{0,1},{1,0},{2,3},{3,2},{4,5},{5,4},{6,7},{7,6},{8,9},{9,8},{10,11... | collective-permute-start | bytes 2359304 | tf_op jit(solution)/shard_map/ppermute | solution.py:417
  167.2 4.6 %collective-permute-start.17 = (bf16[80,4096]{1,0:T(8,128)(2,1)S(1)}, bf16[80,4096]{1,0:T(8,128)(2,1)S(1)}, u32[]{:S(2)}, u32[]{:S(2)}) collective-permute-start(bf16[80,4096]{1,0:T(8,128)(2,1)S(1)} %get-tuple-element.138), channel_id=1, source_target_pairs={{0,2},{2,0},{4,6},{6,4},{8,10},{10,8},{12,14},{14,12},{16,18},{18,... | collective-permute-start | bytes 1966088 | tf_op jit(solution)/shard_map/ppermute | solution.py:388
  168.8 23.5 %collective-permute-start.20 = (bf16[768,512]{1,0:T(8,128)(2,1)S(1)}, bf16[768,512]{1,0:T(8,128)(2,1)S(1)}, u32[]{:S(2)}, u32[]{:S(2)}) collective-permute-start(bf16[768,512]{1,0:T(8,128)(2,1)S(1)} %bitcast.46), channel_id=1, source_target_pairs={{0,1},{1,0},{2,3},{3,2},{4,5},{5,4},{6,7},{7,6},{8,9},{9,8},{10,11... | collective-permute-start | bytes 2359304 | tf_op jit(solution)/shard_map/ppermute | solution.py:417
  170.0 1.7 collective-permute-start.18
  175.5 22.4 %collective-permute-start.24 = (bf16[128,4096]{1,0:T(8,128)(2,1)S(1)}, bf16[128,4096]{1,0:T(8,128)(2,1)S(1)}, u32[]{:S(2)}, u32[]{:S(2)}) collective-permute-start(bf16[128,4096]{1,0:T(8,128)(2,1)S(1)} %shard_map.119), channel_id=1, source_target_pairs={{0,4},{2,10},{8,0},{10,18},{16,8},{18,26},{24,16},{26,30},{28,24},... | collective-permute-start | bytes 3145736 | tf_op jit(solution)/shard_map/ppermute | solution.py:385
  193.2 4.7 %collective-permute-start.21 = (bf16[96,4096]{1,0:T(8,128)(2,1)S(1)}, bf16[96,4096]{1,0:T(8,128)(2,1)S(1)}, u32[]{:S(2)}, u32[]{:S(2)}) collective-permute-start(bf16[96,4096]{1,0:T(8,128)(2,1)S(1)} %get-tuple-element.150), channel_id=1, source_target_pairs={{0,2},{2,0},{4,6},{6,4},{8,10},{10,8},{12,14},{14,12},{16,18},{18,... | collective-permute-start | bytes 2359304 | tf_op jit(solution)/shard_map/ppermute | solution.py:388
  194.1 2.8 %collective-permute-start.22 = (bf16[80,4096]{1,0:T(8,128)(2,1)S(1)}, bf16[80,4096]{1,0:T(8,128)(2,1)S(1)}, u32[]{:S(2)}, u32[]{:S(2)}) collective-permute-start(bf16[80,4096]{1,0:T(8,128)(2,1)S(1)} %get-tuple-element.151), channel_id=1, source_target_pairs={{0,2},{2,0},{4,6},{6,4},{8,10},{10,8},{12,14},{14,12},{16,18},{18,... | collective-permute-start | bytes 1966088 | tf_op jit(solution)/shard_map/ppermute | solution.py:388
  194.1 3.8 %collective-permute-start.23 = (bf16[80,4096]{1,0:T(8,128)(2,1)S(1)}, bf16[80,4096]{1,0:T(8,128)(2,1)S(1)}, u32[]{:S(2)}, u32[]{:S(2)}) collective-permute-start(bf16[80,4096]{1,0:T(8,128)(2,1)S(1)} %get-tuple-element.152), channel_id=1, source_target_pairs={{0,2},{2,0},{4,6},{6,4},{8,10},{10,8},{12,14},{14,12},{16,18},{18,... | collective-permute-start | bytes 1966088 | tf_op jit(solution)/shard_map/ppermute | solution.py:388
  199.1 25.4 %collective-permute-start.28 = (bf16[256,4096]{1,0:T(8,128)(2,1)S(1)}, bf16[256,4096]{1,0:T(8,128)(2,1)S(1)}, u32[]{:S(2)}, u32[]{:S(2)}) collective-permute-start(bf16[256,4096]{1,0:T(8,128)(2,1)S(1)} %shard_map.121), channel_id=1, source_target_pairs={{0,4},{2,10},{8,0},{10,18},{16,8},{18,26},{24,16},{26,30},{28,24},... | collective-permute-start | bytes 6291464 | tf_op jit(solution)/shard_map/ppermute | solution.py:385
  200.5 18.6 %collective-permute-start.25 = (bf16[768,512]{1,0:T(8,128)(2,1)}, bf16[768,512]{1,0:T(8,128)(2,1)S(1)}, u32[]{:S(2)}, u32[]{:S(2)}) collective-permute-start(bf16[768,512]{1,0:T(8,128)(2,1)} %bitcast.44), channel_id=1, source_target_pairs={{0,1},{1,0},{2,3},{3,2},{4,5},{5,4},{6,7},{7,6},{8,9},{9,8},{10,11... | collective-permute-start | bytes 2359304 | tf_op jit(solution)/shard_map/ppermute | solution.py:417
  207.9 19.8 %slice-start = ((s8[12582912]{0:T(1024)(128)(4,1)}), s8[4194304]{0:T(1024)(128)(4,1)S(1)}, s32[]{:S(2)}) async-start(s8[12582912]{0:T(1024)(128)(4,1)} %bitcast.39), calls=%async_computation.2 | async-start | bytes 8388608
  208.0 19.8 %slice-start.1 = ((s8[12582912]{0:T(1024)(128)(4,1)}), s8[4194304]{0:T(1024)(128)(4,1)S(1)}, s32[]{:S(2)}) async-start(s8[12582912]{0:T(1024)(128)(4,1)} %bitcast.39), calls=%async_computation.3 | async-start | bytes 8388608
  219.1 3.8 %collective-permute-start.26 = (bf16[128,4096]{1,0:T(8,128)(2,1)S(1)}, bf16[128,4096]{1,0:T(8,128)(2,1)S(1)}, u32[]{:S(2)}, u32[]{:S(2)}) collective-permute-start(bf16[128,4096]{1,0:T(8,128)(2,1)S(1)} %get-tuple-element.165), channel_id=1, source_target_pairs={{0,2},{2,0},{4,6},{6,4},{8,10},{10,8},{12,14},{14,12},{16,18},{18,... | collective-permute-start | bytes 3145736 | tf_op jit(solution)/shard_map/ppermute | solution.py:388
  220.7 3.8 %collective-permute-start.27 = (bf16[128,4096]{1,0:T(8,128)(2,1)S(1)}, bf16[128,4096]{1,0:T(8,128)(2,1)S(1)}, u32[]{:S(2)}, u32[]{:S(2)}) collective-permute-start(bf16[128,4096]{1,0:T(8,128)(2,1)S(1)} %get-tuple-element.166), channel_id=1, source_target_pairs={{0,2},{2,0},{4,6},{6,4},{8,10},{10,8},{12,14},{14,12},{16,18},{18,... | collective-permute-start | bytes 3145736 | tf_op jit(solution)/shard_map/ppermute | solution.py:388
  225.9 25.2 %collective-permute-start.32 = (bf16[256,4096]{1,0:T(8,128)(2,1)S(1)}, bf16[256,4096]{1,0:T(8,128)(2,1)S(1)}, u32[]{:S(2)}, u32[]{:S(2)}) collective-permute-start(bf16[256,4096]{1,0:T(8,128)(2,1)S(1)} %shard_map.123), channel_id=1, source_target_pairs={{0,4},{2,10},{8,0},{10,18},{16,8},{18,26},{24,16},{26,30},{28,24},... | collective-permute-start | bytes 6291464 | tf_op jit(solution)/shard_map/ppermute | solution.py:385
  227.1 10.2 %collective-permute-start.29 = (bf16[768,256]{1,0:T(8,128)(2,1)S(1)}, bf16[768,256]{1,0:T(8,128)(2,1)S(1)}, u32[]{:S(2)}, u32[]{:S(2)}) collective-permute-start(bf16[768,256]{1,0:T(8,128)(2,1)S(1)} %bitcast.53), channel_id=1, source_target_pairs={{0,1},{1,0},{2,3},{3,2},{4,5},{5,4},{6,7},{7,6},{8,9},{9,8},{10,11... | collective-permute-start | bytes 1179656 | tf_op jit(solution)/shard_map/ppermute | solution.py:417
  237.3 3.9 %collective-permute-start.30 = (bf16[128,4096]{1,0:T(8,128)(2,1)S(1)}, bf16[128,4096]{1,0:T(8,128)(2,1)S(1)}, u32[]{:S(2)}, u32[]{:S(2)}) collective-permute-start(bf16[128,4096]{1,0:T(8,128)(2,1)S(1)} %get-tuple-element.178), channel_id=1, source_target_pairs={{0,2},{2,0},{4,6},{6,4},{8,10},{10,8},{12,14},{14,12},{16,18},{18,... | collective-permute-start | bytes 3145736 | tf_op jit(solution)/shard_map/ppermute | solution.py:388
  238.9 3.8 %collective-permute-start.31 = (bf16[128,4096]{1,0:T(8,128)(2,1)S(1)}, bf16[128,4096]{1,0:T(8,128)(2,1)S(1)}, u32[]{:S(2)}, u32[]{:S(2)}) collective-permute-start(bf16[128,4096]{1,0:T(8,128)(2,1)S(1)} %get-tuple-element.179), channel_id=1, source_target_pairs={{0,2},{2,0},{4,6},{6,4},{8,10},{10,8},{12,14},{14,12},{16,18},{18,... | collective-permute-start | bytes 3145736 | tf_op jit(solution)/shard_map/ppermute | solution.py:388
  253.5 10.7 %copy-start.26 = (f32[8,2,128]{2,1,0:T(2,128)S(1)}, f32[8,2,128]{2,1,0:T(2,128)}, u32[]{:S(2)}) copy-start(f32[8,2,128]{2,1,0:T(2,128)} %get-tuple-element.195) | copy-start | bytes 24580
  253.5 10.9 %copy-start.25 = (f32[8,2,9,128]{3,2,1,0:T(8,128)S(1)}, f32[8,2,9,128]{3,2,1,0:T(8,128)}, u32[]{:S(2)}) copy-start(f32[8,2,9,128]{3,2,1,0:T(8,128)} %get-tuple-element.194) | copy-start | bytes 221188
  253.5 14.2 %collective-permute-start.35 = (bf16[128,4096]{1,0:T(8,128)(2,1)}, bf16[128,4096]{1,0:T(8,128)(2,1)S(1)}, u32[]{:S(2)}, u32[]{:S(2)}) collective-permute-start(bf16[128,4096]{1,0:T(8,128)(2,1)} %get-tuple-element.192), channel_id=1, source_target_pairs={{0,4},{2,10},{8,0},{10,18},{16,8},{18,26},{24,16},{26,30},{28,24},... | collective-permute-start | bytes 3145736 | tf_op jit(solution)/shard_map/ppermute | solution.py:385
  254.7 26.3 %collective-permute-start.36 = (bf16[128,4096]{1,0:T(8,128)(2,1)}, bf16[128,4096]{1,0:T(8,128)(2,1)S(1)}, u32[]{:S(2)}, u32[]{:S(2)}) collective-permute-start(bf16[128,4096]{1,0:T(8,128)(2,1)} %get-tuple-element.193), channel_id=1, source_target_pairs={{0,6},{2,8},{8,2},{10,16},{16,10},{18,24},{24,18},{26,28},{28,26},... | collective-permute-start | bytes 3145736 | tf_op jit(solution)/shard_map/ppermute | solution.py:385
  263.7 2.3 collective-permute-start.33
  263.7 3.0 %collective-permute-start.34 = (bf16[64,4096]{1,0:T(8,128)(2,1)}, bf16[64,4096]{1,0:T(8,128)(2,1)}, u32[]{:S(2)}, u32[]{:S(2)}) collective-permute-start(bf16[64,4096]{1,0:T(8,128)(2,1)} %get-tuple-element.191), channel_id=1, source_target_pairs={{0,2},{2,0},{4,6},{6,4},{8,10},{10,8},{12,14},{14,12},{16,18},{18,... | collective-permute-start | bytes 1572872 | tf_op jit(solution)/shard_map/ppermute | solution.py:388
  (21 other events, 73.4 us)

commit v6 on v5

--- a/solution.py
+++ b/solution.py
@@ -49,17 +49,15 @@
     refs = refs[sets * count :]
     d_count = len(grouped)
     mixed_ref, d_refs, gs_ref, gl_ref = refs[0], refs[1 : 1 + d_count], refs[1 + d_count], refs[2 + d_count]
-    p_s, x_s, y_s, d_s, e_s = refs[3 + d_count :]
+    p_s, f_s, x_s, y_s, d_s, e_s = refs[3 + d_count :]
     blocks = g_ref.shape[0]
     rows = blocks * GROUP
     step = pl.program_id(0)
 
     @pl.when(step == 0)
     def _():
-        p_s[:, :, 0:GROUP, :] = jnp.zeros((per_step, 3, GROUP, LONG), F32)
         x_s[:, 0:GROUP, :] = jnp.zeros((per_step, GROUP, LONG), BF16)
         y_s[:, rows:, :] = jnp.zeros((per_step, GROUP, LONG), BF16)
-        d_s[:, :, rows:, :] = jnp.zeros((per_step, 3, GROUP, LONG), F32)
 
     halves = [(a, h) for a in range(count) for h in range(proj_refs[0][a].shape[2] // LONG)]
     places = [(a, h, where) for where, (a, h) in enumerate(halves)]
@@ -67,7 +65,9 @@
     for b, arrays in enumerate(grouped):
         inside = [where for array in arrays for a, _, where in places if a == array]
         d_places += [(b, h, where) for h, where in enumerate(inside)]
-    lane = lax.broadcasted_iota(jnp.int32, (rows, LONG), 1)
+    lane = lax.broadcasted_iota(jnp.int32, (GROUP, LONG), 1)
+    zero = jnp.zeros((GROUP, LONG), F32)
+    at_block = [slice(n * GROUP, (n + 1) * GROUP) for n in range(blocks)]
     sub8 = lax.broadcasted_iota(jnp.int32, (8, LONG), 0)
     col = lax.broadcasted_iota(jnp.int32, (LONG, LONG), 1)
     row = lax.broadcasted_iota(jnp.int32, (LONG, LONG), 0)
@@ -78,7 +78,7 @@
         [[short_ref[i, step * per_step + j, k] for k in range(SHORT)] for i in range(3)] for j in every
     ]
     for a, h, where in places:
-        at = pl.multiple_of((order[where] + 1) * GROUP, GROUP)
+        at = pl.multiple_of(order[where] * GROUP, GROUP)
         for j in every:
             for i in range(3):
                 part = proj_refs[0][a][i, mine[j], h * LONG : (h + 1) * LONG].astype(F32)
@@ -86,18 +86,20 @@
                     part = part + proj_refs[s][a][i, mine[j], h * LONG : (h + 1) * LONG].astype(F32)
                 p_s[j, i, pl.ds(at, GROUP), :] = part
 
-    feats = []
     for j in every:
-        feat = []
-        for i in range(3):
-            whole = p_s[j, i]
-            one = pltpu.roll(whole, 1, 1)
-            two = pltpu.roll(whole, 2, 1)
-            one = jnp.where(lane < 1, one[:rows], one[GROUP:])
-            two = jnp.where(lane < 2, two[:rows], two[GROUP:])
-            feat.append(taps[j][i][0] * whole[GROUP:] + taps[j][i][1] * one + taps[j][i][2] * two)
-        feats.append(feat)
-        x_s[j, GROUP:, :] = (feat[1] * feat[2]).astype(BF16)
+        before = [(zero, zero)] * 3
+        for at in at_block:
+            feat = []
+            for i in range(3):
+                here = p_s[j, i, at, :]
+                one = pltpu.roll(here, 1, 1)
+                two = pltpu.roll(here, 2, 1)
+                past_one = jnp.where(lane < 1, before[i][0], one)
+                past_two = jnp.where(lane < 2, before[i][1], two)
+                before[i] = (one, two)
+                feat.append(taps[j][i][0] * here + taps[j][i][1] * past_one + taps[j][i][2] * past_two)
+                f_s[j, i, at, :] = feat[i]
+            x_s[j, at.stop : at.stop + GROUP, :] = (feat[1] * feat[2]).astype(BF16)
 
     filters = []
     for j in every:
@@ -111,12 +113,13 @@
 
     x_twos = [jnp.concatenate([x_s[j, GROUP:, :], x_s[j, :rows, :]], axis=1) for j in every]
     inners = [dot(x_twos[j], jnp.concatenate(filters[j], axis=0), ((1,), (0,))) for j in every]
-    d_queries = []
     for j in every:
-        g = g_ref[:, mine[j], :].reshape(rows, LONG).astype(F32)
-        mixed_ref[:, mine[j], :] = (feats[j][0] * inners[j]).astype(BF16).reshape(blocks, GROUP, LONG)
-        y_s[j, :rows, :] = (g * feats[j][0]).astype(BF16)
-        d_queries.append(g * inners[j])
+        for n, at in enumerate(at_block):
+            g = g_ref[n, mine[j], :].astype(F32)
+            feat, inner = f_s[j, 0, at, :], inners[j][at]
+            mixed_ref[n, mine[j], :] = (feat * inner).astype(BF16)
+            y_s[j, at, :] = (g * feat).astype(BF16)
+            d_s[j, at, :] = g * inner
     d_products = []
     for j in every:
         y_two = jnp.concatenate([y_s[j, :rows, :], y_s[j, GROUP:, :]], axis=1)
@@ -133,17 +136,24 @@
         gl_ref[0, j : j + 1, :] = jnp.sum(fold, axis=0, keepdims=True)
 
     for j in every:
-        for i, d in enumerate((d_queries[j], d_products[j] * feats[j][2], d_products[j] * feats[j][1])):
-            d_s[j, i, :rows, :] = d
-            whole = d_s[j, i]
-            one = pltpu.roll(whole, LONG - 1, 1)
-            two = pltpu.roll(whole, LONG - 2, 1)
-            one = jnp.where(lane >= LONG - 1, one[GROUP:], one[:rows])
-            two = jnp.where(lane >= LONG - 2, two[GROUP:], two[:rows])
-            p = p_s[j, i, GROUP:, :]
-            for k, moved in enumerate((d, one, two)):
-                gs_ref[0, j, 3 * i + k : 3 * i + k + 1, :] = jnp.sum(p * moved, axis=0, keepdims=True)
-            e_s[j, i] = (taps[j][i][0] * d + taps[j][i][1] * one + taps[j][i][2] * two).astype(BF16)
+        after = [(zero, zero)] * 3
+        sums = [[zero] * SHORT for _ in range(3)]
+        for at in at_block[::-1]:
+            d_product = d_products[j][at]
+            for i, d in enumerate((d_s[j, at, :], d_product * f_s[j, 2, at, :], d_product * f_s[j, 1, at, :])):
+                one = pltpu.roll(d, LONG - 1, 1)
+                two = pltpu.roll(d, LONG - 2, 1)
+                next_one = jnp.where(lane >= LONG - 1, after[i][0], one)
+                next_two = jnp.where(lane >= LONG - 2, after[i][1], two)
+                after[i] = (one, two)
+                p = p_s[j, i, at, :]
+                sums[i] = [total + p * moved for total, moved in zip(sums[i], (d, next_one, next_two))]
+                e_s[j, i, at, :] = (
+                    taps[j][i][0] * d + taps[j][i][1] * next_one + taps[j][i][2] * next_two
+                ).astype(BF16)
+        for i in range(3):
+            for k in range(SHORT):
+                gs_ref[0, j, 3 * i + k : 3 * i + k + 1, :] = jnp.sum(sums[i][k], axis=0, keepdims=True)
     for a, h, where in d_places:
         at = pl.multiple_of(order[where] * GROUP, GROUP)
         for j in every:
@@ -181,10 +191,11 @@
                 pl.BlockSpec((1, per_step, LONG), lambda i, o: (i, 0, 0)),
             ],
             scratch_shapes=[
-                pltpu.VMEM((per_step, 3, rows + GROUP, LONG), F32),
+                pltpu.VMEM((per_step, 3, rows, LONG), F32),
+                pltpu.VMEM((per_step, 3, rows, LONG), F32),
                 pltpu.VMEM((per_step, rows + GROUP, LONG), BF16),
                 pltpu.VMEM((per_step, rows + GROUP, LONG), BF16),
-                pltpu.VMEM((per_step, 3, rows + GROUP, LONG), F32),
+                pltpu.VMEM((per_step, rows, LONG), F32),
                 pltpu.VMEM((per_step, 3, rows, LONG), BF16),
             ],
         ),
@@ -298,7 +309,7 @@
 def unproject_kernel(flat, near, far, cuts):
     rows, width = flat.shape
     tokens = near.shape[1]
-    tile = min(512, width)
+    tile = min(1024, width)
     return pl.pallas_call(
         unproject_body,
         grid=(width // tile,),
@@ -310,7 +321,7 @@
         out_specs=[pl.BlockSpec((cut, tile), lambda i: (0, i)) for cut in cuts],
         out_shape=[jax.ShapeDtypeStruct((cut, width), BF16) for cut in cuts],
         scratch_shapes=[pltpu.VMEM((tokens, rows), BF16)],
-        compiler_params=pltpu.CompilerParams(vmem_limit_bytes=14 * MIB),
+        compiler_params=pltpu.CompilerParams(vmem_limit_bytes=20 * MIB),
         cost_estimate=SMALL,
     )(near, far, flat)
 
@@ -470,9 +481,9 @@
         if s < half - 1:
             later = meet(rest[-1])
             rest = rest[:-1]
-        cuts = (96, 80, 80) if s == half - 1 and held == 128 else (held, held)
+        cuts = (96, 96, 64) if s == half - 1 and held == 128 else (held, held)
         keep, *give = unproject(met, 2 * held, *cuts)
-        give, later = stage((give, later))
+        give[-1], later = stage((give[-1], later))
         total = add_kernel([keep], [swap(x) for x in give], [coming], cut=2 if s == 1 else 1)
         if s == half - 2:
             mixed_out = copy_kernel(mixed_out)

time: 285 us -> 283 us (level)
  Pallas kernels: 102 us -> 97.9 us
  starting transfers between devices: 49.8 us -> 52.9 us
    pallas_call x5, Pallas kernels: 41.3 us -> 37.2 us  [unproject_kernel(): pl.pallas_call(unproject_body, grid=(width // tile,), in_specs=[pl.BlockS...]
    ppermute x17, waiting for transfers between devices: 16.9 us -> 12.8 us  [swap(): return lax.ppermute(x, 'ctx', [(d, d ^ 1) for d in range(n_ctx)])]
    ppermute x10, waiting for transfers between devices: 51.8 us -> 54.7 us  [one_way(): return lax.ppermute(x, 'ctx', hops)]
    unnamed x63 -> x57, local copies, waits for them, and re-layouts: 28.8 us -> 28.8 us
  transfers between devices with their start and end apart: 39 -> 39, of which waited for: 27 -> 26; matrix products, arithmetic and copies ran while one was open for 2% -> 2% of each run, Pallas kernels for 27% -> 26%
where the time goes in v6:
time: 283 us; the launch traced here: 282 us
  waiting for transfers between devices  99 us (35%)
  Pallas kernels  97.9 us (35%)
  starting transfers between devices  52.9 us (19%)
  local copies, waits for them, and re-layouts  30.5 us (11%)
    ppermute x10, waiting for transfers between devices, one_way(): return lax.ppermute(x, 'ctx', hops)  54.7 us
    pallas_call x5, Pallas kernels, unproject_kernel(): pl.pallas_call(unproject_body, grid=(width // tile,), in_specs=[pl.BlockS...  37.2 us
    pallas_call x5, Pallas kernels, project_kernel(): pl.pallas_call(functools.partial(project_body, len(pieces)), grid=(4,), i...  32 us
    ppermute x10, waiting for transfers between devices, across(): return None if x is None else lax.ppermute(x, 'tp', [(0, 1), (1, 0)])  31.5 us
    unnamed x57, local copies, waits for them, and re-layouts  28.8 us
    pallas_call x1, Pallas kernels, mix(): pl.pallas_call(functools.partial(mix_body, count, sets, per_step, grouped...  16.3 us
    ppermute x10, starting transfers between devices, one_way(): return lax.ppermute(x, 'ctx', hops)  14.5 us
    ppermute x17, starting transfers between devices, swap(): return lax.ppermute(x, 'ctx', [(d, d ^ 1) for d in range(n_ctx)])  12.9 us
  transfers between devices with their start and end apart: 39, of which 26 were waited for; matrix products, arithmetic and copies ran while one was open for 2% of the time, Pallas kernels for 26%

profile of v6, /device:TPU:1, one launch (start us, length us, event | category | flops | bytes accessed | tf_op | source)
XLA Modules:
  0.0 282.1 jit_solution(13404440530034968220)
XLA Ops:
  0.8 2.7 collective-permute-start.1
  6.0 2.2 copy-done.4
  8.2 2.2 copy-done.5
  10.4 2.2 copy-done.6
  12.6 1.7 shard_map.111
  14.3 4.3 %shard_map.112 = (bf16[768,256]{1,0:T(8,128)(2,1)S(1)}, bf16[768,256]{1,0:T(8,128)(2,1)S(1)}) custom-call(bf16[128,4096]{1,0:T(8,128)(2,1)S(1)} %copy-done.7, bf16[128,4096]{1,0:T(8,128)(2,1)S(1)} %collective-permute-done.2.refs_1_, bf16[1536,4096]{1,0:T(8,128)(2,1)S(1)} %bitcast.31), custom_call_target="tpu_custom_call" | custom-call | flops 1 | bytes 1 | tf_op jit(solution)/shard_map/pallas_call | solution.py:276
  18.7 7.8 %collective-permute-done.1 = bf16[128,4096]{1,0:T(8,128)(2,1)S(1)} collective-permute-done((bf16[128,4096]{1,0:T(8,128)(2,1)}, bf16[128,4096]{1,0:T(8,128)(2,1)S(1)}, u32[]{:S(2)}, u32[]{:S(2)}) %collective-permute-start.1) | collective-permute-done | bytes 1048608 | tf_op jit(solution)/shard_map/ppermute | solution.py:396
  28.0 1.4 collective-permute-start.3
  31.8 7.8 %shard_map.113 = (bf16[768,512]{1,0:T(8,128)(2,1)S(1)}, bf16[768,512]{1,0:T(8,128)(2,1)S(1)}) custom-call(bf16[256,4096]{1,0:T(8,128)(2,1)S(1)} %constant_dynamic-update-slice_fusion.refs_0_, bf16[256,4096]{1,0:T(8,128)(2,1)S(1)} %collective-permute-done.4.refs_1_, bf16[1536,4096]{1,0:T(8,128)(2,1)S(1)} %bitcast.32), custom_call_target="tpu_custom_call" | custom-call | flops 1 | bytes 1 | tf_op jit(solution)/shard_map/pallas_call | solution.py:276
  40.4 12.7 %collective-permute-done.3.refs_0_ = bf16[256,4096]{1,0:T(8,128)(2,1)S(1)} collective-permute-done((bf16[256,4096]{1,0:T(8,128)(2,1)S(1)}, bf16[256,4096]{1,0:T(8,128)(2,1)S(1)}, u32[]{:S(2)}, u32[]{:S(2)}) %collective-permute-start.3) | collective-permute-done | bytes 2097184 | tf_op jit(solution)/shard_map/ppermute | solution.py:396
  58.0 7.8 %shard_map.114 = (bf16[768,512]{1,0:T(8,128)(2,1)S(1)}, bf16[768,512]{1,0:T(8,128)(2,1)S(1)}) custom-call(bf16[256,4096]{1,0:T(8,128)(2,1)S(1)} %collective-permute-done.3.refs_0_, bf16[256,4096]{1,0:T(8,128)(2,1)S(1)} %collective-permute-done.7.refs_1_, bf16[1536,4096]{1,0:T(8,128)(2,1)S(1)} %bitcast.33), custom_call_target="tpu_custom_call" | custom-call | flops 1 | bytes 1 | tf_op jit(solution)/shard_map/pallas_call | solution.py:276
  65.7 8.2 %collective-permute-done.8 = bf16[768,512]{1,0:T(8,128)(2,1)S(1)} collective-permute-done((bf16[768,512]{1,0:T(8,128)(2,1)S(1)}, bf16[768,512]{1,0:T(8,128)(2,1)S(1)}, u32[]{:S(2)}, u32[]{:S(2)}) %collective-permute-start.8) | collective-permute-done | bytes 786464 | tf_op jit(solution)/shard_map/ppermute | solution.py:428
  74.0 5.7 %collective-permute-done.6.refs_0_ = bf16[256,4096]{1,0:T(8,128)(2,1)S(1)} collective-permute-done((bf16[256,4096]{1,0:T(8,128)(2,1)S(1)}, bf16[256,4096]{1,0:T(8,128)(2,1)S(1)}, u32[]{:S(2)}, u32[]{:S(2)}) %collective-permute-start.6) | collective-permute-done | bytes 2097184 | tf_op jit(solution)/shard_map/ppermute | solution.py:396
  80.3 1.4 collective-permute-start.9
  84.0 7.8 %shard_map.115 = (bf16[768,512]{1,0:T(8,128)(2,1)S(1)}, bf16[768,512]{1,0:T(8,128)(2,1)S(1)}) custom-call(bf16[256,4096]{1,0:T(8,128)(2,1)S(1)} %collective-permute-done.6.refs_0_, bf16[256,4096]{1,0:T(8,128)(2,1)S(1)} %collective-permute-done.10.refs_1_, bf16[1536,4096]{1,0:T(8,128)(2,1)S(1)} %bitcast.34), custom_call_target="tpu_custom_call" | custom-call | flops 1 | bytes 1 | tf_op jit(solution)/shard_map/pallas_call | solution.py:276
  92.7 2.0 collective-permute-done.9.refs_0_
  94.7 6.4 %all-to-all-start = ((bf16[16,256,128]{2,1,0:T(8,128)(2,1)}), bf16[16,256,128]{2,1,0:T(8,128)(2,1)}, u32[]{:S(2)}, u32[]{:S(2)}) async-start(bf16[16,256,128]{2,1,0:T(8,128)(2,1)} %bitcast.57), calls=%async_computation | async-start | bytes 2097152 | tf_op jit(solution)/shard_map/all_to_all | solution.py:457
  103.5 1.5 collective-permute-done.13.refs_2_
  105.8 4.6 %copy-done.1 = bf16[2,3,256,4096]{3,2,1,0:T(8,128)(2,1)S(1)} copy-done((bf16[2,3,256,4096]{3,2,1,0:T(8,128)(2,1)S(1)}, bf16[2,3,256,4096]{3,2,1,0:T(8,128)(2,1)}, u32[]{:S(2)}) %copy-start.1) | copy-done | bytes 12582936
  110.3 4.3 %shard_map.116 = (bf16[768,256]{1,0:T(8,128)(2,1)S(1)}, bf16[768,256]{1,0:T(8,128)(2,1)S(1)}) custom-call(bf16[128,4096]{1,0:T(8,128)(2,1)S(1)} %collective-permute-done.9.refs_0_, bf16[64,4096]{1,0:T(8,128)(2,1)S(1)} %collective-permute-done.12.refs_1_, bf16[64,4096]{1,0:T(8,128)(2,1)S(1)} %collective-permute-done.13.refs_2_, bf16[1536,4096]{1,0:T(8,128)(2,1)S(1)} %bitcast.35), custom_call_target="tpu_custom_call" | custom-call | flops 1 | bytes 1 | tf_op jit(solution)/shard_map/pallas_call | solution.py:276
  115.4 4.3 %collective-permute-done.14 = bf16[768,512]{1,0:T(8,128)(2,1)S(1)} collective-permute-done((bf16[768,512]{1,0:T(8,128)(2,1)S(1)}, bf16[768,512]{1,0:T(8,128)(2,1)S(1)}, u32[]{:S(2)}, u32[]{:S(2)}) %collective-permute-start.14) | collective-permute-done | bytes 786464 | tf_op jit(solution)/shard_map/ppermute | solution.py:428
  121.0 7.9 %collective-permute-done.15 = bf16[768,256]{1,0:T(8,128)(2,1)S(1)} collective-permute-done((bf16[768,256]{1,0:T(8,128)(2,1)S(1)}, bf16[768,256]{1,0:T(8,128)(2,1)S(1)}, u32[]{:S(2)}, u32[]{:S(2)}) %collective-permute-start.15) | collective-permute-done | bytes 393248 | tf_op jit(solution)/shard_map/ppermute | solution.py:428
  129.6 16.3 %shard_map.117 = (bf16[16,256,128]{2,1,0:T(8,128)(2,1)}, bf16[3,256,256]{2,1,0:T(8,128)(2,1)}, bf16[3,256,512]{2,1,0:T(8,128)(2,1)}, bf16[3,256,512]{2,1,0:T(8,1...) custom-call(s32[16]{0:T(128)} %dynamic-slice_bitcast_fusion.order, ...), custom_call_target="tpu_custom_call" | custom-call | flops 1 | bytes 1 | tf_op jit(solution)/shard_map/pallas_call | solution.py:176
  147.3 8.7 %all-to-all-start.1 = ((bf16[16,256,128]{2,1,0:T(8,128)(2,1)}), bf16[16,256,128]{2,1,0:T(8,128)(2,1)S(1)}, u32[]{:S(2)}, u32[]{:S(2)}) async-start(bf16[16,256,128]{2,1,0:T(8,128)(2,1)} %get-tuple-element.152), calls=%async_computation.1 | async-start | bytes 2097152 | tf_op jit(solution)/shard_map/all_to_all | solution.py:475
  156.3 4.6 %copy-done.2 = bf16[2,3,256,4096]{3,2,1,0:T(8,128)(2,1)S(1)} copy-done((bf16[2,3,256,4096]{3,2,1,0:T(8,128)(2,1)S(1)}, bf16[2,3,256,4096]{3,2,1,0:T(8,128)(2,1)}, u32[]{:S(2)}) %copy-start.2) | copy-done | bytes 12582936
  160.9 5.2 %shard_map.118 = (bf16[128,4096]{1,0:T(8,128)(2,1)S(1)}, bf16[80,4096]{1,0:T(8,128)(2,1)S(1)}, bf16[48,4096]{1,0:T(8,128)(2,1)S(1)}) custom-call(bf16[768,256]{1,0:T(8,128)(2,1)S(1)} %bitcast.54, bf16[768,256]{1,0:T(8,128)(2,1)S(1)} %collective-permute-done.16.far_ref, bf16[1536,4096]{1,0:T(8,128)(2,1)S(1)} %bitcast.36), custom_call_target="tpu_custom_call" | custom-call | flops 1 | bytes 1 | tf_op jit(solution)/shard_map/pallas_call | solution.py:313
  166.1 1.6 collective-permute-start.17
  170.5 4.7 %collective-permute-done.19.far_ref = bf16[768,512]{1,0:T(8,128)(2,1)S(1)} collective-permute-done((bf16[768,512]{1,0:T(8,128)(2,1)S(1)}, bf16[768,512]{1,0:T(8,128)(2,1)S(1)}, u32[]{:S(2)}, u32[]{:S(2)}) %collective-permute-start.19) | collective-permute-done | bytes 786464 | tf_op jit(solution)/shard_map/ppermute | solution.py:428
  176.2 8.7 %shard_map.120 = (bf16[256,4096]{1,0:T(8,128)(2,1)S(1)}, bf16[96,4096]{1,0:T(8,128)(2,1)S(1)}, bf16[96,4096]{1,0:T(8,128)(2,1)S(1)}, bf16[64,4096]{1,0:T(8,128)(2,1)S(1)}) custom-call(bf16[768,512]{1,0:T(8,128)(2,1)S(1)} %bitcast.47, bf16[768,512]{1,0:T(8,128)(2,1)S(1)} %collective-permute-done.19.far_ref, bf16[1536,4096]{1,0:T(8,128)(2,1)S(1)} %bitcast.37), custom_call_target="tpu_custom_call" | custom-call | flops 1 | bytes 1 | tf_op jit(solution)/shard_map/pallas_call | solution.py:313
  184.9 2.3 collective-permute-start.20
  187.3 4.7 %collective-permute-done.22.far_ref = bf16[768,512]{1,0:T(8,128)(2,1)S(1)} collective-permute-done((bf16[768,512]{1,0:T(8,128)(2,1)S(1)}, bf16[768,512]{1,0:T(8,128)(2,1)S(1)}, u32[]{:S(2)}, u32[]{:S(2)}) %collective-permute-start.22) | collective-permute-done | bytes 786464 | tf_op jit(solution)/shard_map/ppermute | solution.py:428
  193.7 1.5 collective-permute-done.23.refs_3_
  198.6 4.6 %copy-done.3 = bf16[2,3,256,4096]{3,2,1,0:T(8,128)(2,1)S(1)} copy-done((bf16[2,3,256,4096]{3,2,1,0:T(8,128)(2,1)S(1)}, bf16[2,3,256,4096]{3,2,1,0:T(8,128)(2,1)}, u32[]{:S(2)}) %copy-start.3) | copy-done | bytes 12582936
  205.4 8.7 %shard_map.122 = (bf16[256,4096]{1,0:T(8,128)(2,1)S(1)}, bf16[128,4096]{1,0:T(8,128)(2,1)S(1)}, bf16[128,4096]{1,0:T(8,128)(2,1)S(1)}) custom-call(bf16[768,512]{1,0:T(8,128)(2,1)S(1)} %bitcast.45, bf16[768,512]{1,0:T(8,128)(2,1)S(1)} %copy-done.12, bf16[1536,4096]{1,0:T(8,128)(2,1)S(1)} %bitcast.38), custom_call_target="tpu_custom_call" | custom-call | flops 1 | bytes 1 | tf_op jit(solution)/shard_map/pallas_call | solution.py:313
  214.9 1.7 collective-permute-done.26.far_ref
  216.6 1.5 collective-permute-start.27
  218.1 1.5 shard_map.124
  225.2 8.7 %shard_map.125 = (bf16[256,4096]{1,0:T(8,128)(2,1)S(1)}, bf16[128,4096]{1,0:T(8,128)(2,1)S(1)}, bf16[128,4096]{1,0:T(8,128)(2,1)S(1)}) custom-call(bf16[768,512]{1,0:T(8,128)(2,1)S(1)} %bitcast.43, bf16[768,512]{1,0:T(8,128)(2,1)S(1)} %collective-permute-done.26.far_ref, bf16[1536,4096]{1,0:T(8,128)(2,1)S(1)} %bitcast.39), custom_call_target="tpu_custom_call" | custom-call | flops 1 | bytes 1 | tf_op jit(solution)/shard_map/pallas_call | solution.py:313
  233.9 1.6 collective-permute-start.29
  236.1 1.7 collective-permute-done.29.refs_1_
  237.8 1.5 collective-permute-done.31.refs_2_
  239.3 9.0 %collective-permute-done.32.refs_3_ = bf16[256,4096]{1,0:T(8,128)(2,1)S(1)} collective-permute-done((bf16[256,4096]{1,0:T(8,128)(2,1)S(1)}, bf16[256,4096]{1,0:T(8,128)(2,1)S(1)}, u32[]{:S(2)}, u32[]{:S(2)}) %collective-permute-start.32) | collective-permute-done | bytes 2097184 | tf_op jit(solution)/shard_map/ppermute | solution.py:396
  248.4 2.4 shard_map.126
  252.1 2.4 collective-permute-start.36
  254.5 5.8 %shard_map.127 = (bf16[128,4096]{1,0:T(8,128)(2,1)S(1)}, bf16[64,4096]{1,0:T(8,128)(2,1)}, bf16[64,4096]{1,0:T(8,128)(2,1)}) custom-call(bf16[768,256]{1,0:T(8,128)(2,1)S(1)} %bitcast.52, bf16[768,256]{1,0:T(8,128)(2,1)S(1)} %collective-permute-done.30.far_ref, bf16[1536,4096]{1,0:T(8,128)(2,1)S(1)} %bitcast.40), custom_call_target="tpu_custom_call" | custom-call | flops 1 | bytes 1 | tf_op jit(solution)/shard_map/pallas_call | solution.py:313
  263.3 1.6 collective-permute-done.35.refs_3_
  264.9 13.5 %collective-permute-done.36.refs_4_ = bf16[128,4096]{1,0:T(8,128)(2,1)S(1)} collective-permute-done((bf16[128,4096]{1,0:T(8,128)(2,1)}, bf16[128,4096]{1,0:T(8,128)(2,1)S(1)}, u32[]{:S(2)}, u32[]{:S(2)}) %collective-permute-start.36) | collective-permute-done | bytes 1048608 | tf_op jit(solution)/shard_map/ppermute | solution.py:396
  278.4 3.7 %shard_map.128 = bf16[128,4096]{1,0:T(8,128)(2,1)} custom-call(bf16[128,4096]{1,0:T(8,128)(2,1)S(1)} %get-tuple-element.181.refs_0_, bf16[64,4096]{1,0:T(8,128)(2,1)} %collective-permute-done.33.refs_1_, bf16[64,4096]{1,0:T(8,128)(2,1)} %collective-permute-done.34.refs_2_, bf16[128,4096]{1,0:T(8,128)(2,1)S(1)} %collective-permute-done.35.refs_3_, ...), custom_call_target="tpu_custom_call" | custom-call | flops 1 | bytes 1 | tf_op jit(solution)/shard_map/pallas_call | solution.py:353
  (115 shorter events, 45.9 us)
Async XLA Ops:
  0.6 13.7 %collective-permute-start.2 = (bf16[128,4096]{1,0:T(8,128)(2,1)}, bf16[128,4096]{1,0:T(8,128)(2,1)S(1)}, u32[]{:S(2)}, u32[]{:S(2)}) collective-permute-start(bf16[128,4096]{1,0:T(8,128)(2,1)} %refs_0_.3), channel_id=1, source_target_pairs={{0,2},{2,0},{4,6},{6,4},{8,10},{10,8},{12,14},{14,12},{16,18},{18,... | collective-permute-start | bytes 3145736 | tf_op jit(solution)/shard_map/ppermute | solution.py:399
  0.8 25.7 %collective-permute-start.1 = (bf16[128,4096]{1,0:T(8,128)(2,1)}, bf16[128,4096]{1,0:T(8,128)(2,1)S(1)}, u32[]{:S(2)}, u32[]{:S(2)}) collective-permute-start(bf16[128,4096]{1,0:T(8,128)(2,1)} %refs_0_.3), channel_id=1, source_target_pairs={{0,6},{2,8},{8,2},{10,16},{16,10},{18,24},{24,18},{26,28},{28,26},... | collective-permute-start | bytes 3145736 | tf_op jit(solution)/shard_map/ppermute | solution.py:396
  3.5 23.9 %collective-permute-start = (bf16[128,4096]{1,0:T(8,128)(2,1)}, bf16[128,4096]{1,0:T(8,128)(2,1)S(1)}, u32[]{:S(2)}, u32[]{:S(2)}) collective-permute-start(bf16[128,4096]{1,0:T(8,128)(2,1)} %refs_0_.3), channel_id=1, source_target_pairs={{0,8},{2,6},{8,16},{10,2},{16,24},{18,10},{24,28},{26,18},{28,20},... | collective-permute-start | bytes 3145736 | tf_op jit(solution)/shard_map/ppermute | solution.py:396
  14.3 69.7 %copy-start = (bf16[2,3,256,4096]{3,2,1,0:T(8,128)(2,1)}, bf16[2,3,256,4096]{3,2,1,0:T(8,128)(2,1)S(1)}, u32[]{:S(2)}) copy-start(bf16[2,3,256,4096]{3,2,1,0:T(8,128)(2,1)S(1)} %shard_map.111) | copy-start | bytes 37748740
  27.6 4.2 %collective-permute-start.4 = (bf16[256,4096]{1,0:T(8,128)(2,1)S(1)}, bf16[256,4096]{1,0:T(8,128)(2,1)S(1)}, u32[]{:S(2)}, u32[]{:S(2)}) collective-permute-start(bf16[256,4096]{1,0:T(8,128)(2,1)S(1)} %constant_dynamic-update-slice_fusion.refs_0_), channel_id=1, source_target_pairs={{0,2},{2,0},{4,6},{6,4},{8,10},{10,8},{12,14},{14,12},{16,18},{18,... | collective-permute-start | bytes 6291464 | tf_op jit(solution)/shard_map/ppermute | solution.py:399
  28.0 25.2 %collective-permute-start.3 = (bf16[256,4096]{1,0:T(8,128)(2,1)S(1)}, bf16[256,4096]{1,0:T(8,128)(2,1)S(1)}, u32[]{:S(2)}, u32[]{:S(2)}) collective-permute-start(bf16[256,4096]{1,0:T(8,128)(2,1)S(1)} %constant_dynamic-update-slice_fusion.refs_0_), channel_id=1, source_target_pairs={{0,8},{2,6},{8,16},{10,2},{16,24},{18,10},{24,28},{26,18},{28,20},... | collective-permute-start | bytes 6291464 | tf_op jit(solution)/shard_map/ppermute | solution.py:396
  29.4 11.0 %collective-permute-start.5 = (bf16[768,256]{1,0:T(8,128)(2,1)S(1)}, bf16[768,256]{1,0:T(8,128)(2,1)S(1)}, u32[]{:S(2)}, u32[]{:S(2)}) collective-permute-start(bf16[768,256]{1,0:T(8,128)(2,1)S(1)} %get-tuple-element.107), channel_id=1, source_target_pairs={{0,1},{1,0},{2,3},{3,2},{4,5},{5,4},{6,7},{7,6},{8,9},{9,8},{10,11... | collective-permute-start | bytes 1179656 | tf_op jit(solution)/shard_map/ppermute | solution.py:428
  40.4 16.3 %copy-start.23 = (bf16[768,256]{1,0:T(8,128)(2,1)}, bf16[768,256]{1,0:T(8,128)(2,1)S(1)}, u32[]{:S(2)}) copy-start(bf16[768,256]{1,0:T(8,128)(2,1)S(1)} %collective-permute-done.5) | copy-start | bytes 1179652
  53.2 4.8 %collective-permute-start.7 = (bf16[256,4096]{1,0:T(8,128)(2,1)S(1)}, bf16[256,4096]{1,0:T(8,128)(2,1)S(1)}, u32[]{:S(2)}, u32[]{:S(2)}) collective-permute-start(bf16[256,4096]{1,0:T(8,128)(2,1)S(1)} %collective-permute-done.3.refs_0_), channel_id=1, source_target_pairs={{0,2},{2,0},{4,6},{6,4},{8,10},{10,8},{12,14},{14,12},{16,18},{18,... | collective-permute-start | bytes 6291464 | tf_op jit(solution)/shard_map/ppermute | solution.py:399
  54.2 25.5 %collective-permute-start.6 = (bf16[256,4096]{1,0:T(8,128)(2,1)S(1)}, bf16[256,4096]{1,0:T(8,128)(2,1)S(1)}, u32[]{:S(2)}, u32[]{:S(2)}) collective-permute-start(bf16[256,4096]{1,0:T(8,128)(2,1)S(1)} %collective-permute-done.3.refs_0_), channel_id=1, source_target_pairs={{0,8},{2,6},{8,16},{10,2},{16,24},{18,10},{24,28},{26,18},{28,20},... | collective-permute-start | bytes 6291464 | tf_op jit(solution)/shard_map/ppermute | solution.py:396
  55.5 18.4 %collective-permute-start.8 = (bf16[768,512]{1,0:T(8,128)(2,1)S(1)}, bf16[768,512]{1,0:T(8,128)(2,1)S(1)}, u32[]{:S(2)}, u32[]{:S(2)}) collective-permute-start(bf16[768,512]{1,0:T(8,128)(2,1)S(1)} %get-tuple-element.112), channel_id=1, source_target_pairs={{0,1},{1,0},{2,3},{3,2},{4,5},{5,4},{6,7},{7,6},{8,9},{9,8},{10,11... | collective-permute-start | bytes 2359304 | tf_op jit(solution)/shard_map/ppermute | solution.py:428
  65.7 26.0 %copy-start.15 = (bf16[768,512]{1,0:T(8,128)(2,1)}, bf16[768,512]{1,0:T(8,128)(2,1)S(1)}, u32[]{:S(2)}) copy-start(bf16[768,512]{1,0:T(8,128)(2,1)S(1)} %get-tuple-element.121) | copy-start | bytes 2359300
  74.0 17.8 %copy-start.21 = (bf16[768,512]{1,0:T(8,128)(2,1)}, bf16[768,512]{1,0:T(8,128)(2,1)S(1)}, u32[]{:S(2)}) copy-start(bf16[768,512]{1,0:T(8,128)(2,1)S(1)} %collective-permute-done.8) | copy-start | bytes 2359300
  79.7 4.3 %collective-permute-start.10 = (bf16[256,4096]{1,0:T(8,128)(2,1)S(1)}, bf16[256,4096]{1,0:T(8,128)(2,1)S(1)}, u32[]{:S(2)}, u32[]{:S(2)}) collective-permute-start(bf16[256,4096]{1,0:T(8,128)(2,1)S(1)} %collective-permute-done.6.refs_0_), channel_id=1, source_target_pairs={{0,2},{2,0},{4,6},{6,4},{8,10},{10,8},{12,14},{14,12},{16,18},{18,... | collective-permute-start | bytes 6291464 | tf_op jit(solution)/shard_map/ppermute | solution.py:399
  80.3 14.4 %collective-permute-start.9 = (bf16[128,4096]{1,0:T(8,128)(2,1)S(1)}, bf16[128,4096]{1,0:T(8,128)(2,1)S(1)}, u32[]{:S(2)}, u32[]{:S(2)}) collective-permute-start(bf16[128,4096]{1,0:T(8,128)(2,1)S(1)} %slice.21), channel_id=1, source_target_pairs={{0,8},{2,6},{8,16},{10,2},{16,24},{18,10},{24,28},{26,18},{28,20},... | collective-permute-start | bytes 3145736 | tf_op jit(solution)/shard_map/ppermute | solution.py:396
  81.7 19.4 %collective-permute-start.11 = (bf16[768,512]{1,0:T(8,128)(2,1)S(1)}, bf16[768,512]{1,0:T(8,128)(2,1)}, u32[]{:S(2)}, u32[]{:S(2)}) collective-permute-start(bf16[768,512]{1,0:T(8,128)(2,1)S(1)} %get-tuple-element.120), channel_id=1, source_target_pairs={{0,1},{1,0},{2,3},{3,2},{4,5},{5,4},{6,7},{7,6},{8,9},{9,8},{10,11... | collective-permute-start | bytes 2359304 | tf_op jit(solution)/shard_map/ppermute | solution.py:428
  94.7 34.2 %all-to-all-start = ((bf16[16,256,128]{2,1,0:T(8,128)(2,1)}), bf16[16,256,128]{2,1,0:T(8,128)(2,1)}, u32[]{:S(2)}, u32[]{:S(2)}) async-start(bf16[16,256,128]{2,1,0:T(8,128)(2,1)} %bitcast.57), calls=%async_computation | async-start | bytes 2097152 | tf_op jit(solution)/shard_map/all_to_all | solution.py:457
  101.1 18.6 %collective-permute-start.14 = (bf16[768,512]{1,0:T(8,128)(2,1)S(1)}, bf16[768,512]{1,0:T(8,128)(2,1)S(1)}, u32[]{:S(2)}, u32[]{:S(2)}) collective-permute-start(bf16[768,512]{1,0:T(8,128)(2,1)S(1)} %get-tuple-element.129), channel_id=1, source_target_pairs={{0,1},{1,0},{2,3},{3,2},{4,5},{5,4},{6,7},{7,6},{8,9},{9,8},{10,11... | collective-permute-start | bytes 2359304 | tf_op jit(solution)/shard_map/ppermute | solution.py:428
  102.5 2.5 collective-permute-start.13
  103.5 2.3 collective-permute-start.12
  119.7 9.2 %copy-start.22 = (bf16[768,512]{1,0:T(8,128)(2,1)}, bf16[768,512]{1,0:T(8,128)(2,1)S(1)}, u32[]{:S(2)}) copy-start(bf16[768,512]{1,0:T(8,128)(2,1)S(1)} %collective-permute-done.14) | copy-start | bytes 2359300
  119.7 9.2 %collective-permute-start.15 = (bf16[768,256]{1,0:T(8,128)(2,1)S(1)}, bf16[768,256]{1,0:T(8,128)(2,1)S(1)}, u32[]{:S(2)}, u32[]{:S(2)}) collective-permute-start(bf16[768,256]{1,0:T(8,128)(2,1)S(1)} %get-tuple-element.131), channel_id=1, source_target_pairs={{0,1},{1,0},{2,3},{3,2},{4,5},{5,4},{6,7},{7,6},{8,9},{9,8},{10,11... | collective-permute-start | bytes 1179656 | tf_op jit(solution)/shard_map/ppermute | solution.py:428
  146.0 10.0 %copy-start.13 = (bf16[3,256,512]{2,1,0:T(8,128)(2,1)S(1)}, bf16[3,256,512]{2,1,0:T(8,128)(2,1)}, u32[]{:S(2)}) copy-start(bf16[3,256,512]{2,1,0:T(8,128)(2,1)} %get-tuple-element.136) | copy-start | bytes 2359300
  146.0 10.3 %copy-start.18 = (bf16[3,256,256]{2,1,0:T(8,128)(2,1)S(1)}, bf16[3,256,256]{2,1,0:T(8,128)(2,1)}, u32[]{:S(2)}) copy-start(bf16[3,256,256]{2,1,0:T(8,128)(2,1)} %get-tuple-element.132) | copy-start | bytes 1179652
  146.0 10.3 %collective-permute-start.16 = (bf16[768,256]{1,0:T(8,128)(2,1)}, bf16[768,256]{1,0:T(8,128)(2,1)S(1)}, u32[]{:S(2)}, u32[]{:S(2)}) collective-permute-start(bf16[768,256]{1,0:T(8,128)(2,1)} %bitcast.53), channel_id=1, source_target_pairs={{0,1},{1,0},{2,3},{3,2},{4,5},{5,4},{6,7},{7,6},{8,9},{9,8},{10,11... | collective-permute-start | bytes 1179656 | tf_op jit(solution)/shard_map/ppermute | solution.py:428
  147.3 49.2 %all-to-all-start.1 = ((bf16[16,256,128]{2,1,0:T(8,128)(2,1)}), bf16[16,256,128]{2,1,0:T(8,128)(2,1)S(1)}, u32[]{:S(2)}, u32[]{:S(2)}) async-start(bf16[16,256,128]{2,1,0:T(8,128)(2,1)} %get-tuple-element.152), calls=%async_computation.1 | async-start | bytes 2097152 | tf_op jit(solution)/shard_map/all_to_all | solution.py:475
  156.0 19.2 %collective-permute-start.19 = (bf16[768,512]{1,0:T(8,128)(2,1)S(1)}, bf16[768,512]{1,0:T(8,128)(2,1)S(1)}, u32[]{:S(2)}, u32[]{:S(2)}) collective-permute-start(bf16[768,512]{1,0:T(8,128)(2,1)S(1)} %bitcast.46), channel_id=1, source_target_pairs={{0,1},{1,0},{2,3},{3,2},{4,5},{5,4},{6,7},{7,6},{8,9},{9,8},{10,11... | collective-permute-start | bytes 2359304 | tf_op jit(solution)/shard_map/ppermute | solution.py:428
  166.1 3.9 %collective-permute-start.17 = (bf16[80,4096]{1,0:T(8,128)(2,1)S(1)}, bf16[80,4096]{1,0:T(8,128)(2,1)S(1)}, u32[]{:S(2)}, u32[]{:S(2)}) collective-permute-start(bf16[80,4096]{1,0:T(8,128)(2,1)S(1)} %get-tuple-element.134), channel_id=1, source_target_pairs={{0,2},{2,0},{4,6},{6,4},{8,10},{10,8},{12,14},{14,12},{16,18},{18,... | collective-permute-start | bytes 1966088 | tf_op jit(solution)/shard_map/ppermute | solution.py:399
  167.6 2.3 collective-permute-start.18
  167.7 24.3 %collective-permute-start.22 = (bf16[768,512]{1,0:T(8,128)(2,1)S(1)}, bf16[768,512]{1,0:T(8,128)(2,1)S(1)}, u32[]{:S(2)}, u32[]{:S(2)}) collective-permute-start(bf16[768,512]{1,0:T(8,128)(2,1)S(1)} %bitcast.44), channel_id=1, source_target_pairs={{0,1},{1,0},{2,3},{3,2},{4,5},{5,4},{6,7},{7,6},{8,9},{9,8},{10,11... | collective-permute-start | bytes 2359304 | tf_op jit(solution)/shard_map/ppermute | solution.py:428
  175.1 20.2 %collective-permute-start.24 = (bf16[128,4096]{1,0:T(8,128)(2,1)S(1)}, bf16[128,4096]{1,0:T(8,128)(2,1)S(1)}, u32[]{:S(2)}, u32[]{:S(2)}) collective-permute-start(bf16[128,4096]{1,0:T(8,128)(2,1)S(1)} %shard_map.119), channel_id=1, source_target_pairs={{0,4},{2,10},{8,0},{10,18},{16,8},{18,26},{24,16},{26,30},{28,24},... | collective-permute-start | bytes 3145736 | tf_op jit(solution)/shard_map/ppermute | solution.py:396
  184.9 10.4 %collective-permute-start.20 = (bf16[96,4096]{1,0:T(8,128)(2,1)S(1)}, bf16[96,4096]{1,0:T(8,128)(2,1)S(1)}, u32[]{:S(2)}, u32[]{:S(2)}) collective-permute-start(bf16[96,4096]{1,0:T(8,128)(2,1)S(1)} %get-tuple-element.142), channel_id=1, source_target_pairs={{0,2},{2,0},{4,6},{6,4},{8,10},{10,8},{12,14},{14,12},{16,18},{18,... | collective-permute-start | bytes 2359304 | tf_op jit(solution)/shard_map/ppermute | solution.py:399
  187.3 8.0 %collective-permute-start.21 = (bf16[96,4096]{1,0:T(8,128)(2,1)S(1)}, bf16[96,4096]{1,0:T(8,128)(2,1)S(1)}, u32[]{:S(2)}, u32[]{:S(2)}) collective-permute-start(bf16[96,4096]{1,0:T(8,128)(2,1)S(1)} %get-tuple-element.143), channel_id=1, source_target_pairs={{0,2},{2,0},{4,6},{6,4},{8,10},{10,8},{12,14},{14,12},{16,18},{18,... | collective-permute-start | bytes 2359304 | tf_op jit(solution)/shard_map/ppermute | solution.py:399
  192.9 2.4 collective-permute-start.23
  196.5 25.2 %collective-permute-start.28 = (bf16[256,4096]{1,0:T(8,128)(2,1)S(1)}, bf16[256,4096]{1,0:T(8,128)(2,1)S(1)}, u32[]{:S(2)}, u32[]{:S(2)}) collective-permute-start(bf16[256,4096]{1,0:T(8,128)(2,1)S(1)} %shard_map.121), channel_id=1, source_target_pairs={{0,4},{2,10},{8,0},{10,18},{16,8},{18,26},{24,16},{26,30},{28,24},... | collective-permute-start | bytes 6291464 | tf_op jit(solution)/shard_map/ppermute | solution.py:396
  197.9 18.6 %collective-permute-start.26 = (bf16[768,512]{1,0:T(8,128)(2,1)}, bf16[768,512]{1,0:T(8,128)(2,1)S(1)}, u32[]{:S(2)}, u32[]{:S(2)}) collective-permute-start(bf16[768,512]{1,0:T(8,128)(2,1)} %bitcast.42), channel_id=1, source_target_pairs={{0,1},{1,0},{2,3},{3,2},{4,5},{5,4},{6,7},{7,6},{8,9},{9,8},{10,11... | collective-permute-start | bytes 2359304 | tf_op jit(solution)/shard_map/ppermute | solution.py:428
  214.1 5.5 %collective-permute-start.25 = (bf16[128,4096]{1,0:T(8,128)(2,1)S(1)}, bf16[128,4096]{1,0:T(8,128)(2,1)S(1)}, u32[]{:S(2)}, u32[]{:S(2)}) collective-permute-start(bf16[128,4096]{1,0:T(8,128)(2,1)S(1)} %get-tuple-element.156), channel_id=1, source_target_pairs={{0,2},{2,0},{4,6},{6,4},{8,10},{10,8},{12,14},{14,12},{16,18},{18,... | collective-permute-start | bytes 3145736 | tf_op jit(solution)/shard_map/ppermute | solution.py:399
  216.6 3.8 %collective-permute-start.27 = (bf16[128,4096]{1,0:T(8,128)(2,1)S(1)}, bf16[128,4096]{1,0:T(8,128)(2,1)S(1)}, u32[]{:S(2)}, u32[]{:S(2)}) collective-permute-start(bf16[128,4096]{1,0:T(8,128)(2,1)S(1)} %get-tuple-element.159), channel_id=1, source_target_pairs={{0,2},{2,0},{4,6},{6,4},{8,10},{10,8},{12,14},{14,12},{16,18},{18,... | collective-permute-start | bytes 3145736 | tf_op jit(solution)/shard_map/ppermute | solution.py:399
  223.2 25.2 %collective-permute-start.32 = (bf16[256,4096]{1,0:T(8,128)(2,1)S(1)}, bf16[256,4096]{1,0:T(8,128)(2,1)S(1)}, u32[]{:S(2)}, u32[]{:S(2)}) collective-permute-start(bf16[256,4096]{1,0:T(8,128)(2,1)S(1)} %shard_map.123), channel_id=1, source_target_pairs={{0,4},{2,10},{8,0},{10,18},{16,8},{18,26},{24,16},{26,30},{28,24},... | collective-permute-start | bytes 6291464 | tf_op jit(solution)/shard_map/ppermute | solution.py:396
  224.6 11.0 %collective-permute-start.30 = (bf16[768,256]{1,0:T(8,128)(2,1)S(1)}, bf16[768,256]{1,0:T(8,128)(2,1)S(1)}, u32[]{:S(2)}, u32[]{:S(2)}) collective-permute-start(bf16[768,256]{1,0:T(8,128)(2,1)S(1)} %bitcast.51), channel_id=1, source_target_pairs={{0,1},{1,0},{2,3},{3,2},{4,5},{5,4},{6,7},{7,6},{8,9},{9,8},{10,11... | collective-permute-start | bytes 1179656 | tf_op jit(solution)/shard_map/ppermute | solution.py:428
  233.9 3.9 %collective-permute-start.29 = (bf16[128,4096]{1,0:T(8,128)(2,1)S(1)}, bf16[128,4096]{1,0:T(8,128)(2,1)S(1)}, u32[]{:S(2)}, u32[]{:S(2)}) collective-permute-start(bf16[128,4096]{1,0:T(8,128)(2,1)S(1)} %get-tuple-element.168), channel_id=1, source_target_pairs={{0,2},{2,0},{4,6},{6,4},{8,10},{10,8},{12,14},{14,12},{16,18},{18,... | collective-permute-start | bytes 3145736 | tf_op jit(solution)/shard_map/ppermute | solution.py:399
  235.6 3.8 %collective-permute-start.31 = (bf16[128,4096]{1,0:T(8,128)(2,1)S(1)}, bf16[128,4096]{1,0:T(8,128)(2,1)S(1)}, u32[]{:S(2)}, u32[]{:S(2)}) collective-permute-start(bf16[128,4096]{1,0:T(8,128)(2,1)S(1)} %get-tuple-element.171), channel_id=1, source_target_pairs={{0,2},{2,0},{4,6},{6,4},{8,10},{10,8},{12,14},{14,12},{16,18},{18,... | collective-permute-start | bytes 3145736 | tf_op jit(solution)/shard_map/ppermute | solution.py:399
  250.8 10.0 %copy-start.26 = (f32[8,2,128]{2,1,0:T(2,128)S(1)}, f32[8,2,128]{2,1,0:T(2,128)}, u32[]{:S(2)}) copy-start(f32[8,2,128]{2,1,0:T(2,128)} %get-tuple-element.187) | copy-start | bytes 24580
  250.8 10.2 %copy-start.25 = (f32[8,2,9,128]{3,2,1,0:T(8,128)S(1)}, f32[8,2,9,128]{3,2,1,0:T(8,128)}, u32[]{:S(2)}) copy-start(f32[8,2,9,128]{3,2,1,0:T(8,128)} %get-tuple-element.186) | copy-start | bytes 221188
  250.8 14.2 %collective-permute-start.35 = (bf16[128,4096]{1,0:T(8,128)(2,1)}, bf16[128,4096]{1,0:T(8,128)(2,1)S(1)}, u32[]{:S(2)}, u32[]{:S(2)}) collective-permute-start(bf16[128,4096]{1,0:T(8,128)(2,1)} %get-tuple-element.184), channel_id=1, source_target_pairs={{0,4},{2,10},{8,0},{10,18},{16,8},{18,26},{24,16},{26,30},{28,24},... | collective-permute-start | bytes 3145736 | tf_op jit(solution)/shard_map/ppermute | solution.py:396
  252.1 26.3 %collective-permute-start.36 = (bf16[128,4096]{1,0:T(8,128)(2,1)}, bf16[128,4096]{1,0:T(8,128)(2,1)S(1)}, u32[]{:S(2)}, u32[]{:S(2)}) collective-permute-start(bf16[128,4096]{1,0:T(8,128)(2,1)} %get-tuple-element.185), channel_id=1, source_target_pairs={{0,6},{2,8},{8,2},{10,16},{16,10},{18,24},{24,18},{26,28},{28,26},... | collective-permute-start | bytes 3145736 | tf_op jit(solution)/shard_map/ppermute | solution.py:396
  260.3 2.3 collective-permute-start.33
  260.3 3.0 %collective-permute-start.34 = (bf16[64,4096]{1,0:T(8,128)(2,1)}, bf16[64,4096]{1,0:T(8,128)(2,1)}, u32[]{:S(2)}, u32[]{:S(2)}) collective-permute-start(bf16[64,4096]{1,0:T(8,128)(2,1)} %get-tuple-element.183), channel_id=1, source_target_pairs={{0,2},{2,0},{4,6},{6,4},{8,10},{10,8},{12,14},{14,12},{16,18},{18,... | collective-permute-start | bytes 1572872 | tf_op jit(solution)/shard_map/ppermute | solution.py:399
  (18 other events, 50.3 us)

commit v7 on v6

--- a/solution.py
+++ b/solution.py
@@ -443,22 +443,30 @@
 
     arrived = [one_way(tokens_in), one_way(tokens_in, to_mate=True, turned=True)]
     near, far = project([tokens_in, swap(tokens_in)])
-    arrived, near, far = stage((arrived, near, far))
+    crossed = across(far)
+    arrived, near = stage((arrived, near))
     arrived = jnp.concatenate(arrived, axis=0)
     projected = []
     for s in range(1, half):
         coming = one_way(arrived if s < half - 1 else arrived[:held])
-        projected.append((near, across(far)))
-        near, far = project([arrived, swap(arrived)])
+        shared, crossed = stage((arrived, crossed))
+        projected.append((near, crossed))
+        cuts = (96, 80, 80) if s == half - 1 and held == 128 else (held, held)
+        mates = [swap(x) for x in jnp.split(shared, np.cumsum(cuts)[:-1], axis=0)]
         if s < half - 1:
-            arrived, near, far, projected[-1] = stage((coming, near, far, projected[-1]))
+            near, far = project([arrived, *mates])
+            crossed = across(far)
+            arrived, near = stage((coming, near))
+    here, far = project([arrived])
+    first = across(far)
+    near, far = project(mates)
     crossed = across(far)
-    arrived, near, grad_out = stage((coming, near, grad_out))
+    arrived, near, first, grad_out = stage((coming, near, first, grad_out))
+    projected.append((here, first))
     incoming = lax.all_to_all(
         grad_out.reshape(n_ctx, channels, held), "ctx", split_axis=0, concat_axis=0, tiled=True
     )
-    shared, projected[-1] = stage((arrived, projected[-1]))
-    last, far = project([arrived, swap(shared[: held // 2]), swap(shared[held // 2 :])])
+    last, far = project([arrived, swap(arrived[: held // 2]), swap(arrived[held // 2 :])])
     far, crossed = stage((far, crossed))
     projected += [(near, crossed), (last, across(far))]
 
@@ -468,7 +476,7 @@
         long_kernel,
         incoming,
         [[y.reshape(3, channels, -1) for y in side] for side in zip(*projected) if side[0] is not None],
-        [[s] for s in range(half + 1)],
+        [[s] for s in range(half - 1)] + [[half - 1, half], [half + 1]],
     )
 
     first, met, later = [meet(d_proj[s]) for s in (half, half - 1, half - 2)]

time: 283 us -> 305 us (1.078)
  waiting for transfers between devices: 99 us -> 114 us
  starting transfers between devices: 52.9 us -> 57.1 us
    ppermute x10 -> x11, waiting for transfers between devices: 31.5 us -> 65 us  [across(): return None if x is None else lax.ppermute(x, 'tp', [(0, 1), (1, 0)])]
    ppermute x10, waiting for transfers between devices: 54.7 us -> 34.1 us  [one_way(): return lax.ppermute(x, 'ctx', hops)]
    ppermute x10 -> x11, starting transfers between devices: 10.4 us -> 14.7 us  [across(): return None if x is None else lax.ppermute(x, 'tp', [(0, 1), (1, 0)])]
    ppermute x10, starting transfers between devices: 14.5 us -> 18.2 us  [one_way(): return lax.ppermute(x, 'ctx', hops)]
    ppermute x17 -> x21, waiting for transfers between devices: 12.8 us -> 14.9 us  [swap(): return lax.ppermute(x, 'ctx', [(d, d ^ 1) for d in range(n_ctx)])]
    ppermute x17 -> x21, starting transfers between devices: 12.9 us -> 11.1 us  [swap(): return lax.ppermute(x, 'ctx', [(d, d ^ 1) for d in range(n_ctx)])]
    pallas_call x5 -> x6, Pallas kernels: 32 us -> 33.4 us  [project_kernel(): pl.pallas_call(functools.partial(project_body, len(pieces)), grid=(4,), i...]
    unnamed x57 -> x63, local copies, waits for them, and re-layouts: 28.8 us -> 29.7 us
  transfers between devices with their start and end apart: 39 -> 44, of which waited for: 26 -> 29; matrix products, arithmetic and copies ran while one was open for 2% -> 2% of each run, Pallas kernels for 26% -> 25%
where the time goes in v7:
time: 305 us; the launch traced here: 304 us
  waiting for transfers between devices  114 us (37%)
  Pallas kernels  99.4 us (33%)
  starting transfers between devices  57.1 us (19%)
  local copies, waits for them, and re-layouts  32 us (10%)
    ppermute x11, waiting for transfers between devices, across(): return None if x is None else lax.ppermute(x, 'tp', [(0, 1), (1, 0)])  65 us
    pallas_call x5, Pallas kernels, unproject_kernel(): pl.pallas_call(unproject_body, grid=(width // tile,), in_specs=[pl.BlockS...  37.2 us
    ppermute x10, waiting for transfers between devices, one_way(): return lax.ppermute(x, 'ctx', hops)  34.1 us
    pallas_call x6, Pallas kernels, project_kernel(): pl.pallas_call(functools.partial(project_body, len(pieces)), grid=(4,), i...  33.4 us
    unnamed x63, local copies, waits for them, and re-layouts  29.7 us
    ppermute x10, starting transfers between devices, one_way(): return lax.ppermute(x, 'ctx', hops)  18.2 us
    pallas_call x1, Pallas kernels, mix(): pl.pallas_call(functools.partial(mix_body, count, sets, per_step, grouped...  16.4 us
    ppermute x21, waiting for transfers between devices, swap(): return lax.ppermute(x, 'ctx', [(d, d ^ 1) for d in range(n_ctx)])  14.9 us
  transfers between devices with their start and end apart: 44, of which 29 were waited for; matrix products, arithmetic and copies ran while one was open for 2% of the time, Pallas kernels for 25%

profile of v7, /device:TPU:1, one launch (start us, length us, event | category | flops | bytes accessed | tf_op | source)
XLA Modules:
  0.0 304.4 jit_solution(12686991585767152087)
XLA Ops:
  0.8 2.7 collective-permute-start.1
  6.1 2.2 copy-done.4
  8.3 2.2 copy-done.5
  10.4 2.2 copy-done.6
  12.6 1.7 shard_map.111
  14.4 4.4 %shard_map.112 = (bf16[768,256]{1,0:T(8,128)(2,1)S(1)}, bf16[768,256]{1,0:T(8,128)(2,1)S(1)}) custom-call(bf16[128,4096]{1,0:T(8,128)(2,1)S(1)} %copy-done.7, bf16[128,4096]{1,0:T(8,128)(2,1)S(1)} %collective-permute-done.2.refs_1_, bf16[1536,4096]{1,0:T(8,128)(2,1)S(1)} %bitcast.33), custom_call_target="tpu_custom_call" | custom-call | flops 1 | bytes 1 | tf_op jit(solution)/shard_map/pallas_call | solution.py:276
  18.8 7.7 %collective-permute-done.1 = bf16[128,4096]{1,0:T(8,128)(2,1)S(1)} collective-permute-done((bf16[128,4096]{1,0:T(8,128)(2,1)}, bf16[128,4096]{1,0:T(8,128)(2,1)S(1)}, u32[]{:S(2)}, u32[]{:S(2)}) %collective-permute-start.1) | collective-permute-done | bytes 1048608 | tf_op jit(solution)/shard_map/ppermute | solution.py:396
  27.4 1.7 collective-permute-start.4
  30.2 8.2 %collective-permute-done.4 = bf16[768,256]{1,0:T(8,128)(2,1)} collective-permute-done((bf16[768,256]{1,0:T(8,128)(2,1)S(1)}, bf16[768,256]{1,0:T(8,128)(2,1)}, u32[]{:S(2)}, u32[]{:S(2)}) %collective-permute-start.4) | collective-permute-done | bytes 393248 | tf_op jit(solution)/shard_map/ppermute | solution.py:428
  39.6 2.2 collective-permute-done.6.refs_2_
  43.4 7.8 %shard_map.113 = (bf16[768,512]{1,0:T(8,128)(2,1)S(1)}, bf16[768,512]{1,0:T(8,128)(2,1)S(1)}) custom-call(bf16[256,4096]{1,0:T(8,128)(2,1)S(1)} %constant_dynamic-update-slice_fusion.refs_0_, bf16[128,4096]{1,0:T(8,128)(2,1)S(1)} %collective-permute-done.5.refs_1_, bf16[128,4096]{1,0:T(8,128)(2,1)S(1)} %collective-permute-done.6.refs_2_, ...), custom_call_target="tpu_custom_call" | custom-call | flops 1 | bytes 1 | tf_op jit(solution)/shard_map/pallas_call | solution.py:276
  55.4 15.5 %collective-permute-done.8 = bf16[768,512]{1,0:T(8,128)(2,1)S(1)} collective-permute-done((bf16[768,512]{1,0:T(8,128)(2,1)S(1)}, bf16[768,512]{1,0:T(8,128)(2,1)S(1)}, u32[]{:S(2)}, u32[]{:S(2)}) %collective-permute-start.8) | collective-permute-done | bytes 786464 | tf_op jit(solution)/shard_map/ppermute | solution.py:428
  72.9 2.3 collective-permute-done.10.refs_2_
  76.7 7.8 %shard_map.114 = (bf16[768,512]{1,0:T(8,128)(2,1)S(1)}, bf16[768,512]{1,0:T(8,128)(2,1)S(1)}) custom-call(bf16[256,4096]{1,0:T(8,128)(2,1)S(1)} %collective-permute-done.3.refs_0_, bf16[128,4096]{1,0:T(8,128)(2,1)S(1)} %collective-permute-done.9.refs_1_, bf16[128,4096]{1,0:T(8,128)(2,1)S(1)} %collective-permute-done.10.refs_2_, bf16[1536,4096]{1,0:T(8,128)(2,1)S(1)} %bitcast.35), custom_call_target="tpu_custom_call" | custom-call | flops 1 | bytes 1 | tf_op jit(solution)/shard_map/pallas_call | solution.py:276
  86.2 17.2 %collective-permute-done.12 = bf16[768,512]{1,0:T(8,128)(2,1)S(1)} collective-permute-done((bf16[768,512]{1,0:T(8,128)(2,1)S(1)}, bf16[768,512]{1,0:T(8,128)(2,1)S(1)}, u32[]{:S(2)}, u32[]{:S(2)}) %collective-permute-start.12) | collective-permute-done | bytes 786464 | tf_op jit(solution)/shard_map/ppermute | solution.py:428
  106.9 4.3 %shard_map.116 = (bf16[768,256]{1,0:T(8,128)(2,1)S(1)}, bf16[768,256]{1,0:T(8,128)(2,1)S(1)}) custom-call(bf16[256,4096]{1,0:T(8,128)(2,1)S(1)} %collective-permute-done.7.refs_0_, bf16[1536,4096]{1,0:T(8,128)(2,1)S(1)} %bitcast.36), custom_call_target="tpu_custom_call" | custom-call | flops 1 | bytes 1 | tf_op jit(solution)/shard_map/pallas_call | solution.py:276
  112.5 4.7 %shard_map.115 = (bf16[768,256]{1,0:T(8,128)(2,1)S(1)}, bf16[768,256]{1,0:T(8,128)(2,1)S(1)}) custom-call(bf16[96,4096]{1,0:T(8,128)(2,1)S(1)} %collective-permute-done.13.refs_0_, bf16[80,4096]{1,0:T(8,128)(2,1)S(1)} %collective-permute-done.14.refs_1_, bf16[80,4096]{1,0:T(8,128)(2,1)S(1)} %collective-permute-done.15.refs_2_, bf16[1536,4096]{1,0:T(8,128)(2,1)S(1)} %bitcast.37), custom_call_target="tpu_custom_call" | custom-call | flops 1 | bytes 1 | tf_op jit(solution)/shard_map/pallas_call | solution.py:276
  118.0 3.5 %collective-permute-done.16 = bf16[768,256]{1,0:T(8,128)(2,1)S(1)} collective-permute-done((bf16[768,256]{1,0:T(8,128)(2,1)S(1)}, bf16[768,256]{1,0:T(8,128)(2,1)S(1)}, u32[]{:S(2)}, u32[]{:S(2)}) %collective-permute-start.16) | collective-permute-done | bytes 393248 | tf_op jit(solution)/shard_map/ppermute | solution.py:428
  121.5 6.2 %all-to-all-start = ((bf16[16,256,128]{2,1,0:T(8,128)(2,1)}), bf16[16,256,128]{2,1,0:T(8,128)(2,1)S(1)}, u32[]{:S(2)}, u32[]{:S(2)}) async-start(bf16[16,256,128]{2,1,0:T(8,128)(2,1)} %bitcast.6), calls=%async_computation | async-start | bytes 2097152 | tf_op jit(solution)/shard_map/all_to_all | solution.py:466
  130.5 4.6 %copy-done.1 = bf16[2,3,256,4096]{3,2,1,0:T(8,128)(2,1)S(1)} copy-done((bf16[2,3,256,4096]{3,2,1,0:T(8,128)(2,1)S(1)}, bf16[2,3,256,4096]{3,2,1,0:T(8,128)(2,1)}, u32[]{:S(2)}) %copy-start.1) | copy-done | bytes 12582936
  135.1 4.3 %shard_map.117 = (bf16[768,256]{1,0:T(8,128)(2,1)S(1)}, bf16[768,256]{1,0:T(8,128)(2,1)S(1)}) custom-call(bf16[128,4096]{1,0:T(8,128)(2,1)S(1)} %collective-permute-done.11.refs_0_, bf16[64,4096]{1,0:T(8,128)(2,1)S(1)} %collective-permute-done.17.refs_1_, bf16[64,4096]{1,0:T(8,128)(2,1)S(1)} %collective-permute-done.18.refs_2_, bf16[1536,4096]{1,0:T(8,128)(2,1)S(1)} %bitcast.38), custom_call_target="tpu_custom_call" | custom-call | flops 1 | bytes 1 | tf_op jit(solution)/shard_map/pallas_call | solution.py:276
  141.4 9.4 %collective-permute-done.20 = bf16[768,256]{1,0:T(8,128)(2,1)S(1)} collective-permute-done((bf16[768,256]{1,0:T(8,128)(2,1)S(1)}, bf16[768,256]{1,0:T(8,128)(2,1)S(1)}, u32[]{:S(2)}, u32[]{:S(2)}) %collective-permute-start.20) | collective-permute-done | bytes 393248 | tf_op jit(solution)/shard_map/ppermute | solution.py:428
  151.9 16.4 %shard_map.118 = (bf16[16,256,128]{2,1,0:T(8,128)(2,1)}, bf16[3,256,256]{2,1,0:T(8,128)(2,1)}, bf16[3,256,512]{2,1,0:T(8,128)(2,1)}, bf16[3,256,512]{2,1,0:T(8,1...) custom-call(s32[16]{0:T(128)} %dynamic-slice_bitcast_fusion.order, ...), custom_call_target="tpu_custom_call" | custom-call | flops 1 | bytes 1 | tf_op jit(solution)/shard_map/pallas_call | solution.py:176
  169.6 6.9 %all-to-all-start.1 = ((bf16[16,256,128]{2,1,0:T(8,128)(2,1)}), bf16[16,256,128]{2,1,0:T(8,128)(2,1)S(1)}, u32[]{:S(2)}, u32[]{:S(2)}) async-start(bf16[16,256,128]{2,1,0:T(8,128)(2,1)} %get-tuple-element.150), calls=%async_computation.1 | async-start | bytes 2097152 | tf_op jit(solution)/shard_map/all_to_all | solution.py:483
  178.2 4.6 %copy-done.2 = bf16[2,3,256,4096]{3,2,1,0:T(8,128)(2,1)S(1)} copy-done((bf16[2,3,256,4096]{3,2,1,0:T(8,128)(2,1)S(1)}, bf16[2,3,256,4096]{3,2,1,0:T(8,128)(2,1)}, u32[]{:S(2)}) %copy-start.2) | copy-done | bytes 12582936
  182.8 5.2 %shard_map.119 = (bf16[128,4096]{1,0:T(8,128)(2,1)S(1)}, bf16[80,4096]{1,0:T(8,128)(2,1)S(1)}, bf16[48,4096]{1,0:T(8,128)(2,1)S(1)}) custom-call(bf16[768,256]{1,0:T(8,128)(2,1)S(1)} %bitcast.56, bf16[768,256]{1,0:T(8,128)(2,1)S(1)} %collective-permute-done.21.far_ref, bf16[1536,4096]{1,0:T(8,128)(2,1)S(1)} %bitcast.39), custom_call_target="tpu_custom_call" | custom-call | flops 1 | bytes 1 | tf_op jit(solution)/shard_map/pallas_call | solution.py:313
  188.0 2.4 collective-permute-start.22
  190.5 2.1 collective-permute-start.27
  193.2 3.0 collective-permute-done.24.far_ref
  196.3 3.2 %collective-permute-start.29 = (bf16[128,4096]{1,0:T(8,128)(2,1)S(1)}, bf16[128,4096]{1,0:T(8,128)(2,1)S(1)}, u32[]{:S(2)}, u32[]{:S(2)}) collective-permute-start(bf16[128,4096]{1,0:T(8,128)(2,1)S(1)} %shard_map.120), channel_id=1, source_target_pairs={{0,4},{2,10},{8,0},{10,18},{16,8},{18,26},{24,16},{26,30},{28,24},... | collective-permute-start | bytes 3145736 | tf_op jit(solution)/shard_map/ppermute | solution.py:396
  199.4 8.7 %shard_map.121 = (bf16[256,4096]{1,0:T(8,128)(2,1)S(1)}, bf16[96,4096]{1,0:T(8,128)(2,1)S(1)}, bf16[96,4096]{1,0:T(8,128)(2,1)S(1)}, bf16[64,4096]{1,0:T(8,128)(2,1)S(1)}) custom-call(bf16[768,512]{1,0:T(8,128)(2,1)S(1)} %bitcast.50, bf16[768,512]{1,0:T(8,128)(2,1)S(1)} %collective-permute-done.24.far_ref, bf16[1536,4096]{1,0:T(8,128)(2,1)S(1)} %bitcast.40), custom_call_target="tpu_custom_call" | custom-call | flops 1 | bytes 1 | tf_op jit(solution)/shard_map/pallas_call | solution.py:313
  208.8 4.4 %collective-permute-done.27.far_ref = bf16[768,512]{1,0:T(8,128)(2,1)S(1)} collective-permute-done((bf16[768,512]{1,0:T(8,128)(2,1)S(1)}, bf16[768,512]{1,0:T(8,128)(2,1)S(1)}, u32[]{:S(2)}, u32[]{:S(2)}) %collective-permute-start.27) | collective-permute-done | bytes 786464 | tf_op jit(solution)/shard_map/ppermute | solution.py:428
  214.7 1.5 collective-permute-done.28.refs_3_
  217.5 3.1 %collective-permute-start.33 = (bf16[256,4096]{1,0:T(8,128)(2,1)S(1)}, bf16[256,4096]{1,0:T(8,128)(2,1)S(1)}, u32[]{:S(2)}, u32[]{:S(2)}) collective-permute-start(bf16[256,4096]{1,0:T(8,128)(2,1)S(1)} %shard_map.122), channel_id=1, source_target_pairs={{0,4},{2,10},{8,0},{10,18},{16,8},{18,26},{24,16},{26,30},{28,24},... | collective-permute-start | bytes 6291464 | tf_op jit(solution)/shard_map/ppermute | solution.py:396
  221.8 4.6 %copy-done.3 = bf16[2,3,256,4096]{3,2,1,0:T(8,128)(2,1)S(1)} copy-done((bf16[2,3,256,4096]{3,2,1,0:T(8,128)(2,1)S(1)}, bf16[2,3,256,4096]{3,2,1,0:T(8,128)(2,1)}, u32[]{:S(2)}) %copy-start.3) | copy-done | bytes 12582936
  228.7 8.7 %shard_map.123 = (bf16[256,4096]{1,0:T(8,128)(2,1)S(1)}, bf16[128,4096]{1,0:T(8,128)(2,1)S(1)}, bf16[128,4096]{1,0:T(8,128)(2,1)S(1)}) custom-call(bf16[768,512]{1,0:T(8,128)(2,1)S(1)} %bitcast.48, bf16[768,512]{1,0:T(8,128)(2,1)S(1)} %copy-done.12, bf16[1536,4096]{1,0:T(8,128)(2,1)S(1)} %bitcast.41), custom_call_target="tpu_custom_call" | custom-call | flops 1 | bytes 1 | tf_op jit(solution)/shard_map/pallas_call | solution.py:313
  237.5 2.6 collective-permute-done.31.far_ref
  245.0 2.3 collective-permute-start.37
  248.5 8.7 %shard_map.126 = (bf16[256,4096]{1,0:T(8,128)(2,1)S(1)}, bf16[128,4096]{1,0:T(8,128)(2,1)S(1)}, bf16[128,4096]{1,0:T(8,128)(2,1)S(1)}) custom-call(bf16[768,512]{1,0:T(8,128)(2,1)S(1)} %bitcast.46, bf16[768,512]{1,0:T(8,128)(2,1)S(1)} %collective-permute-done.31.far_ref, bf16[1536,4096]{1,0:T(8,128)(2,1)S(1)} %bitcast.42), custom_call_target="tpu_custom_call" | custom-call | flops 1 | bytes 1 | tf_op jit(solution)/shard_map/pallas_call | solution.py:313
  258.8 1.6 collective-permute-done.34.refs_1_
  261.9 8.5 %collective-permute-done.37.refs_3_ = bf16[256,4096]{1,0:T(8,128)(2,1)S(1)} collective-permute-done((bf16[256,4096]{1,0:T(8,128)(2,1)S(1)}, bf16[256,4096]{1,0:T(8,128)(2,1)S(1)}, u32[]{:S(2)}, u32[]{:S(2)}) %collective-permute-start.37) | collective-permute-done | bytes 2097184 | tf_op jit(solution)/shard_map/ppermute | solution.py:396
  270.4 2.4 shard_map.127
  272.8 2.0 collective-permute-start.40
  274.8 2.0 collective-permute-start.41
  276.9 5.8 %shard_map.128 = (bf16[128,4096]{1,0:T(8,128)(2,1)S(1)}, bf16[64,4096]{1,0:T(8,128)(2,1)}, bf16[64,4096]{1,0:T(8,128)(2,1)}) custom-call(bf16[768,256]{1,0:T(8,128)(2,1)S(1)} %bitcast.54, bf16[768,256]{1,0:T(8,128)(2,1)S(1)} %collective-permute-done.35.far_ref, bf16[1536,4096]{1,0:T(8,128)(2,1)S(1)} %bitcast.43), custom_call_target="tpu_custom_call" | custom-call | flops 1 | bytes 1 | tf_op jit(solution)/shard_map/pallas_call | solution.py:313
  285.7 1.6 collective-permute-done.40.refs_3_
  287.3 13.5 %collective-permute-done.41.refs_4_ = bf16[128,4096]{1,0:T(8,128)(2,1)S(1)} collective-permute-done((bf16[128,4096]{1,0:T(8,128)(2,1)}, bf16[128,4096]{1,0:T(8,128)(2,1)S(1)}, u32[]{:S(2)}, u32[]{:S(2)}) %collective-permute-start.41) | collective-permute-done | bytes 1048608 | tf_op jit(solution)/shard_map/ppermute | solution.py:396
  300.7 3.7 %shard_map.129 = bf16[128,4096]{1,0:T(8,128)(2,1)} custom-call(bf16[128,4096]{1,0:T(8,128)(2,1)S(1)} %get-tuple-element.179.refs_0_, bf16[64,4096]{1,0:T(8,128)(2,1)} %collective-permute-done.38.refs_1_, bf16[64,4096]{1,0:T(8,128)(2,1)} %collective-permute-done.39.refs_2_, bf16[128,4096]{1,0:T(8,128)(2,1)S(1)} %collective-permute-done.40.refs_3_, ...), custom_call_target="tpu_custom_call" | custom-call | flops 1 | bytes 1 | tf_op jit(solution)/shard_map/pallas_call | solution.py:353
  (136 shorter events, 51.1 us)
Async XLA Ops:
  0.6 13.7 %collective-permute-start.2 = (bf16[128,4096]{1,0:T(8,128)(2,1)}, bf16[128,4096]{1,0:T(8,128)(2,1)S(1)}, u32[]{:S(2)}, u32[]{:S(2)}) collective-permute-start(bf16[128,4096]{1,0:T(8,128)(2,1)} %refs_0_.3), channel_id=1, source_target_pairs={{0,2},{2,0},{4,6},{6,4},{8,10},{10,8},{12,14},{14,12},{16,18},{18,... | collective-permute-start | bytes 3145736 | tf_op jit(solution)/shard_map/ppermute | solution.py:399
  0.8 25.7 %collective-permute-start.1 = (bf16[128,4096]{1,0:T(8,128)(2,1)}, bf16[128,4096]{1,0:T(8,128)(2,1)S(1)}, u32[]{:S(2)}, u32[]{:S(2)}) collective-permute-start(bf16[128,4096]{1,0:T(8,128)(2,1)} %refs_0_.3), channel_id=1, source_target_pairs={{0,6},{2,8},{8,2},{10,16},{16,10},{18,24},{24,18},{26,28},{28,26},... | collective-permute-start | bytes 3145736 | tf_op jit(solution)/shard_map/ppermute | solution.py:396
  3.5 23.9 %collective-permute-start = (bf16[128,4096]{1,0:T(8,128)(2,1)}, bf16[128,4096]{1,0:T(8,128)(2,1)S(1)}, u32[]{:S(2)}, u32[]{:S(2)}) collective-permute-start(bf16[128,4096]{1,0:T(8,128)(2,1)} %refs_0_.3), channel_id=1, source_target_pairs={{0,8},{2,6},{8,16},{10,2},{16,24},{18,10},{24,28},{26,18},{28,20},... | collective-permute-start | bytes 3145736 | tf_op jit(solution)/shard_map/ppermute | solution.py:396
  14.3 98.2 %copy-start = (bf16[2,3,256,4096]{3,2,1,0:T(8,128)(2,1)}, bf16[2,3,256,4096]{3,2,1,0:T(8,128)(2,1)S(1)}, u32[]{:S(2)}) copy-start(bf16[2,3,256,4096]{3,2,1,0:T(8,128)(2,1)S(1)} %shard_map.111) | copy-start | bytes 37748740
  18.7 10.5 %copy-start.18 = (bf16[768,256]{1,0:T(8,128)(2,1)}, bf16[768,256]{1,0:T(8,128)(2,1)S(1)}, u32[]{:S(2)}) copy-start(bf16[768,256]{1,0:T(8,128)(2,1)S(1)} %get-tuple-element.115) | copy-start | bytes 1179652
  27.4 11.0 %collective-permute-start.4 = (bf16[768,256]{1,0:T(8,128)(2,1)S(1)}, bf16[768,256]{1,0:T(8,128)(2,1)}, u32[]{:S(2)}, u32[]{:S(2)}) collective-permute-start(bf16[768,256]{1,0:T(8,128)(2,1)S(1)} %get-tuple-element.102), channel_id=1, source_target_pairs={{0,1},{1,0},{2,3},{3,2},{4,5},{5,4},{6,7},{7,6},{8,9},{9,8},{10,11... | collective-permute-start | bytes 1179656 | tf_op jit(solution)/shard_map/ppermute | solution.py:428
  29.3 25.2 %collective-permute-start.3 = (bf16[256,4096]{1,0:T(8,128)(2,1)S(1)}, bf16[256,4096]{1,0:T(8,128)(2,1)S(1)}, u32[]{:S(2)}, u32[]{:S(2)}) collective-permute-start(bf16[256,4096]{1,0:T(8,128)(2,1)S(1)} %constant_dynamic-update-slice_fusion.refs_0_), channel_id=1, source_target_pairs={{0,8},{2,6},{8,16},{10,2},{16,24},{18,10},{24,28},{26,18},{28,20},... | collective-permute-start | bytes 6291464 | tf_op jit(solution)/shard_map/ppermute | solution.py:396
  38.6 3.2 %collective-permute-start.6 = (bf16[128,4096]{1,0:T(8,128)(2,1)S(1)}, bf16[128,4096]{1,0:T(8,128)(2,1)S(1)}, u32[]{:S(2)}, u32[]{:S(2)}) collective-permute-start(bf16[128,4096]{1,0:T(8,128)(2,1)S(1)} %get-tuple-element.198), channel_id=1, source_target_pairs={{0,2},{2,0},{4,6},{6,4},{8,10},{10,8},{12,14},{14,12},{16,18},{18,... | collective-permute-start | bytes 3145736 | tf_op jit(solution)/shard_map/ppermute | solution.py:399
  39.6 3.8 %collective-permute-start.5 = (bf16[128,4096]{1,0:T(8,128)(2,1)S(1)}, bf16[128,4096]{1,0:T(8,128)(2,1)S(1)}, u32[]{:S(2)}, u32[]{:S(2)}) collective-permute-start(bf16[128,4096]{1,0:T(8,128)(2,1)S(1)} %get-tuple-element.199), channel_id=1, source_target_pairs={{0,2},{2,0},{4,6},{6,4},{8,10},{10,8},{12,14},{14,12},{16,18},{18,... | collective-permute-start | bytes 3145736 | tf_op jit(solution)/shard_map/ppermute | solution.py:399
  52.1 18.8 %collective-permute-start.8 = (bf16[768,512]{1,0:T(8,128)(2,1)S(1)}, bf16[768,512]{1,0:T(8,128)(2,1)S(1)}, u32[]{:S(2)}, u32[]{:S(2)}) collective-permute-start(bf16[768,512]{1,0:T(8,128)(2,1)S(1)} %get-tuple-element.106), channel_id=1, source_target_pairs={{0,1},{1,0},{2,3},{3,2},{4,5},{5,4},{6,7},{7,6},{8,9},{9,8},{10,11... | collective-permute-start | bytes 2359304 | tf_op jit(solution)/shard_map/ppermute | solution.py:428
  54.5 31.6 %collective-permute-start.7 = (bf16[256,4096]{1,0:T(8,128)(2,1)S(1)}, bf16[256,4096]{1,0:T(8,128)(2,1)S(1)}, u32[]{:S(2)}, u32[]{:S(2)}) collective-permute-start(bf16[256,4096]{1,0:T(8,128)(2,1)S(1)} %collective-permute-done.3.refs_0_), channel_id=1, source_target_pairs={{0,8},{2,6},{8,16},{10,2},{16,24},{18,10},{24,28},{26,18},{28,20},... | collective-permute-start | bytes 6291464 | tf_op jit(solution)/shard_map/ppermute | solution.py:396
  71.7 3.5 %collective-permute-start.10 = (bf16[128,4096]{1,0:T(8,128)(2,1)S(1)}, bf16[128,4096]{1,0:T(8,128)(2,1)S(1)}, u32[]{:S(2)}, u32[]{:S(2)}) collective-permute-start(bf16[128,4096]{1,0:T(8,128)(2,1)S(1)} %get-tuple-element.196), channel_id=1, source_target_pairs={{0,2},{2,0},{4,6},{6,4},{8,10},{10,8},{12,14},{14,12},{16,18},{18,... | collective-permute-start | bytes 3145736 | tf_op jit(solution)/shard_map/ppermute | solution.py:399
  72.9 3.8 %collective-permute-start.9 = (bf16[128,4096]{1,0:T(8,128)(2,1)S(1)}, bf16[128,4096]{1,0:T(8,128)(2,1)S(1)}, u32[]{:S(2)}, u32[]{:S(2)}) collective-permute-start(bf16[128,4096]{1,0:T(8,128)(2,1)S(1)} %get-tuple-element.197), channel_id=1, source_target_pairs={{0,2},{2,0},{4,6},{6,4},{8,10},{10,8},{12,14},{14,12},{16,18},{18,... | collective-permute-start | bytes 3145736 | tf_op jit(solution)/shard_map/ppermute | solution.py:399
  84.5 21.4 %copy-start.15 = (bf16[768,512]{1,0:T(8,128)(2,1)}, bf16[768,512]{1,0:T(8,128)(2,1)S(1)}, u32[]{:S(2)}) copy-start(bf16[768,512]{1,0:T(8,128)(2,1)S(1)} %get-tuple-element.117) | copy-start | bytes 2359300
  84.6 18.8 %collective-permute-start.12 = (bf16[768,512]{1,0:T(8,128)(2,1)S(1)}, bf16[768,512]{1,0:T(8,128)(2,1)S(1)}, u32[]{:S(2)}, u32[]{:S(2)}) collective-permute-start(bf16[768,512]{1,0:T(8,128)(2,1)S(1)} %get-tuple-element.110), channel_id=1, source_target_pairs={{0,1},{1,0},{2,3},{3,2},{4,5},{5,4},{6,7},{7,6},{8,9},{9,8},{10,11... | collective-permute-start | bytes 2359304 | tf_op jit(solution)/shard_map/ppermute | solution.py:428
  103.4 9.1 %collective-permute-start.13 = (bf16[96,4096]{1,0:T(8,128)(2,1)S(1)}, bf16[96,4096]{1,0:T(8,128)(2,1)S(1)}, u32[]{:S(2)}, u32[]{:S(2)}) collective-permute-start(bf16[96,4096]{1,0:T(8,128)(2,1)S(1)} %split.25), channel_id=1, source_target_pairs={{0,2},{2,0},{4,6},{6,4},{8,10},{10,8},{12,14},{14,12},{16,18},{18,... | collective-permute-start | bytes 2359304 | tf_op jit(solution)/shard_map/ppermute | solution.py:399
  104.7 16.8 %collective-permute-start.11 = (bf16[128,4096]{1,0:T(8,128)(2,1)S(1)}, bf16[128,4096]{1,0:T(8,128)(2,1)S(1)}, u32[]{:S(2)}, u32[]{:S(2)}) collective-permute-start(bf16[128,4096]{1,0:T(8,128)(2,1)S(1)} %slice.21), channel_id=1, source_target_pairs={{0,8},{2,6},{8,16},{10,2},{16,24},{18,10},{24,28},{26,18},{28,20},... | collective-permute-start | bytes 3145736 | tf_op jit(solution)/shard_map/ppermute | solution.py:396
  105.9 6.6 %collective-permute-start.15 = (bf16[80,4096]{1,0:T(8,128)(2,1)S(1)}, bf16[80,4096]{1,0:T(8,128)(2,1)S(1)}, u32[]{:S(2)}, u32[]{:S(2)}) collective-permute-start(bf16[80,4096]{1,0:T(8,128)(2,1)S(1)} %get-tuple-element.194), channel_id=1, source_target_pairs={{0,2},{2,0},{4,6},{6,4},{8,10},{10,8},{12,14},{14,12},{16,18},{18,... | collective-permute-start | bytes 1966088 | tf_op jit(solution)/shard_map/ppermute | solution.py:399
  106.8 5.7 %collective-permute-start.14 = (bf16[80,4096]{1,0:T(8,128)(2,1)S(1)}, bf16[80,4096]{1,0:T(8,128)(2,1)S(1)}, u32[]{:S(2)}, u32[]{:S(2)}) collective-permute-start(bf16[80,4096]{1,0:T(8,128)(2,1)S(1)} %get-tuple-element.195), channel_id=1, source_target_pairs={{0,2},{2,0},{4,6},{6,4},{8,10},{10,8},{12,14},{14,12},{16,18},{18,... | collective-permute-start | bytes 1966088 | tf_op jit(solution)/shard_map/ppermute | solution.py:399
  111.2 10.3 %collective-permute-start.16 = (bf16[768,256]{1,0:T(8,128)(2,1)S(1)}, bf16[768,256]{1,0:T(8,128)(2,1)S(1)}, u32[]{:S(2)}, u32[]{:S(2)}) collective-permute-start(bf16[768,256]{1,0:T(8,128)(2,1)S(1)} %get-tuple-element.113), channel_id=1, source_target_pairs={{0,1},{1,0},{2,3},{3,2},{4,5},{5,4},{6,7},{7,6},{8,9},{9,8},{10,11... | collective-permute-start | bytes 1179656 | tf_op jit(solution)/shard_map/ppermute | solution.py:428
  121.5 29.3 %all-to-all-start = ((bf16[16,256,128]{2,1,0:T(8,128)(2,1)}), bf16[16,256,128]{2,1,0:T(8,128)(2,1)S(1)}, u32[]{:S(2)}, u32[]{:S(2)}) async-start(bf16[16,256,128]{2,1,0:T(8,128)(2,1)} %bitcast.6), calls=%async_computation | async-start | bytes 2097152 | tf_op jit(solution)/shard_map/all_to_all | solution.py:466
  127.8 2.0 collective-permute-start.18
  128.0 2.6 collective-permute-start.17
  128.4 11.8 %collective-permute-start.19 = (bf16[768,256]{1,0:T(8,128)(2,1)S(1)}, bf16[768,256]{1,0:T(8,128)(2,1)S(1)}, u32[]{:S(2)}, u32[]{:S(2)}) collective-permute-start(bf16[768,256]{1,0:T(8,128)(2,1)S(1)} %get-tuple-element.127), channel_id=1, source_target_pairs={{0,1},{1,0},{2,3},{3,2},{4,5},{5,4},{6,7},{7,6},{8,9},{9,8},{10,11... | collective-permute-start | bytes 1179656 | tf_op jit(solution)/shard_map/ppermute | solution.py:428
  140.2 10.7 %copy-start.26 = (bf16[768,256]{1,0:T(8,128)(2,1)}, bf16[768,256]{1,0:T(8,128)(2,1)S(1)}, u32[]{:S(2)}) copy-start(bf16[768,256]{1,0:T(8,128)(2,1)S(1)} %collective-permute-done.19) | copy-start | bytes 1179652
  140.2 10.6 %collective-permute-start.20 = (bf16[768,256]{1,0:T(8,128)(2,1)S(1)}, bf16[768,256]{1,0:T(8,128)(2,1)S(1)}, u32[]{:S(2)}, u32[]{:S(2)}) collective-permute-start(bf16[768,256]{1,0:T(8,128)(2,1)S(1)} %get-tuple-element.129), channel_id=1, source_target_pairs={{0,1},{1,0},{2,3},{3,2},{4,5},{5,4},{6,7},{7,6},{8,9},{9,8},{10,11... | collective-permute-start | bytes 1179656 | tf_op jit(solution)/shard_map/ppermute | solution.py:428
  168.3 9.9 %collective-permute-start.21 = (bf16[768,256]{1,0:T(8,128)(2,1)}, bf16[768,256]{1,0:T(8,128)(2,1)S(1)}, u32[]{:S(2)}, u32[]{:S(2)}) collective-permute-start(bf16[768,256]{1,0:T(8,128)(2,1)} %bitcast.55), channel_id=1, source_target_pairs={{0,1},{1,0},{2,3},{3,2},{4,5},{5,4},{6,7},{7,6},{8,9},{9,8},{10,11... | collective-permute-start | bytes 1179656 | tf_op jit(solution)/shard_map/ppermute | solution.py:428
  169.6 47.9 %all-to-all-start.1 = ((bf16[16,256,128]{2,1,0:T(8,128)(2,1)}), bf16[16,256,128]{2,1,0:T(8,128)(2,1)S(1)}, u32[]{:S(2)}, u32[]{:S(2)}) async-start(bf16[16,256,128]{2,1,0:T(8,128)(2,1)} %get-tuple-element.150), calls=%async_computation.1 | async-start | bytes 2097152 | tf_op jit(solution)/shard_map/all_to_all | solution.py:483
  176.5 19.7 %collective-permute-start.24 = (bf16[768,512]{1,0:T(8,128)(2,1)S(1)}, bf16[768,512]{1,0:T(8,128)(2,1)S(1)}, u32[]{:S(2)}, u32[]{:S(2)}) collective-permute-start(bf16[768,512]{1,0:T(8,128)(2,1)S(1)} %bitcast.49), channel_id=1, source_target_pairs={{0,1},{1,0},{2,3},{3,2},{4,5},{5,4},{6,7},{7,6},{8,9},{9,8},{10,11... | collective-permute-start | bytes 2359304 | tf_op jit(solution)/shard_map/ppermute | solution.py:428
  188.0 4.7 %collective-permute-start.22 = (bf16[80,4096]{1,0:T(8,128)(2,1)S(1)}, bf16[80,4096]{1,0:T(8,128)(2,1)S(1)}, u32[]{:S(2)}, u32[]{:S(2)}) collective-permute-start(bf16[80,4096]{1,0:T(8,128)(2,1)S(1)} %get-tuple-element.132), channel_id=1, source_target_pairs={{0,2},{2,0},{4,6},{6,4},{8,10},{10,8},{12,14},{14,12},{16,18},{18,... | collective-permute-start | bytes 1966088 | tf_op jit(solution)/shard_map/ppermute | solution.py:399
  190.4 2.3 collective-permute-start.23
  190.5 22.6 %collective-permute-start.27 = (bf16[768,512]{1,0:T(8,128)(2,1)S(1)}, bf16[768,512]{1,0:T(8,128)(2,1)S(1)}, u32[]{:S(2)}, u32[]{:S(2)}) collective-permute-start(bf16[768,512]{1,0:T(8,128)(2,1)S(1)} %bitcast.47), channel_id=1, source_target_pairs={{0,1},{1,0},{2,3},{3,2},{4,5},{5,4},{6,7},{7,6},{8,9},{9,8},{10,11... | collective-permute-start | bytes 2359304 | tf_op jit(solution)/shard_map/ppermute | solution.py:428
  196.3 20.0 %collective-permute-start.29 = (bf16[128,4096]{1,0:T(8,128)(2,1)S(1)}, bf16[128,4096]{1,0:T(8,128)(2,1)S(1)}, u32[]{:S(2)}, u32[]{:S(2)}) collective-permute-start(bf16[128,4096]{1,0:T(8,128)(2,1)S(1)} %shard_map.120), channel_id=1, source_target_pairs={{0,4},{2,10},{8,0},{10,18},{16,8},{18,26},{24,16},{26,30},{28,24},... | collective-permute-start | bytes 3145736 | tf_op jit(solution)/shard_map/ppermute | solution.py:396
  208.2 8.1 %collective-permute-start.25 = (bf16[96,4096]{1,0:T(8,128)(2,1)S(1)}, bf16[96,4096]{1,0:T(8,128)(2,1)S(1)}, u32[]{:S(2)}, u32[]{:S(2)}) collective-permute-start(bf16[96,4096]{1,0:T(8,128)(2,1)S(1)} %get-tuple-element.140), channel_id=1, source_target_pairs={{0,2},{2,0},{4,6},{6,4},{8,10},{10,8},{12,14},{14,12},{16,18},{18,... | collective-permute-start | bytes 2359304 | tf_op jit(solution)/shard_map/ppermute | solution.py:399
  208.3 7.9 %collective-permute-start.26 = (bf16[96,4096]{1,0:T(8,128)(2,1)S(1)}, bf16[96,4096]{1,0:T(8,128)(2,1)S(1)}, u32[]{:S(2)}, u32[]{:S(2)}) collective-permute-start(bf16[96,4096]{1,0:T(8,128)(2,1)S(1)} %get-tuple-element.141), channel_id=1, source_target_pairs={{0,2},{2,0},{4,6},{6,4},{8,10},{10,8},{12,14},{14,12},{16,18},{18,... | collective-permute-start | bytes 2359304 | tf_op jit(solution)/shard_map/ppermute | solution.py:399
  214.0 2.3 collective-permute-start.28
  217.5 26.1 %collective-permute-start.33 = (bf16[256,4096]{1,0:T(8,128)(2,1)S(1)}, bf16[256,4096]{1,0:T(8,128)(2,1)S(1)}, u32[]{:S(2)}, u32[]{:S(2)}) collective-permute-start(bf16[256,4096]{1,0:T(8,128)(2,1)S(1)} %shard_map.122), channel_id=1, source_target_pairs={{0,4},{2,10},{8,0},{10,18},{16,8},{18,26},{24,16},{26,30},{28,24},... | collective-permute-start | bytes 6291464 | tf_op jit(solution)/shard_map/ppermute | solution.py:396
  220.6 19.5 %collective-permute-start.31 = (bf16[768,512]{1,0:T(8,128)(2,1)}, bf16[768,512]{1,0:T(8,128)(2,1)S(1)}, u32[]{:S(2)}, u32[]{:S(2)}) collective-permute-start(bf16[768,512]{1,0:T(8,128)(2,1)} %bitcast.45), channel_id=1, source_target_pairs={{0,1},{1,0},{2,3},{3,2},{4,5},{5,4},{6,7},{7,6},{8,9},{9,8},{10,11... | collective-permute-start | bytes 2359304 | tf_op jit(solution)/shard_map/ppermute | solution.py:428
  237.4 4.3 %collective-permute-start.30 = (bf16[128,4096]{1,0:T(8,128)(2,1)S(1)}, bf16[128,4096]{1,0:T(8,128)(2,1)S(1)}, u32[]{:S(2)}, u32[]{:S(2)}) collective-permute-start(bf16[128,4096]{1,0:T(8,128)(2,1)S(1)} %get-tuple-element.154), channel_id=1, source_target_pairs={{0,2},{2,0},{4,6},{6,4},{8,10},{10,8},{12,14},{14,12},{16,18},{18,... | collective-permute-start | bytes 3145736 | tf_op jit(solution)/shard_map/ppermute | solution.py:399
  240.1 2.7 collective-permute-start.32
  245.0 25.4 %collective-permute-start.37 = (bf16[256,4096]{1,0:T(8,128)(2,1)S(1)}, bf16[256,4096]{1,0:T(8,128)(2,1)S(1)}, u32[]{:S(2)}, u32[]{:S(2)}) collective-permute-start(bf16[256,4096]{1,0:T(8,128)(2,1)S(1)} %shard_map.124), channel_id=1, source_target_pairs={{0,4},{2,10},{8,0},{10,18},{16,8},{18,26},{24,16},{26,30},{28,24},... | collective-permute-start | bytes 6291464 | tf_op jit(solution)/shard_map/ppermute | solution.py:396
  247.2 10.8 %collective-permute-start.35 = (bf16[768,256]{1,0:T(8,128)(2,1)S(1)}, bf16[768,256]{1,0:T(8,128)(2,1)S(1)}, u32[]{:S(2)}, u32[]{:S(2)}) collective-permute-start(bf16[768,256]{1,0:T(8,128)(2,1)S(1)} %bitcast.53), channel_id=1, source_target_pairs={{0,1},{1,0},{2,3},{3,2},{4,5},{5,4},{6,7},{7,6},{8,9},{9,8},{10,11... | collective-permute-start | bytes 1179656 | tf_op jit(solution)/shard_map/ppermute | solution.py:428
  257.2 3.1 %collective-permute-start.34 = (bf16[128,4096]{1,0:T(8,128)(2,1)S(1)}, bf16[128,4096]{1,0:T(8,128)(2,1)S(1)}, u32[]{:S(2)}, u32[]{:S(2)}) collective-permute-start(bf16[128,4096]{1,0:T(8,128)(2,1)S(1)} %get-tuple-element.166), channel_id=1, source_target_pairs={{0,2},{2,0},{4,6},{6,4},{8,10},{10,8},{12,14},{14,12},{16,18},{18,... | collective-permute-start | bytes 3145736 | tf_op jit(solution)/shard_map/ppermute | solution.py:399
  258.1 3.8 %collective-permute-start.36 = (bf16[128,4096]{1,0:T(8,128)(2,1)S(1)}, bf16[128,4096]{1,0:T(8,128)(2,1)S(1)}, u32[]{:S(2)}, u32[]{:S(2)}) collective-permute-start(bf16[128,4096]{1,0:T(8,128)(2,1)S(1)} %get-tuple-element.169), channel_id=1, source_target_pairs={{0,2},{2,0},{4,6},{6,4},{8,10},{10,8},{12,14},{14,12},{16,18},{18,... | collective-permute-start | bytes 3145736 | tf_op jit(solution)/shard_map/ppermute | solution.py:399
  272.8 14.4 %collective-permute-start.40 = (bf16[128,4096]{1,0:T(8,128)(2,1)}, bf16[128,4096]{1,0:T(8,128)(2,1)S(1)}, u32[]{:S(2)}, u32[]{:S(2)}) collective-permute-start(bf16[128,4096]{1,0:T(8,128)(2,1)} %get-tuple-element.182), channel_id=1, source_target_pairs={{0,4},{2,10},{8,0},{10,18},{16,8},{18,26},{24,16},{26,30},{28,24},... | collective-permute-start | bytes 3145736 | tf_op jit(solution)/shard_map/ppermute | solution.py:396
  274.8 25.9 %collective-permute-start.41 = (bf16[128,4096]{1,0:T(8,128)(2,1)}, bf16[128,4096]{1,0:T(8,128)(2,1)S(1)}, u32[]{:S(2)}, u32[]{:S(2)}) collective-permute-start(bf16[128,4096]{1,0:T(8,128)(2,1)} %get-tuple-element.183), channel_id=1, source_target_pairs={{0,6},{2,8},{8,2},{10,16},{16,10},{18,24},{24,18},{26,28},{28,26},... | collective-permute-start | bytes 3145736 | tf_op jit(solution)/shard_map/ppermute | solution.py:396
  282.7 2.3 collective-permute-start.38
  282.7 3.0 collective-permute-start.39
  (26 other events, 100.3 us)

commit v8 on v6

--- a/solution.py
+++ b/solution.py
@@ -44,7 +44,11 @@
     return lax.dot_general(a, b, (dims, ((), ())), preferred_element_type=F32)
 
 
-def mix_body(count, sets, per_step, grouped, order, short_ref, long_ref, g_ref, *refs):
+def turn_taps(taps):
+    return jnp.roll(jnp.flip(taps, axis=1), 1, axis=1)
+
+
+def mix_body(count, sets, per_turn, grouped, order, short_ref, long_ref, turned_ref, g_ref, *refs):
     proj_refs = [refs[s * count : (s + 1) * count] for s in range(sets)]
     refs = refs[sets * count :]
     d_count = len(grouped)
@@ -56,8 +60,8 @@
 
     @pl.when(step == 0)
     def _():
-        x_s[:, 0:GROUP, :] = jnp.zeros((per_step, GROUP, LONG), BF16)
-        y_s[:, rows:, :] = jnp.zeros((per_step, GROUP, LONG), BF16)
+        x_s[:, 0:GROUP, :] = jnp.zeros((per_turn, GROUP, LONG), BF16)
+        y_s[:, rows:, :] = jnp.zeros((per_turn, GROUP, LONG), BF16)
 
     halves = [(a, h) for a in range(count) for h in range(proj_refs[0][a].shape[2] // LONG)]
     places = [(a, h, where) for where, (a, h) in enumerate(halves)]
@@ -72,100 +76,108 @@
     col = lax.broadcasted_iota(jnp.int32, (LONG, LONG), 1)
     row = lax.broadcasted_iota(jnp.int32, (LONG, LONG), 0)
 
-    every = range(per_step)
-    mine = [slice(j * GROUP, (j + 1) * GROUP) for j in every]
-    taps = [
-        [[short_ref[i, step * per_step + j, k] for k in range(SHORT)] for i in range(3)] for j in every
-    ]
-    for a, h, where in places:
-        at = pl.multiple_of(order[where] * GROUP, GROUP)
+    per_step = gl_ref.shape[1]
+
+    @pl.loop(0, per_step // per_turn)
+    def _(turn):
+        every = range(per_turn)
+        mine = [pl.ds(pl.multiple_of((turn * per_turn + j) * GROUP, GROUP), GROUP) for j in every]
+        lines = [turn * per_turn + j for j in every]
+        taps = [
+            [[short_ref[i, step * per_step + lines[j], k] for k in range(SHORT)] for i in range(3)] for j in every
+        ]
+        for a, h, where in places:
+            at = pl.multiple_of(order[where] * GROUP, GROUP)
+            for j in every:
+                for i in range(3):
+                    part = proj_refs[0][a][i, mine[j], h * LONG : (h + 1) * LONG].astype(F32)
+                    for s in range(1, sets):
+                        part = part + proj_refs[s][a][i, mine[j], h * LONG : (h + 1) * LONG].astype(F32)
+                    p_s[j, i, pl.ds(at, GROUP), :] = part
+
         for j in every:
+            before = [(zero, zero)] * 3
+            for at in at_block:
+                feat = []
+                for i in range(3):
+                    here = p_s[j, i, at, :]
+                    one = pltpu.roll(here, 1, 1)
+                    two = pltpu.roll(here, 2, 1)
+                    past_one = jnp.where(lane < 1, before[i][0], one)
+                    past_two = jnp.where(lane < 2, before[i][1], two)
+                    before[i] = (one, two)
+                    feat.append(taps[j][i][0] * here + taps[j][i][1] * past_one + taps[j][i][2] * past_two)
+                    f_s[j, i, at, :] = feat[i]
+                x_s[j, at.stop : at.stop + GROUP, :] = (feat[1] * feat[2]).astype(BF16)
+
+        filters, turned = [], []
+        for j in every:
+            for ref, made in ((long_ref, filters), (turned_ref, turned)):
+                base = jnp.broadcast_to(ref[0, pl.ds(lines[j], 1), :], (8, LONG))
+                for bit in (1, 2, 4):
+                    base = jnp.where((sub8 & bit) != 0, pltpu.roll(base, bit, 1), base)
+                full = jnp.concatenate([base] + [pltpu.roll(base, 8 * m, 1) for m in range(1, LONG // 8)], axis=0)
+                inside = col >= row if made is filters else col <= row
+                near = jnp.where(inside, full, 0.0).astype(BF16)
+                far = jnp.where(inside, 0.0, full).astype(BF16)
+                made.append(jnp.concatenate([near, far], axis=0))
+
+        x_twos = [jnp.concatenate([x_s[j, GROUP:, :], x_s[j, :rows, :]], axis=1) for j in every]
+        inners = [dot(x_twos[j], filters[j], ((1,), (0,))) for j in every]
+        for j in every:
+            for n, at in enumerate(at_block):
+                g = g_ref[n, mine[j], :].astype(F32)
+                feat, inner = f_s[j, 0, at, :], inners[j][at]
+                mixed_ref[n, mine[j], :] = (feat * inner).astype(BF16)
+                y_s[j, at, :] = (g * feat).astype(BF16)
+                d_s[j, at, :] = g * inner
+        d_products = []
+        for j in every:
+            y_two = jnp.concatenate([y_s[j, :rows, :], y_s[j, GROUP:, :]], axis=1)
+            d_products.append(dot(y_two, turned[j], ((1,), (0,))))
+        folds = [dot(y_s[j, :rows, :], x_twos[j], ((0,), (0,))) for j in every]
+        for j in every:
+            fold = jnp.where(col <= row, folds[j][:, :LONG], folds[j][:, LONG:])
+            width = LONG
+            while width > 8:
+                width //= 2
+                fold = fold[:width] + pltpu.roll(fold[width:], LONG - width, 1)
+            for bit in (4, 2, 1):
+                fold = jnp.where((sub8 & bit) != 0, pltpu.roll(fold, LONG - bit, 1), fold)
+            gl_ref[0, pl.ds(lines[j], 1), :] = jnp.sum(fold, axis=0, keepdims=True)
+
+        for j in every:
+            after = [(zero, zero)] * 3
+            sums = [[zero] * SHORT for _ in range(3)]
+            for at in at_block[::-1]:
+                d_product = d_products[j][at]
+                for i, d in enumerate((d_s[j, at, :], d_product * f_s[j, 2, at, :], d_product * f_s[j, 1, at, :])):
+                    one = pltpu.roll(d, LONG - 1, 1)
+                    two = pltpu.roll(d, LONG - 2, 1)
+                    next_one = jnp.where(lane >= LONG - 1, after[i][0], one)
+                    next_two = jnp.where(lane >= LONG - 2, after[i][1], two)
+                    after[i] = (one, two)
+                    p = p_s[j, i, at, :]
+                    sums[i] = [total + p * moved for total, moved in zip(sums[i], (d, next_one, next_two))]
+                    e_s[j, i, at, :] = (
+                        taps[j][i][0] * d + taps[j][i][1] * next_one + taps[j][i][2] * next_two
+                    ).astype(BF16)
             for i in range(3):
-                part = proj_refs[0][a][i, mine[j], h * LONG : (h + 1) * LONG].astype(F32)
-                for s in range(1, sets):
-                    part = part + proj_refs[s][a][i, mine[j], h * LONG : (h + 1) * LONG].astype(F32)
-                p_s[j, i, pl.ds(at, GROUP), :] = part
-
-    for j in every:
-        before = [(zero, zero)] * 3
-        for at in at_block:
-            feat = []
-            for i in range(3):
-                here = p_s[j, i, at, :]
-                one = pltpu.roll(here, 1, 1)
-                two = pltpu.roll(here, 2, 1)
-                past_one = jnp.where(lane < 1, before[i][0], one)
-                past_two = jnp.where(lane < 2, before[i][1], two)
-                before[i] = (one, two)
-                feat.append(taps[j][i][0] * here + taps[j][i][1] * past_one + taps[j][i][2] * past_two)
-                f_s[j, i, at, :] = feat[i]
-            x_s[j, at.stop : at.stop + GROUP, :] = (feat[1] * feat[2]).astype(BF16)
-
-    filters = []
-    for j in every:
-        base = jnp.broadcast_to(long_ref[0, j : j + 1, :], (8, LONG))
-        for bit in (1, 2, 4):
-            base = jnp.where((sub8 & bit) != 0, pltpu.roll(base, bit, 1), base)
-        full = jnp.concatenate([base] + [pltpu.roll(base, 8 * m, 1) for m in range(1, LONG // 8)], axis=0)
-        near = jnp.where(col >= row, full, 0.0).astype(BF16)
-        far = jnp.where(col < row, full, 0.0).astype(BF16)
-        filters.append((near, far))
-
-    x_twos = [jnp.concatenate([x_s[j, GROUP:, :], x_s[j, :rows, :]], axis=1) for j in every]
-    inners = [dot(x_twos[j], jnp.concatenate(filters[j], axis=0), ((1,), (0,))) for j in every]
-    for j in every:
-        for n, at in enumerate(at_block):
-            g = g_ref[n, mine[j], :].astype(F32)
-            feat, inner = f_s[j, 0, at, :], inners[j][at]
-            mixed_ref[n, mine[j], :] = (feat * inner).astype(BF16)
-            y_s[j, at, :] = (g * feat).astype(BF16)
-            d_s[j, at, :] = g * inner
-    d_products = []
-    for j in every:
-        y_two = jnp.concatenate([y_s[j, :rows, :], y_s[j, GROUP:, :]], axis=1)
-        d_products.append(dot(y_two, jnp.concatenate(filters[j], axis=1), ((1,), (1,))))
-    folds = [dot(y_s[j, :rows, :], x_twos[j], ((0,), (0,))) for j in every]
-    for j in every:
-        fold = jnp.where(col <= row, folds[j][:, :LONG], folds[j][:, LONG:])
-        width = LONG
-        while width > 8:
-            width //= 2
-            fold = fold[:width] + pltpu.roll(fold[width:], LONG - width, 1)
-        for bit in (4, 2, 1):
-            fold = jnp.where((sub8 & bit) != 0, pltpu.roll(fold, LONG - bit, 1), fold)
-        gl_ref[0, j : j + 1, :] = jnp.sum(fold, axis=0, keepdims=True)
-
-    for j in every:
-        after = [(zero, zero)] * 3
-        sums = [[zero] * SHORT for _ in range(3)]
-        for at in at_block[::-1]:
-            d_product = d_products[j][at]
-            for i, d in enumerate((d_s[j, at, :], d_product * f_s[j, 2, at, :], d_product * f_s[j, 1, at, :])):
-                one = pltpu.roll(d, LONG - 1, 1)
-                two = pltpu.roll(d, LONG - 2, 1)
-                next_one = jnp.where(lane >= LONG - 1, after[i][0], one)
-                next_two = jnp.where(lane >= LONG - 2, after[i][1], two)
-                after[i] = (one, two)
-                p = p_s[j, i, at, :]
-                sums[i] = [total + p * moved for total, moved in zip(sums[i], (d, next_one, next_two))]
-                e_s[j, i, at, :] = (
-                    taps[j][i][0] * d + taps[j][i][1] * next_one + taps[j][i][2] * next_two
-                ).astype(BF16)
-        for i in range(3):
-            for k in range(SHORT):
-                gs_ref[0, j, 3 * i + k : 3 * i + k + 1, :] = jnp.sum(sums[i][k], axis=0, keepdims=True)
-    for a, h, where in d_places:
-        at = pl.multiple_of(order[where] * GROUP, GROUP)
-        for j in every:
-            for i in range(3):
-                d_refs[a][i, mine[j], h * LONG : (h + 1) * LONG] = e_s[j, i, pl.ds(at, GROUP), :]
-
-
-def mix(order, short_kernel, long_kernel, g, proj_sets, grouped):
+                for k in range(SHORT):
+                    gs_ref[0, lines[j], 3 * i + k : 3 * i + k + 1, :] = jnp.sum(sums[i][k], axis=0, keepdims=True)
+        for a, h, where in d_places:
+            at = pl.multiple_of(order[where] * GROUP, GROUP)
+            for j in every:
+                for i in range(3):
+                    d_refs[a][i, mine[j], h * LONG : (h + 1) * LONG] = e_s[j, i, pl.ds(at, GROUP), :]
+
+
+def mix(order, short_kernel, long_kernel, turned_kernel, g, proj_sets, grouped):
     blocks, channels, _ = g.shape
     count, sets = len(proj_sets[0]), len(proj_sets)
     groups = channels // GROUP
-    per_step = next(n for n in (2, 1) if groups % n == 0)
+    per_turn = next(n for n in (2, 1) if groups % n == 0)
+    per_step = next(n for n in (4, 2, 1) if groups % n == 0)
     steps = groups // per_step
     rows = blocks * GROUP
     high = per_step * GROUP
@@ -174,12 +186,13 @@
     d_specs = [pl.BlockSpec((3, high, w), lambda i, o: (0, i, 0)) for w in d_widths]
     token_spec = pl.BlockSpec((blocks, high, LONG), lambda i, o: (0, i, 0))
     outs = pl.pallas_call(
-        functools.partial(mix_body, count, sets, per_step, grouped),
+        functools.partial(mix_body, count, sets, per_turn, grouped),
         grid_spec=pltpu.PrefetchScalarGridSpec(
             num_scalar_prefetch=1,
             grid=(steps,),
             in_specs=[
                 pl.BlockSpec(memory_space=pltpu.SMEM),
+                pl.BlockSpec((1, per_step, LONG), lambda i, o: (i, 0, 0)),
                 pl.BlockSpec((1, per_step, LONG), lambda i, o: (i, 0, 0)),
                 token_spec,
             ]
@@ -191,12 +204,12 @@
                 pl.BlockSpec((1, per_step, LONG), lambda i, o: (i, 0, 0)),
             ],
             scratch_shapes=[
-                pltpu.VMEM((per_step, 3, rows, LONG), F32),
-                pltpu.VMEM((per_step, 3, rows, LONG), F32),
-                pltpu.VMEM((per_step, rows + GROUP, LONG), BF16),
-                pltpu.VMEM((per_step, rows + GROUP, LONG), BF16),
-                pltpu.VMEM((per_step, rows, LONG), F32),
-                pltpu.VMEM((per_step, 3, rows, LONG), BF16),
+                pltpu.VMEM((per_turn, 3, rows, LONG), F32),
+                pltpu.VMEM((per_turn, 3, rows, LONG), F32),
+                pltpu.VMEM((per_turn, rows + GROUP, LONG), BF16),
+                pltpu.VMEM((per_turn, rows + GROUP, LONG), BF16),
+                pltpu.VMEM((per_turn, rows, LONG), F32),
+                pltpu.VMEM((per_turn, 3, rows, LONG), BF16),
             ],
         ),
         out_shape=[jax.ShapeDtypeStruct((blocks, channels, LONG), BF16)]
@@ -207,10 +220,10 @@
         ],
         compiler_params=pltpu.CompilerParams(vmem_limit_bytes=58 * MIB),
         cost_estimate=SMALL,
-    )(order, short_kernel, long_kernel.reshape(steps, per_step, LONG), g, *[x for s in proj_sets for x in s])
+    )(order, short_kernel, long_kernel.reshape(steps, per_step, LONG), turned_kernel.reshape(steps, per_step, LONG), g, *[x for s in proj_sets for x in s])
     mixed, d_proj, (gs, gl) = outs[0], outs[1:-2], outs[-2:]
     grad_short = jnp.sum(gs, axis=-1).reshape(groups, 3, SHORT).transpose(1, 0, 2)
-    grad_long = jnp.roll(jnp.flip(gl.reshape(groups, LONG), axis=1), 1, axis=1)
+    grad_long = turn_taps(gl.reshape(groups, LONG))
     return mixed, d_proj, grad_short, grad_long
 
 
@@ -409,11 +422,12 @@
         table[device] = [2 * ring[(place + hop) % chips] + (core ^ other) for hop, other in items]
     order = lax.dynamic_index_in_dim(jnp.asarray(table), lax.axis_index("ctx"), 0, keepdims=False)
     short_kernel, long_kernel = short_taps.reshape(3, -1, SHORT), long_taps.reshape(-1, LONG)
+    turned_kernel = turn_taps(long_kernel)
 
     stay = 3 * channels
     if n_tp == 2:
         t = lax.axis_index("tp").astype(jnp.int32)
-        t, order, short_kernel, long_kernel = lax.optimization_barrier((t, order, short_kernel, long_kernel))
+        t, order, short_kernel, turned_kernel = lax.optimization_barrier((t, order, short_kernel, turned_kernel))
         flat = restack(t, weights)
     else:
         flat = jnp.stack(weights).reshape(-1, width)
@@ -459,13 +473,13 @@
     )
     shared, projected[-1] = stage((arrived, projected[-1]))
     last, far = project([arrived, swap(shared[: held // 2]), swap(shared[held // 2 :])])
-    far, crossed = stage((far, crossed))
     projected += [(near, crossed), (last, across(far))]
 
     mixed, d_proj, grad_short, grad_long = mix(
         order,
         short_kernel,
         long_kernel,
+        turned_kernel,
         incoming,
         [[y.reshape(3, channels, -1) for y in side] for side in zip(*projected) if side[0] is not None],
         [[s] for s in range(half + 1)],

time: 283 us -> 282 us (level)
  waiting for transfers between devices: 99 us -> 95.2 us
    ppermute x10, waiting for transfers between devices: 54.7 us -> 51.7 us  [one_way(): return lax.ppermute(x, 'ctx', hops)]
  transfers between devices with their start and end apart: 39 -> 39, of which waited for: 26 -> 27; matrix products, arithmetic and copies ran while one was open for 2% -> 2% of each run, Pallas kernels for 26% -> 26%
where the time goes in v8:
time: 282 us; the launch traced here: 281 us
  Pallas kernels  98.2 us (35%)
  waiting for transfers between devices  95.2 us (34%)
  starting transfers between devices  53.4 us (19%)
  local copies, waits for them, and re-layouts  31.4 us (11%)
    ppermute x10, waiting for transfers between devices, one_way(): return lax.ppermute(x, 'ctx', hops)  51.7 us
    pallas_call x5, Pallas kernels, unproject_kernel(): pl.pallas_call(unproject_body, grid=(width // tile,), in_specs=[pl.BlockS...  37.2 us
    ppermute x10, waiting for transfers between devices, across(): return None if x is None else lax.ppermute(x, 'tp', [(0, 1), (1, 0)])  32.3 us
    pallas_call x5, Pallas kernels, project_kernel(): pl.pallas_call(functools.partial(project_body, len(pieces)), grid=(4,), i...  32 us
    unnamed x57, local copies, waits for them, and re-layouts  28.8 us
    pallas_call x1, Pallas kernels, mix(): pl.pallas_call(functools.partial(mix_body, count, sets, per_turn, grouped...  16.6 us
    ppermute x10, starting transfers between devices, one_way(): return lax.ppermute(x, 'ctx', hops)  14.2 us
    ppermute x17, starting transfers between devices, swap(): return lax.ppermute(x, 'ctx', [(d, d ^ 1) for d in range(n_ctx)])  13.4 us
  transfers between devices with their start and end apart: 39, of which 27 were waited for; matrix products, arithmetic and copies ran while one was open for 2% of the time, Pallas kernels for 26%

profile of v8, /device:TPU:1, one launch (start us, length us, event | category | flops | bytes accessed | tf_op | source)
XLA Modules:
  0.0 281.3 jit_solution(807383780801418685)
XLA Ops:
  0.8 2.7 collective-permute-start.1
  8.3 2.2 copy-done.4
  10.4 2.2 copy-done.5
  12.6 2.2 copy-done.6
  14.8 1.7 shard_map.111
  16.6 4.3 %shard_map.112 = (bf16[768,256]{1,0:T(8,128)(2,1)S(1)}, bf16[768,256]{1,0:T(8,128)(2,1)S(1)}) custom-call(bf16[128,4096]{1,0:T(8,128)(2,1)S(1)} %copy-done.7, bf16[128,4096]{1,0:T(8,128)(2,1)S(1)} %collective-permute-done.2.refs_1_, bf16[1536,4096]{1,0:T(8,128)(2,1)S(1)} %bitcast.35), custom_call_target="tpu_custom_call" | custom-call | flops 1 | bytes 1 | tf_op jit(solution)/shard_map/pallas_call | solution.py:289
  20.9 5.6 %collective-permute-done.1 = bf16[128,4096]{1,0:T(8,128)(2,1)S(1)} collective-permute-done((bf16[128,4096]{1,0:T(8,128)(2,1)}, bf16[128,4096]{1,0:T(8,128)(2,1)S(1)}, u32[]{:S(2)}, u32[]{:S(2)}) %collective-permute-start.1) | collective-permute-done | bytes 1048608 | tf_op jit(solution)/shard_map/ppermute | solution.py:409
  28.0 1.4 collective-permute-start.3
  31.8 7.8 %shard_map.113 = (bf16[768,512]{1,0:T(8,128)(2,1)S(1)}, bf16[768,512]{1,0:T(8,128)(2,1)S(1)}) custom-call(bf16[256,4096]{1,0:T(8,128)(2,1)S(1)} %constant_dynamic-update-slice_fusion.refs_0_, bf16[256,4096]{1,0:T(8,128)(2,1)S(1)} %collective-permute-done.4.refs_1_, bf16[1536,4096]{1,0:T(8,128)(2,1)S(1)} %bitcast.36), custom_call_target="tpu_custom_call" | custom-call | flops 1 | bytes 1 | tf_op jit(solution)/shard_map/pallas_call | solution.py:289
  40.4 12.7 %collective-permute-done.3.refs_0_ = bf16[256,4096]{1,0:T(8,128)(2,1)S(1)} collective-permute-done((bf16[256,4096]{1,0:T(8,128)(2,1)S(1)}, bf16[256,4096]{1,0:T(8,128)(2,1)S(1)}, u32[]{:S(2)}, u32[]{:S(2)}) %collective-permute-start.3) | collective-permute-done | bytes 2097184 | tf_op jit(solution)/shard_map/ppermute | solution.py:409
  58.0 7.8 %shard_map.114 = (bf16[768,512]{1,0:T(8,128)(2,1)S(1)}, bf16[768,512]{1,0:T(8,128)(2,1)S(1)}) custom-call(bf16[256,4096]{1,0:T(8,128)(2,1)S(1)} %collective-permute-done.3.refs_0_, bf16[256,4096]{1,0:T(8,128)(2,1)S(1)} %collective-permute-done.7.refs_1_, bf16[1536,4096]{1,0:T(8,128)(2,1)S(1)} %bitcast.37), custom_call_target="tpu_custom_call" | custom-call | flops 1 | bytes 1 | tf_op jit(solution)/shard_map/pallas_call | solution.py:289
  65.7 8.2 %collective-permute-done.8 = bf16[768,512]{1,0:T(8,128)(2,1)S(1)} collective-permute-done((bf16[768,512]{1,0:T(8,128)(2,1)S(1)}, bf16[768,512]{1,0:T(8,128)(2,1)S(1)}, u32[]{:S(2)}, u32[]{:S(2)}) %collective-permute-start.8) | collective-permute-done | bytes 786464 | tf_op jit(solution)/shard_map/ppermute | solution.py:442
  74.0 5.7 %collective-permute-done.6.refs_0_ = bf16[256,4096]{1,0:T(8,128)(2,1)S(1)} collective-permute-done((bf16[256,4096]{1,0:T(8,128)(2,1)S(1)}, bf16[256,4096]{1,0:T(8,128)(2,1)S(1)}, u32[]{:S(2)}, u32[]{:S(2)}) %collective-permute-start.6) | collective-permute-done | bytes 2097184 | tf_op jit(solution)/shard_map/ppermute | solution.py:409
  80.3 1.4 collective-permute-start.9
  84.0 7.8 %shard_map.115 = (bf16[768,512]{1,0:T(8,128)(2,1)S(1)}, bf16[768,512]{1,0:T(8,128)(2,1)S(1)}) custom-call(bf16[256,4096]{1,0:T(8,128)(2,1)S(1)} %collective-permute-done.6.refs_0_, bf16[256,4096]{1,0:T(8,128)(2,1)S(1)} %collective-permute-done.10.refs_1_, bf16[1536,4096]{1,0:T(8,128)(2,1)S(1)} %bitcast.38), custom_call_target="tpu_custom_call" | custom-call | flops 1 | bytes 1 | tf_op jit(solution)/shard_map/pallas_call | solution.py:289
  92.7 2.0 collective-permute-done.9.refs_0_
  94.7 6.4 %all-to-all-start = ((bf16[16,256,128]{2,1,0:T(8,128)(2,1)}), bf16[16,256,128]{2,1,0:T(8,128)(2,1)}, u32[]{:S(2)}, u32[]{:S(2)}) async-start(bf16[16,256,128]{2,1,0:T(8,128)(2,1)} %bitcast.61), calls=%async_computation | async-start | bytes 2097152 | tf_op jit(solution)/shard_map/all_to_all | solution.py:471
  104.2 4.6 %copy-done.1 = bf16[2,3,256,4096]{3,2,1,0:T(8,128)(2,1)S(1)} copy-done((bf16[2,3,256,4096]{3,2,1,0:T(8,128)(2,1)S(1)}, bf16[2,3,256,4096]{3,2,1,0:T(8,128)(2,1)}, u32[]{:S(2)}) %copy-start.1) | copy-done | bytes 12582936
  108.8 4.3 %shard_map.116 = (bf16[768,256]{1,0:T(8,128)(2,1)S(1)}, bf16[768,256]{1,0:T(8,128)(2,1)S(1)}) custom-call(bf16[128,4096]{1,0:T(8,128)(2,1)S(1)} %collective-permute-done.9.refs_0_, bf16[64,4096]{1,0:T(8,128)(2,1)S(1)} %collective-permute-done.12.refs_1_, bf16[64,4096]{1,0:T(8,128)(2,1)S(1)} %collective-permute-done.13.refs_2_, bf16[1536,4096]{1,0:T(8,128)(2,1)S(1)} %bitcast.39), custom_call_target="tpu_custom_call" | custom-call | flops 1 | bytes 1 | tf_op jit(solution)/shard_map/pallas_call | solution.py:289
  115.1 5.6 %collective-permute-done.14 = bf16[768,512]{1,0:T(8,128)(2,1)S(1)} collective-permute-done((bf16[768,512]{1,0:T(8,128)(2,1)S(1)}, bf16[768,512]{1,0:T(8,128)(2,1)S(1)}, u32[]{:S(2)}, u32[]{:S(2)}) %collective-permute-start.14) | collective-permute-done | bytes 786464 | tf_op jit(solution)/shard_map/ppermute | solution.py:442
  120.7 8.4 %collective-permute-done.15 = bf16[768,256]{1,0:T(8,128)(2,1)S(1)} collective-permute-done((bf16[768,256]{1,0:T(8,128)(2,1)S(1)}, bf16[768,256]{1,0:T(8,128)(2,1)S(1)}, u32[]{:S(2)}, u32[]{:S(2)}) %collective-permute-start.15) | collective-permute-done | bytes 393248 | tf_op jit(solution)/shard_map/ppermute | solution.py:442
  129.9 16.6 %shard_map.117 = (bf16[16,256,128]{2,1,0:T(8,128)(2,1)}, bf16[3,256,256]{2,1,0:T(8,128)(2,1)}, bf16[3,256,512]{2,1,0:T(8,128)(2,1)}, bf16[3,256,512]{2,1,0:T(8,1...) custom-call(s32[16]{0:T(128)} %dynamic-slice_bitcast_fusion.order, ...), custom_call_target="tpu_custom_call" | custom-call | flops 1 | bytes 1 | tf_op jit(solution)/shard_map/pallas_call | solution.py:188
  147.8 7.0 %all-to-all-start.1 = ((bf16[16,256,128]{2,1,0:T(8,128)(2,1)}), bf16[16,256,128]{2,1,0:T(8,128)(2,1)S(1)}, u32[]{:S(2)}, u32[]{:S(2)}) async-start(bf16[16,256,128]{2,1,0:T(8,128)(2,1)} %get-tuple-element.148), calls=%async_computation.1 | async-start | bytes 2097152 | tf_op jit(solution)/shard_map/all_to_all | solution.py:489
  156.1 4.6 %copy-done.2 = bf16[2,3,256,4096]{3,2,1,0:T(8,128)(2,1)S(1)} copy-done((bf16[2,3,256,4096]{3,2,1,0:T(8,128)(2,1)S(1)}, bf16[2,3,256,4096]{3,2,1,0:T(8,128)(2,1)}, u32[]{:S(2)}) %copy-start.2) | copy-done | bytes 12582936
  160.7 5.2 %shard_map.118 = (bf16[128,4096]{1,0:T(8,128)(2,1)S(1)}, bf16[80,4096]{1,0:T(8,128)(2,1)S(1)}, bf16[48,4096]{1,0:T(8,128)(2,1)S(1)}) custom-call(bf16[768,256]{1,0:T(8,128)(2,1)S(1)} %bitcast.59, bf16[768,256]{1,0:T(8,128)(2,1)S(1)} %collective-permute-done.16.far_ref, bf16[1536,4096]{1,0:T(8,128)(2,1)S(1)} %bitcast.40), custom_call_target="tpu_custom_call" | custom-call | flops 1 | bytes 1 | tf_op jit(solution)/shard_map/pallas_call | solution.py:326
  165.9 2.6 collective-permute-start.17
  168.6 2.1 collective-permute-start.22
  171.4 3.2 %collective-permute-done.19.far_ref = bf16[768,512]{1,0:T(8,128)(2,1)S(1)} collective-permute-done((bf16[768,512]{1,0:T(8,128)(2,1)S(1)}, bf16[768,512]{1,0:T(8,128)(2,1)S(1)}, u32[]{:S(2)}, u32[]{:S(2)}) %collective-permute-start.19) | collective-permute-done | bytes 786464 | tf_op jit(solution)/shard_map/ppermute | solution.py:442
  175.4 8.7 %shard_map.120 = (bf16[256,4096]{1,0:T(8,128)(2,1)S(1)}, bf16[96,4096]{1,0:T(8,128)(2,1)S(1)}, bf16[96,4096]{1,0:T(8,128)(2,1)S(1)}, bf16[64,4096]{1,0:T(8,128)(2,1)S(1)}) custom-call(bf16[768,512]{1,0:T(8,128)(2,1)S(1)} %bitcast.54, bf16[768,512]{1,0:T(8,128)(2,1)S(1)} %collective-permute-done.19.far_ref, bf16[1536,4096]{1,0:T(8,128)(2,1)S(1)} %bitcast.41), custom_call_target="tpu_custom_call" | custom-call | flops 1 | bytes 1 | tf_op jit(solution)/shard_map/pallas_call | solution.py:326
  184.2 1.9 collective-permute-start.20
  186.2 5.2 %collective-permute-done.22.far_ref = bf16[768,512]{1,0:T(8,128)(2,1)S(1)} collective-permute-done((bf16[768,512]{1,0:T(8,128)(2,1)S(1)}, bf16[768,512]{1,0:T(8,128)(2,1)S(1)}, u32[]{:S(2)}, u32[]{:S(2)}) %collective-permute-start.22) | collective-permute-done | bytes 786464 | tf_op jit(solution)/shard_map/ppermute | solution.py:442
  192.9 1.5 collective-permute-done.23.refs_3_
  198.2 4.6 %copy-done.3 = bf16[2,3,256,4096]{3,2,1,0:T(8,128)(2,1)S(1)} copy-done((bf16[2,3,256,4096]{3,2,1,0:T(8,128)(2,1)S(1)}, bf16[2,3,256,4096]{3,2,1,0:T(8,128)(2,1)}, u32[]{:S(2)}) %copy-start.3) | copy-done | bytes 12582936
  205.1 8.7 %shard_map.122 = (bf16[256,4096]{1,0:T(8,128)(2,1)S(1)}, bf16[128,4096]{1,0:T(8,128)(2,1)S(1)}, bf16[128,4096]{1,0:T(8,128)(2,1)S(1)}) custom-call(bf16[768,512]{1,0:T(8,128)(2,1)S(1)} %bitcast.49, bf16[768,512]{1,0:T(8,128)(2,1)S(1)} %copy-done.14, bf16[1536,4096]{1,0:T(8,128)(2,1)S(1)} %bitcast.42), custom_call_target="tpu_custom_call" | custom-call | flops 1 | bytes 1 | tf_op jit(solution)/shard_map/pallas_call | solution.py:326
  215.6 1.5 collective-permute-start.27
  217.2 1.5 shard_map.124
  219.5 1.5 collective-permute-done.28.refs_3_
  224.9 8.7 %shard_map.125 = (bf16[256,4096]{1,0:T(8,128)(2,1)S(1)}, bf16[128,4096]{1,0:T(8,128)(2,1)S(1)}, bf16[128,4096]{1,0:T(8,128)(2,1)S(1)}) custom-call(bf16[768,512]{1,0:T(8,128)(2,1)S(1)} %bitcast.47, bf16[768,512]{1,0:T(8,128)(2,1)S(1)} %collective-permute-done.26.far_ref, bf16[1536,4096]{1,0:T(8,128)(2,1)S(1)} %bitcast.43), custom_call_target="tpu_custom_call" | custom-call | flops 1 | bytes 1 | tf_op jit(solution)/shard_map/pallas_call | solution.py:326
  233.6 1.9 collective-permute-start.29
  235.7 2.2 collective-permute-done.29.refs_1_
  237.9 1.5 collective-permute-done.31.refs_2_
  239.4 8.2 %collective-permute-done.32.refs_3_ = bf16[256,4096]{1,0:T(8,128)(2,1)S(1)} collective-permute-done((bf16[256,4096]{1,0:T(8,128)(2,1)S(1)}, bf16[256,4096]{1,0:T(8,128)(2,1)S(1)}, u32[]{:S(2)}, u32[]{:S(2)}) %collective-permute-start.32) | collective-permute-done | bytes 2097184 | tf_op jit(solution)/shard_map/ppermute | solution.py:409
  247.6 2.4 shard_map.126
  251.2 2.5 collective-permute-start.36
  253.7 5.8 %shard_map.127 = (bf16[128,4096]{1,0:T(8,128)(2,1)S(1)}, bf16[64,4096]{1,0:T(8,128)(2,1)}, bf16[64,4096]{1,0:T(8,128)(2,1)}) custom-call(bf16[768,256]{1,0:T(8,128)(2,1)S(1)} %bitcast.56, bf16[768,256]{1,0:T(8,128)(2,1)S(1)} %collective-permute-done.30.far_ref, bf16[1536,4096]{1,0:T(8,128)(2,1)S(1)} %bitcast.44), custom_call_target="tpu_custom_call" | custom-call | flops 1 | bytes 1 | tf_op jit(solution)/shard_map/pallas_call | solution.py:326
  262.5 1.6 collective-permute-done.35.refs_3_
  264.1 13.5 %collective-permute-done.36.refs_4_ = bf16[128,4096]{1,0:T(8,128)(2,1)S(1)} collective-permute-done((bf16[128,4096]{1,0:T(8,128)(2,1)}, bf16[128,4096]{1,0:T(8,128)(2,1)S(1)}, u32[]{:S(2)}, u32[]{:S(2)}) %collective-permute-start.36) | collective-permute-done | bytes 1048608 | tf_op jit(solution)/shard_map/ppermute | solution.py:409
  277.6 3.7 %shard_map.128 = bf16[128,4096]{1,0:T(8,128)(2,1)} custom-call(bf16[128,4096]{1,0:T(8,128)(2,1)S(1)} %get-tuple-element.177.refs_0_, bf16[64,4096]{1,0:T(8,128)(2,1)} %collective-permute-done.33.refs_1_, bf16[64,4096]{1,0:T(8,128)(2,1)} %collective-permute-done.34.refs_2_, bf16[128,4096]{1,0:T(8,128)(2,1)S(1)} %collective-permute-done.35.refs_3_, ...), custom_call_target="tpu_custom_call" | custom-call | flops 1 | bytes 1 | tf_op jit(solution)/shard_map/pallas_call | solution.py:366
  (118 shorter events, 46.7 us)
Async XLA Ops:
  0.6 15.9 %collective-permute-start.2 = (bf16[128,4096]{1,0:T(8,128)(2,1)}, bf16[128,4096]{1,0:T(8,128)(2,1)S(1)}, u32[]{:S(2)}, u32[]{:S(2)}) collective-permute-start(bf16[128,4096]{1,0:T(8,128)(2,1)} %refs_0_.3), channel_id=1, source_target_pairs={{0,2},{2,0},{4,6},{6,4},{8,10},{10,8},{12,14},{14,12},{16,18},{18,... | collective-permute-start | bytes 3145736 | tf_op jit(solution)/shard_map/ppermute | solution.py:412
  0.8 25.7 %collective-permute-start.1 = (bf16[128,4096]{1,0:T(8,128)(2,1)}, bf16[128,4096]{1,0:T(8,128)(2,1)S(1)}, u32[]{:S(2)}, u32[]{:S(2)}) collective-permute-start(bf16[128,4096]{1,0:T(8,128)(2,1)} %refs_0_.3), channel_id=1, source_target_pairs={{0,6},{2,8},{8,2},{10,16},{16,10},{18,24},{24,18},{26,28},{28,26},... | collective-permute-start | bytes 3145736 | tf_op jit(solution)/shard_map/ppermute | solution.py:409
  3.5 23.9 %collective-permute-start = (bf16[128,4096]{1,0:T(8,128)(2,1)}, bf16[128,4096]{1,0:T(8,128)(2,1)S(1)}, u32[]{:S(2)}, u32[]{:S(2)}) collective-permute-start(bf16[128,4096]{1,0:T(8,128)(2,1)} %refs_0_.3), channel_id=1, source_target_pairs={{0,8},{2,6},{8,16},{10,2},{16,24},{18,10},{24,28},{26,18},{28,20},... | collective-permute-start | bytes 3145736 | tf_op jit(solution)/shard_map/ppermute | solution.py:409
  16.5 67.5 %copy-start = (bf16[2,3,256,4096]{3,2,1,0:T(8,128)(2,1)}, bf16[2,3,256,4096]{3,2,1,0:T(8,128)(2,1)S(1)}, u32[]{:S(2)}) copy-start(bf16[2,3,256,4096]{3,2,1,0:T(8,128)(2,1)S(1)} %shard_map.111) | copy-start | bytes 37748740
  27.6 4.2 %collective-permute-start.4 = (bf16[256,4096]{1,0:T(8,128)(2,1)S(1)}, bf16[256,4096]{1,0:T(8,128)(2,1)S(1)}, u32[]{:S(2)}, u32[]{:S(2)}) collective-permute-start(bf16[256,4096]{1,0:T(8,128)(2,1)S(1)} %constant_dynamic-update-slice_fusion.refs_0_), channel_id=1, source_target_pairs={{0,2},{2,0},{4,6},{6,4},{8,10},{10,8},{12,14},{14,12},{16,18},{18,... | collective-permute-start | bytes 6291464 | tf_op jit(solution)/shard_map/ppermute | solution.py:412
  28.0 25.2 %collective-permute-start.3 = (bf16[256,4096]{1,0:T(8,128)(2,1)S(1)}, bf16[256,4096]{1,0:T(8,128)(2,1)S(1)}, u32[]{:S(2)}, u32[]{:S(2)}) collective-permute-start(bf16[256,4096]{1,0:T(8,128)(2,1)S(1)} %constant_dynamic-update-slice_fusion.refs_0_), channel_id=1, source_target_pairs={{0,8},{2,6},{8,16},{10,2},{16,24},{18,10},{24,28},{26,18},{28,20},... | collective-permute-start | bytes 6291464 | tf_op jit(solution)/shard_map/ppermute | solution.py:409
  29.4 11.1 %collective-permute-start.5 = (bf16[768,256]{1,0:T(8,128)(2,1)S(1)}, bf16[768,256]{1,0:T(8,128)(2,1)S(1)}, u32[]{:S(2)}, u32[]{:S(2)}) collective-permute-start(bf16[768,256]{1,0:T(8,128)(2,1)S(1)} %get-tuple-element.105), channel_id=1, source_target_pairs={{0,1},{1,0},{2,3},{3,2},{4,5},{5,4},{6,7},{7,6},{8,9},{9,8},{10,11... | collective-permute-start | bytes 1179656 | tf_op jit(solution)/shard_map/ppermute | solution.py:442
  40.4 16.3 %copy-start.23 = (bf16[768,256]{1,0:T(8,128)(2,1)}, bf16[768,256]{1,0:T(8,128)(2,1)S(1)}, u32[]{:S(2)}) copy-start(bf16[768,256]{1,0:T(8,128)(2,1)S(1)} %collective-permute-done.5) | copy-start | bytes 1179652
  53.2 4.8 %collective-permute-start.7 = (bf16[256,4096]{1,0:T(8,128)(2,1)S(1)}, bf16[256,4096]{1,0:T(8,128)(2,1)S(1)}, u32[]{:S(2)}, u32[]{:S(2)}) collective-permute-start(bf16[256,4096]{1,0:T(8,128)(2,1)S(1)} %collective-permute-done.3.refs_0_), channel_id=1, source_target_pairs={{0,2},{2,0},{4,6},{6,4},{8,10},{10,8},{12,14},{14,12},{16,18},{18,... | collective-permute-start | bytes 6291464 | tf_op jit(solution)/shard_map/ppermute | solution.py:412
  54.2 25.5 %collective-permute-start.6 = (bf16[256,4096]{1,0:T(8,128)(2,1)S(1)}, bf16[256,4096]{1,0:T(8,128)(2,1)S(1)}, u32[]{:S(2)}, u32[]{:S(2)}) collective-permute-start(bf16[256,4096]{1,0:T(8,128)(2,1)S(1)} %collective-permute-done.3.refs_0_), channel_id=1, source_target_pairs={{0,8},{2,6},{8,16},{10,2},{16,24},{18,10},{24,28},{26,18},{28,20},... | collective-permute-start | bytes 6291464 | tf_op jit(solution)/shard_map/ppermute | solution.py:409
  55.5 18.4 %collective-permute-start.8 = (bf16[768,512]{1,0:T(8,128)(2,1)S(1)}, bf16[768,512]{1,0:T(8,128)(2,1)S(1)}, u32[]{:S(2)}, u32[]{:S(2)}) collective-permute-start(bf16[768,512]{1,0:T(8,128)(2,1)S(1)} %get-tuple-element.110), channel_id=1, source_target_pairs={{0,1},{1,0},{2,3},{3,2},{4,5},{5,4},{6,7},{7,6},{8,9},{9,8},{10,11... | collective-permute-start | bytes 2359304 | tf_op jit(solution)/shard_map/ppermute | solution.py:442
  65.7 26.0 %copy-start.12 = (bf16[768,512]{1,0:T(8,128)(2,1)}, bf16[768,512]{1,0:T(8,128)(2,1)S(1)}, u32[]{:S(2)}) copy-start(bf16[768,512]{1,0:T(8,128)(2,1)S(1)} %get-tuple-element.119) | copy-start | bytes 2359300
  74.0 17.8 %copy-start.21 = (bf16[768,512]{1,0:T(8,128)(2,1)}, bf16[768,512]{1,0:T(8,128)(2,1)S(1)}, u32[]{:S(2)}) copy-start(bf16[768,512]{1,0:T(8,128)(2,1)S(1)} %collective-permute-done.8) | copy-start | bytes 2359300
  79.7 4.3 %collective-permute-start.10 = (bf16[256,4096]{1,0:T(8,128)(2,1)S(1)}, bf16[256,4096]{1,0:T(8,128)(2,1)S(1)}, u32[]{:S(2)}, u32[]{:S(2)}) collective-permute-start(bf16[256,4096]{1,0:T(8,128)(2,1)S(1)} %collective-permute-done.6.refs_0_), channel_id=1, source_target_pairs={{0,2},{2,0},{4,6},{6,4},{8,10},{10,8},{12,14},{14,12},{16,18},{18,... | collective-permute-start | bytes 6291464 | tf_op jit(solution)/shard_map/ppermute | solution.py:412
  80.3 14.4 %collective-permute-start.9 = (bf16[128,4096]{1,0:T(8,128)(2,1)S(1)}, bf16[128,4096]{1,0:T(8,128)(2,1)S(1)}, u32[]{:S(2)}, u32[]{:S(2)}) collective-permute-start(bf16[128,4096]{1,0:T(8,128)(2,1)S(1)} %slice.34), channel_id=1, source_target_pairs={{0,8},{2,6},{8,16},{10,2},{16,24},{18,10},{24,28},{26,18},{28,20},... | collective-permute-start | bytes 3145736 | tf_op jit(solution)/shard_map/ppermute | solution.py:409
  81.7 19.4 %collective-permute-start.11 = (bf16[768,512]{1,0:T(8,128)(2,1)S(1)}, bf16[768,512]{1,0:T(8,128)(2,1)}, u32[]{:S(2)}, u32[]{:S(2)}) collective-permute-start(bf16[768,512]{1,0:T(8,128)(2,1)S(1)} %get-tuple-element.118), channel_id=1, source_target_pairs={{0,1},{1,0},{2,3},{3,2},{4,5},{5,4},{6,7},{7,6},{8,9},{9,8},{10,11... | collective-permute-start | bytes 2359304 | tf_op jit(solution)/shard_map/ppermute | solution.py:442
  94.7 34.4 %all-to-all-start = ((bf16[16,256,128]{2,1,0:T(8,128)(2,1)}), bf16[16,256,128]{2,1,0:T(8,128)(2,1)}, u32[]{:S(2)}, u32[]{:S(2)}) async-start(bf16[16,256,128]{2,1,0:T(8,128)(2,1)} %bitcast.61), calls=%async_computation | async-start | bytes 2097152 | tf_op jit(solution)/shard_map/all_to_all | solution.py:471
  101.2 2.2 collective-permute-start.13
  101.9 2.3 collective-permute-start.12
  102.0 18.7 %collective-permute-start.14 = (bf16[768,512]{1,0:T(8,128)(2,1)S(1)}, bf16[768,512]{1,0:T(8,128)(2,1)S(1)}, u32[]{:S(2)}, u32[]{:S(2)}) collective-permute-start(bf16[768,512]{1,0:T(8,128)(2,1)S(1)} %get-tuple-element.126), channel_id=1, source_target_pairs={{0,1},{1,0},{2,3},{3,2},{4,5},{5,4},{6,7},{7,6},{8,9},{9,8},{10,11... | collective-permute-start | bytes 2359304 | tf_op jit(solution)/shard_map/ppermute | solution.py:442
  113.9 15.2 %collective-permute-start.15 = (bf16[768,256]{1,0:T(8,128)(2,1)S(1)}, bf16[768,256]{1,0:T(8,128)(2,1)S(1)}, u32[]{:S(2)}, u32[]{:S(2)}) collective-permute-start(bf16[768,256]{1,0:T(8,128)(2,1)S(1)} %get-tuple-element.127), channel_id=1, source_target_pairs={{0,1},{1,0},{2,3},{3,2},{4,5},{5,4},{6,7},{7,6},{8,9},{9,8},{10,11... | collective-permute-start | bytes 1179656 | tf_op jit(solution)/shard_map/ppermute | solution.py:442
  120.7 8.4 %copy-start.22 = (bf16[768,512]{1,0:T(8,128)(2,1)}, bf16[768,512]{1,0:T(8,128)(2,1)S(1)}, u32[]{:S(2)}) copy-start(bf16[768,512]{1,0:T(8,128)(2,1)S(1)} %collective-permute-done.14) | copy-start | bytes 2359300
  146.5 8.3 %copy-start.16 = (bf16[3,256,512]{2,1,0:T(8,128)(2,1)S(1)}, bf16[3,256,512]{2,1,0:T(8,128)(2,1)}, u32[]{:S(2)}) copy-start(bf16[3,256,512]{2,1,0:T(8,128)(2,1)} %get-tuple-element.132) | copy-start | bytes 2359300
  146.5 9.6 %copy-start.19 = (bf16[3,256,256]{2,1,0:T(8,128)(2,1)S(1)}, bf16[3,256,256]{2,1,0:T(8,128)(2,1)}, u32[]{:S(2)}) copy-start(bf16[3,256,256]{2,1,0:T(8,128)(2,1)} %get-tuple-element.128) | copy-start | bytes 1179652
  146.5 9.6 %collective-permute-start.16 = (bf16[768,256]{1,0:T(8,128)(2,1)}, bf16[768,256]{1,0:T(8,128)(2,1)S(1)}, u32[]{:S(2)}, u32[]{:S(2)}) collective-permute-start(bf16[768,256]{1,0:T(8,128)(2,1)} %bitcast.58), channel_id=1, source_target_pairs={{0,1},{1,0},{2,3},{3,2},{4,5},{5,4},{6,7},{7,6},{8,9},{9,8},{10,11... | collective-permute-start | bytes 1179656 | tf_op jit(solution)/shard_map/ppermute | solution.py:442
  147.8 47.9 %all-to-all-start.1 = ((bf16[16,256,128]{2,1,0:T(8,128)(2,1)}), bf16[16,256,128]{2,1,0:T(8,128)(2,1)S(1)}, u32[]{:S(2)}, u32[]{:S(2)}) async-start(bf16[16,256,128]{2,1,0:T(8,128)(2,1)} %get-tuple-element.148), calls=%async_computation.1 | async-start | bytes 2097152 | tf_op jit(solution)/shard_map/all_to_all | solution.py:489
  154.8 19.7 %collective-permute-start.19 = (bf16[768,512]{1,0:T(8,128)(2,1)S(1)}, bf16[768,512]{1,0:T(8,128)(2,1)S(1)}, u32[]{:S(2)}, u32[]{:S(2)}) collective-permute-start(bf16[768,512]{1,0:T(8,128)(2,1)S(1)} %bitcast.53), channel_id=1, source_target_pairs={{0,1},{1,0},{2,3},{3,2},{4,5},{5,4},{6,7},{7,6},{8,9},{9,8},{10,11... | collective-permute-start | bytes 2359304 | tf_op jit(solution)/shard_map/ppermute | solution.py:442
  165.9 4.9 %collective-permute-start.17 = (bf16[80,4096]{1,0:T(8,128)(2,1)S(1)}, bf16[80,4096]{1,0:T(8,128)(2,1)S(1)}, u32[]{:S(2)}, u32[]{:S(2)}) collective-permute-start(bf16[80,4096]{1,0:T(8,128)(2,1)S(1)} %get-tuple-element.130), channel_id=1, source_target_pairs={{0,2},{2,0},{4,6},{6,4},{8,10},{10,8},{12,14},{14,12},{16,18},{18,... | collective-permute-start | bytes 1966088 | tf_op jit(solution)/shard_map/ppermute | solution.py:412
  168.5 2.3 collective-permute-start.18
  168.6 22.8 %collective-permute-start.22 = (bf16[768,512]{1,0:T(8,128)(2,1)S(1)}, bf16[768,512]{1,0:T(8,128)(2,1)S(1)}, u32[]{:S(2)}, u32[]{:S(2)}) collective-permute-start(bf16[768,512]{1,0:T(8,128)(2,1)S(1)} %bitcast.48), channel_id=1, source_target_pairs={{0,1},{1,0},{2,3},{3,2},{4,5},{5,4},{6,7},{7,6},{8,9},{9,8},{10,11... | collective-permute-start | bytes 2359304 | tf_op jit(solution)/shard_map/ppermute | solution.py:442
  174.5 19.9 %collective-permute-start.24 = (bf16[128,4096]{1,0:T(8,128)(2,1)S(1)}, bf16[128,4096]{1,0:T(8,128)(2,1)S(1)}, u32[]{:S(2)}, u32[]{:S(2)}) collective-permute-start(bf16[128,4096]{1,0:T(8,128)(2,1)S(1)} %shard_map.119), channel_id=1, source_target_pairs={{0,4},{2,10},{8,0},{10,18},{16,8},{18,26},{24,16},{26,30},{28,24},... | collective-permute-start | bytes 3145736 | tf_op jit(solution)/shard_map/ppermute | solution.py:409
  184.2 10.3 %collective-permute-start.20 = (bf16[96,4096]{1,0:T(8,128)(2,1)S(1)}, bf16[96,4096]{1,0:T(8,128)(2,1)S(1)}, u32[]{:S(2)}, u32[]{:S(2)}) collective-permute-start(bf16[96,4096]{1,0:T(8,128)(2,1)S(1)} %get-tuple-element.138), channel_id=1, source_target_pairs={{0,2},{2,0},{4,6},{6,4},{8,10},{10,8},{12,14},{14,12},{16,18},{18,... | collective-permute-start | bytes 2359304 | tf_op jit(solution)/shard_map/ppermute | solution.py:412
  186.1 8.3 %collective-permute-start.21 = (bf16[96,4096]{1,0:T(8,128)(2,1)S(1)}, bf16[96,4096]{1,0:T(8,128)(2,1)S(1)}, u32[]{:S(2)}, u32[]{:S(2)}) collective-permute-start(bf16[96,4096]{1,0:T(8,128)(2,1)S(1)} %get-tuple-element.139), channel_id=1, source_target_pairs={{0,2},{2,0},{4,6},{6,4},{8,10},{10,8},{12,14},{14,12},{16,18},{18,... | collective-permute-start | bytes 2359304 | tf_op jit(solution)/shard_map/ppermute | solution.py:412
  192.3 2.2 collective-permute-start.23
  195.7 25.2 %collective-permute-start.28 = (bf16[256,4096]{1,0:T(8,128)(2,1)S(1)}, bf16[256,4096]{1,0:T(8,128)(2,1)S(1)}, u32[]{:S(2)}, u32[]{:S(2)}) collective-permute-start(bf16[256,4096]{1,0:T(8,128)(2,1)S(1)} %shard_map.121), channel_id=1, source_target_pairs={{0,4},{2,10},{8,0},{10,18},{16,8},{18,26},{24,16},{26,30},{28,24},... | collective-permute-start | bytes 6291464 | tf_op jit(solution)/shard_map/ppermute | solution.py:409
  197.0 18.6 %collective-permute-start.26 = (bf16[768,512]{1,0:T(8,128)(2,1)}, bf16[768,512]{1,0:T(8,128)(2,1)S(1)}, u32[]{:S(2)}, u32[]{:S(2)}) collective-permute-start(bf16[768,512]{1,0:T(8,128)(2,1)} %bitcast.46), channel_id=1, source_target_pairs={{0,1},{1,0},{2,3},{3,2},{4,5},{5,4},{6,7},{7,6},{8,9},{9,8},{10,11... | collective-permute-start | bytes 2359304 | tf_op jit(solution)/shard_map/ppermute | solution.py:442
  213.8 4.9 %collective-permute-start.25 = (bf16[128,4096]{1,0:T(8,128)(2,1)S(1)}, bf16[128,4096]{1,0:T(8,128)(2,1)S(1)}, u32[]{:S(2)}, u32[]{:S(2)}) collective-permute-start(bf16[128,4096]{1,0:T(8,128)(2,1)S(1)} %get-tuple-element.152), channel_id=1, source_target_pairs={{0,2},{2,0},{4,6},{6,4},{8,10},{10,8},{12,14},{14,12},{16,18},{18,... | collective-permute-start | bytes 3145736 | tf_op jit(solution)/shard_map/ppermute | solution.py:412
  215.6 3.8 %collective-permute-start.27 = (bf16[128,4096]{1,0:T(8,128)(2,1)S(1)}, bf16[128,4096]{1,0:T(8,128)(2,1)S(1)}, u32[]{:S(2)}, u32[]{:S(2)}) collective-permute-start(bf16[128,4096]{1,0:T(8,128)(2,1)S(1)} %get-tuple-element.155), channel_id=1, source_target_pairs={{0,2},{2,0},{4,6},{6,4},{8,10},{10,8},{12,14},{14,12},{16,18},{18,... | collective-permute-start | bytes 3145736 | tf_op jit(solution)/shard_map/ppermute | solution.py:412
  222.3 25.2 %collective-permute-start.32 = (bf16[256,4096]{1,0:T(8,128)(2,1)S(1)}, bf16[256,4096]{1,0:T(8,128)(2,1)S(1)}, u32[]{:S(2)}, u32[]{:S(2)}) collective-permute-start(bf16[256,4096]{1,0:T(8,128)(2,1)S(1)} %shard_map.123), channel_id=1, source_target_pairs={{0,4},{2,10},{8,0},{10,18},{16,8},{18,26},{24,16},{26,30},{28,24},... | collective-permute-start | bytes 6291464 | tf_op jit(solution)/shard_map/ppermute | solution.py:409
  223.6 11.9 %collective-permute-start.30 = (bf16[768,256]{1,0:T(8,128)(2,1)S(1)}, bf16[768,256]{1,0:T(8,128)(2,1)S(1)}, u32[]{:S(2)}, u32[]{:S(2)}) collective-permute-start(bf16[768,256]{1,0:T(8,128)(2,1)S(1)} %bitcast.55), channel_id=1, source_target_pairs={{0,1},{1,0},{2,3},{3,2},{4,5},{5,4},{6,7},{7,6},{8,9},{9,8},{10,11... | collective-permute-start | bytes 1179656 | tf_op jit(solution)/shard_map/ppermute | solution.py:442
  233.6 4.2 %collective-permute-start.29 = (bf16[128,4096]{1,0:T(8,128)(2,1)S(1)}, bf16[128,4096]{1,0:T(8,128)(2,1)S(1)}, u32[]{:S(2)}, u32[]{:S(2)}) collective-permute-start(bf16[128,4096]{1,0:T(8,128)(2,1)S(1)} %get-tuple-element.164), channel_id=1, source_target_pairs={{0,2},{2,0},{4,6},{6,4},{8,10},{10,8},{12,14},{14,12},{16,18},{18,... | collective-permute-start | bytes 3145736 | tf_op jit(solution)/shard_map/ppermute | solution.py:412
  235.6 3.8 %collective-permute-start.31 = (bf16[128,4096]{1,0:T(8,128)(2,1)S(1)}, bf16[128,4096]{1,0:T(8,128)(2,1)S(1)}, u32[]{:S(2)}, u32[]{:S(2)}) collective-permute-start(bf16[128,4096]{1,0:T(8,128)(2,1)S(1)} %get-tuple-element.167), channel_id=1, source_target_pairs={{0,2},{2,0},{4,6},{6,4},{8,10},{10,8},{12,14},{14,12},{16,18},{18,... | collective-permute-start | bytes 3145736 | tf_op jit(solution)/shard_map/ppermute | solution.py:412
  250.0 10.0 %copy-start.26 = (f32[4,4,128]{2,1,0:T(4,128)S(1)}, f32[4,4,128]{2,1,0:T(4,128)}, u32[]{:S(2)}) copy-start(f32[4,4,128]{2,1,0:T(4,128)} %get-tuple-element.183) | copy-start | bytes 24580
  250.0 10.2 %copy-start.25 = (f32[4,4,9,128]{3,2,1,0:T(8,128)S(1)}, f32[4,4,9,128]{3,2,1,0:T(8,128)}, u32[]{:S(2)}) copy-start(f32[4,4,9,128]{3,2,1,0:T(8,128)} %get-tuple-element.182) | copy-start | bytes 221188
  250.0 14.2 %collective-permute-start.35 = (bf16[128,4096]{1,0:T(8,128)(2,1)}, bf16[128,4096]{1,0:T(8,128)(2,1)S(1)}, u32[]{:S(2)}, u32[]{:S(2)}) collective-permute-start(bf16[128,4096]{1,0:T(8,128)(2,1)} %get-tuple-element.180), channel_id=1, source_target_pairs={{0,4},{2,10},{8,0},{10,18},{16,8},{18,26},{24,16},{26,30},{28,24},... | collective-permute-start | bytes 3145736 | tf_op jit(solution)/shard_map/ppermute | solution.py:409
  251.2 26.4 %collective-permute-start.36 = (bf16[128,4096]{1,0:T(8,128)(2,1)}, bf16[128,4096]{1,0:T(8,128)(2,1)S(1)}, u32[]{:S(2)}, u32[]{:S(2)}) collective-permute-start(bf16[128,4096]{1,0:T(8,128)(2,1)} %get-tuple-element.181), channel_id=1, source_target_pairs={{0,6},{2,8},{8,2},{10,16},{16,10},{18,24},{24,18},{26,28},{28,26},... | collective-permute-start | bytes 3145736 | tf_op jit(solution)/shard_map/ppermute | solution.py:409
  259.5 2.3 collective-permute-start.33
  259.5 3.0 %collective-permute-start.34 = (bf16[64,4096]{1,0:T(8,128)(2,1)}, bf16[64,4096]{1,0:T(8,128)(2,1)}, u32[]{:S(2)}, u32[]{:S(2)}) collective-permute-start(bf16[64,4096]{1,0:T(8,128)(2,1)} %get-tuple-element.179), channel_id=1, source_target_pairs={{0,2},{2,0},{4,6},{6,4},{8,10},{10,8},{12,14},{14,12},{16,18},{18,... | collective-permute-start | bytes 1572872 | tf_op jit(solution)/shard_map/ppermute | solution.py:412
  (18 other events, 49.6 us)

commit v9 on v8

--- a/solution.py
+++ b/solution.py
@@ -48,20 +48,29 @@
     return jnp.roll(jnp.flip(taps, axis=1), 1, axis=1)
 
 
-def mix_body(count, sets, per_turn, grouped, order, short_ref, long_ref, turned_ref, g_ref, *refs):
+def shift_matrix(way):
+    at = np.arange(2 * LONG)
+    place = np.where(at < LONG, at, at - (2 * LONG if way < 0 else 0))
+    out = np.arange(LONG)
+    return np.concatenate([place[:, None] - out[None, :] == way * k for k in (1, 2)], axis=1).astype(np.float32)
+
+
+def mix_body(count, sets, per_turn, grouped, order, short_ref, long_ref, turned_ref, past_ref, next_ref, g_ref, *refs):
     proj_refs = [refs[s * count : (s + 1) * count] for s in range(sets)]
     refs = refs[sets * count :]
     d_count = len(grouped)
     mixed_ref, d_refs, gs_ref, gl_ref = refs[0], refs[1 : 1 + d_count], refs[1 + d_count], refs[2 + d_count]
-    p_s, f_s, x_s, y_s, d_s, e_s = refs[3 + d_count :]
+    p_s, m_s, f_s, x_s, y_s, q_s, d_s, e_s = refs[3 + d_count :]
     blocks = g_ref.shape[0]
     rows = blocks * GROUP
     step = pl.program_id(0)
 
     @pl.when(step == 0)
     def _():
+        p_s[:, :, 0:GROUP, :] = jnp.zeros((per_turn, 3, GROUP, LONG), BF16)
         x_s[:, 0:GROUP, :] = jnp.zeros((per_turn, GROUP, LONG), BF16)
         y_s[:, rows:, :] = jnp.zeros((per_turn, GROUP, LONG), BF16)
+        d_s[:, :, rows:, :] = jnp.zeros((per_turn, 3, GROUP, LONG), BF16)
 
     halves = [(a, h) for a in range(count) for h in range(proj_refs[0][a].shape[2] // LONG)]
     places = [(a, h, where) for where, (a, h) in enumerate(halves)]
@@ -69,7 +78,6 @@
     for b, arrays in enumerate(grouped):
         inside = [where for array in arrays for a, _, where in places if a == array]
         d_places += [(b, h, where) for h, where in enumerate(inside)]
-    lane = lax.broadcasted_iota(jnp.int32, (GROUP, LONG), 1)
     zero = jnp.zeros((GROUP, LONG), F32)
     at_block = [slice(n * GROUP, (n + 1) * GROUP) for n in range(blocks)]
     sub8 = lax.broadcasted_iota(jnp.int32, (8, LONG), 0)
@@ -87,26 +95,25 @@
             [[short_ref[i, step * per_step + lines[j], k] for k in range(SHORT)] for i in range(3)] for j in every
         ]
         for a, h, where in places:
-            at = pl.multiple_of(order[where] * GROUP, GROUP)
+            at = pl.multiple_of((order[where] + 1) * GROUP, GROUP)
             for j in every:
                 for i in range(3):
                     part = proj_refs[0][a][i, mine[j], h * LONG : (h + 1) * LONG].astype(F32)
                     for s in range(1, sets):
                         part = part + proj_refs[s][a][i, mine[j], h * LONG : (h + 1) * LONG].astype(F32)
-                    p_s[j, i, pl.ds(at, GROUP), :] = part
-
-        for j in every:
-            before = [(zero, zero)] * 3
+                    p_s[j, i, pl.ds(at, GROUP), :] = part.astype(BF16)
+
+        for j in every:
+            for i in range(3):
+                two_blocks = jnp.concatenate([p_s[j, i, GROUP:, :], p_s[j, i, :rows, :]], axis=1)
+                m_s[j, i] = dot(two_blocks, past_ref[...], ((1,), (0,))).astype(BF16)
+        for j in every:
             for at in at_block:
                 feat = []
                 for i in range(3):
-                    here = p_s[j, i, at, :]
-                    one = pltpu.roll(here, 1, 1)
-                    two = pltpu.roll(here, 2, 1)
-                    past_one = jnp.where(lane < 1, before[i][0], one)
-                    past_two = jnp.where(lane < 2, before[i][1], two)
-                    before[i] = (one, two)
-                    feat.append(taps[j][i][0] * here + taps[j][i][1] * past_one + taps[j][i][2] * past_two)
+                    here = p_s[j, i, at.stop : at.stop + GROUP, :].astype(F32)
+                    past = m_s[j, i, at, :].astype(F32)
+                    feat.append(taps[j][i][0] * here + taps[j][i][1] * past[:, :LONG] + taps[j][i][2] * past[:, LONG:])
                     f_s[j, i, at, :] = feat[i]
                 x_s[j, at.stop : at.stop + GROUP, :] = (feat[1] * feat[2]).astype(BF16)
 
@@ -130,7 +137,7 @@
                 feat, inner = f_s[j, 0, at, :], inners[j][at]
                 mixed_ref[n, mine[j], :] = (feat * inner).astype(BF16)
                 y_s[j, at, :] = (g * feat).astype(BF16)
-                d_s[j, at, :] = g * inner
+                q_s[j, at, :] = g * inner
         d_products = []
         for j in every:
             y_two = jnp.concatenate([y_s[j, :rows, :], y_s[j, GROUP:, :]], axis=1)
@@ -147,24 +154,28 @@
             gl_ref[0, pl.ds(lines[j], 1), :] = jnp.sum(fold, axis=0, keepdims=True)
 
         for j in every:
-            after = [(zero, zero)] * 3
             sums = [[zero] * SHORT for _ in range(3)]
-            for at in at_block[::-1]:
+            for at in at_block:
                 d_product = d_products[j][at]
-                for i, d in enumerate((d_s[j, at, :], d_product * f_s[j, 2, at, :], d_product * f_s[j, 1, at, :])):
-                    one = pltpu.roll(d, LONG - 1, 1)
-                    two = pltpu.roll(d, LONG - 2, 1)
-                    next_one = jnp.where(lane >= LONG - 1, after[i][0], one)
-                    next_two = jnp.where(lane >= LONG - 2, after[i][1], two)
-                    after[i] = (one, two)
-                    p = p_s[j, i, at, :]
-                    sums[i] = [total + p * moved for total, moved in zip(sums[i], (d, next_one, next_two))]
-                    e_s[j, i, at, :] = (
-                        taps[j][i][0] * d + taps[j][i][1] * next_one + taps[j][i][2] * next_two
-                    ).astype(BF16)
+                for i, d in enumerate((q_s[j, at, :], d_product * f_s[j, 2, at, :], d_product * f_s[j, 1, at, :])):
+                    here = p_s[j, i, at.stop : at.stop + GROUP, :].astype(F32)
+                    past = m_s[j, i, at, :].astype(F32)
+                    seen = (here, past[:, :LONG], past[:, LONG:])
+                    sums[i] = [total + d * p for total, p in zip(sums[i], seen)]
+                    d_s[j, i, at, :] = d.astype(BF16)
             for i in range(3):
                 for k in range(SHORT):
                     gs_ref[0, lines[j], 3 * i + k : 3 * i + k + 1, :] = jnp.sum(sums[i][k], axis=0, keepdims=True)
+        for j in every:
+            for i in range(3):
+                two_blocks = jnp.concatenate([d_s[j, i, :rows, :], d_s[j, i, GROUP:, :]], axis=1)
+                coming = dot(two_blocks, next_ref[...], ((1,), (0,)))
+                for at in at_block:
+                    here = d_s[j, i, at, :].astype(F32)
+                    near, far = coming[at, :LONG], coming[at, LONG:]
+                    e_s[j, i, at, :] = (
+                        taps[j][i][0] * here + taps[j][i][1] * near + taps[j][i][2] * far
+                    ).astype(BF16)
         for a, h, where in d_places:
             at = pl.multiple_of(order[where] * GROUP, GROUP)
             for j in every:
@@ -185,6 +196,7 @@
     d_widths = [sum(proj_sets[0][a].shape[2] for a in arrays) for arrays in grouped]
     d_specs = [pl.BlockSpec((3, high, w), lambda i, o: (0, i, 0)) for w in d_widths]
     token_spec = pl.BlockSpec((blocks, high, LONG), lambda i, o: (0, i, 0))
+    shifts = [jnp.asarray(shift_matrix(way), BF16) for way in (-1, 1)]
     outs = pl.pallas_call(
         functools.partial(mix_body, count, sets, per_turn, grouped),
         grid_spec=pltpu.PrefetchScalarGridSpec(
@@ -194,6 +206,8 @@
                 pl.BlockSpec(memory_space=pltpu.SMEM),
                 pl.BlockSpec((1, per_step, LONG), lambda i, o: (i, 0, 0)),
                 pl.BlockSpec((1, per_step, LONG), lambda i, o: (i, 0, 0)),
+                pl.BlockSpec((2 * LONG, 2 * LONG), lambda i, o: (0, 0)),
+                pl.BlockSpec((2 * LONG, 2 * LONG), lambda i, o: (0, 0)),
                 token_spec,
             ]
             + proj_specs * sets,
@@ -204,11 +218,13 @@
                 pl.BlockSpec((1, per_step, LONG), lambda i, o: (i, 0, 0)),
             ],
             scratch_shapes=[
-                pltpu.VMEM((per_turn, 3, rows, LONG), F32),
+                pltpu.VMEM((per_turn, 3, rows + GROUP, LONG), BF16),
+                pltpu.VMEM((per_turn, 3, rows, 2 * LONG), BF16),
                 pltpu.VMEM((per_turn, 3, rows, LONG), F32),
                 pltpu.VMEM((per_turn, rows + GROUP, LONG), BF16),
                 pltpu.VMEM((per_turn, rows + GROUP, LONG), BF16),
                 pltpu.VMEM((per_turn, rows, LONG), F32),
+                pltpu.VMEM((per_turn, 3, rows + GROUP, LONG), BF16),
                 pltpu.VMEM((per_turn, 3, rows, LONG), BF16),
             ],
         ),
@@ -220,7 +236,7 @@
         ],
         compiler_params=pltpu.CompilerParams(vmem_limit_bytes=58 * MIB),
         cost_estimate=SMALL,
-    )(order, short_kernel, long_kernel.reshape(steps, per_step, LONG), turned_kernel.reshape(steps, per_step, LONG), g, *[x for s in proj_sets for x in s])
+    )(order, short_kernel, long_kernel.reshape(steps, per_step, LONG), turned_kernel.reshape(steps, per_step, LONG), *shifts, g, *[x for s in proj_sets for x in s])
     mixed, d_proj, (gs, gl) = outs[0], outs[1:-2], outs[-2:]
     grad_short = jnp.sum(gs, axis=-1).reshape(groups, 3, SHORT).transpose(1, 0, 2)
     grad_long = turn_taps(gl.reshape(groups, LONG))

time: 282 us -> 281 us (level)
  no operation moved by 1% of the time
where the time goes in v9:
time: 281 us; the launch traced here: 280 us
  Pallas kernels  97.1 us (35%)
  waiting for transfers between devices  95.1 us (34%)
  starting transfers between devices  53.4 us (19%)
  local copies, waits for them, and re-layouts  31.4 us (11%)
    ppermute x10, waiting for transfers between devices, one_way(): return lax.ppermute(x, 'ctx', hops)  51.7 us
    pallas_call x5, Pallas kernels, unproject_kernel(): pl.pallas_call(unproject_body, grid=(width // tile,), in_specs=[pl.BlockS...  37.2 us
    ppermute x10, waiting for transfers between devices, across(): return None if x is None else lax.ppermute(x, 'tp', [(0, 1), (1, 0)])  32.3 us
    pallas_call x5, Pallas kernels, project_kernel(): pl.pallas_call(functools.partial(project_body, len(pieces)), grid=(4,), i...  32 us
    unnamed x57, local copies, waits for them, and re-layouts  28.8 us
    pallas_call x1, Pallas kernels, mix(): pl.pallas_call(functools.partial(mix_body, count, sets, per_turn, grouped...  15.5 us
    ppermute x10, starting transfers between devices, one_way(): return lax.ppermute(x, 'ctx', hops)  14.2 us
    ppermute x17, starting transfers between devices, swap(): return lax.ppermute(x, 'ctx', [(d, d ^ 1) for d in range(n_ctx)])  13.4 us
  transfers between devices with their start and end apart: 39, of which 27 were waited for; matrix products, arithmetic and copies ran while one was open for 2% of the time, Pallas kernels for 26%

profile of v9, /device:TPU:1, one launch (start us, length us, event | category | flops | bytes accessed | tf_op | source)
XLA Modules:
  0.0 280.1 jit_solution(1837262672693599764)
XLA Ops:
  0.8 2.7 collective-permute-start.1
  8.3 2.2 copy-done.4
  10.4 2.2 copy-done.5
  12.6 2.2 copy-done.6
  14.8 1.7 shard_map.129
  16.6 4.3 %shard_map.130 = (bf16[768,256]{1,0:T(8,128)(2,1)S(1)}, bf16[768,256]{1,0:T(8,128)(2,1)S(1)}) custom-call(bf16[128,4096]{1,0:T(8,128)(2,1)S(1)} %copy-done.7, bf16[128,4096]{1,0:T(8,128)(2,1)S(1)} %collective-permute-done.2.refs_1_, bf16[1536,4096]{1,0:T(8,128)(2,1)S(1)} %bitcast.35), custom_call_target="tpu_custom_call" | custom-call | flops 1 | bytes 1 | tf_op jit(solution)/shard_map/pallas_call | solution.py:305
  20.9 5.6 %collective-permute-done.1 = bf16[128,4096]{1,0:T(8,128)(2,1)S(1)} collective-permute-done((bf16[128,4096]{1,0:T(8,128)(2,1)}, bf16[128,4096]{1,0:T(8,128)(2,1)S(1)}, u32[]{:S(2)}, u32[]{:S(2)}) %collective-permute-start.1) | collective-permute-done | bytes 1048608 | tf_op jit(solution)/shard_map/ppermute | solution.py:425
  28.0 1.4 collective-permute-start.3
  31.8 7.8 %shard_map.131 = (bf16[768,512]{1,0:T(8,128)(2,1)S(1)}, bf16[768,512]{1,0:T(8,128)(2,1)S(1)}) custom-call(bf16[256,4096]{1,0:T(8,128)(2,1)S(1)} %constant_dynamic-update-slice_fusion.refs_0_, bf16[256,4096]{1,0:T(8,128)(2,1)S(1)} %collective-permute-done.4.refs_1_, bf16[1536,4096]{1,0:T(8,128)(2,1)S(1)} %bitcast.36), custom_call_target="tpu_custom_call" | custom-call | flops 1 | bytes 1 | tf_op jit(solution)/shard_map/pallas_call | solution.py:305
  40.4 12.7 %collective-permute-done.3.refs_0_ = bf16[256,4096]{1,0:T(8,128)(2,1)S(1)} collective-permute-done((bf16[256,4096]{1,0:T(8,128)(2,1)S(1)}, bf16[256,4096]{1,0:T(8,128)(2,1)S(1)}, u32[]{:S(2)}, u32[]{:S(2)}) %collective-permute-start.3) | collective-permute-done | bytes 2097184 | tf_op jit(solution)/shard_map/ppermute | solution.py:425
  58.0 7.8 %shard_map.132 = (bf16[768,512]{1,0:T(8,128)(2,1)S(1)}, bf16[768,512]{1,0:T(8,128)(2,1)S(1)}) custom-call(bf16[256,4096]{1,0:T(8,128)(2,1)S(1)} %collective-permute-done.3.refs_0_, bf16[256,4096]{1,0:T(8,128)(2,1)S(1)} %collective-permute-done.7.refs_1_, bf16[1536,4096]{1,0:T(8,128)(2,1)S(1)} %bitcast.37), custom_call_target="tpu_custom_call" | custom-call | flops 1 | bytes 1 | tf_op jit(solution)/shard_map/pallas_call | solution.py:305
  65.7 8.2 %collective-permute-done.8 = bf16[768,512]{1,0:T(8,128)(2,1)S(1)} collective-permute-done((bf16[768,512]{1,0:T(8,128)(2,1)S(1)}, bf16[768,512]{1,0:T(8,128)(2,1)S(1)}, u32[]{:S(2)}, u32[]{:S(2)}) %collective-permute-start.8) | collective-permute-done | bytes 786464 | tf_op jit(solution)/shard_map/ppermute | solution.py:458
  74.0 5.7 %collective-permute-done.6.refs_0_ = bf16[256,4096]{1,0:T(8,128)(2,1)S(1)} collective-permute-done((bf16[256,4096]{1,0:T(8,128)(2,1)S(1)}, bf16[256,4096]{1,0:T(8,128)(2,1)S(1)}, u32[]{:S(2)}, u32[]{:S(2)}) %collective-permute-start.6) | collective-permute-done | bytes 2097184 | tf_op jit(solution)/shard_map/ppermute | solution.py:425
  80.3 1.4 collective-permute-start.9
  84.0 7.8 %shard_map.133 = (bf16[768,512]{1,0:T(8,128)(2,1)S(1)}, bf16[768,512]{1,0:T(8,128)(2,1)S(1)}) custom-call(bf16[256,4096]{1,0:T(8,128)(2,1)S(1)} %collective-permute-done.6.refs_0_, bf16[256,4096]{1,0:T(8,128)(2,1)S(1)} %collective-permute-done.10.refs_1_, bf16[1536,4096]{1,0:T(8,128)(2,1)S(1)} %bitcast.38), custom_call_target="tpu_custom_call" | custom-call | flops 1 | bytes 1 | tf_op jit(solution)/shard_map/pallas_call | solution.py:305
  92.7 2.0 collective-permute-done.9.refs_0_
  94.7 6.4 %all-to-all-start = ((bf16[16,256,128]{2,1,0:T(8,128)(2,1)}), bf16[16,256,128]{2,1,0:T(8,128)(2,1)}, u32[]{:S(2)}, u32[]{:S(2)}) async-start(bf16[16,256,128]{2,1,0:T(8,128)(2,1)} %bitcast.61), calls=%async_computation | async-start | bytes 2097152 | tf_op jit(solution)/shard_map/all_to_all | solution.py:487
  104.2 4.6 %copy-done.1 = bf16[2,3,256,4096]{3,2,1,0:T(8,128)(2,1)S(1)} copy-done((bf16[2,3,256,4096]{3,2,1,0:T(8,128)(2,1)S(1)}, bf16[2,3,256,4096]{3,2,1,0:T(8,128)(2,1)}, u32[]{:S(2)}) %copy-start.1) | copy-done | bytes 12582936
  108.8 4.3 %shard_map.134 = (bf16[768,256]{1,0:T(8,128)(2,1)S(1)}, bf16[768,256]{1,0:T(8,128)(2,1)S(1)}) custom-call(bf16[128,4096]{1,0:T(8,128)(2,1)S(1)} %collective-permute-done.9.refs_0_, bf16[64,4096]{1,0:T(8,128)(2,1)S(1)} %collective-permute-done.12.refs_1_, bf16[64,4096]{1,0:T(8,128)(2,1)S(1)} %collective-permute-done.13.refs_2_, bf16[1536,4096]{1,0:T(8,128)(2,1)S(1)} %bitcast.39), custom_call_target="tpu_custom_call" | custom-call | flops 1 | bytes 1 | tf_op jit(solution)/shard_map/pallas_call | solution.py:305
  115.1 5.6 %collective-permute-done.14 = bf16[768,512]{1,0:T(8,128)(2,1)S(1)} collective-permute-done((bf16[768,512]{1,0:T(8,128)(2,1)S(1)}, bf16[768,512]{1,0:T(8,128)(2,1)S(1)}, u32[]{:S(2)}, u32[]{:S(2)}) %collective-permute-start.14) | collective-permute-done | bytes 786464 | tf_op jit(solution)/shard_map/ppermute | solution.py:458
  120.7 8.4 %collective-permute-done.15 = bf16[768,256]{1,0:T(8,128)(2,1)S(1)} collective-permute-done((bf16[768,256]{1,0:T(8,128)(2,1)S(1)}, bf16[768,256]{1,0:T(8,128)(2,1)S(1)}, u32[]{:S(2)}, u32[]{:S(2)}) %collective-permute-start.15) | collective-permute-done | bytes 393248 | tf_op jit(solution)/shard_map/ppermute | solution.py:458
  129.9 15.5 %shard_map.135 = (bf16[16,256,128]{2,1,0:T(8,128)(2,1)}, bf16[3,256,256]{2,1,0:T(8,128)(2,1)}, bf16[3,256,512]{2,1,0:T(8,128)(2,1)}, bf16[3,256,512]{2,1,0:T(8,1...) custom-call(s32[16]{0:T(128)} %dynamic-slice_bitcast_fusion.order, ...), custom_call_target="tpu_custom_call" | custom-call | flops 1 | bytes 1 | tf_op jit(solution)/shard_map/pallas_call | solution.py:200
  146.7 7.0 %all-to-all-start.1 = ((bf16[16,256,128]{2,1,0:T(8,128)(2,1)}), bf16[16,256,128]{2,1,0:T(8,128)(2,1)S(1)}, u32[]{:S(2)}, u32[]{:S(2)}) async-start(bf16[16,256,128]{2,1,0:T(8,128)(2,1)} %get-tuple-element.148), calls=%async_computation.1 | async-start | bytes 2097152 | tf_op jit(solution)/shard_map/all_to_all | solution.py:505
  155.0 4.6 %copy-done.2 = bf16[2,3,256,4096]{3,2,1,0:T(8,128)(2,1)S(1)} copy-done((bf16[2,3,256,4096]{3,2,1,0:T(8,128)(2,1)S(1)}, bf16[2,3,256,4096]{3,2,1,0:T(8,128)(2,1)}, u32[]{:S(2)}) %copy-start.2) | copy-done | bytes 12582936
  159.6 5.2 %shard_map.136 = (bf16[128,4096]{1,0:T(8,128)(2,1)S(1)}, bf16[80,4096]{1,0:T(8,128)(2,1)S(1)}, bf16[48,4096]{1,0:T(8,128)(2,1)S(1)}) custom-call(bf16[768,256]{1,0:T(8,128)(2,1)S(1)} %bitcast.59, bf16[768,256]{1,0:T(8,128)(2,1)S(1)} %collective-permute-done.16.far_ref, bf16[1536,4096]{1,0:T(8,128)(2,1)S(1)} %bitcast.40), custom_call_target="tpu_custom_call" | custom-call | flops 1 | bytes 1 | tf_op jit(solution)/shard_map/pallas_call | solution.py:342
  164.8 2.7 collective-permute-start.17
  167.5 2.1 collective-permute-start.22
  170.3 3.1 %collective-permute-done.19.far_ref = bf16[768,512]{1,0:T(8,128)(2,1)S(1)} collective-permute-done((bf16[768,512]{1,0:T(8,128)(2,1)S(1)}, bf16[768,512]{1,0:T(8,128)(2,1)S(1)}, u32[]{:S(2)}, u32[]{:S(2)}) %collective-permute-start.19) | collective-permute-done | bytes 786464 | tf_op jit(solution)/shard_map/ppermute | solution.py:458
  174.4 8.7 %shard_map.138 = (bf16[256,4096]{1,0:T(8,128)(2,1)S(1)}, bf16[96,4096]{1,0:T(8,128)(2,1)S(1)}, bf16[96,4096]{1,0:T(8,128)(2,1)S(1)}, bf16[64,4096]{1,0:T(8,128)(2,1)S(1)}) custom-call(bf16[768,512]{1,0:T(8,128)(2,1)S(1)} %bitcast.54, bf16[768,512]{1,0:T(8,128)(2,1)S(1)} %collective-permute-done.19.far_ref, bf16[1536,4096]{1,0:T(8,128)(2,1)S(1)} %bitcast.41), custom_call_target="tpu_custom_call" | custom-call | flops 1 | bytes 1 | tf_op jit(solution)/shard_map/pallas_call | solution.py:342
  183.1 1.9 collective-permute-start.20
  185.1 5.2 %collective-permute-done.22.far_ref = bf16[768,512]{1,0:T(8,128)(2,1)S(1)} collective-permute-done((bf16[768,512]{1,0:T(8,128)(2,1)S(1)}, bf16[768,512]{1,0:T(8,128)(2,1)S(1)}, u32[]{:S(2)}, u32[]{:S(2)}) %collective-permute-start.22) | collective-permute-done | bytes 786464 | tf_op jit(solution)/shard_map/ppermute | solution.py:458
  191.8 1.5 collective-permute-done.23.refs_3_
  197.1 4.6 %copy-done.3 = bf16[2,3,256,4096]{3,2,1,0:T(8,128)(2,1)S(1)} copy-done((bf16[2,3,256,4096]{3,2,1,0:T(8,128)(2,1)S(1)}, bf16[2,3,256,4096]{3,2,1,0:T(8,128)(2,1)}, u32[]{:S(2)}) %copy-start.3) | copy-done | bytes 12582936
  204.0 8.7 %shard_map.140 = (bf16[256,4096]{1,0:T(8,128)(2,1)S(1)}, bf16[128,4096]{1,0:T(8,128)(2,1)S(1)}, bf16[128,4096]{1,0:T(8,128)(2,1)S(1)}) custom-call(bf16[768,512]{1,0:T(8,128)(2,1)S(1)} %bitcast.49, bf16[768,512]{1,0:T(8,128)(2,1)S(1)} %copy-done.15, bf16[1536,4096]{1,0:T(8,128)(2,1)S(1)} %bitcast.42), custom_call_target="tpu_custom_call" | custom-call | flops 1 | bytes 1 | tf_op jit(solution)/shard_map/pallas_call | solution.py:342
  214.5 1.5 collective-permute-start.27
  216.1 1.5 shard_map.142
  218.3 1.5 collective-permute-done.28.refs_3_
  223.8 8.7 %shard_map.143 = (bf16[256,4096]{1,0:T(8,128)(2,1)S(1)}, bf16[128,4096]{1,0:T(8,128)(2,1)S(1)}, bf16[128,4096]{1,0:T(8,128)(2,1)S(1)}) custom-call(bf16[768,512]{1,0:T(8,128)(2,1)S(1)} %bitcast.47, bf16[768,512]{1,0:T(8,128)(2,1)S(1)} %collective-permute-done.26.far_ref, bf16[1536,4096]{1,0:T(8,128)(2,1)S(1)} %bitcast.43), custom_call_target="tpu_custom_call" | custom-call | flops 1 | bytes 1 | tf_op jit(solution)/shard_map/pallas_call | solution.py:342
  232.5 1.9 collective-permute-start.29
  234.5 2.2 collective-permute-done.29.refs_1_
  236.7 1.5 collective-permute-done.31.refs_2_
  238.2 8.2 %collective-permute-done.32.refs_3_ = bf16[256,4096]{1,0:T(8,128)(2,1)S(1)} collective-permute-done((bf16[256,4096]{1,0:T(8,128)(2,1)S(1)}, bf16[256,4096]{1,0:T(8,128)(2,1)S(1)}, u32[]{:S(2)}, u32[]{:S(2)}) %collective-permute-start.32) | collective-permute-done | bytes 2097184 | tf_op jit(solution)/shard_map/ppermute | solution.py:425
  246.4 2.4 shard_map.144
  250.1 2.5 collective-permute-start.36
  252.5 5.8 %shard_map.145 = (bf16[128,4096]{1,0:T(8,128)(2,1)S(1)}, bf16[64,4096]{1,0:T(8,128)(2,1)}, bf16[64,4096]{1,0:T(8,128)(2,1)}) custom-call(bf16[768,256]{1,0:T(8,128)(2,1)S(1)} %bitcast.56, bf16[768,256]{1,0:T(8,128)(2,1)S(1)} %collective-permute-done.30.far_ref, bf16[1536,4096]{1,0:T(8,128)(2,1)S(1)} %bitcast.44), custom_call_target="tpu_custom_call" | custom-call | flops 1 | bytes 1 | tf_op jit(solution)/shard_map/pallas_call | solution.py:342
  261.4 1.6 collective-permute-done.35.refs_3_
  263.0 13.5 %collective-permute-done.36.refs_4_ = bf16[128,4096]{1,0:T(8,128)(2,1)S(1)} collective-permute-done((bf16[128,4096]{1,0:T(8,128)(2,1)}, bf16[128,4096]{1,0:T(8,128)(2,1)S(1)}, u32[]{:S(2)}, u32[]{:S(2)}) %collective-permute-start.36) | collective-permute-done | bytes 1048608 | tf_op jit(solution)/shard_map/ppermute | solution.py:425
  276.5 3.7 %shard_map.146 = bf16[128,4096]{1,0:T(8,128)(2,1)} custom-call(bf16[128,4096]{1,0:T(8,128)(2,1)S(1)} %get-tuple-element.177.refs_0_, bf16[64,4096]{1,0:T(8,128)(2,1)} %collective-permute-done.33.refs_1_, bf16[64,4096]{1,0:T(8,128)(2,1)} %collective-permute-done.34.refs_2_, bf16[128,4096]{1,0:T(8,128)(2,1)S(1)} %collective-permute-done.35.refs_3_, ...), custom_call_target="tpu_custom_call" | custom-call | flops 1 | bytes 1 | tf_op jit(solution)/shard_map/pallas_call | solution.py:382
  (118 shorter events, 46.8 us)
Async XLA Ops:
  0.6 15.9 %collective-permute-start.2 = (bf16[128,4096]{1,0:T(8,128)(2,1)}, bf16[128,4096]{1,0:T(8,128)(2,1)S(1)}, u32[]{:S(2)}, u32[]{:S(2)}) collective-permute-start(bf16[128,4096]{1,0:T(8,128)(2,1)} %refs_0_.3), channel_id=1, source_target_pairs={{0,2},{2,0},{4,6},{6,4},{8,10},{10,8},{12,14},{14,12},{16,18},{18,... | collective-permute-start | bytes 3145736 | tf_op jit(solution)/shard_map/ppermute | solution.py:428
  0.8 25.7 %collective-permute-start.1 = (bf16[128,4096]{1,0:T(8,128)(2,1)}, bf16[128,4096]{1,0:T(8,128)(2,1)S(1)}, u32[]{:S(2)}, u32[]{:S(2)}) collective-permute-start(bf16[128,4096]{1,0:T(8,128)(2,1)} %refs_0_.3), channel_id=1, source_target_pairs={{0,6},{2,8},{8,2},{10,16},{16,10},{18,24},{24,18},{26,28},{28,26},... | collective-permute-start | bytes 3145736 | tf_op jit(solution)/shard_map/ppermute | solution.py:425
  3.5 23.9 %collective-permute-start = (bf16[128,4096]{1,0:T(8,128)(2,1)}, bf16[128,4096]{1,0:T(8,128)(2,1)S(1)}, u32[]{:S(2)}, u32[]{:S(2)}) collective-permute-start(bf16[128,4096]{1,0:T(8,128)(2,1)} %refs_0_.3), channel_id=1, source_target_pairs={{0,8},{2,6},{8,16},{10,2},{16,24},{18,10},{24,28},{26,18},{28,20},... | collective-permute-start | bytes 3145736 | tf_op jit(solution)/shard_map/ppermute | solution.py:425
  16.5 67.5 %copy-start = (bf16[2,3,256,4096]{3,2,1,0:T(8,128)(2,1)}, bf16[2,3,256,4096]{3,2,1,0:T(8,128)(2,1)S(1)}, u32[]{:S(2)}) copy-start(bf16[2,3,256,4096]{3,2,1,0:T(8,128)(2,1)S(1)} %shard_map.129) | copy-start | bytes 37748740
  27.6 4.2 %collective-permute-start.4 = (bf16[256,4096]{1,0:T(8,128)(2,1)S(1)}, bf16[256,4096]{1,0:T(8,128)(2,1)S(1)}, u32[]{:S(2)}, u32[]{:S(2)}) collective-permute-start(bf16[256,4096]{1,0:T(8,128)(2,1)S(1)} %constant_dynamic-update-slice_fusion.refs_0_), channel_id=1, source_target_pairs={{0,2},{2,0},{4,6},{6,4},{8,10},{10,8},{12,14},{14,12},{16,18},{18,... | collective-permute-start | bytes 6291464 | tf_op jit(solution)/shard_map/ppermute | solution.py:428
  28.0 25.2 %collective-permute-start.3 = (bf16[256,4096]{1,0:T(8,128)(2,1)S(1)}, bf16[256,4096]{1,0:T(8,128)(2,1)S(1)}, u32[]{:S(2)}, u32[]{:S(2)}) collective-permute-start(bf16[256,4096]{1,0:T(8,128)(2,1)S(1)} %constant_dynamic-update-slice_fusion.refs_0_), channel_id=1, source_target_pairs={{0,8},{2,6},{8,16},{10,2},{16,24},{18,10},{24,28},{26,18},{28,20},... | collective-permute-start | bytes 6291464 | tf_op jit(solution)/shard_map/ppermute | solution.py:425
  29.4 11.1 %collective-permute-start.5 = (bf16[768,256]{1,0:T(8,128)(2,1)S(1)}, bf16[768,256]{1,0:T(8,128)(2,1)S(1)}, u32[]{:S(2)}, u32[]{:S(2)}) collective-permute-start(bf16[768,256]{1,0:T(8,128)(2,1)S(1)} %get-tuple-element.105), channel_id=1, source_target_pairs={{0,1},{1,0},{2,3},{3,2},{4,5},{5,4},{6,7},{7,6},{8,9},{9,8},{10,11... | collective-permute-start | bytes 1179656 | tf_op jit(solution)/shard_map/ppermute | solution.py:458
  40.4 16.3 %copy-start.23 = (bf16[768,256]{1,0:T(8,128)(2,1)}, bf16[768,256]{1,0:T(8,128)(2,1)S(1)}, u32[]{:S(2)}) copy-start(bf16[768,256]{1,0:T(8,128)(2,1)S(1)} %collective-permute-done.5) | copy-start | bytes 1179652
  53.2 4.8 %collective-permute-start.7 = (bf16[256,4096]{1,0:T(8,128)(2,1)S(1)}, bf16[256,4096]{1,0:T(8,128)(2,1)S(1)}, u32[]{:S(2)}, u32[]{:S(2)}) collective-permute-start(bf16[256,4096]{1,0:T(8,128)(2,1)S(1)} %collective-permute-done.3.refs_0_), channel_id=1, source_target_pairs={{0,2},{2,0},{4,6},{6,4},{8,10},{10,8},{12,14},{14,12},{16,18},{18,... | collective-permute-start | bytes 6291464 | tf_op jit(solution)/shard_map/ppermute | solution.py:428
  54.2 25.5 %collective-permute-start.6 = (bf16[256,4096]{1,0:T(8,128)(2,1)S(1)}, bf16[256,4096]{1,0:T(8,128)(2,1)S(1)}, u32[]{:S(2)}, u32[]{:S(2)}) collective-permute-start(bf16[256,4096]{1,0:T(8,128)(2,1)S(1)} %collective-permute-done.3.refs_0_), channel_id=1, source_target_pairs={{0,8},{2,6},{8,16},{10,2},{16,24},{18,10},{24,28},{26,18},{28,20},... | collective-permute-start | bytes 6291464 | tf_op jit(solution)/shard_map/ppermute | solution.py:425
  55.5 18.4 %collective-permute-start.8 = (bf16[768,512]{1,0:T(8,128)(2,1)S(1)}, bf16[768,512]{1,0:T(8,128)(2,1)S(1)}, u32[]{:S(2)}, u32[]{:S(2)}) collective-permute-start(bf16[768,512]{1,0:T(8,128)(2,1)S(1)} %get-tuple-element.110), channel_id=1, source_target_pairs={{0,1},{1,0},{2,3},{3,2},{4,5},{5,4},{6,7},{7,6},{8,9},{9,8},{10,11... | collective-permute-start | bytes 2359304 | tf_op jit(solution)/shard_map/ppermute | solution.py:458
  65.7 26.0 %copy-start.12 = (bf16[768,512]{1,0:T(8,128)(2,1)}, bf16[768,512]{1,0:T(8,128)(2,1)S(1)}, u32[]{:S(2)}) copy-start(bf16[768,512]{1,0:T(8,128)(2,1)S(1)} %get-tuple-element.119) | copy-start | bytes 2359300
  74.0 17.8 %copy-start.21 = (bf16[768,512]{1,0:T(8,128)(2,1)}, bf16[768,512]{1,0:T(8,128)(2,1)S(1)}, u32[]{:S(2)}) copy-start(bf16[768,512]{1,0:T(8,128)(2,1)S(1)} %collective-permute-done.8) | copy-start | bytes 2359300
  79.7 4.3 %collective-permute-start.10 = (bf16[256,4096]{1,0:T(8,128)(2,1)S(1)}, bf16[256,4096]{1,0:T(8,128)(2,1)S(1)}, u32[]{:S(2)}, u32[]{:S(2)}) collective-permute-start(bf16[256,4096]{1,0:T(8,128)(2,1)S(1)} %collective-permute-done.6.refs_0_), channel_id=1, source_target_pairs={{0,2},{2,0},{4,6},{6,4},{8,10},{10,8},{12,14},{14,12},{16,18},{18,... | collective-permute-start | bytes 6291464 | tf_op jit(solution)/shard_map/ppermute | solution.py:428
  80.3 14.4 %collective-permute-start.9 = (bf16[128,4096]{1,0:T(8,128)(2,1)S(1)}, bf16[128,4096]{1,0:T(8,128)(2,1)S(1)}, u32[]{:S(2)}, u32[]{:S(2)}) collective-permute-start(bf16[128,4096]{1,0:T(8,128)(2,1)S(1)} %slice.34), channel_id=1, source_target_pairs={{0,8},{2,6},{8,16},{10,2},{16,24},{18,10},{24,28},{26,18},{28,20},... | collective-permute-start | bytes 3145736 | tf_op jit(solution)/shard_map/ppermute | solution.py:425
  81.7 19.4 %collective-permute-start.11 = (bf16[768,512]{1,0:T(8,128)(2,1)S(1)}, bf16[768,512]{1,0:T(8,128)(2,1)}, u32[]{:S(2)}, u32[]{:S(2)}) collective-permute-start(bf16[768,512]{1,0:T(8,128)(2,1)S(1)} %get-tuple-element.118), channel_id=1, source_target_pairs={{0,1},{1,0},{2,3},{3,2},{4,5},{5,4},{6,7},{7,6},{8,9},{9,8},{10,11... | collective-permute-start | bytes 2359304 | tf_op jit(solution)/shard_map/ppermute | solution.py:458
  94.7 34.4 %all-to-all-start = ((bf16[16,256,128]{2,1,0:T(8,128)(2,1)}), bf16[16,256,128]{2,1,0:T(8,128)(2,1)}, u32[]{:S(2)}, u32[]{:S(2)}) async-start(bf16[16,256,128]{2,1,0:T(8,128)(2,1)} %bitcast.61), calls=%async_computation | async-start | bytes 2097152 | tf_op jit(solution)/shard_map/all_to_all | solution.py:487
  101.2 2.2 collective-permute-start.13
  101.9 2.3 collective-permute-start.12
  102.0 18.7 %collective-permute-start.14 = (bf16[768,512]{1,0:T(8,128)(2,1)S(1)}, bf16[768,512]{1,0:T(8,128)(2,1)S(1)}, u32[]{:S(2)}, u32[]{:S(2)}) collective-permute-start(bf16[768,512]{1,0:T(8,128)(2,1)S(1)} %get-tuple-element.126), channel_id=1, source_target_pairs={{0,1},{1,0},{2,3},{3,2},{4,5},{5,4},{6,7},{7,6},{8,9},{9,8},{10,11... | collective-permute-start | bytes 2359304 | tf_op jit(solution)/shard_map/ppermute | solution.py:458
  113.9 15.2 %collective-permute-start.15 = (bf16[768,256]{1,0:T(8,128)(2,1)S(1)}, bf16[768,256]{1,0:T(8,128)(2,1)S(1)}, u32[]{:S(2)}, u32[]{:S(2)}) collective-permute-start(bf16[768,256]{1,0:T(8,128)(2,1)S(1)} %get-tuple-element.127), channel_id=1, source_target_pairs={{0,1},{1,0},{2,3},{3,2},{4,5},{5,4},{6,7},{7,6},{8,9},{9,8},{10,11... | collective-permute-start | bytes 1179656 | tf_op jit(solution)/shard_map/ppermute | solution.py:458
  120.7 8.4 %copy-start.22 = (bf16[768,512]{1,0:T(8,128)(2,1)}, bf16[768,512]{1,0:T(8,128)(2,1)S(1)}, u32[]{:S(2)}) copy-start(bf16[768,512]{1,0:T(8,128)(2,1)S(1)} %collective-permute-done.14) | copy-start | bytes 2359300
  145.4 8.3 %copy-start.16 = (bf16[3,256,512]{2,1,0:T(8,128)(2,1)S(1)}, bf16[3,256,512]{2,1,0:T(8,128)(2,1)}, u32[]{:S(2)}) copy-start(bf16[3,256,512]{2,1,0:T(8,128)(2,1)} %get-tuple-element.132) | copy-start | bytes 2359300
  145.4 9.6 %copy-start.19 = (bf16[3,256,256]{2,1,0:T(8,128)(2,1)S(1)}, bf16[3,256,256]{2,1,0:T(8,128)(2,1)}, u32[]{:S(2)}) copy-start(bf16[3,256,256]{2,1,0:T(8,128)(2,1)} %get-tuple-element.128) | copy-start | bytes 1179652
  145.4 9.6 %collective-permute-start.16 = (bf16[768,256]{1,0:T(8,128)(2,1)}, bf16[768,256]{1,0:T(8,128)(2,1)S(1)}, u32[]{:S(2)}, u32[]{:S(2)}) collective-permute-start(bf16[768,256]{1,0:T(8,128)(2,1)} %bitcast.58), channel_id=1, source_target_pairs={{0,1},{1,0},{2,3},{3,2},{4,5},{5,4},{6,7},{7,6},{8,9},{9,8},{10,11... | collective-permute-start | bytes 1179656 | tf_op jit(solution)/shard_map/ppermute | solution.py:458
  146.7 47.9 %all-to-all-start.1 = ((bf16[16,256,128]{2,1,0:T(8,128)(2,1)}), bf16[16,256,128]{2,1,0:T(8,128)(2,1)S(1)}, u32[]{:S(2)}, u32[]{:S(2)}) async-start(bf16[16,256,128]{2,1,0:T(8,128)(2,1)} %get-tuple-element.148), calls=%async_computation.1 | async-start | bytes 2097152 | tf_op jit(solution)/shard_map/all_to_all | solution.py:505
  153.7 19.7 %collective-permute-start.19 = (bf16[768,512]{1,0:T(8,128)(2,1)S(1)}, bf16[768,512]{1,0:T(8,128)(2,1)S(1)}, u32[]{:S(2)}, u32[]{:S(2)}) collective-permute-start(bf16[768,512]{1,0:T(8,128)(2,1)S(1)} %bitcast.53), channel_id=1, source_target_pairs={{0,1},{1,0},{2,3},{3,2},{4,5},{5,4},{6,7},{7,6},{8,9},{9,8},{10,11... | collective-permute-start | bytes 2359304 | tf_op jit(solution)/shard_map/ppermute | solution.py:458
  164.8 5.0 %collective-permute-start.17 = (bf16[80,4096]{1,0:T(8,128)(2,1)S(1)}, bf16[80,4096]{1,0:T(8,128)(2,1)S(1)}, u32[]{:S(2)}, u32[]{:S(2)}) collective-permute-start(bf16[80,4096]{1,0:T(8,128)(2,1)S(1)} %get-tuple-element.130), channel_id=1, source_target_pairs={{0,2},{2,0},{4,6},{6,4},{8,10},{10,8},{12,14},{14,12},{16,18},{18,... | collective-permute-start | bytes 1966088 | tf_op jit(solution)/shard_map/ppermute | solution.py:428
  167.4 2.3 collective-permute-start.18
  167.5 22.7 %collective-permute-start.22 = (bf16[768,512]{1,0:T(8,128)(2,1)S(1)}, bf16[768,512]{1,0:T(8,128)(2,1)S(1)}, u32[]{:S(2)}, u32[]{:S(2)}) collective-permute-start(bf16[768,512]{1,0:T(8,128)(2,1)S(1)} %bitcast.48), channel_id=1, source_target_pairs={{0,1},{1,0},{2,3},{3,2},{4,5},{5,4},{6,7},{7,6},{8,9},{9,8},{10,11... | collective-permute-start | bytes 2359304 | tf_op jit(solution)/shard_map/ppermute | solution.py:458
  173.4 19.9 %collective-permute-start.24 = (bf16[128,4096]{1,0:T(8,128)(2,1)S(1)}, bf16[128,4096]{1,0:T(8,128)(2,1)S(1)}, u32[]{:S(2)}, u32[]{:S(2)}) collective-permute-start(bf16[128,4096]{1,0:T(8,128)(2,1)S(1)} %shard_map.137), channel_id=1, source_target_pairs={{0,4},{2,10},{8,0},{10,18},{16,8},{18,26},{24,16},{26,30},{28,24},... | collective-permute-start | bytes 3145736 | tf_op jit(solution)/shard_map/ppermute | solution.py:425
  183.1 10.2 %collective-permute-start.20 = (bf16[96,4096]{1,0:T(8,128)(2,1)S(1)}, bf16[96,4096]{1,0:T(8,128)(2,1)S(1)}, u32[]{:S(2)}, u32[]{:S(2)}) collective-permute-start(bf16[96,4096]{1,0:T(8,128)(2,1)S(1)} %get-tuple-element.138), channel_id=1, source_target_pairs={{0,2},{2,0},{4,6},{6,4},{8,10},{10,8},{12,14},{14,12},{16,18},{18,... | collective-permute-start | bytes 2359304 | tf_op jit(solution)/shard_map/ppermute | solution.py:428
  185.0 8.4 %collective-permute-start.21 = (bf16[96,4096]{1,0:T(8,128)(2,1)S(1)}, bf16[96,4096]{1,0:T(8,128)(2,1)S(1)}, u32[]{:S(2)}, u32[]{:S(2)}) collective-permute-start(bf16[96,4096]{1,0:T(8,128)(2,1)S(1)} %get-tuple-element.139), channel_id=1, source_target_pairs={{0,2},{2,0},{4,6},{6,4},{8,10},{10,8},{12,14},{14,12},{16,18},{18,... | collective-permute-start | bytes 2359304 | tf_op jit(solution)/shard_map/ppermute | solution.py:428
  191.1 2.2 collective-permute-start.23
  194.6 25.2 %collective-permute-start.28 = (bf16[256,4096]{1,0:T(8,128)(2,1)S(1)}, bf16[256,4096]{1,0:T(8,128)(2,1)S(1)}, u32[]{:S(2)}, u32[]{:S(2)}) collective-permute-start(bf16[256,4096]{1,0:T(8,128)(2,1)S(1)} %shard_map.139), channel_id=1, source_target_pairs={{0,4},{2,10},{8,0},{10,18},{16,8},{18,26},{24,16},{26,30},{28,24},... | collective-permute-start | bytes 6291464 | tf_op jit(solution)/shard_map/ppermute | solution.py:425
  195.9 18.6 %collective-permute-start.26 = (bf16[768,512]{1,0:T(8,128)(2,1)}, bf16[768,512]{1,0:T(8,128)(2,1)S(1)}, u32[]{:S(2)}, u32[]{:S(2)}) collective-permute-start(bf16[768,512]{1,0:T(8,128)(2,1)} %bitcast.46), channel_id=1, source_target_pairs={{0,1},{1,0},{2,3},{3,2},{4,5},{5,4},{6,7},{7,6},{8,9},{9,8},{10,11... | collective-permute-start | bytes 2359304 | tf_op jit(solution)/shard_map/ppermute | solution.py:458
  212.7 4.9 %collective-permute-start.25 = (bf16[128,4096]{1,0:T(8,128)(2,1)S(1)}, bf16[128,4096]{1,0:T(8,128)(2,1)S(1)}, u32[]{:S(2)}, u32[]{:S(2)}) collective-permute-start(bf16[128,4096]{1,0:T(8,128)(2,1)S(1)} %get-tuple-element.152), channel_id=1, source_target_pairs={{0,2},{2,0},{4,6},{6,4},{8,10},{10,8},{12,14},{14,12},{16,18},{18,... | collective-permute-start | bytes 3145736 | tf_op jit(solution)/shard_map/ppermute | solution.py:428
  214.5 3.8 %collective-permute-start.27 = (bf16[128,4096]{1,0:T(8,128)(2,1)S(1)}, bf16[128,4096]{1,0:T(8,128)(2,1)S(1)}, u32[]{:S(2)}, u32[]{:S(2)}) collective-permute-start(bf16[128,4096]{1,0:T(8,128)(2,1)S(1)} %get-tuple-element.155), channel_id=1, source_target_pairs={{0,2},{2,0},{4,6},{6,4},{8,10},{10,8},{12,14},{14,12},{16,18},{18,... | collective-permute-start | bytes 3145736 | tf_op jit(solution)/shard_map/ppermute | solution.py:428
  221.2 25.2 %collective-permute-start.32 = (bf16[256,4096]{1,0:T(8,128)(2,1)S(1)}, bf16[256,4096]{1,0:T(8,128)(2,1)S(1)}, u32[]{:S(2)}, u32[]{:S(2)}) collective-permute-start(bf16[256,4096]{1,0:T(8,128)(2,1)S(1)} %shard_map.141), channel_id=1, source_target_pairs={{0,4},{2,10},{8,0},{10,18},{16,8},{18,26},{24,16},{26,30},{28,24},... | collective-permute-start | bytes 6291464 | tf_op jit(solution)/shard_map/ppermute | solution.py:425
  222.5 11.9 %collective-permute-start.30 = (bf16[768,256]{1,0:T(8,128)(2,1)S(1)}, bf16[768,256]{1,0:T(8,128)(2,1)S(1)}, u32[]{:S(2)}, u32[]{:S(2)}) collective-permute-start(bf16[768,256]{1,0:T(8,128)(2,1)S(1)} %bitcast.55), channel_id=1, source_target_pairs={{0,1},{1,0},{2,3},{3,2},{4,5},{5,4},{6,7},{7,6},{8,9},{9,8},{10,11... | collective-permute-start | bytes 1179656 | tf_op jit(solution)/shard_map/ppermute | solution.py:458
  232.5 4.2 %collective-permute-start.29 = (bf16[128,4096]{1,0:T(8,128)(2,1)S(1)}, bf16[128,4096]{1,0:T(8,128)(2,1)S(1)}, u32[]{:S(2)}, u32[]{:S(2)}) collective-permute-start(bf16[128,4096]{1,0:T(8,128)(2,1)S(1)} %get-tuple-element.164), channel_id=1, source_target_pairs={{0,2},{2,0},{4,6},{6,4},{8,10},{10,8},{12,14},{14,12},{16,18},{18,... | collective-permute-start | bytes 3145736 | tf_op jit(solution)/shard_map/ppermute | solution.py:428
  234.4 3.8 %collective-permute-start.31 = (bf16[128,4096]{1,0:T(8,128)(2,1)S(1)}, bf16[128,4096]{1,0:T(8,128)(2,1)S(1)}, u32[]{:S(2)}, u32[]{:S(2)}) collective-permute-start(bf16[128,4096]{1,0:T(8,128)(2,1)S(1)} %get-tuple-element.167), channel_id=1, source_target_pairs={{0,2},{2,0},{4,6},{6,4},{8,10},{10,8},{12,14},{14,12},{16,18},{18,... | collective-permute-start | bytes 3145736 | tf_op jit(solution)/shard_map/ppermute | solution.py:428
  248.8 10.0 %copy-start.26 = (f32[4,4,128]{2,1,0:T(4,128)S(1)}, f32[4,4,128]{2,1,0:T(4,128)}, u32[]{:S(2)}) copy-start(f32[4,4,128]{2,1,0:T(4,128)} %get-tuple-element.183) | copy-start | bytes 24580
  248.8 10.2 %copy-start.25 = (f32[4,4,9,128]{3,2,1,0:T(8,128)S(1)}, f32[4,4,9,128]{3,2,1,0:T(8,128)}, u32[]{:S(2)}) copy-start(f32[4,4,9,128]{3,2,1,0:T(8,128)} %get-tuple-element.182) | copy-start | bytes 221188
  248.8 14.2 %collective-permute-start.35 = (bf16[128,4096]{1,0:T(8,128)(2,1)}, bf16[128,4096]{1,0:T(8,128)(2,1)S(1)}, u32[]{:S(2)}, u32[]{:S(2)}) collective-permute-start(bf16[128,4096]{1,0:T(8,128)(2,1)} %get-tuple-element.180), channel_id=1, source_target_pairs={{0,4},{2,10},{8,0},{10,18},{16,8},{18,26},{24,16},{26,30},{28,24},... | collective-permute-start | bytes 3145736 | tf_op jit(solution)/shard_map/ppermute | solution.py:425
  250.1 26.4 %collective-permute-start.36 = (bf16[128,4096]{1,0:T(8,128)(2,1)}, bf16[128,4096]{1,0:T(8,128)(2,1)S(1)}, u32[]{:S(2)}, u32[]{:S(2)}) collective-permute-start(bf16[128,4096]{1,0:T(8,128)(2,1)} %get-tuple-element.181), channel_id=1, source_target_pairs={{0,6},{2,8},{8,2},{10,16},{16,10},{18,24},{24,18},{26,28},{28,26},... | collective-permute-start | bytes 3145736 | tf_op jit(solution)/shard_map/ppermute | solution.py:425
  258.3 2.3 collective-permute-start.33
  258.4 3.0 %collective-permute-start.34 = (bf16[64,4096]{1,0:T(8,128)(2,1)}, bf16[64,4096]{1,0:T(8,128)(2,1)}, u32[]{:S(2)}, u32[]{:S(2)}) collective-permute-start(bf16[64,4096]{1,0:T(8,128)(2,1)} %get-tuple-element.179), channel_id=1, source_target_pairs={{0,2},{2,0},{4,6},{6,4},{8,10},{10,8},{12,14},{14,12},{16,18},{18,... | collective-permute-start | bytes 1572872 | tf_op jit(solution)/shard_map/ppermute | solution.py:428
  (18 other events, 49.7 us)

commit v10 on v9

--- a/solution.py
+++ b/solution.py
@@ -503,6 +503,7 @@
 
     first, met, later = [meet(d_proj[s]) for s in (half, half - 1, half - 2)]
     mixed_out = lax.all_to_all(mixed, "ctx", split_axis=0, concat_axis=0, tiled=True).reshape(-1, held)
+    first, grad_short, grad_long = stage((first, grad_short, grad_long))
     keep, *give = unproject(first, held, *((80, 48) if held == 128 else (held // 2, held // 2)))
     total = add_kernel([keep], [swap(x) for x in give])
     total, met, rest = stage((total, met, d_proj[: half - 2]))

time: 281 us -> 278 us (0.989)
  Pallas kernels: 97.1 us -> 93.8 us
  transfers between devices with their start and end apart: 39 -> 39, of which waited for: 27 -> 27; matrix products, arithmetic and copies ran while one was open for 2% -> 3% of each run, Pallas kernels for 26% -> 26%
where the time goes in v10:
time: 278 us; the launch traced here: 277 us
  waiting for transfers between devices  95.7 us (34%)
  Pallas kernels  93.8 us (34%)
  starting transfers between devices  50.8 us (18%)
  local copies, waits for them, and re-layouts  33.4 us (12%)
    ppermute x10, waiting for transfers between devices, one_way(): return lax.ppermute(x, 'ctx', hops)  52.4 us
    pallas_call x5, Pallas kernels, unproject_kernel(): pl.pallas_call(unproject_body, grid=(width // tile,), in_specs=[pl.BlockS...  36.5 us
    pallas_call x5, Pallas kernels, project_kernel(): pl.pallas_call(functools.partial(project_body, len(pieces)), grid=(4,), i...  32 us
    ppermute x10, waiting for transfers between devices, across(): return None if x is None else lax.ppermute(x, 'tp', [(0, 1), (1, 0)])  30.8 us
    unnamed x57, local copies, waits for them, and re-layouts  28.8 us
    pallas_call x1, Pallas kernels, mix(): pl.pallas_call(functools.partial(mix_body, count, sets, per_turn, grouped...  15.5 us
    ppermute x10, starting transfers between devices, one_way(): return lax.ppermute(x, 'ctx', hops)  14.3 us
    ppermute x17, waiting for transfers between devices, swap(): return lax.ppermute(x, 'ctx', [(d, d ^ 1) for d in range(n_ctx)])  12.5 us
  transfers between devices with their start and end apart: 39, of which 27 were waited for; matrix products, arithmetic and copies ran while one was open for 3% of the time, Pallas kernels for 26%

profile of v10, /device:TPU:1, one launch (start us, length us, event | category | flops | bytes accessed | tf_op | source)
XLA Modules:
  0.0 277.4 jit_solution(17174439730069960389)
XLA Ops:
  0.8 2.7 collective-permute-start.1
  8.3 2.2 copy-done.4
  10.4 2.2 copy-done.5
  12.6 2.2 copy-done.6
  14.8 1.7 shard_map.129
  16.6 4.3 %shard_map.130 = (bf16[768,256]{1,0:T(8,128)(2,1)S(1)}, bf16[768,256]{1,0:T(8,128)(2,1)S(1)}) custom-call(bf16[128,4096]{1,0:T(8,128)(2,1)S(1)} %copy-done.7, bf16[128,4096]{1,0:T(8,128)(2,1)S(1)} %collective-permute-done.2.refs_1_, bf16[1536,4096]{1,0:T(8,128)(2,1)S(1)} %bitcast.33), custom_call_target="tpu_custom_call" | custom-call | flops 1 | bytes 1 | tf_op jit(solution)/shard_map/pallas_call | solution.py:305
  20.9 5.6 %collective-permute-done.1 = bf16[128,4096]{1,0:T(8,128)(2,1)S(1)} collective-permute-done((bf16[128,4096]{1,0:T(8,128)(2,1)}, bf16[128,4096]{1,0:T(8,128)(2,1)S(1)}, u32[]{:S(2)}, u32[]{:S(2)}) %collective-permute-start.1) | collective-permute-done | bytes 1048608 | tf_op jit(solution)/shard_map/ppermute | solution.py:425
  28.0 1.4 collective-permute-start.3
  31.8 7.8 %shard_map.131 = (bf16[768,512]{1,0:T(8,128)(2,1)S(1)}, bf16[768,512]{1,0:T(8,128)(2,1)S(1)}) custom-call(bf16[256,4096]{1,0:T(8,128)(2,1)S(1)} %constant_dynamic-update-slice_fusion.refs_0_, bf16[256,4096]{1,0:T(8,128)(2,1)S(1)} %collective-permute-done.4.refs_1_, bf16[1536,4096]{1,0:T(8,128)(2,1)S(1)} %bitcast.34), custom_call_target="tpu_custom_call" | custom-call | flops 1 | bytes 1 | tf_op jit(solution)/shard_map/pallas_call | solution.py:305
  40.4 12.7 %collective-permute-done.3.refs_0_ = bf16[256,4096]{1,0:T(8,128)(2,1)S(1)} collective-permute-done((bf16[256,4096]{1,0:T(8,128)(2,1)S(1)}, bf16[256,4096]{1,0:T(8,128)(2,1)S(1)}, u32[]{:S(2)}, u32[]{:S(2)}) %collective-permute-start.3) | collective-permute-done | bytes 2097184 | tf_op jit(solution)/shard_map/ppermute | solution.py:425
  58.0 7.8 %shard_map.132 = (bf16[768,512]{1,0:T(8,128)(2,1)S(1)}, bf16[768,512]{1,0:T(8,128)(2,1)S(1)}) custom-call(bf16[256,4096]{1,0:T(8,128)(2,1)S(1)} %collective-permute-done.3.refs_0_, bf16[256,4096]{1,0:T(8,128)(2,1)S(1)} %collective-permute-done.7.refs_1_, bf16[1536,4096]{1,0:T(8,128)(2,1)S(1)} %bitcast.35), custom_call_target="tpu_custom_call" | custom-call | flops 1 | bytes 1 | tf_op jit(solution)/shard_map/pallas_call | solution.py:305
  65.7 8.2 %collective-permute-done.8 = bf16[768,512]{1,0:T(8,128)(2,1)S(1)} collective-permute-done((bf16[768,512]{1,0:T(8,128)(2,1)S(1)}, bf16[768,512]{1,0:T(8,128)(2,1)S(1)}, u32[]{:S(2)}, u32[]{:S(2)}) %collective-permute-start.8) | collective-permute-done | bytes 786464 | tf_op jit(solution)/shard_map/ppermute | solution.py:458
  74.0 5.7 %collective-permute-done.6.refs_0_ = bf16[256,4096]{1,0:T(8,128)(2,1)S(1)} collective-permute-done((bf16[256,4096]{1,0:T(8,128)(2,1)S(1)}, bf16[256,4096]{1,0:T(8,128)(2,1)S(1)}, u32[]{:S(2)}, u32[]{:S(2)}) %collective-permute-start.6) | collective-permute-done | bytes 2097184 | tf_op jit(solution)/shard_map/ppermute | solution.py:425
  80.3 1.4 collective-permute-start.9
  84.0 7.8 %shard_map.133 = (bf16[768,512]{1,0:T(8,128)(2,1)S(1)}, bf16[768,512]{1,0:T(8,128)(2,1)S(1)}) custom-call(bf16[256,4096]{1,0:T(8,128)(2,1)S(1)} %collective-permute-done.6.refs_0_, bf16[256,4096]{1,0:T(8,128)(2,1)S(1)} %collective-permute-done.10.refs_1_, bf16[1536,4096]{1,0:T(8,128)(2,1)S(1)} %bitcast.36), custom_call_target="tpu_custom_call" | custom-call | flops 1 | bytes 1 | tf_op jit(solution)/shard_map/pallas_call | solution.py:305
  92.7 2.0 collective-permute-done.9.refs_0_
  94.7 6.4 %all-to-all-start = ((bf16[16,256,128]{2,1,0:T(8,128)(2,1)}), bf16[16,256,128]{2,1,0:T(8,128)(2,1)}, u32[]{:S(2)}, u32[]{:S(2)}) async-start(bf16[16,256,128]{2,1,0:T(8,128)(2,1)} %bitcast.59), calls=%async_computation | async-start | bytes 2097152 | tf_op jit(solution)/shard_map/all_to_all | solution.py:487
  104.2 4.6 %copy-done.1 = bf16[2,3,256,4096]{3,2,1,0:T(8,128)(2,1)S(1)} copy-done((bf16[2,3,256,4096]{3,2,1,0:T(8,128)(2,1)S(1)}, bf16[2,3,256,4096]{3,2,1,0:T(8,128)(2,1)}, u32[]{:S(2)}) %copy-start.1) | copy-done | bytes 12582936
  108.8 4.3 %shard_map.134 = (bf16[768,256]{1,0:T(8,128)(2,1)S(1)}, bf16[768,256]{1,0:T(8,128)(2,1)S(1)}) custom-call(bf16[128,4096]{1,0:T(8,128)(2,1)S(1)} %collective-permute-done.9.refs_0_, bf16[64,4096]{1,0:T(8,128)(2,1)S(1)} %collective-permute-done.12.refs_1_, bf16[64,4096]{1,0:T(8,128)(2,1)S(1)} %collective-permute-done.13.refs_2_, bf16[1536,4096]{1,0:T(8,128)(2,1)S(1)} %bitcast.37), custom_call_target="tpu_custom_call" | custom-call | flops 1 | bytes 1 | tf_op jit(solution)/shard_map/pallas_call | solution.py:305
  115.1 5.6 %collective-permute-done.14 = bf16[768,512]{1,0:T(8,128)(2,1)S(1)} collective-permute-done((bf16[768,512]{1,0:T(8,128)(2,1)S(1)}, bf16[768,512]{1,0:T(8,128)(2,1)S(1)}, u32[]{:S(2)}, u32[]{:S(2)}) %collective-permute-start.14) | collective-permute-done | bytes 786464 | tf_op jit(solution)/shard_map/ppermute | solution.py:458
  120.7 8.4 %collective-permute-done.15 = bf16[768,256]{1,0:T(8,128)(2,1)S(1)} collective-permute-done((bf16[768,256]{1,0:T(8,128)(2,1)S(1)}, bf16[768,256]{1,0:T(8,128)(2,1)S(1)}, u32[]{:S(2)}, u32[]{:S(2)}) %collective-permute-start.15) | collective-permute-done | bytes 393248 | tf_op jit(solution)/shard_map/ppermute | solution.py:458
  129.9 15.5 %shard_map.135 = (bf16[16,256,128]{2,1,0:T(8,128)(2,1)}, bf16[3,256,256]{2,1,0:T(8,128)(2,1)}, bf16[3,256,512]{2,1,0:T(8,128)(2,1)}, bf16[3,256,512]{2,1,0:T(8,1...) custom-call(s32[16]{0:T(128)} %dynamic-slice_bitcast_fusion.order, ...), custom_call_target="tpu_custom_call" | custom-call | flops 1 | bytes 1 | tf_op jit(solution)/shard_map/pallas_call | solution.py:200
  146.7 7.0 %all-to-all-start.1 = ((bf16[16,256,128]{2,1,0:T(8,128)(2,1)}), bf16[16,256,128]{2,1,0:T(8,128)(2,1)S(1)}, u32[]{:S(2)}, u32[]{:S(2)}) async-start(bf16[16,256,128]{2,1,0:T(8,128)(2,1)} %get-tuple-element.156), calls=%async_computation.1 | async-start | bytes 2097152 | tf_op jit(solution)/shard_map/all_to_all | solution.py:505
  157.8 4.6 %copy-done.2 = bf16[2,3,256,4096]{3,2,1,0:T(8,128)(2,1)S(1)} copy-done((bf16[2,3,256,4096]{3,2,1,0:T(8,128)(2,1)S(1)}, bf16[2,3,256,4096]{3,2,1,0:T(8,128)(2,1)}, u32[]{:S(2)}) %copy-start.2) | copy-done | bytes 12582936
  162.3 5.2 %shard_map.136 = (bf16[128,4096]{1,0:T(8,128)(2,1)S(1)}, bf16[80,4096]{1,0:T(8,128)(2,1)S(1)}, bf16[48,4096]{1,0:T(8,128)(2,1)S(1)}) custom-call(bf16[768,256]{1,0:T(8,128)(2,1)S(1)} %bitcast.57, bf16[768,256]{1,0:T(8,128)(2,1)S(1)} %collective-permute-done.16.far_ref, bf16[1536,4096]{1,0:T(8,128)(2,1)S(1)} %bitcast.38), custom_call_target="tpu_custom_call" | custom-call | flops 1 | bytes 1 | tf_op jit(solution)/shard_map/pallas_call | solution.py:342
  168.1 1.6 collective-permute-start.22
  170.8 2.6 collective-permute-done.19.far_ref
  174.4 8.7 %shard_map.138 = (bf16[256,4096]{1,0:T(8,128)(2,1)S(1)}, bf16[96,4096]{1,0:T(8,128)(2,1)S(1)}, bf16[96,4096]{1,0:T(8,128)(2,1)S(1)}, bf16[64,4096]{1,0:T(8,128)(2,1)S(1)}) custom-call(bf16[768,512]{1,0:T(8,128)(2,1)S(1)} %bitcast.51, bf16[768,512]{1,0:T(8,128)(2,1)S(1)} %collective-permute-done.19.far_ref, bf16[1536,4096]{1,0:T(8,128)(2,1)S(1)} %bitcast.39), custom_call_target="tpu_custom_call" | custom-call | flops 1 | bytes 1 | tf_op jit(solution)/shard_map/pallas_call | solution.py:342
  183.1 1.9 collective-permute-start.20
  185.1 5.2 %collective-permute-done.22.far_ref = bf16[768,512]{1,0:T(8,128)(2,1)S(1)} collective-permute-done((bf16[768,512]{1,0:T(8,128)(2,1)S(1)}, bf16[768,512]{1,0:T(8,128)(2,1)S(1)}, u32[]{:S(2)}, u32[]{:S(2)}) %collective-permute-start.22) | collective-permute-done | bytes 786464 | tf_op jit(solution)/shard_map/ppermute | solution.py:458
  191.8 1.5 collective-permute-done.23.refs_3_
  197.1 4.6 %copy-done.3 = bf16[2,3,256,4096]{3,2,1,0:T(8,128)(2,1)S(1)} copy-done((bf16[2,3,256,4096]{3,2,1,0:T(8,128)(2,1)S(1)}, bf16[2,3,256,4096]{3,2,1,0:T(8,128)(2,1)}, u32[]{:S(2)}) %copy-start.3) | copy-done | bytes 12582936
  204.0 8.7 %shard_map.140 = (bf16[256,4096]{1,0:T(8,128)(2,1)S(1)}, bf16[128,4096]{1,0:T(8,128)(2,1)S(1)}, bf16[128,4096]{1,0:T(8,128)(2,1)S(1)}) custom-call(bf16[768,512]{1,0:T(8,128)(2,1)S(1)} %bitcast.47, bf16[768,512]{1,0:T(8,128)(2,1)S(1)} %copy-done.15, bf16[1536,4096]{1,0:T(8,128)(2,1)S(1)} %bitcast.40), custom_call_target="tpu_custom_call" | custom-call | flops 1 | bytes 1 | tf_op jit(solution)/shard_map/pallas_call | solution.py:342
  214.5 1.5 collective-permute-start.27
  216.1 1.5 shard_map.142
  218.4 1.5 collective-permute-done.28.refs_3_
  219.8 1.4 shard_map.141
  223.8 8.7 %shard_map.143 = (bf16[256,4096]{1,0:T(8,128)(2,1)S(1)}, bf16[128,4096]{1,0:T(8,128)(2,1)S(1)}, bf16[128,4096]{1,0:T(8,128)(2,1)S(1)}) custom-call(bf16[768,512]{1,0:T(8,128)(2,1)S(1)} %bitcast.45, bf16[768,512]{1,0:T(8,128)(2,1)S(1)} %collective-permute-done.26.far_ref, bf16[1536,4096]{1,0:T(8,128)(2,1)S(1)} %bitcast.41), custom_call_target="tpu_custom_call" | custom-call | flops 1 | bytes 1 | tf_op jit(solution)/shard_map/pallas_call | solution.py:342
  232.5 1.9 collective-permute-start.29
  234.6 2.2 collective-permute-done.29.refs_1_
  236.7 1.5 collective-permute-done.31.refs_2_
  238.2 8.2 %collective-permute-done.32.refs_3_ = bf16[256,4096]{1,0:T(8,128)(2,1)S(1)} collective-permute-done((bf16[256,4096]{1,0:T(8,128)(2,1)S(1)}, bf16[256,4096]{1,0:T(8,128)(2,1)S(1)}, u32[]{:S(2)}, u32[]{:S(2)}) %collective-permute-start.32) | collective-permute-done | bytes 2097184 | tf_op jit(solution)/shard_map/ppermute | solution.py:425
  246.5 1.4 shard_map.144
  249.2 2.5 collective-permute-start.36
  251.6 5.2 %shard_map.145 = (bf16[128,4096]{1,0:T(8,128)(2,1)S(1)}, bf16[64,4096]{1,0:T(8,128)(2,1)S(1)}, bf16[64,4096]{1,0:T(8,128)(2,1)S(1)}) custom-call(bf16[768,256]{1,0:T(8,128)(2,1)S(1)} %bitcast.54, bf16[768,256]{1,0:T(8,128)(2,1)S(1)} %collective-permute-done.30.far_ref, bf16[1536,4096]{1,0:T(8,128)(2,1)S(1)} %bitcast.42), custom_call_target="tpu_custom_call" | custom-call | flops 1 | bytes 1 | tf_op jit(solution)/shard_map/pallas_call | solution.py:342
  259.5 2.3 collective-permute-done.35.refs_3_
  261.8 13.5 %collective-permute-done.36.refs_4_ = bf16[128,4096]{1,0:T(8,128)(2,1)S(1)} collective-permute-done((bf16[128,4096]{1,0:T(8,128)(2,1)S(1)}, bf16[128,4096]{1,0:T(8,128)(2,1)S(1)}, u32[]{:S(2)}, u32[]{:S(2)}) %collective-permute-start.36) | collective-permute-done | bytes 1048608 | tf_op jit(solution)/shard_map/ppermute | solution.py:425
  275.3 2.1 shard_map.146
  (118 shorter events, 48.9 us)
Async XLA Ops:
  0.6 15.9 %collective-permute-start.2 = (bf16[128,4096]{1,0:T(8,128)(2,1)}, bf16[128,4096]{1,0:T(8,128)(2,1)S(1)}, u32[]{:S(2)}, u32[]{:S(2)}) collective-permute-start(bf16[128,4096]{1,0:T(8,128)(2,1)} %refs_0_.3), channel_id=1, source_target_pairs={{0,2},{2,0},{4,6},{6,4},{8,10},{10,8},{12,14},{14,12},{16,18},{18,... | collective-permute-start | bytes 3145736 | tf_op jit(solution)/shard_map/ppermute | solution.py:428
  0.8 25.7 %collective-permute-start.1 = (bf16[128,4096]{1,0:T(8,128)(2,1)}, bf16[128,4096]{1,0:T(8,128)(2,1)S(1)}, u32[]{:S(2)}, u32[]{:S(2)}) collective-permute-start(bf16[128,4096]{1,0:T(8,128)(2,1)} %refs_0_.3), channel_id=1, source_target_pairs={{0,6},{2,8},{8,2},{10,16},{16,10},{18,24},{24,18},{26,28},{28,26},... | collective-permute-start | bytes 3145736 | tf_op jit(solution)/shard_map/ppermute | solution.py:425
  3.5 23.9 %collective-permute-start = (bf16[128,4096]{1,0:T(8,128)(2,1)}, bf16[128,4096]{1,0:T(8,128)(2,1)S(1)}, u32[]{:S(2)}, u32[]{:S(2)}) collective-permute-start(bf16[128,4096]{1,0:T(8,128)(2,1)} %refs_0_.3), channel_id=1, source_target_pairs={{0,8},{2,6},{8,16},{10,2},{16,24},{18,10},{24,28},{26,18},{28,20},... | collective-permute-start | bytes 3145736 | tf_op jit(solution)/shard_map/ppermute | solution.py:425
  16.5 67.5 %copy-start = (bf16[2,3,256,4096]{3,2,1,0:T(8,128)(2,1)}, bf16[2,3,256,4096]{3,2,1,0:T(8,128)(2,1)S(1)}, u32[]{:S(2)}) copy-start(bf16[2,3,256,4096]{3,2,1,0:T(8,128)(2,1)S(1)} %shard_map.129) | copy-start | bytes 37748740
  27.6 4.2 %collective-permute-start.4 = (bf16[256,4096]{1,0:T(8,128)(2,1)S(1)}, bf16[256,4096]{1,0:T(8,128)(2,1)S(1)}, u32[]{:S(2)}, u32[]{:S(2)}) collective-permute-start(bf16[256,4096]{1,0:T(8,128)(2,1)S(1)} %constant_dynamic-update-slice_fusion.refs_0_), channel_id=1, source_target_pairs={{0,2},{2,0},{4,6},{6,4},{8,10},{10,8},{12,14},{14,12},{16,18},{18,... | collective-permute-start | bytes 6291464 | tf_op jit(solution)/shard_map/ppermute | solution.py:428
  28.0 25.2 %collective-permute-start.3 = (bf16[256,4096]{1,0:T(8,128)(2,1)S(1)}, bf16[256,4096]{1,0:T(8,128)(2,1)S(1)}, u32[]{:S(2)}, u32[]{:S(2)}) collective-permute-start(bf16[256,4096]{1,0:T(8,128)(2,1)S(1)} %constant_dynamic-update-slice_fusion.refs_0_), channel_id=1, source_target_pairs={{0,8},{2,6},{8,16},{10,2},{16,24},{18,10},{24,28},{26,18},{28,20},... | collective-permute-start | bytes 6291464 | tf_op jit(solution)/shard_map/ppermute | solution.py:425
  29.4 11.1 %collective-permute-start.5 = (bf16[768,256]{1,0:T(8,128)(2,1)S(1)}, bf16[768,256]{1,0:T(8,128)(2,1)S(1)}, u32[]{:S(2)}, u32[]{:S(2)}) collective-permute-start(bf16[768,256]{1,0:T(8,128)(2,1)S(1)} %get-tuple-element.109), channel_id=1, source_target_pairs={{0,1},{1,0},{2,3},{3,2},{4,5},{5,4},{6,7},{7,6},{8,9},{9,8},{10,11... | collective-permute-start | bytes 1179656 | tf_op jit(solution)/shard_map/ppermute | solution.py:458
  40.4 16.3 %copy-start.23 = (bf16[768,256]{1,0:T(8,128)(2,1)}, bf16[768,256]{1,0:T(8,128)(2,1)S(1)}, u32[]{:S(2)}) copy-start(bf16[768,256]{1,0:T(8,128)(2,1)S(1)} %collective-permute-done.5) | copy-start | bytes 1179652
  53.2 4.8 %collective-permute-start.7 = (bf16[256,4096]{1,0:T(8,128)(2,1)S(1)}, bf16[256,4096]{1,0:T(8,128)(2,1)S(1)}, u32[]{:S(2)}, u32[]{:S(2)}) collective-permute-start(bf16[256,4096]{1,0:T(8,128)(2,1)S(1)} %collective-permute-done.3.refs_0_), channel_id=1, source_target_pairs={{0,2},{2,0},{4,6},{6,4},{8,10},{10,8},{12,14},{14,12},{16,18},{18,... | collective-permute-start | bytes 6291464 | tf_op jit(solution)/shard_map/ppermute | solution.py:428
  54.2 25.5 %collective-permute-start.6 = (bf16[256,4096]{1,0:T(8,128)(2,1)S(1)}, bf16[256,4096]{1,0:T(8,128)(2,1)S(1)}, u32[]{:S(2)}, u32[]{:S(2)}) collective-permute-start(bf16[256,4096]{1,0:T(8,128)(2,1)S(1)} %collective-permute-done.3.refs_0_), channel_id=1, source_target_pairs={{0,8},{2,6},{8,16},{10,2},{16,24},{18,10},{24,28},{26,18},{28,20},... | collective-permute-start | bytes 6291464 | tf_op jit(solution)/shard_map/ppermute | solution.py:425
  55.5 18.4 %collective-permute-start.8 = (bf16[768,512]{1,0:T(8,128)(2,1)S(1)}, bf16[768,512]{1,0:T(8,128)(2,1)S(1)}, u32[]{:S(2)}, u32[]{:S(2)}) collective-permute-start(bf16[768,512]{1,0:T(8,128)(2,1)S(1)} %get-tuple-element.114), channel_id=1, source_target_pairs={{0,1},{1,0},{2,3},{3,2},{4,5},{5,4},{6,7},{7,6},{8,9},{9,8},{10,11... | collective-permute-start | bytes 2359304 | tf_op jit(solution)/shard_map/ppermute | solution.py:458
  65.7 26.0 %copy-start.12 = (bf16[768,512]{1,0:T(8,128)(2,1)}, bf16[768,512]{1,0:T(8,128)(2,1)S(1)}, u32[]{:S(2)}) copy-start(bf16[768,512]{1,0:T(8,128)(2,1)S(1)} %get-tuple-element.123) | copy-start | bytes 2359300
  74.0 17.8 %copy-start.21 = (bf16[768,512]{1,0:T(8,128)(2,1)}, bf16[768,512]{1,0:T(8,128)(2,1)S(1)}, u32[]{:S(2)}) copy-start(bf16[768,512]{1,0:T(8,128)(2,1)S(1)} %collective-permute-done.8) | copy-start | bytes 2359300
  79.7 4.3 %collective-permute-start.10 = (bf16[256,4096]{1,0:T(8,128)(2,1)S(1)}, bf16[256,4096]{1,0:T(8,128)(2,1)S(1)}, u32[]{:S(2)}, u32[]{:S(2)}) collective-permute-start(bf16[256,4096]{1,0:T(8,128)(2,1)S(1)} %collective-permute-done.6.refs_0_), channel_id=1, source_target_pairs={{0,2},{2,0},{4,6},{6,4},{8,10},{10,8},{12,14},{14,12},{16,18},{18,... | collective-permute-start | bytes 6291464 | tf_op jit(solution)/shard_map/ppermute | solution.py:428
  80.3 14.4 %collective-permute-start.9 = (bf16[128,4096]{1,0:T(8,128)(2,1)S(1)}, bf16[128,4096]{1,0:T(8,128)(2,1)S(1)}, u32[]{:S(2)}, u32[]{:S(2)}) collective-permute-start(bf16[128,4096]{1,0:T(8,128)(2,1)S(1)} %slice.34), channel_id=1, source_target_pairs={{0,8},{2,6},{8,16},{10,2},{16,24},{18,10},{24,28},{26,18},{28,20},... | collective-permute-start | bytes 3145736 | tf_op jit(solution)/shard_map/ppermute | solution.py:425
  81.7 19.4 %collective-permute-start.11 = (bf16[768,512]{1,0:T(8,128)(2,1)S(1)}, bf16[768,512]{1,0:T(8,128)(2,1)}, u32[]{:S(2)}, u32[]{:S(2)}) collective-permute-start(bf16[768,512]{1,0:T(8,128)(2,1)S(1)} %get-tuple-element.122), channel_id=1, source_target_pairs={{0,1},{1,0},{2,3},{3,2},{4,5},{5,4},{6,7},{7,6},{8,9},{9,8},{10,11... | collective-permute-start | bytes 2359304 | tf_op jit(solution)/shard_map/ppermute | solution.py:458
  94.7 34.4 %all-to-all-start = ((bf16[16,256,128]{2,1,0:T(8,128)(2,1)}), bf16[16,256,128]{2,1,0:T(8,128)(2,1)}, u32[]{:S(2)}, u32[]{:S(2)}) async-start(bf16[16,256,128]{2,1,0:T(8,128)(2,1)} %bitcast.59), calls=%async_computation | async-start | bytes 2097152 | tf_op jit(solution)/shard_map/all_to_all | solution.py:487
  101.2 2.2 collective-permute-start.13
  101.9 2.3 collective-permute-start.12
  102.0 18.7 %collective-permute-start.14 = (bf16[768,512]{1,0:T(8,128)(2,1)S(1)}, bf16[768,512]{1,0:T(8,128)(2,1)S(1)}, u32[]{:S(2)}, u32[]{:S(2)}) collective-permute-start(bf16[768,512]{1,0:T(8,128)(2,1)S(1)} %get-tuple-element.130), channel_id=1, source_target_pairs={{0,1},{1,0},{2,3},{3,2},{4,5},{5,4},{6,7},{7,6},{8,9},{9,8},{10,11... | collective-permute-start | bytes 2359304 | tf_op jit(solution)/shard_map/ppermute | solution.py:458
  113.9 15.2 %collective-permute-start.15 = (bf16[768,256]{1,0:T(8,128)(2,1)S(1)}, bf16[768,256]{1,0:T(8,128)(2,1)S(1)}, u32[]{:S(2)}, u32[]{:S(2)}) collective-permute-start(bf16[768,256]{1,0:T(8,128)(2,1)S(1)} %get-tuple-element.131), channel_id=1, source_target_pairs={{0,1},{1,0},{2,3},{3,2},{4,5},{5,4},{6,7},{7,6},{8,9},{9,8},{10,11... | collective-permute-start | bytes 1179656 | tf_op jit(solution)/shard_map/ppermute | solution.py:458
  120.7 8.4 %copy-start.22 = (bf16[768,512]{1,0:T(8,128)(2,1)}, bf16[768,512]{1,0:T(8,128)(2,1)S(1)}, u32[]{:S(2)}) copy-start(bf16[768,512]{1,0:T(8,128)(2,1)S(1)} %collective-permute-done.14) | copy-start | bytes 2359300
  145.4 8.3 %copy-start.13 = (bf16[3,256,512]{2,1,0:T(8,128)(2,1)S(1)}, bf16[3,256,512]{2,1,0:T(8,128)(2,1)}, u32[]{:S(2)}) copy-start(bf16[3,256,512]{2,1,0:T(8,128)(2,1)} %get-tuple-element.140) | copy-start | bytes 2359300
  145.4 8.6 %copy-start.26 = (f32[4,4,128]{2,1,0:T(4,128)S(1)}, f32[4,4,128]{2,1,0:T(4,128)}, u32[]{:S(2)}) copy-start(f32[4,4,128]{2,1,0:T(4,128)} %get-tuple-element.134) | copy-start | bytes 24580
  145.4 10.1 %copy-start.25 = (f32[4,4,9,128]{3,2,1,0:T(8,128)S(1)}, f32[4,4,9,128]{3,2,1,0:T(8,128)}, u32[]{:S(2)}) copy-start(f32[4,4,9,128]{3,2,1,0:T(8,128)} %get-tuple-element.133) | copy-start | bytes 221188
  145.4 12.3 %copy-start.19 = (bf16[3,256,256]{2,1,0:T(8,128)(2,1)S(1)}, bf16[3,256,256]{2,1,0:T(8,128)(2,1)}, u32[]{:S(2)}) copy-start(bf16[3,256,256]{2,1,0:T(8,128)(2,1)} %get-tuple-element.132) | copy-start | bytes 1179652
  145.4 12.3 %collective-permute-start.16 = (bf16[768,256]{1,0:T(8,128)(2,1)}, bf16[768,256]{1,0:T(8,128)(2,1)S(1)}, u32[]{:S(2)}, u32[]{:S(2)}) collective-permute-start(bf16[768,256]{1,0:T(8,128)(2,1)} %bitcast.56), channel_id=1, source_target_pairs={{0,1},{1,0},{2,3},{3,2},{4,5},{5,4},{6,7},{7,6},{8,9},{9,8},{10,11... | collective-permute-start | bytes 1179656 | tf_op jit(solution)/shard_map/ppermute | solution.py:458
  146.7 47.9 %all-to-all-start.1 = ((bf16[16,256,128]{2,1,0:T(8,128)(2,1)}), bf16[16,256,128]{2,1,0:T(8,128)(2,1)S(1)}, u32[]{:S(2)}, u32[]{:S(2)}) async-start(bf16[16,256,128]{2,1,0:T(8,128)(2,1)} %get-tuple-element.156), calls=%async_computation.1 | async-start | bytes 2097152 | tf_op jit(solution)/shard_map/all_to_all | solution.py:505
  153.7 19.7 %collective-permute-start.19 = (bf16[768,512]{1,0:T(8,128)(2,1)S(1)}, bf16[768,512]{1,0:T(8,128)(2,1)S(1)}, u32[]{:S(2)}, u32[]{:S(2)}) collective-permute-start(bf16[768,512]{1,0:T(8,128)(2,1)S(1)} %bitcast.50), channel_id=1, source_target_pairs={{0,1},{1,0},{2,3},{3,2},{4,5},{5,4},{6,7},{7,6},{8,9},{9,8},{10,11... | collective-permute-start | bytes 2359304 | tf_op jit(solution)/shard_map/ppermute | solution.py:458
  167.5 2.7 collective-permute-start.17
  167.9 2.3 collective-permute-start.18
  168.1 22.2 %collective-permute-start.22 = (bf16[768,512]{1,0:T(8,128)(2,1)S(1)}, bf16[768,512]{1,0:T(8,128)(2,1)S(1)}, u32[]{:S(2)}, u32[]{:S(2)}) collective-permute-start(bf16[768,512]{1,0:T(8,128)(2,1)S(1)} %bitcast.46), channel_id=1, source_target_pairs={{0,1},{1,0},{2,3},{3,2},{4,5},{5,4},{6,7},{7,6},{8,9},{9,8},{10,11... | collective-permute-start | bytes 2359304 | tf_op jit(solution)/shard_map/ppermute | solution.py:458
  173.4 19.9 %collective-permute-start.24 = (bf16[128,4096]{1,0:T(8,128)(2,1)S(1)}, bf16[128,4096]{1,0:T(8,128)(2,1)S(1)}, u32[]{:S(2)}, u32[]{:S(2)}) collective-permute-start(bf16[128,4096]{1,0:T(8,128)(2,1)S(1)} %shard_map.137), channel_id=1, source_target_pairs={{0,4},{2,10},{8,0},{10,18},{16,8},{18,26},{24,16},{26,30},{28,24},... | collective-permute-start | bytes 3145736 | tf_op jit(solution)/shard_map/ppermute | solution.py:425
  183.1 10.2 %collective-permute-start.20 = (bf16[96,4096]{1,0:T(8,128)(2,1)S(1)}, bf16[96,4096]{1,0:T(8,128)(2,1)S(1)}, u32[]{:S(2)}, u32[]{:S(2)}) collective-permute-start(bf16[96,4096]{1,0:T(8,128)(2,1)S(1)} %get-tuple-element.146), channel_id=1, source_target_pairs={{0,2},{2,0},{4,6},{6,4},{8,10},{10,8},{12,14},{14,12},{16,18},{18,... | collective-permute-start | bytes 2359304 | tf_op jit(solution)/shard_map/ppermute | solution.py:428
  185.0 8.4 %collective-permute-start.21 = (bf16[96,4096]{1,0:T(8,128)(2,1)S(1)}, bf16[96,4096]{1,0:T(8,128)(2,1)S(1)}, u32[]{:S(2)}, u32[]{:S(2)}) collective-permute-start(bf16[96,4096]{1,0:T(8,128)(2,1)S(1)} %get-tuple-element.147), channel_id=1, source_target_pairs={{0,2},{2,0},{4,6},{6,4},{8,10},{10,8},{12,14},{14,12},{16,18},{18,... | collective-permute-start | bytes 2359304 | tf_op jit(solution)/shard_map/ppermute | solution.py:428
  191.2 2.2 collective-permute-start.23
  194.6 25.2 %collective-permute-start.28 = (bf16[256,4096]{1,0:T(8,128)(2,1)S(1)}, bf16[256,4096]{1,0:T(8,128)(2,1)S(1)}, u32[]{:S(2)}, u32[]{:S(2)}) collective-permute-start(bf16[256,4096]{1,0:T(8,128)(2,1)S(1)} %shard_map.139), channel_id=1, source_target_pairs={{0,4},{2,10},{8,0},{10,18},{16,8},{18,26},{24,16},{26,30},{28,24},... | collective-permute-start | bytes 6291464 | tf_op jit(solution)/shard_map/ppermute | solution.py:425
  195.9 18.6 %collective-permute-start.26 = (bf16[768,512]{1,0:T(8,128)(2,1)}, bf16[768,512]{1,0:T(8,128)(2,1)S(1)}, u32[]{:S(2)}, u32[]{:S(2)}) collective-permute-start(bf16[768,512]{1,0:T(8,128)(2,1)} %bitcast.44), channel_id=1, source_target_pairs={{0,1},{1,0},{2,3},{3,2},{4,5},{5,4},{6,7},{7,6},{8,9},{9,8},{10,11... | collective-permute-start | bytes 2359304 | tf_op jit(solution)/shard_map/ppermute | solution.py:458
  212.7 4.9 %collective-permute-start.25 = (bf16[128,4096]{1,0:T(8,128)(2,1)S(1)}, bf16[128,4096]{1,0:T(8,128)(2,1)S(1)}, u32[]{:S(2)}, u32[]{:S(2)}) collective-permute-start(bf16[128,4096]{1,0:T(8,128)(2,1)S(1)} %get-tuple-element.160), channel_id=1, source_target_pairs={{0,2},{2,0},{4,6},{6,4},{8,10},{10,8},{12,14},{14,12},{16,18},{18,... | collective-permute-start | bytes 3145736 | tf_op jit(solution)/shard_map/ppermute | solution.py:428
  214.5 3.8 %collective-permute-start.27 = (bf16[128,4096]{1,0:T(8,128)(2,1)S(1)}, bf16[128,4096]{1,0:T(8,128)(2,1)S(1)}, u32[]{:S(2)}, u32[]{:S(2)}) collective-permute-start(bf16[128,4096]{1,0:T(8,128)(2,1)S(1)} %get-tuple-element.163), channel_id=1, source_target_pairs={{0,2},{2,0},{4,6},{6,4},{8,10},{10,8},{12,14},{14,12},{16,18},{18,... | collective-permute-start | bytes 3145736 | tf_op jit(solution)/shard_map/ppermute | solution.py:428
  221.2 25.2 %collective-permute-start.32 = (bf16[256,4096]{1,0:T(8,128)(2,1)S(1)}, bf16[256,4096]{1,0:T(8,128)(2,1)S(1)}, u32[]{:S(2)}, u32[]{:S(2)}) collective-permute-start(bf16[256,4096]{1,0:T(8,128)(2,1)S(1)} %shard_map.141), channel_id=1, source_target_pairs={{0,4},{2,10},{8,0},{10,18},{16,8},{18,26},{24,16},{26,30},{28,24},... | collective-permute-start | bytes 6291464 | tf_op jit(solution)/shard_map/ppermute | solution.py:425
  222.5 11.9 %collective-permute-start.30 = (bf16[768,256]{1,0:T(8,128)(2,1)S(1)}, bf16[768,256]{1,0:T(8,128)(2,1)S(1)}, u32[]{:S(2)}, u32[]{:S(2)}) collective-permute-start(bf16[768,256]{1,0:T(8,128)(2,1)S(1)} %bitcast.53), channel_id=1, source_target_pairs={{0,1},{1,0},{2,3},{3,2},{4,5},{5,4},{6,7},{7,6},{8,9},{9,8},{10,11... | collective-permute-start | bytes 1179656 | tf_op jit(solution)/shard_map/ppermute | solution.py:458
  232.5 4.2 %collective-permute-start.29 = (bf16[128,4096]{1,0:T(8,128)(2,1)S(1)}, bf16[128,4096]{1,0:T(8,128)(2,1)S(1)}, u32[]{:S(2)}, u32[]{:S(2)}) collective-permute-start(bf16[128,4096]{1,0:T(8,128)(2,1)S(1)} %get-tuple-element.172), channel_id=1, source_target_pairs={{0,2},{2,0},{4,6},{6,4},{8,10},{10,8},{12,14},{14,12},{16,18},{18,... | collective-permute-start | bytes 3145736 | tf_op jit(solution)/shard_map/ppermute | solution.py:428
  234.5 3.8 %collective-permute-start.31 = (bf16[128,4096]{1,0:T(8,128)(2,1)S(1)}, bf16[128,4096]{1,0:T(8,128)(2,1)S(1)}, u32[]{:S(2)}, u32[]{:S(2)}) collective-permute-start(bf16[128,4096]{1,0:T(8,128)(2,1)S(1)} %get-tuple-element.175), channel_id=1, source_target_pairs={{0,2},{2,0},{4,6},{6,4},{8,10},{10,8},{12,14},{14,12},{16,18},{18,... | collective-permute-start | bytes 3145736 | tf_op jit(solution)/shard_map/ppermute | solution.py:428
  247.8 14.0 %collective-permute-start.35 = (bf16[128,4096]{1,0:T(8,128)(2,1)S(1)}, bf16[128,4096]{1,0:T(8,128)(2,1)S(1)}, u32[]{:S(2)}, u32[]{:S(2)}) collective-permute-start(bf16[128,4096]{1,0:T(8,128)(2,1)S(1)} %get-tuple-element.188), channel_id=1, source_target_pairs={{0,4},{2,10},{8,0},{10,18},{16,8},{18,26},{24,16},{26,30},{28,24},... | collective-permute-start | bytes 3145736 | tf_op jit(solution)/shard_map/ppermute | solution.py:425
  249.2 26.2 %collective-permute-start.36 = (bf16[128,4096]{1,0:T(8,128)(2,1)S(1)}, bf16[128,4096]{1,0:T(8,128)(2,1)S(1)}, u32[]{:S(2)}, u32[]{:S(2)}) collective-permute-start(bf16[128,4096]{1,0:T(8,128)(2,1)S(1)} %get-tuple-element.189), channel_id=1, source_target_pairs={{0,6},{2,8},{8,2},{10,16},{16,10},{18,24},{24,18},{26,28},{28,26},... | collective-permute-start | bytes 3145736 | tf_op jit(solution)/shard_map/ppermute | solution.py:425
  256.8 2.0 collective-permute-start.33
  256.9 2.6 collective-permute-start.34
  (18 other events, 47.5 us)

commit v11 on v10

--- a/solution.py
+++ b/solution.py
@@ -103,10 +103,11 @@
                         part = part + proj_refs[s][a][i, mine[j], h * LONG : (h + 1) * LONG].astype(F32)
                     p_s[j, i, pl.ds(at, GROUP), :] = part.astype(BF16)
 
-        for j in every:
-            for i in range(3):
-                two_blocks = jnp.concatenate([p_s[j, i, GROUP:, :], p_s[j, i, :rows, :]], axis=1)
-                m_s[j, i] = dot(two_blocks, past_ref[...], ((1,), (0,))).astype(BF16)
+        signals = [(j, i) for j in every for i in range(3)]
+        two_blocks = [jnp.concatenate([p_s[j, i, GROUP:, :], p_s[j, i, :rows, :]], axis=1) for j, i in signals]
+        past = dot(jnp.concatenate(two_blocks, axis=0), past_ref[...], ((1,), (0,))).astype(BF16)
+        for n, (j, i) in enumerate(signals):
+            m_s[j, i] = past[n * rows : (n + 1) * rows]
         for j in every:
             for at in at_block:
                 feat = []
@@ -166,16 +167,15 @@
             for i in range(3):
                 for k in range(SHORT):
                     gs_ref[0, lines[j], 3 * i + k : 3 * i + k + 1, :] = jnp.sum(sums[i][k], axis=0, keepdims=True)
-        for j in every:
-            for i in range(3):
-                two_blocks = jnp.concatenate([d_s[j, i, :rows, :], d_s[j, i, GROUP:, :]], axis=1)
-                coming = dot(two_blocks, next_ref[...], ((1,), (0,)))
-                for at in at_block:
-                    here = d_s[j, i, at, :].astype(F32)
-                    near, far = coming[at, :LONG], coming[at, LONG:]
-                    e_s[j, i, at, :] = (
-                        taps[j][i][0] * here + taps[j][i][1] * near + taps[j][i][2] * far
-                    ).astype(BF16)
+        two_blocks = [jnp.concatenate([d_s[j, i, :rows, :], d_s[j, i, GROUP:, :]], axis=1) for j, i in signals]
+        coming = dot(jnp.concatenate(two_blocks, axis=0), next_ref[...], ((1,), (0,)))
+        for n, (j, i) in enumerate(signals):
+            for at in at_block:
+                here = d_s[j, i, at, :].astype(F32)
+                moved = coming[n * rows + at.start : n * rows + at.stop]
+                e_s[j, i, at, :] = (
+                    taps[j][i][0] * here + taps[j][i][1] * moved[:, :LONG] + taps[j][i][2] * moved[:, LONG:]
+                ).astype(BF16)
         for a, h, where in d_places:
             at = pl.multiple_of(order[where] * GROUP, GROUP)
             for j in every:

time: 278 us -> 279 us (level)
  no operation moved by 1% of the time
where the time goes in v11:
time: 279 us; the launch traced here: 278 us
  waiting for transfers between devices  95.7 us (34%)
  Pallas kernels  94.6 us (34%)
  starting transfers between devices  50.7 us (18%)
  local copies, waits for them, and re-layouts  33.4 us (12%)
    ppermute x10, waiting for transfers between devices, one_way(): return lax.ppermute(x, 'ctx', hops)  52.4 us
    pallas_call x5, Pallas kernels, unproject_kernel(): pl.pallas_call(unproject_body, grid=(width // tile,), in_specs=[pl.BlockS...  36.5 us
    pallas_call x5, Pallas kernels, project_kernel(): pl.pallas_call(functools.partial(project_body, len(pieces)), grid=(4,), i...  32 us
    ppermute x10, waiting for transfers between devices, across(): return None if x is None else lax.ppermute(x, 'tp', [(0, 1), (1, 0)])  30.7 us
    unnamed x57, local copies, waits for them, and re-layouts  28.8 us
    pallas_call x1, Pallas kernels, mix(): pl.pallas_call(functools.partial(mix_body, count, sets, per_turn, grouped...  16.3 us
    ppermute x10, starting transfers between devices, one_way(): return lax.ppermute(x, 'ctx', hops)  14.2 us
    ppermute x17, waiting for transfers between devices, swap(): return lax.ppermute(x, 'ctx', [(d, d ^ 1) for d in range(n_ctx)])  12.5 us
  transfers between devices with their start and end apart: 39, of which 27 were waited for; matrix products, arithmetic and copies ran while one was open for 3% of the time, Pallas kernels for 26%

profile of v11, /device:TPU:1, one launch (start us, length us, event | category | flops | bytes accessed | tf_op | source)
XLA Modules:
  0.0 278.1 jit_solution(12352975047830775464)
XLA Ops:
  0.8 2.7 collective-permute-start.1
  8.3 2.2 copy-done.4
  10.4 2.2 copy-done.5
  12.6 2.2 copy-done.6
  14.8 1.7 shard_map.129
  16.6 4.3 %shard_map.130 = (bf16[768,256]{1,0:T(8,128)(2,1)S(1)}, bf16[768,256]{1,0:T(8,128)(2,1)S(1)}) custom-call(bf16[128,4096]{1,0:T(8,128)(2,1)S(1)} %copy-done.7, bf16[128,4096]{1,0:T(8,128)(2,1)S(1)} %collective-permute-done.2.refs_1_, bf16[1536,4096]{1,0:T(8,128)(2,1)S(1)} %bitcast.33), custom_call_target="tpu_custom_call" | custom-call | flops 1 | bytes 1 | tf_op jit(solution)/shard_map/pallas_call | solution.py:305
  20.9 5.6 %collective-permute-done.1 = bf16[128,4096]{1,0:T(8,128)(2,1)S(1)} collective-permute-done((bf16[128,4096]{1,0:T(8,128)(2,1)}, bf16[128,4096]{1,0:T(8,128)(2,1)S(1)}, u32[]{:S(2)}, u32[]{:S(2)}) %collective-permute-start.1) | collective-permute-done | bytes 1048608 | tf_op jit(solution)/shard_map/ppermute | solution.py:425
  28.0 1.4 collective-permute-start.3
  31.8 7.8 %shard_map.131 = (bf16[768,512]{1,0:T(8,128)(2,1)S(1)}, bf16[768,512]{1,0:T(8,128)(2,1)S(1)}) custom-call(bf16[256,4096]{1,0:T(8,128)(2,1)S(1)} %constant_dynamic-update-slice_fusion.refs_0_, bf16[256,4096]{1,0:T(8,128)(2,1)S(1)} %collective-permute-done.4.refs_1_, bf16[1536,4096]{1,0:T(8,128)(2,1)S(1)} %bitcast.34), custom_call_target="tpu_custom_call" | custom-call | flops 1 | bytes 1 | tf_op jit(solution)/shard_map/pallas_call | solution.py:305
  40.4 12.7 %collective-permute-done.3.refs_0_ = bf16[256,4096]{1,0:T(8,128)(2,1)S(1)} collective-permute-done((bf16[256,4096]{1,0:T(8,128)(2,1)S(1)}, bf16[256,4096]{1,0:T(8,128)(2,1)S(1)}, u32[]{:S(2)}, u32[]{:S(2)}) %collective-permute-start.3) | collective-permute-done | bytes 2097184 | tf_op jit(solution)/shard_map/ppermute | solution.py:425
  58.0 7.8 %shard_map.132 = (bf16[768,512]{1,0:T(8,128)(2,1)S(1)}, bf16[768,512]{1,0:T(8,128)(2,1)S(1)}) custom-call(bf16[256,4096]{1,0:T(8,128)(2,1)S(1)} %collective-permute-done.3.refs_0_, bf16[256,4096]{1,0:T(8,128)(2,1)S(1)} %collective-permute-done.7.refs_1_, bf16[1536,4096]{1,0:T(8,128)(2,1)S(1)} %bitcast.35), custom_call_target="tpu_custom_call" | custom-call | flops 1 | bytes 1 | tf_op jit(solution)/shard_map/pallas_call | solution.py:305
  65.7 8.2 %collective-permute-done.8 = bf16[768,512]{1,0:T(8,128)(2,1)S(1)} collective-permute-done((bf16[768,512]{1,0:T(8,128)(2,1)S(1)}, bf16[768,512]{1,0:T(8,128)(2,1)S(1)}, u32[]{:S(2)}, u32[]{:S(2)}) %collective-permute-start.8) | collective-permute-done | bytes 786464 | tf_op jit(solution)/shard_map/ppermute | solution.py:458
  74.0 5.7 %collective-permute-done.6.refs_0_ = bf16[256,4096]{1,0:T(8,128)(2,1)S(1)} collective-permute-done((bf16[256,4096]{1,0:T(8,128)(2,1)S(1)}, bf16[256,4096]{1,0:T(8,128)(2,1)S(1)}, u32[]{:S(2)}, u32[]{:S(2)}) %collective-permute-start.6) | collective-permute-done | bytes 2097184 | tf_op jit(solution)/shard_map/ppermute | solution.py:425
  80.3 1.4 collective-permute-start.9
  84.0 7.8 %shard_map.133 = (bf16[768,512]{1,0:T(8,128)(2,1)S(1)}, bf16[768,512]{1,0:T(8,128)(2,1)S(1)}) custom-call(bf16[256,4096]{1,0:T(8,128)(2,1)S(1)} %collective-permute-done.6.refs_0_, bf16[256,4096]{1,0:T(8,128)(2,1)S(1)} %collective-permute-done.10.refs_1_, bf16[1536,4096]{1,0:T(8,128)(2,1)S(1)} %bitcast.36), custom_call_target="tpu_custom_call" | custom-call | flops 1 | bytes 1 | tf_op jit(solution)/shard_map/pallas_call | solution.py:305
  92.7 2.0 collective-permute-done.9.refs_0_
  94.7 6.4 %all-to-all-start = ((bf16[16,256,128]{2,1,0:T(8,128)(2,1)}), bf16[16,256,128]{2,1,0:T(8,128)(2,1)}, u32[]{:S(2)}, u32[]{:S(2)}) async-start(bf16[16,256,128]{2,1,0:T(8,128)(2,1)} %bitcast.59), calls=%async_computation | async-start | bytes 2097152 | tf_op jit(solution)/shard_map/all_to_all | solution.py:487
  104.2 4.6 %copy-done.1 = bf16[2,3,256,4096]{3,2,1,0:T(8,128)(2,1)S(1)} copy-done((bf16[2,3,256,4096]{3,2,1,0:T(8,128)(2,1)S(1)}, bf16[2,3,256,4096]{3,2,1,0:T(8,128)(2,1)}, u32[]{:S(2)}) %copy-start.1) | copy-done | bytes 12582936
  108.8 4.3 %shard_map.134 = (bf16[768,256]{1,0:T(8,128)(2,1)S(1)}, bf16[768,256]{1,0:T(8,128)(2,1)S(1)}) custom-call(bf16[128,4096]{1,0:T(8,128)(2,1)S(1)} %collective-permute-done.9.refs_0_, bf16[64,4096]{1,0:T(8,128)(2,1)S(1)} %collective-permute-done.12.refs_1_, bf16[64,4096]{1,0:T(8,128)(2,1)S(1)} %collective-permute-done.13.refs_2_, bf16[1536,4096]{1,0:T(8,128)(2,1)S(1)} %bitcast.37), custom_call_target="tpu_custom_call" | custom-call | flops 1 | bytes 1 | tf_op jit(solution)/shard_map/pallas_call | solution.py:305
  115.1 5.6 %collective-permute-done.14 = bf16[768,512]{1,0:T(8,128)(2,1)S(1)} collective-permute-done((bf16[768,512]{1,0:T(8,128)(2,1)S(1)}, bf16[768,512]{1,0:T(8,128)(2,1)S(1)}, u32[]{:S(2)}, u32[]{:S(2)}) %collective-permute-start.14) | collective-permute-done | bytes 786464 | tf_op jit(solution)/shard_map/ppermute | solution.py:458
  120.7 8.4 %collective-permute-done.15 = bf16[768,256]{1,0:T(8,128)(2,1)S(1)} collective-permute-done((bf16[768,256]{1,0:T(8,128)(2,1)S(1)}, bf16[768,256]{1,0:T(8,128)(2,1)S(1)}, u32[]{:S(2)}, u32[]{:S(2)}) %collective-permute-start.15) | collective-permute-done | bytes 393248 | tf_op jit(solution)/shard_map/ppermute | solution.py:458
  129.9 16.3 %shard_map.135 = (bf16[16,256,128]{2,1,0:T(8,128)(2,1)}, bf16[3,256,256]{2,1,0:T(8,128)(2,1)}, bf16[3,256,512]{2,1,0:T(8,128)(2,1)}, bf16[3,256,512]{2,1,0:T(8,1...) custom-call(s32[16]{0:T(128)} %dynamic-slice_bitcast_fusion.order, ...), custom_call_target="tpu_custom_call" | custom-call | flops 1 | bytes 1 | tf_op jit(solution)/shard_map/pallas_call | solution.py:200
  147.5 7.0 %all-to-all-start.1 = ((bf16[16,256,128]{2,1,0:T(8,128)(2,1)}), bf16[16,256,128]{2,1,0:T(8,128)(2,1)S(1)}, u32[]{:S(2)}, u32[]{:S(2)}) async-start(bf16[16,256,128]{2,1,0:T(8,128)(2,1)} %get-tuple-element.156), calls=%async_computation.1 | async-start | bytes 2097152 | tf_op jit(solution)/shard_map/all_to_all | solution.py:505
  158.6 4.6 %copy-done.2 = bf16[2,3,256,4096]{3,2,1,0:T(8,128)(2,1)S(1)} copy-done((bf16[2,3,256,4096]{3,2,1,0:T(8,128)(2,1)S(1)}, bf16[2,3,256,4096]{3,2,1,0:T(8,128)(2,1)}, u32[]{:S(2)}) %copy-start.2) | copy-done | bytes 12582936
  163.1 5.2 %shard_map.136 = (bf16[128,4096]{1,0:T(8,128)(2,1)S(1)}, bf16[80,4096]{1,0:T(8,128)(2,1)S(1)}, bf16[48,4096]{1,0:T(8,128)(2,1)S(1)}) custom-call(bf16[768,256]{1,0:T(8,128)(2,1)S(1)} %bitcast.57, bf16[768,256]{1,0:T(8,128)(2,1)S(1)} %collective-permute-done.16.far_ref, bf16[1536,4096]{1,0:T(8,128)(2,1)S(1)} %bitcast.38), custom_call_target="tpu_custom_call" | custom-call | flops 1 | bytes 1 | tf_op jit(solution)/shard_map/pallas_call | solution.py:342
  168.9 1.5 collective-permute-start.22
  171.6 2.6 collective-permute-done.19.far_ref
  175.1 8.7 %shard_map.138 = (bf16[256,4096]{1,0:T(8,128)(2,1)S(1)}, bf16[96,4096]{1,0:T(8,128)(2,1)S(1)}, bf16[96,4096]{1,0:T(8,128)(2,1)S(1)}, bf16[64,4096]{1,0:T(8,128)(2,1)S(1)}) custom-call(bf16[768,512]{1,0:T(8,128)(2,1)S(1)} %bitcast.51, bf16[768,512]{1,0:T(8,128)(2,1)S(1)} %collective-permute-done.19.far_ref, bf16[1536,4096]{1,0:T(8,128)(2,1)S(1)} %bitcast.39), custom_call_target="tpu_custom_call" | custom-call | flops 1 | bytes 1 | tf_op jit(solution)/shard_map/pallas_call | solution.py:342
  183.8 2.0 collective-permute-start.20
  185.9 5.2 %collective-permute-done.22.far_ref = bf16[768,512]{1,0:T(8,128)(2,1)S(1)} collective-permute-done((bf16[768,512]{1,0:T(8,128)(2,1)S(1)}, bf16[768,512]{1,0:T(8,128)(2,1)S(1)}, u32[]{:S(2)}, u32[]{:S(2)}) %collective-permute-start.22) | collective-permute-done | bytes 786464 | tf_op jit(solution)/shard_map/ppermute | solution.py:458
  192.6 1.5 collective-permute-done.23.refs_3_
  197.9 4.6 %copy-done.3 = bf16[2,3,256,4096]{3,2,1,0:T(8,128)(2,1)S(1)} copy-done((bf16[2,3,256,4096]{3,2,1,0:T(8,128)(2,1)S(1)}, bf16[2,3,256,4096]{3,2,1,0:T(8,128)(2,1)}, u32[]{:S(2)}) %copy-start.3) | copy-done | bytes 12582936
  204.7 8.7 %shard_map.140 = (bf16[256,4096]{1,0:T(8,128)(2,1)S(1)}, bf16[128,4096]{1,0:T(8,128)(2,1)S(1)}, bf16[128,4096]{1,0:T(8,128)(2,1)S(1)}) custom-call(bf16[768,512]{1,0:T(8,128)(2,1)S(1)} %bitcast.47, bf16[768,512]{1,0:T(8,128)(2,1)S(1)} %copy-done.15, bf16[1536,4096]{1,0:T(8,128)(2,1)S(1)} %bitcast.40), custom_call_target="tpu_custom_call" | custom-call | flops 1 | bytes 1 | tf_op jit(solution)/shard_map/pallas_call | solution.py:342
  215.3 1.5 collective-permute-start.27
  216.8 1.5 shard_map.142
  219.1 1.5 collective-permute-done.28.refs_3_
  220.6 1.4 shard_map.141
  224.5 8.7 %shard_map.143 = (bf16[256,4096]{1,0:T(8,128)(2,1)S(1)}, bf16[128,4096]{1,0:T(8,128)(2,1)S(1)}, bf16[128,4096]{1,0:T(8,128)(2,1)S(1)}) custom-call(bf16[768,512]{1,0:T(8,128)(2,1)S(1)} %bitcast.45, bf16[768,512]{1,0:T(8,128)(2,1)S(1)} %collective-permute-done.26.far_ref, bf16[1536,4096]{1,0:T(8,128)(2,1)S(1)} %bitcast.41), custom_call_target="tpu_custom_call" | custom-call | flops 1 | bytes 1 | tf_op jit(solution)/shard_map/pallas_call | solution.py:342
  233.3 1.9 collective-permute-start.29
  235.3 2.2 collective-permute-done.29.refs_1_
  237.5 1.5 collective-permute-done.31.refs_2_
  239.0 8.2 %collective-permute-done.32.refs_3_ = bf16[256,4096]{1,0:T(8,128)(2,1)S(1)} collective-permute-done((bf16[256,4096]{1,0:T(8,128)(2,1)S(1)}, bf16[256,4096]{1,0:T(8,128)(2,1)S(1)}, u32[]{:S(2)}, u32[]{:S(2)}) %collective-permute-start.32) | collective-permute-done | bytes 2097184 | tf_op jit(solution)/shard_map/ppermute | solution.py:425
  247.2 1.4 shard_map.144
  249.9 2.5 collective-permute-start.36
  252.4 5.2 %shard_map.145 = (bf16[128,4096]{1,0:T(8,128)(2,1)S(1)}, bf16[64,4096]{1,0:T(8,128)(2,1)S(1)}, bf16[64,4096]{1,0:T(8,128)(2,1)S(1)}) custom-call(bf16[768,256]{1,0:T(8,128)(2,1)S(1)} %bitcast.54, bf16[768,256]{1,0:T(8,128)(2,1)S(1)} %collective-permute-done.30.far_ref, bf16[1536,4096]{1,0:T(8,128)(2,1)S(1)} %bitcast.42), custom_call_target="tpu_custom_call" | custom-call | flops 1 | bytes 1 | tf_op jit(solution)/shard_map/pallas_call | solution.py:342
  260.3 2.3 collective-permute-done.35.refs_3_
  262.6 13.5 %collective-permute-done.36.refs_4_ = bf16[128,4096]{1,0:T(8,128)(2,1)S(1)} collective-permute-done((bf16[128,4096]{1,0:T(8,128)(2,1)S(1)}, bf16[128,4096]{1,0:T(8,128)(2,1)S(1)}, u32[]{:S(2)}, u32[]{:S(2)}) %collective-permute-start.36) | collective-permute-done | bytes 1048608 | tf_op jit(solution)/shard_map/ppermute | solution.py:425
  276.1 2.1 shard_map.146
  (118 shorter events, 49.0 us)
Async XLA Ops:
  0.6 15.9 %collective-permute-start.2 = (bf16[128,4096]{1,0:T(8,128)(2,1)}, bf16[128,4096]{1,0:T(8,128)(2,1)S(1)}, u32[]{:S(2)}, u32[]{:S(2)}) collective-permute-start(bf16[128,4096]{1,0:T(8,128)(2,1)} %refs_0_.3), channel_id=1, source_target_pairs={{0,2},{2,0},{4,6},{6,4},{8,10},{10,8},{12,14},{14,12},{16,18},{18,... | collective-permute-start | bytes 3145736 | tf_op jit(solution)/shard_map/ppermute | solution.py:428
  0.8 25.7 %collective-permute-start.1 = (bf16[128,4096]{1,0:T(8,128)(2,1)}, bf16[128,4096]{1,0:T(8,128)(2,1)S(1)}, u32[]{:S(2)}, u32[]{:S(2)}) collective-permute-start(bf16[128,4096]{1,0:T(8,128)(2,1)} %refs_0_.3), channel_id=1, source_target_pairs={{0,6},{2,8},{8,2},{10,16},{16,10},{18,24},{24,18},{26,28},{28,26},... | collective-permute-start | bytes 3145736 | tf_op jit(solution)/shard_map/ppermute | solution.py:425
  3.5 23.9 %collective-permute-start = (bf16[128,4096]{1,0:T(8,128)(2,1)}, bf16[128,4096]{1,0:T(8,128)(2,1)S(1)}, u32[]{:S(2)}, u32[]{:S(2)}) collective-permute-start(bf16[128,4096]{1,0:T(8,128)(2,1)} %refs_0_.3), channel_id=1, source_target_pairs={{0,8},{2,6},{8,16},{10,2},{16,24},{18,10},{24,28},{26,18},{28,20},... | collective-permute-start | bytes 3145736 | tf_op jit(solution)/shard_map/ppermute | solution.py:425
  16.5 67.5 %copy-start = (bf16[2,3,256,4096]{3,2,1,0:T(8,128)(2,1)}, bf16[2,3,256,4096]{3,2,1,0:T(8,128)(2,1)S(1)}, u32[]{:S(2)}) copy-start(bf16[2,3,256,4096]{3,2,1,0:T(8,128)(2,1)S(1)} %shard_map.129) | copy-start | bytes 37748740
  27.6 4.2 %collective-permute-start.4 = (bf16[256,4096]{1,0:T(8,128)(2,1)S(1)}, bf16[256,4096]{1,0:T(8,128)(2,1)S(1)}, u32[]{:S(2)}, u32[]{:S(2)}) collective-permute-start(bf16[256,4096]{1,0:T(8,128)(2,1)S(1)} %constant_dynamic-update-slice_fusion.refs_0_), channel_id=1, source_target_pairs={{0,2},{2,0},{4,6},{6,4},{8,10},{10,8},{12,14},{14,12},{16,18},{18,... | collective-permute-start | bytes 6291464 | tf_op jit(solution)/shard_map/ppermute | solution.py:428
  28.0 25.2 %collective-permute-start.3 = (bf16[256,4096]{1,0:T(8,128)(2,1)S(1)}, bf16[256,4096]{1,0:T(8,128)(2,1)S(1)}, u32[]{:S(2)}, u32[]{:S(2)}) collective-permute-start(bf16[256,4096]{1,0:T(8,128)(2,1)S(1)} %constant_dynamic-update-slice_fusion.refs_0_), channel_id=1, source_target_pairs={{0,8},{2,6},{8,16},{10,2},{16,24},{18,10},{24,28},{26,18},{28,20},... | collective-permute-start | bytes 6291464 | tf_op jit(solution)/shard_map/ppermute | solution.py:425
  29.4 11.1 %collective-permute-start.5 = (bf16[768,256]{1,0:T(8,128)(2,1)S(1)}, bf16[768,256]{1,0:T(8,128)(2,1)S(1)}, u32[]{:S(2)}, u32[]{:S(2)}) collective-permute-start(bf16[768,256]{1,0:T(8,128)(2,1)S(1)} %get-tuple-element.109), channel_id=1, source_target_pairs={{0,1},{1,0},{2,3},{3,2},{4,5},{5,4},{6,7},{7,6},{8,9},{9,8},{10,11... | collective-permute-start | bytes 1179656 | tf_op jit(solution)/shard_map/ppermute | solution.py:458
  40.4 16.3 %copy-start.23 = (bf16[768,256]{1,0:T(8,128)(2,1)}, bf16[768,256]{1,0:T(8,128)(2,1)S(1)}, u32[]{:S(2)}) copy-start(bf16[768,256]{1,0:T(8,128)(2,1)S(1)} %collective-permute-done.5) | copy-start | bytes 1179652
  53.2 4.8 %collective-permute-start.7 = (bf16[256,4096]{1,0:T(8,128)(2,1)S(1)}, bf16[256,4096]{1,0:T(8,128)(2,1)S(1)}, u32[]{:S(2)}, u32[]{:S(2)}) collective-permute-start(bf16[256,4096]{1,0:T(8,128)(2,1)S(1)} %collective-permute-done.3.refs_0_), channel_id=1, source_target_pairs={{0,2},{2,0},{4,6},{6,4},{8,10},{10,8},{12,14},{14,12},{16,18},{18,... | collective-permute-start | bytes 6291464 | tf_op jit(solution)/shard_map/ppermute | solution.py:428
  54.2 25.5 %collective-permute-start.6 = (bf16[256,4096]{1,0:T(8,128)(2,1)S(1)}, bf16[256,4096]{1,0:T(8,128)(2,1)S(1)}, u32[]{:S(2)}, u32[]{:S(2)}) collective-permute-start(bf16[256,4096]{1,0:T(8,128)(2,1)S(1)} %collective-permute-done.3.refs_0_), channel_id=1, source_target_pairs={{0,8},{2,6},{8,16},{10,2},{16,24},{18,10},{24,28},{26,18},{28,20},... | collective-permute-start | bytes 6291464 | tf_op jit(solution)/shard_map/ppermute | solution.py:425
  55.5 18.4 %collective-permute-start.8 = (bf16[768,512]{1,0:T(8,128)(2,1)S(1)}, bf16[768,512]{1,0:T(8,128)(2,1)S(1)}, u32[]{:S(2)}, u32[]{:S(2)}) collective-permute-start(bf16[768,512]{1,0:T(8,128)(2,1)S(1)} %get-tuple-element.114), channel_id=1, source_target_pairs={{0,1},{1,0},{2,3},{3,2},{4,5},{5,4},{6,7},{7,6},{8,9},{9,8},{10,11... | collective-permute-start | bytes 2359304 | tf_op jit(solution)/shard_map/ppermute | solution.py:458
  65.7 26.0 %copy-start.12 = (bf16[768,512]{1,0:T(8,128)(2,1)}, bf16[768,512]{1,0:T(8,128)(2,1)S(1)}, u32[]{:S(2)}) copy-start(bf16[768,512]{1,0:T(8,128)(2,1)S(1)} %get-tuple-element.123) | copy-start | bytes 2359300
  74.0 17.8 %copy-start.21 = (bf16[768,512]{1,0:T(8,128)(2,1)}, bf16[768,512]{1,0:T(8,128)(2,1)S(1)}, u32[]{:S(2)}) copy-start(bf16[768,512]{1,0:T(8,128)(2,1)S(1)} %collective-permute-done.8) | copy-start | bytes 2359300
  79.7 4.3 %collective-permute-start.10 = (bf16[256,4096]{1,0:T(8,128)(2,1)S(1)}, bf16[256,4096]{1,0:T(8,128)(2,1)S(1)}, u32[]{:S(2)}, u32[]{:S(2)}) collective-permute-start(bf16[256,4096]{1,0:T(8,128)(2,1)S(1)} %collective-permute-done.6.refs_0_), channel_id=1, source_target_pairs={{0,2},{2,0},{4,6},{6,4},{8,10},{10,8},{12,14},{14,12},{16,18},{18,... | collective-permute-start | bytes 6291464 | tf_op jit(solution)/shard_map/ppermute | solution.py:428
  80.3 14.4 %collective-permute-start.9 = (bf16[128,4096]{1,0:T(8,128)(2,1)S(1)}, bf16[128,4096]{1,0:T(8,128)(2,1)S(1)}, u32[]{:S(2)}, u32[]{:S(2)}) collective-permute-start(bf16[128,4096]{1,0:T(8,128)(2,1)S(1)} %slice.34), channel_id=1, source_target_pairs={{0,8},{2,6},{8,16},{10,2},{16,24},{18,10},{24,28},{26,18},{28,20},... | collective-permute-start | bytes 3145736 | tf_op jit(solution)/shard_map/ppermute | solution.py:425
  81.7 19.4 %collective-permute-start.11 = (bf16[768,512]{1,0:T(8,128)(2,1)S(1)}, bf16[768,512]{1,0:T(8,128)(2,1)}, u32[]{:S(2)}, u32[]{:S(2)}) collective-permute-start(bf16[768,512]{1,0:T(8,128)(2,1)S(1)} %get-tuple-element.122), channel_id=1, source_target_pairs={{0,1},{1,0},{2,3},{3,2},{4,5},{5,4},{6,7},{7,6},{8,9},{9,8},{10,11... | collective-permute-start | bytes 2359304 | tf_op jit(solution)/shard_map/ppermute | solution.py:458
  94.7 34.4 %all-to-all-start = ((bf16[16,256,128]{2,1,0:T(8,128)(2,1)}), bf16[16,256,128]{2,1,0:T(8,128)(2,1)}, u32[]{:S(2)}, u32[]{:S(2)}) async-start(bf16[16,256,128]{2,1,0:T(8,128)(2,1)} %bitcast.59), calls=%async_computation | async-start | bytes 2097152 | tf_op jit(solution)/shard_map/all_to_all | solution.py:487
  101.2 2.2 collective-permute-start.13
  101.9 2.3 collective-permute-start.12
  102.0 18.7 %collective-permute-start.14 = (bf16[768,512]{1,0:T(8,128)(2,1)S(1)}, bf16[768,512]{1,0:T(8,128)(2,1)S(1)}, u32[]{:S(2)}, u32[]{:S(2)}) collective-permute-start(bf16[768,512]{1,0:T(8,128)(2,1)S(1)} %get-tuple-element.130), channel_id=1, source_target_pairs={{0,1},{1,0},{2,3},{3,2},{4,5},{5,4},{6,7},{7,6},{8,9},{9,8},{10,11... | collective-permute-start | bytes 2359304 | tf_op jit(solution)/shard_map/ppermute | solution.py:458
  113.9 15.2 %collective-permute-start.15 = (bf16[768,256]{1,0:T(8,128)(2,1)S(1)}, bf16[768,256]{1,0:T(8,128)(2,1)S(1)}, u32[]{:S(2)}, u32[]{:S(2)}) collective-permute-start(bf16[768,256]{1,0:T(8,128)(2,1)S(1)} %get-tuple-element.131), channel_id=1, source_target_pairs={{0,1},{1,0},{2,3},{3,2},{4,5},{5,4},{6,7},{7,6},{8,9},{9,8},{10,11... | collective-permute-start | bytes 1179656 | tf_op jit(solution)/shard_map/ppermute | solution.py:458
  120.7 8.4 %copy-start.22 = (bf16[768,512]{1,0:T(8,128)(2,1)}, bf16[768,512]{1,0:T(8,128)(2,1)S(1)}, u32[]{:S(2)}) copy-start(bf16[768,512]{1,0:T(8,128)(2,1)S(1)} %collective-permute-done.14) | copy-start | bytes 2359300
  146.1 8.4 %copy-start.13 = (bf16[3,256,512]{2,1,0:T(8,128)(2,1)S(1)}, bf16[3,256,512]{2,1,0:T(8,128)(2,1)}, u32[]{:S(2)}) copy-start(bf16[3,256,512]{2,1,0:T(8,128)(2,1)} %get-tuple-element.140) | copy-start | bytes 2359300
  146.1 8.7 %copy-start.26 = (f32[4,4,128]{2,1,0:T(4,128)S(1)}, f32[4,4,128]{2,1,0:T(4,128)}, u32[]{:S(2)}) copy-start(f32[4,4,128]{2,1,0:T(4,128)} %get-tuple-element.134) | copy-start | bytes 24580
  146.2 10.1 %copy-start.25 = (f32[4,4,9,128]{3,2,1,0:T(8,128)S(1)}, f32[4,4,9,128]{3,2,1,0:T(8,128)}, u32[]{:S(2)}) copy-start(f32[4,4,9,128]{3,2,1,0:T(8,128)} %get-tuple-element.133) | copy-start | bytes 221188
  146.2 12.4 %copy-start.19 = (bf16[3,256,256]{2,1,0:T(8,128)(2,1)S(1)}, bf16[3,256,256]{2,1,0:T(8,128)(2,1)}, u32[]{:S(2)}) copy-start(bf16[3,256,256]{2,1,0:T(8,128)(2,1)} %get-tuple-element.132) | copy-start | bytes 1179652
  146.2 12.4 %collective-permute-start.16 = (bf16[768,256]{1,0:T(8,128)(2,1)}, bf16[768,256]{1,0:T(8,128)(2,1)S(1)}, u32[]{:S(2)}, u32[]{:S(2)}) collective-permute-start(bf16[768,256]{1,0:T(8,128)(2,1)} %bitcast.56), channel_id=1, source_target_pairs={{0,1},{1,0},{2,3},{3,2},{4,5},{5,4},{6,7},{7,6},{8,9},{9,8},{10,11... | collective-permute-start | bytes 1179656 | tf_op jit(solution)/shard_map/ppermute | solution.py:458
  147.5 47.9 %all-to-all-start.1 = ((bf16[16,256,128]{2,1,0:T(8,128)(2,1)}), bf16[16,256,128]{2,1,0:T(8,128)(2,1)S(1)}, u32[]{:S(2)}, u32[]{:S(2)}) async-start(bf16[16,256,128]{2,1,0:T(8,128)(2,1)} %get-tuple-element.156), calls=%async_computation.1 | async-start | bytes 2097152 | tf_op jit(solution)/shard_map/all_to_all | solution.py:505
  154.5 19.7 %collective-permute-start.19 = (bf16[768,512]{1,0:T(8,128)(2,1)S(1)}, bf16[768,512]{1,0:T(8,128)(2,1)S(1)}, u32[]{:S(2)}, u32[]{:S(2)}) collective-permute-start(bf16[768,512]{1,0:T(8,128)(2,1)S(1)} %bitcast.50), channel_id=1, source_target_pairs={{0,1},{1,0},{2,3},{3,2},{4,5},{5,4},{6,7},{7,6},{8,9},{9,8},{10,11... | collective-permute-start | bytes 2359304 | tf_op jit(solution)/shard_map/ppermute | solution.py:458
  168.3 2.7 collective-permute-start.17
  168.7 2.3 collective-permute-start.18
  168.9 22.1 %collective-permute-start.22 = (bf16[768,512]{1,0:T(8,128)(2,1)S(1)}, bf16[768,512]{1,0:T(8,128)(2,1)S(1)}, u32[]{:S(2)}, u32[]{:S(2)}) collective-permute-start(bf16[768,512]{1,0:T(8,128)(2,1)S(1)} %bitcast.46), channel_id=1, source_target_pairs={{0,1},{1,0},{2,3},{3,2},{4,5},{5,4},{6,7},{7,6},{8,9},{9,8},{10,11... | collective-permute-start | bytes 2359304 | tf_op jit(solution)/shard_map/ppermute | solution.py:458
  174.2 19.9 %collective-permute-start.24 = (bf16[128,4096]{1,0:T(8,128)(2,1)S(1)}, bf16[128,4096]{1,0:T(8,128)(2,1)S(1)}, u32[]{:S(2)}, u32[]{:S(2)}) collective-permute-start(bf16[128,4096]{1,0:T(8,128)(2,1)S(1)} %shard_map.137), channel_id=1, source_target_pairs={{0,4},{2,10},{8,0},{10,18},{16,8},{18,26},{24,16},{26,30},{28,24},... | collective-permute-start | bytes 3145736 | tf_op jit(solution)/shard_map/ppermute | solution.py:425
  183.8 10.3 %collective-permute-start.20 = (bf16[96,4096]{1,0:T(8,128)(2,1)S(1)}, bf16[96,4096]{1,0:T(8,128)(2,1)S(1)}, u32[]{:S(2)}, u32[]{:S(2)}) collective-permute-start(bf16[96,4096]{1,0:T(8,128)(2,1)S(1)} %get-tuple-element.146), channel_id=1, source_target_pairs={{0,2},{2,0},{4,6},{6,4},{8,10},{10,8},{12,14},{14,12},{16,18},{18,... | collective-permute-start | bytes 2359304 | tf_op jit(solution)/shard_map/ppermute | solution.py:428
  185.8 8.3 %collective-permute-start.21 = (bf16[96,4096]{1,0:T(8,128)(2,1)S(1)}, bf16[96,4096]{1,0:T(8,128)(2,1)S(1)}, u32[]{:S(2)}, u32[]{:S(2)}) collective-permute-start(bf16[96,4096]{1,0:T(8,128)(2,1)S(1)} %get-tuple-element.147), channel_id=1, source_target_pairs={{0,2},{2,0},{4,6},{6,4},{8,10},{10,8},{12,14},{14,12},{16,18},{18,... | collective-permute-start | bytes 2359304 | tf_op jit(solution)/shard_map/ppermute | solution.py:428
  191.9 2.2 collective-permute-start.23
  195.3 25.2 %collective-permute-start.28 = (bf16[256,4096]{1,0:T(8,128)(2,1)S(1)}, bf16[256,4096]{1,0:T(8,128)(2,1)S(1)}, u32[]{:S(2)}, u32[]{:S(2)}) collective-permute-start(bf16[256,4096]{1,0:T(8,128)(2,1)S(1)} %shard_map.139), channel_id=1, source_target_pairs={{0,4},{2,10},{8,0},{10,18},{16,8},{18,26},{24,16},{26,30},{28,24},... | collective-permute-start | bytes 6291464 | tf_op jit(solution)/shard_map/ppermute | solution.py:425
  196.7 18.6 %collective-permute-start.26 = (bf16[768,512]{1,0:T(8,128)(2,1)}, bf16[768,512]{1,0:T(8,128)(2,1)S(1)}, u32[]{:S(2)}, u32[]{:S(2)}) collective-permute-start(bf16[768,512]{1,0:T(8,128)(2,1)} %bitcast.44), channel_id=1, source_target_pairs={{0,1},{1,0},{2,3},{3,2},{4,5},{5,4},{6,7},{7,6},{8,9},{9,8},{10,11... | collective-permute-start | bytes 2359304 | tf_op jit(solution)/shard_map/ppermute | solution.py:458
  213.5 4.9 %collective-permute-start.25 = (bf16[128,4096]{1,0:T(8,128)(2,1)S(1)}, bf16[128,4096]{1,0:T(8,128)(2,1)S(1)}, u32[]{:S(2)}, u32[]{:S(2)}) collective-permute-start(bf16[128,4096]{1,0:T(8,128)(2,1)S(1)} %get-tuple-element.160), channel_id=1, source_target_pairs={{0,2},{2,0},{4,6},{6,4},{8,10},{10,8},{12,14},{14,12},{16,18},{18,... | collective-permute-start | bytes 3145736 | tf_op jit(solution)/shard_map/ppermute | solution.py:428
  215.3 3.8 %collective-permute-start.27 = (bf16[128,4096]{1,0:T(8,128)(2,1)S(1)}, bf16[128,4096]{1,0:T(8,128)(2,1)S(1)}, u32[]{:S(2)}, u32[]{:S(2)}) collective-permute-start(bf16[128,4096]{1,0:T(8,128)(2,1)S(1)} %get-tuple-element.163), channel_id=1, source_target_pairs={{0,2},{2,0},{4,6},{6,4},{8,10},{10,8},{12,14},{14,12},{16,18},{18,... | collective-permute-start | bytes 3145736 | tf_op jit(solution)/shard_map/ppermute | solution.py:428
  222.0 25.2 %collective-permute-start.32 = (bf16[256,4096]{1,0:T(8,128)(2,1)S(1)}, bf16[256,4096]{1,0:T(8,128)(2,1)S(1)}, u32[]{:S(2)}, u32[]{:S(2)}) collective-permute-start(bf16[256,4096]{1,0:T(8,128)(2,1)S(1)} %shard_map.141), channel_id=1, source_target_pairs={{0,4},{2,10},{8,0},{10,18},{16,8},{18,26},{24,16},{26,30},{28,24},... | collective-permute-start | bytes 6291464 | tf_op jit(solution)/shard_map/ppermute | solution.py:425
  223.3 11.9 %collective-permute-start.30 = (bf16[768,256]{1,0:T(8,128)(2,1)S(1)}, bf16[768,256]{1,0:T(8,128)(2,1)S(1)}, u32[]{:S(2)}, u32[]{:S(2)}) collective-permute-start(bf16[768,256]{1,0:T(8,128)(2,1)S(1)} %bitcast.53), channel_id=1, source_target_pairs={{0,1},{1,0},{2,3},{3,2},{4,5},{5,4},{6,7},{7,6},{8,9},{9,8},{10,11... | collective-permute-start | bytes 1179656 | tf_op jit(solution)/shard_map/ppermute | solution.py:458
  233.3 4.2 %collective-permute-start.29 = (bf16[128,4096]{1,0:T(8,128)(2,1)S(1)}, bf16[128,4096]{1,0:T(8,128)(2,1)S(1)}, u32[]{:S(2)}, u32[]{:S(2)}) collective-permute-start(bf16[128,4096]{1,0:T(8,128)(2,1)S(1)} %get-tuple-element.172), channel_id=1, source_target_pairs={{0,2},{2,0},{4,6},{6,4},{8,10},{10,8},{12,14},{14,12},{16,18},{18,... | collective-permute-start | bytes 3145736 | tf_op jit(solution)/shard_map/ppermute | solution.py:428
  235.2 3.8 %collective-permute-start.31 = (bf16[128,4096]{1,0:T(8,128)(2,1)S(1)}, bf16[128,4096]{1,0:T(8,128)(2,1)S(1)}, u32[]{:S(2)}, u32[]{:S(2)}) collective-permute-start(bf16[128,4096]{1,0:T(8,128)(2,1)S(1)} %get-tuple-element.175), channel_id=1, source_target_pairs={{0,2},{2,0},{4,6},{6,4},{8,10},{10,8},{12,14},{14,12},{16,18},{18,... | collective-permute-start | bytes 3145736 | tf_op jit(solution)/shard_map/ppermute | solution.py:428
  248.6 14.0 %collective-permute-start.35 = (bf16[128,4096]{1,0:T(8,128)(2,1)S(1)}, bf16[128,4096]{1,0:T(8,128)(2,1)S(1)}, u32[]{:S(2)}, u32[]{:S(2)}) collective-permute-start(bf16[128,4096]{1,0:T(8,128)(2,1)S(1)} %get-tuple-element.188), channel_id=1, source_target_pairs={{0,4},{2,10},{8,0},{10,18},{16,8},{18,26},{24,16},{26,30},{28,24},... | collective-permute-start | bytes 3145736 | tf_op jit(solution)/shard_map/ppermute | solution.py:425
  249.9 26.2 %collective-permute-start.36 = (bf16[128,4096]{1,0:T(8,128)(2,1)S(1)}, bf16[128,4096]{1,0:T(8,128)(2,1)S(1)}, u32[]{:S(2)}, u32[]{:S(2)}) collective-permute-start(bf16[128,4096]{1,0:T(8,128)(2,1)S(1)} %get-tuple-element.189), channel_id=1, source_target_pairs={{0,6},{2,8},{8,2},{10,16},{16,10},{18,24},{24,18},{26,28},{28,26},... | collective-permute-start | bytes 3145736 | tf_op jit(solution)/shard_map/ppermute | solution.py:425
  257.5 2.0 collective-permute-start.33
  257.6 2.6 collective-permute-start.34
  (18 other events, 47.5 us)

commit v12 on v10

--- a/solution.py
+++ b/solution.py
@@ -187,7 +187,7 @@
     blocks, channels, _ = g.shape
     count, sets = len(proj_sets[0]), len(proj_sets)
     groups = channels // GROUP
-    per_turn = next(n for n in (2, 1) if groups % n == 0)
+    per_turn = 1
     per_step = next(n for n in (4, 2, 1) if groups % n == 0)
     steps = groups // per_step
     rows = blocks * GROUP

time: 278 us -> 284 us (1.022)
  Pallas kernels: 93.8 us -> 99.7 us
    pallas_call x1, Pallas kernels: 15.5 us -> 21.4 us  [mix(): pl.pallas_call(functools.partial(mix_body, count, sets, per_turn, grouped...]
where the time goes in v12:
time: 284 us; the launch traced here: 283 us
  Pallas kernels  99.7 us (35%)
  waiting for transfers between devices  95.6 us (34%)
  starting transfers between devices  50.8 us (18%)
  local copies, waits for them, and re-layouts  33.4 us (12%)
    ppermute x10, waiting for transfers between devices, one_way(): return lax.ppermute(x, 'ctx', hops)  52.4 us
    pallas_call x5, Pallas kernels, unproject_kernel(): pl.pallas_call(unproject_body, grid=(width // tile,), in_specs=[pl.BlockS...  36.5 us
    pallas_call x5, Pallas kernels, project_kernel(): pl.pallas_call(functools.partial(project_body, len(pieces)), grid=(4,), i...  32 us
    ppermute x10, waiting for transfers between devices, across(): return None if x is None else lax.ppermute(x, 'tp', [(0, 1), (1, 0)])  30.6 us
    unnamed x57, local copies, waits for them, and re-layouts  28.8 us
    pallas_call x1, Pallas kernels, mix(): pl.pallas_call(functools.partial(mix_body, count, sets, per_turn, grouped...  21.4 us
    ppermute x10, starting transfers between devices, one_way(): return lax.ppermute(x, 'ctx', hops)  14.2 us
    ppermute x17, waiting for transfers between devices, swap(): return lax.ppermute(x, 'ctx', [(d, d ^ 1) for d in range(n_ctx)])  12.6 us
  transfers between devices with their start and end apart: 39, of which 27 were waited for; matrix products, arithmetic and copies ran while one was open for 3% of the time, Pallas kernels for 26%

profile of v12, /device:TPU:1, one launch (start us, length us, event | category | flops | bytes accessed | tf_op | source)
XLA Modules:
  0.0 283.3 jit_solution(9082360388042266236)
XLA Ops:
  0.8 2.7 collective-permute-start.1
  8.3 2.2 copy-done.4
  10.4 2.2 copy-done.5
  12.6 2.2 copy-done.6
  14.8 1.7 shard_map.129
  16.6 4.3 %shard_map.130 = (bf16[768,256]{1,0:T(8,128)(2,1)S(1)}, bf16[768,256]{1,0:T(8,128)(2,1)S(1)}) custom-call(bf16[128,4096]{1,0:T(8,128)(2,1)S(1)} %copy-done.7, bf16[128,4096]{1,0:T(8,128)(2,1)S(1)} %collective-permute-done.2.refs_1_, bf16[1536,4096]{1,0:T(8,128)(2,1)S(1)} %bitcast.33), custom_call_target="tpu_custom_call" | custom-call | flops 1 | bytes 1 | tf_op jit(solution)/shard_map/pallas_call | solution.py:305
  20.9 5.6 %collective-permute-done.1 = bf16[128,4096]{1,0:T(8,128)(2,1)S(1)} collective-permute-done((bf16[128,4096]{1,0:T(8,128)(2,1)}, bf16[128,4096]{1,0:T(8,128)(2,1)S(1)}, u32[]{:S(2)}, u32[]{:S(2)}) %collective-permute-start.1) | collective-permute-done | bytes 1048608 | tf_op jit(solution)/shard_map/ppermute | solution.py:425
  28.0 1.4 collective-permute-start.3
  31.8 7.8 %shard_map.131 = (bf16[768,512]{1,0:T(8,128)(2,1)S(1)}, bf16[768,512]{1,0:T(8,128)(2,1)S(1)}) custom-call(bf16[256,4096]{1,0:T(8,128)(2,1)S(1)} %constant_dynamic-update-slice_fusion.refs_0_, bf16[256,4096]{1,0:T(8,128)(2,1)S(1)} %collective-permute-done.4.refs_1_, bf16[1536,4096]{1,0:T(8,128)(2,1)S(1)} %bitcast.34), custom_call_target="tpu_custom_call" | custom-call | flops 1 | bytes 1 | tf_op jit(solution)/shard_map/pallas_call | solution.py:305
  40.4 12.7 %collective-permute-done.3.refs_0_ = bf16[256,4096]{1,0:T(8,128)(2,1)S(1)} collective-permute-done((bf16[256,4096]{1,0:T(8,128)(2,1)S(1)}, bf16[256,4096]{1,0:T(8,128)(2,1)S(1)}, u32[]{:S(2)}, u32[]{:S(2)}) %collective-permute-start.3) | collective-permute-done | bytes 2097184 | tf_op jit(solution)/shard_map/ppermute | solution.py:425
  58.0 7.8 %shard_map.132 = (bf16[768,512]{1,0:T(8,128)(2,1)S(1)}, bf16[768,512]{1,0:T(8,128)(2,1)S(1)}) custom-call(bf16[256,4096]{1,0:T(8,128)(2,1)S(1)} %collective-permute-done.3.refs_0_, bf16[256,4096]{1,0:T(8,128)(2,1)S(1)} %collective-permute-done.7.refs_1_, bf16[1536,4096]{1,0:T(8,128)(2,1)S(1)} %bitcast.35), custom_call_target="tpu_custom_call" | custom-call | flops 1 | bytes 1 | tf_op jit(solution)/shard_map/pallas_call | solution.py:305
  65.7 8.2 %collective-permute-done.8 = bf16[768,512]{1,0:T(8,128)(2,1)S(1)} collective-permute-done((bf16[768,512]{1,0:T(8,128)(2,1)S(1)}, bf16[768,512]{1,0:T(8,128)(2,1)S(1)}, u32[]{:S(2)}, u32[]{:S(2)}) %collective-permute-start.8) | collective-permute-done | bytes 786464 | tf_op jit(solution)/shard_map/ppermute | solution.py:458
  74.0 5.7 %collective-permute-done.6.refs_0_ = bf16[256,4096]{1,0:T(8,128)(2,1)S(1)} collective-permute-done((bf16[256,4096]{1,0:T(8,128)(2,1)S(1)}, bf16[256,4096]{1,0:T(8,128)(2,1)S(1)}, u32[]{:S(2)}, u32[]{:S(2)}) %collective-permute-start.6) | collective-permute-done | bytes 2097184 | tf_op jit(solution)/shard_map/ppermute | solution.py:425
  80.3 1.4 collective-permute-start.9
  84.0 7.8 %shard_map.133 = (bf16[768,512]{1,0:T(8,128)(2,1)S(1)}, bf16[768,512]{1,0:T(8,128)(2,1)S(1)}) custom-call(bf16[256,4096]{1,0:T(8,128)(2,1)S(1)} %collective-permute-done.6.refs_0_, bf16[256,4096]{1,0:T(8,128)(2,1)S(1)} %collective-permute-done.10.refs_1_, bf16[1536,4096]{1,0:T(8,128)(2,1)S(1)} %bitcast.36), custom_call_target="tpu_custom_call" | custom-call | flops 1 | bytes 1 | tf_op jit(solution)/shard_map/pallas_call | solution.py:305
  92.7 2.0 collective-permute-done.9.refs_0_
  94.7 6.4 %all-to-all-start = ((bf16[16,256,128]{2,1,0:T(8,128)(2,1)}), bf16[16,256,128]{2,1,0:T(8,128)(2,1)}, u32[]{:S(2)}, u32[]{:S(2)}) async-start(bf16[16,256,128]{2,1,0:T(8,128)(2,1)} %bitcast.59), calls=%async_computation | async-start | bytes 2097152 | tf_op jit(solution)/shard_map/all_to_all | solution.py:487
  104.2 4.6 %copy-done.1 = bf16[2,3,256,4096]{3,2,1,0:T(8,128)(2,1)S(1)} copy-done((bf16[2,3,256,4096]{3,2,1,0:T(8,128)(2,1)S(1)}, bf16[2,3,256,4096]{3,2,1,0:T(8,128)(2,1)}, u32[]{:S(2)}) %copy-start.1) | copy-done | bytes 12582936
  108.8 4.3 %shard_map.134 = (bf16[768,256]{1,0:T(8,128)(2,1)S(1)}, bf16[768,256]{1,0:T(8,128)(2,1)S(1)}) custom-call(bf16[128,4096]{1,0:T(8,128)(2,1)S(1)} %collective-permute-done.9.refs_0_, bf16[64,4096]{1,0:T(8,128)(2,1)S(1)} %collective-permute-done.12.refs_1_, bf16[64,4096]{1,0:T(8,128)(2,1)S(1)} %collective-permute-done.13.refs_2_, bf16[1536,4096]{1,0:T(8,128)(2,1)S(1)} %bitcast.37), custom_call_target="tpu_custom_call" | custom-call | flops 1 | bytes 1 | tf_op jit(solution)/shard_map/pallas_call | solution.py:305
  115.1 5.6 %collective-permute-done.14 = bf16[768,512]{1,0:T(8,128)(2,1)S(1)} collective-permute-done((bf16[768,512]{1,0:T(8,128)(2,1)S(1)}, bf16[768,512]{1,0:T(8,128)(2,1)S(1)}, u32[]{:S(2)}, u32[]{:S(2)}) %collective-permute-start.14) | collective-permute-done | bytes 786464 | tf_op jit(solution)/shard_map/ppermute | solution.py:458
  120.7 8.4 %collective-permute-done.15 = bf16[768,256]{1,0:T(8,128)(2,1)S(1)} collective-permute-done((bf16[768,256]{1,0:T(8,128)(2,1)S(1)}, bf16[768,256]{1,0:T(8,128)(2,1)S(1)}, u32[]{:S(2)}, u32[]{:S(2)}) %collective-permute-start.15) | collective-permute-done | bytes 393248 | tf_op jit(solution)/shard_map/ppermute | solution.py:458
  129.9 21.4 %shard_map.135 = (bf16[16,256,128]{2,1,0:T(8,128)(2,1)}, bf16[3,256,256]{2,1,0:T(8,128)(2,1)}, bf16[3,256,512]{2,1,0:T(8,128)(2,1)}, bf16[3,256,512]{2,1,0:T(8,1...) custom-call(s32[16]{0:T(128)} %dynamic-slice_bitcast_fusion.order, ...), custom_call_target="tpu_custom_call" | custom-call | flops 1 | bytes 1 | tf_op jit(solution)/shard_map/pallas_call | solution.py:200
  152.6 7.0 %all-to-all-start.1 = ((bf16[16,256,128]{2,1,0:T(8,128)(2,1)}), bf16[16,256,128]{2,1,0:T(8,128)(2,1)S(1)}, u32[]{:S(2)}, u32[]{:S(2)}) async-start(bf16[16,256,128]{2,1,0:T(8,128)(2,1)} %get-tuple-element.156), calls=%async_computation.1 | async-start | bytes 2097152 | tf_op jit(solution)/shard_map/all_to_all | solution.py:505
  163.7 4.6 %copy-done.2 = bf16[2,3,256,4096]{3,2,1,0:T(8,128)(2,1)S(1)} copy-done((bf16[2,3,256,4096]{3,2,1,0:T(8,128)(2,1)S(1)}, bf16[2,3,256,4096]{3,2,1,0:T(8,128)(2,1)}, u32[]{:S(2)}) %copy-start.2) | copy-done | bytes 12582936
  168.3 5.2 %shard_map.136 = (bf16[128,4096]{1,0:T(8,128)(2,1)S(1)}, bf16[80,4096]{1,0:T(8,128)(2,1)S(1)}, bf16[48,4096]{1,0:T(8,128)(2,1)S(1)}) custom-call(bf16[768,256]{1,0:T(8,128)(2,1)S(1)} %bitcast.57, bf16[768,256]{1,0:T(8,128)(2,1)S(1)} %collective-permute-done.16.far_ref, bf16[1536,4096]{1,0:T(8,128)(2,1)S(1)} %bitcast.38), custom_call_target="tpu_custom_call" | custom-call | flops 1 | bytes 1 | tf_op jit(solution)/shard_map/pallas_call | solution.py:342
  174.0 1.4 collective-permute-start.22
  176.7 2.6 collective-permute-done.19.far_ref
  180.2 8.7 %shard_map.138 = (bf16[256,4096]{1,0:T(8,128)(2,1)S(1)}, bf16[96,4096]{1,0:T(8,128)(2,1)S(1)}, bf16[96,4096]{1,0:T(8,128)(2,1)S(1)}, bf16[64,4096]{1,0:T(8,128)(2,1)S(1)}) custom-call(bf16[768,512]{1,0:T(8,128)(2,1)S(1)} %bitcast.51, bf16[768,512]{1,0:T(8,128)(2,1)S(1)} %collective-permute-done.19.far_ref, bf16[1536,4096]{1,0:T(8,128)(2,1)S(1)} %bitcast.39), custom_call_target="tpu_custom_call" | custom-call | flops 1 | bytes 1 | tf_op jit(solution)/shard_map/pallas_call | solution.py:342
  188.9 2.0 collective-permute-start.20
  191.0 5.1 %collective-permute-done.22.far_ref = bf16[768,512]{1,0:T(8,128)(2,1)S(1)} collective-permute-done((bf16[768,512]{1,0:T(8,128)(2,1)S(1)}, bf16[768,512]{1,0:T(8,128)(2,1)S(1)}, u32[]{:S(2)}, u32[]{:S(2)}) %collective-permute-start.22) | collective-permute-done | bytes 786464 | tf_op jit(solution)/shard_map/ppermute | solution.py:458
  197.7 1.5 collective-permute-done.23.refs_3_
  203.0 4.6 %copy-done.3 = bf16[2,3,256,4096]{3,2,1,0:T(8,128)(2,1)S(1)} copy-done((bf16[2,3,256,4096]{3,2,1,0:T(8,128)(2,1)S(1)}, bf16[2,3,256,4096]{3,2,1,0:T(8,128)(2,1)}, u32[]{:S(2)}) %copy-start.3) | copy-done | bytes 12582936
  209.9 8.7 %shard_map.140 = (bf16[256,4096]{1,0:T(8,128)(2,1)S(1)}, bf16[128,4096]{1,0:T(8,128)(2,1)S(1)}, bf16[128,4096]{1,0:T(8,128)(2,1)S(1)}) custom-call(bf16[768,512]{1,0:T(8,128)(2,1)S(1)} %bitcast.47, bf16[768,512]{1,0:T(8,128)(2,1)S(1)} %copy-done.15, bf16[1536,4096]{1,0:T(8,128)(2,1)S(1)} %bitcast.40), custom_call_target="tpu_custom_call" | custom-call | flops 1 | bytes 1 | tf_op jit(solution)/shard_map/pallas_call | solution.py:342
  220.4 1.5 collective-permute-start.27
  222.0 1.5 shard_map.142
  224.2 1.5 collective-permute-done.28.refs_3_
  225.7 1.4 shard_map.141
  229.7 8.7 %shard_map.143 = (bf16[256,4096]{1,0:T(8,128)(2,1)S(1)}, bf16[128,4096]{1,0:T(8,128)(2,1)S(1)}, bf16[128,4096]{1,0:T(8,128)(2,1)S(1)}) custom-call(bf16[768,512]{1,0:T(8,128)(2,1)S(1)} %bitcast.45, bf16[768,512]{1,0:T(8,128)(2,1)S(1)} %collective-permute-done.26.far_ref, bf16[1536,4096]{1,0:T(8,128)(2,1)S(1)} %bitcast.41), custom_call_target="tpu_custom_call" | custom-call | flops 1 | bytes 1 | tf_op jit(solution)/shard_map/pallas_call | solution.py:342
  238.4 1.9 collective-permute-start.29
  240.4 2.2 collective-permute-done.29.refs_1_
  242.6 1.5 collective-permute-done.31.refs_2_
  244.1 8.2 %collective-permute-done.32.refs_3_ = bf16[256,4096]{1,0:T(8,128)(2,1)S(1)} collective-permute-done((bf16[256,4096]{1,0:T(8,128)(2,1)S(1)}, bf16[256,4096]{1,0:T(8,128)(2,1)S(1)}, u32[]{:S(2)}, u32[]{:S(2)}) %collective-permute-start.32) | collective-permute-done | bytes 2097184 | tf_op jit(solution)/shard_map/ppermute | solution.py:425
  252.3 1.4 shard_map.144
  255.0 2.5 collective-permute-start.36
  257.5 5.2 %shard_map.145 = (bf16[128,4096]{1,0:T(8,128)(2,1)S(1)}, bf16[64,4096]{1,0:T(8,128)(2,1)S(1)}, bf16[64,4096]{1,0:T(8,128)(2,1)S(1)}) custom-call(bf16[768,256]{1,0:T(8,128)(2,1)S(1)} %bitcast.54, bf16[768,256]{1,0:T(8,128)(2,1)S(1)} %collective-permute-done.30.far_ref, bf16[1536,4096]{1,0:T(8,128)(2,1)S(1)} %bitcast.42), custom_call_target="tpu_custom_call" | custom-call | flops 1 | bytes 1 | tf_op jit(solution)/shard_map/pallas_call | solution.py:342
  265.4 2.3 collective-permute-done.35.refs_3_
  267.7 13.5 %collective-permute-done.36.refs_4_ = bf16[128,4096]{1,0:T(8,128)(2,1)S(1)} collective-permute-done((bf16[128,4096]{1,0:T(8,128)(2,1)S(1)}, bf16[128,4096]{1,0:T(8,128)(2,1)S(1)}, u32[]{:S(2)}, u32[]{:S(2)}) %collective-permute-start.36) | collective-permute-done | bytes 1048608 | tf_op jit(solution)/shard_map/ppermute | solution.py:425
  281.2 2.1 shard_map.146
  (118 shorter events, 49.0 us)
Async XLA Ops:
  0.6 15.9 %collective-permute-start.2 = (bf16[128,4096]{1,0:T(8,128)(2,1)}, bf16[128,4096]{1,0:T(8,128)(2,1)S(1)}, u32[]{:S(2)}, u32[]{:S(2)}) collective-permute-start(bf16[128,4096]{1,0:T(8,128)(2,1)} %refs_0_.3), channel_id=1, source_target_pairs={{0,2},{2,0},{4,6},{6,4},{8,10},{10,8},{12,14},{14,12},{16,18},{18,... | collective-permute-start | bytes 3145736 | tf_op jit(solution)/shard_map/ppermute | solution.py:428
  0.8 25.7 %collective-permute-start.1 = (bf16[128,4096]{1,0:T(8,128)(2,1)}, bf16[128,4096]{1,0:T(8,128)(2,1)S(1)}, u32[]{:S(2)}, u32[]{:S(2)}) collective-permute-start(bf16[128,4096]{1,0:T(8,128)(2,1)} %refs_0_.3), channel_id=1, source_target_pairs={{0,6},{2,8},{8,2},{10,16},{16,10},{18,24},{24,18},{26,28},{28,26},... | collective-permute-start | bytes 3145736 | tf_op jit(solution)/shard_map/ppermute | solution.py:425
  3.5 23.9 %collective-permute-start = (bf16[128,4096]{1,0:T(8,128)(2,1)}, bf16[128,4096]{1,0:T(8,128)(2,1)S(1)}, u32[]{:S(2)}, u32[]{:S(2)}) collective-permute-start(bf16[128,4096]{1,0:T(8,128)(2,1)} %refs_0_.3), channel_id=1, source_target_pairs={{0,8},{2,6},{8,16},{10,2},{16,24},{18,10},{24,28},{26,18},{28,20},... | collective-permute-start | bytes 3145736 | tf_op jit(solution)/shard_map/ppermute | solution.py:425
  16.5 67.5 %copy-start = (bf16[2,3,256,4096]{3,2,1,0:T(8,128)(2,1)}, bf16[2,3,256,4096]{3,2,1,0:T(8,128)(2,1)S(1)}, u32[]{:S(2)}) copy-start(bf16[2,3,256,4096]{3,2,1,0:T(8,128)(2,1)S(1)} %shard_map.129) | copy-start | bytes 37748740
  27.6 4.2 %collective-permute-start.4 = (bf16[256,4096]{1,0:T(8,128)(2,1)S(1)}, bf16[256,4096]{1,0:T(8,128)(2,1)S(1)}, u32[]{:S(2)}, u32[]{:S(2)}) collective-permute-start(bf16[256,4096]{1,0:T(8,128)(2,1)S(1)} %constant_dynamic-update-slice_fusion.refs_0_), channel_id=1, source_target_pairs={{0,2},{2,0},{4,6},{6,4},{8,10},{10,8},{12,14},{14,12},{16,18},{18,... | collective-permute-start | bytes 6291464 | tf_op jit(solution)/shard_map/ppermute | solution.py:428
  28.0 25.2 %collective-permute-start.3 = (bf16[256,4096]{1,0:T(8,128)(2,1)S(1)}, bf16[256,4096]{1,0:T(8,128)(2,1)S(1)}, u32[]{:S(2)}, u32[]{:S(2)}) collective-permute-start(bf16[256,4096]{1,0:T(8,128)(2,1)S(1)} %constant_dynamic-update-slice_fusion.refs_0_), channel_id=1, source_target_pairs={{0,8},{2,6},{8,16},{10,2},{16,24},{18,10},{24,28},{26,18},{28,20},... | collective-permute-start | bytes 6291464 | tf_op jit(solution)/shard_map/ppermute | solution.py:425
  29.4 11.1 %collective-permute-start.5 = (bf16[768,256]{1,0:T(8,128)(2,1)S(1)}, bf16[768,256]{1,0:T(8,128)(2,1)S(1)}, u32[]{:S(2)}, u32[]{:S(2)}) collective-permute-start(bf16[768,256]{1,0:T(8,128)(2,1)S(1)} %get-tuple-element.109), channel_id=1, source_target_pairs={{0,1},{1,0},{2,3},{3,2},{4,5},{5,4},{6,7},{7,6},{8,9},{9,8},{10,11... | collective-permute-start | bytes 1179656 | tf_op jit(solution)/shard_map/ppermute | solution.py:458
  40.4 16.3 %copy-start.23 = (bf16[768,256]{1,0:T(8,128)(2,1)}, bf16[768,256]{1,0:T(8,128)(2,1)S(1)}, u32[]{:S(2)}) copy-start(bf16[768,256]{1,0:T(8,128)(2,1)S(1)} %collective-permute-done.5) | copy-start | bytes 1179652
  53.2 4.8 %collective-permute-start.7 = (bf16[256,4096]{1,0:T(8,128)(2,1)S(1)}, bf16[256,4096]{1,0:T(8,128)(2,1)S(1)}, u32[]{:S(2)}, u32[]{:S(2)}) collective-permute-start(bf16[256,4096]{1,0:T(8,128)(2,1)S(1)} %collective-permute-done.3.refs_0_), channel_id=1, source_target_pairs={{0,2},{2,0},{4,6},{6,4},{8,10},{10,8},{12,14},{14,12},{16,18},{18,... | collective-permute-start | bytes 6291464 | tf_op jit(solution)/shard_map/ppermute | solution.py:428
  54.2 25.5 %collective-permute-start.6 = (bf16[256,4096]{1,0:T(8,128)(2,1)S(1)}, bf16[256,4096]{1,0:T(8,128)(2,1)S(1)}, u32[]{:S(2)}, u32[]{:S(2)}) collective-permute-start(bf16[256,4096]{1,0:T(8,128)(2,1)S(1)} %collective-permute-done.3.refs_0_), channel_id=1, source_target_pairs={{0,8},{2,6},{8,16},{10,2},{16,24},{18,10},{24,28},{26,18},{28,20},... | collective-permute-start | bytes 6291464 | tf_op jit(solution)/shard_map/ppermute | solution.py:425
  55.5 18.4 %collective-permute-start.8 = (bf16[768,512]{1,0:T(8,128)(2,1)S(1)}, bf16[768,512]{1,0:T(8,128)(2,1)S(1)}, u32[]{:S(2)}, u32[]{:S(2)}) collective-permute-start(bf16[768,512]{1,0:T(8,128)(2,1)S(1)} %get-tuple-element.114), channel_id=1, source_target_pairs={{0,1},{1,0},{2,3},{3,2},{4,5},{5,4},{6,7},{7,6},{8,9},{9,8},{10,11... | collective-permute-start | bytes 2359304 | tf_op jit(solution)/shard_map/ppermute | solution.py:458
  65.7 26.0 %copy-start.12 = (bf16[768,512]{1,0:T(8,128)(2,1)}, bf16[768,512]{1,0:T(8,128)(2,1)S(1)}, u32[]{:S(2)}) copy-start(bf16[768,512]{1,0:T(8,128)(2,1)S(1)} %get-tuple-element.123) | copy-start | bytes 2359300
  74.0 17.8 %copy-start.21 = (bf16[768,512]{1,0:T(8,128)(2,1)}, bf16[768,512]{1,0:T(8,128)(2,1)S(1)}, u32[]{:S(2)}) copy-start(bf16[768,512]{1,0:T(8,128)(2,1)S(1)} %collective-permute-done.8) | copy-start | bytes 2359300
  79.7 4.3 %collective-permute-start.10 = (bf16[256,4096]{1,0:T(8,128)(2,1)S(1)}, bf16[256,4096]{1,0:T(8,128)(2,1)S(1)}, u32[]{:S(2)}, u32[]{:S(2)}) collective-permute-start(bf16[256,4096]{1,0:T(8,128)(2,1)S(1)} %collective-permute-done.6.refs_0_), channel_id=1, source_target_pairs={{0,2},{2,0},{4,6},{6,4},{8,10},{10,8},{12,14},{14,12},{16,18},{18,... | collective-permute-start | bytes 6291464 | tf_op jit(solution)/shard_map/ppermute | solution.py:428
  80.3 14.4 %collective-permute-start.9 = (bf16[128,4096]{1,0:T(8,128)(2,1)S(1)}, bf16[128,4096]{1,0:T(8,128)(2,1)S(1)}, u32[]{:S(2)}, u32[]{:S(2)}) collective-permute-start(bf16[128,4096]{1,0:T(8,128)(2,1)S(1)} %slice.34), channel_id=1, source_target_pairs={{0,8},{2,6},{8,16},{10,2},{16,24},{18,10},{24,28},{26,18},{28,20},... | collective-permute-start | bytes 3145736 | tf_op jit(solution)/shard_map/ppermute | solution.py:425
  81.7 19.4 %collective-permute-start.11 = (bf16[768,512]{1,0:T(8,128)(2,1)S(1)}, bf16[768,512]{1,0:T(8,128)(2,1)}, u32[]{:S(2)}, u32[]{:S(2)}) collective-permute-start(bf16[768,512]{1,0:T(8,128)(2,1)S(1)} %get-tuple-element.122), channel_id=1, source_target_pairs={{0,1},{1,0},{2,3},{3,2},{4,5},{5,4},{6,7},{7,6},{8,9},{9,8},{10,11... | collective-permute-start | bytes 2359304 | tf_op jit(solution)/shard_map/ppermute | solution.py:458
  94.7 34.4 %all-to-all-start = ((bf16[16,256,128]{2,1,0:T(8,128)(2,1)}), bf16[16,256,128]{2,1,0:T(8,128)(2,1)}, u32[]{:S(2)}, u32[]{:S(2)}) async-start(bf16[16,256,128]{2,1,0:T(8,128)(2,1)} %bitcast.59), calls=%async_computation | async-start | bytes 2097152 | tf_op jit(solution)/shard_map/all_to_all | solution.py:487
  101.2 2.2 collective-permute-start.13
  101.9 2.3 collective-permute-start.12
  102.0 18.7 %collective-permute-start.14 = (bf16[768,512]{1,0:T(8,128)(2,1)S(1)}, bf16[768,512]{1,0:T(8,128)(2,1)S(1)}, u32[]{:S(2)}, u32[]{:S(2)}) collective-permute-start(bf16[768,512]{1,0:T(8,128)(2,1)S(1)} %get-tuple-element.130), channel_id=1, source_target_pairs={{0,1},{1,0},{2,3},{3,2},{4,5},{5,4},{6,7},{7,6},{8,9},{9,8},{10,11... | collective-permute-start | bytes 2359304 | tf_op jit(solution)/shard_map/ppermute | solution.py:458
  113.9 15.2 %collective-permute-start.15 = (bf16[768,256]{1,0:T(8,128)(2,1)S(1)}, bf16[768,256]{1,0:T(8,128)(2,1)S(1)}, u32[]{:S(2)}, u32[]{:S(2)}) collective-permute-start(bf16[768,256]{1,0:T(8,128)(2,1)S(1)} %get-tuple-element.131), channel_id=1, source_target_pairs={{0,1},{1,0},{2,3},{3,2},{4,5},{5,4},{6,7},{7,6},{8,9},{9,8},{10,11... | collective-permute-start | bytes 1179656 | tf_op jit(solution)/shard_map/ppermute | solution.py:458
  120.7 8.4 %copy-start.22 = (bf16[768,512]{1,0:T(8,128)(2,1)}, bf16[768,512]{1,0:T(8,128)(2,1)S(1)}, u32[]{:S(2)}) copy-start(bf16[768,512]{1,0:T(8,128)(2,1)S(1)} %collective-permute-done.14) | copy-start | bytes 2359300
  151.3 8.4 %copy-start.13 = (bf16[3,256,512]{2,1,0:T(8,128)(2,1)S(1)}, bf16[3,256,512]{2,1,0:T(8,128)(2,1)}, u32[]{:S(2)}) copy-start(bf16[3,256,512]{2,1,0:T(8,128)(2,1)} %get-tuple-element.140) | copy-start | bytes 2359300
  151.3 8.7 %copy-start.26 = (f32[4,4,128]{2,1,0:T(4,128)S(1)}, f32[4,4,128]{2,1,0:T(4,128)}, u32[]{:S(2)}) copy-start(f32[4,4,128]{2,1,0:T(4,128)} %get-tuple-element.134) | copy-start | bytes 24580
  151.3 10.1 %copy-start.25 = (f32[4,4,9,128]{3,2,1,0:T(8,128)S(1)}, f32[4,4,9,128]{3,2,1,0:T(8,128)}, u32[]{:S(2)}) copy-start(f32[4,4,9,128]{3,2,1,0:T(8,128)} %get-tuple-element.133) | copy-start | bytes 221188
  151.3 12.4 %copy-start.19 = (bf16[3,256,256]{2,1,0:T(8,128)(2,1)S(1)}, bf16[3,256,256]{2,1,0:T(8,128)(2,1)}, u32[]{:S(2)}) copy-start(bf16[3,256,256]{2,1,0:T(8,128)(2,1)} %get-tuple-element.132) | copy-start | bytes 1179652
  151.3 12.4 %collective-permute-start.16 = (bf16[768,256]{1,0:T(8,128)(2,1)}, bf16[768,256]{1,0:T(8,128)(2,1)S(1)}, u32[]{:S(2)}, u32[]{:S(2)}) collective-permute-start(bf16[768,256]{1,0:T(8,128)(2,1)} %bitcast.56), channel_id=1, source_target_pairs={{0,1},{1,0},{2,3},{3,2},{4,5},{5,4},{6,7},{7,6},{8,9},{9,8},{10,11... | collective-permute-start | bytes 1179656 | tf_op jit(solution)/shard_map/ppermute | solution.py:458
  152.6 47.9 %all-to-all-start.1 = ((bf16[16,256,128]{2,1,0:T(8,128)(2,1)}), bf16[16,256,128]{2,1,0:T(8,128)(2,1)S(1)}, u32[]{:S(2)}, u32[]{:S(2)}) async-start(bf16[16,256,128]{2,1,0:T(8,128)(2,1)} %get-tuple-element.156), calls=%async_computation.1 | async-start | bytes 2097152 | tf_op jit(solution)/shard_map/all_to_all | solution.py:505
  159.7 19.6 %collective-permute-start.19 = (bf16[768,512]{1,0:T(8,128)(2,1)S(1)}, bf16[768,512]{1,0:T(8,128)(2,1)S(1)}, u32[]{:S(2)}, u32[]{:S(2)}) collective-permute-start(bf16[768,512]{1,0:T(8,128)(2,1)S(1)} %bitcast.50), channel_id=1, source_target_pairs={{0,1},{1,0},{2,3},{3,2},{4,5},{5,4},{6,7},{7,6},{8,9},{9,8},{10,11... | collective-permute-start | bytes 2359304 | tf_op jit(solution)/shard_map/ppermute | solution.py:458
  173.5 2.7 collective-permute-start.17
  173.9 2.3 collective-permute-start.18
  174.0 22.1 %collective-permute-start.22 = (bf16[768,512]{1,0:T(8,128)(2,1)S(1)}, bf16[768,512]{1,0:T(8,128)(2,1)S(1)}, u32[]{:S(2)}, u32[]{:S(2)}) collective-permute-start(bf16[768,512]{1,0:T(8,128)(2,1)S(1)} %bitcast.46), channel_id=1, source_target_pairs={{0,1},{1,0},{2,3},{3,2},{4,5},{5,4},{6,7},{7,6},{8,9},{9,8},{10,11... | collective-permute-start | bytes 2359304 | tf_op jit(solution)/shard_map/ppermute | solution.py:458
  179.3 20.0 %collective-permute-start.24 = (bf16[128,4096]{1,0:T(8,128)(2,1)S(1)}, bf16[128,4096]{1,0:T(8,128)(2,1)S(1)}, u32[]{:S(2)}, u32[]{:S(2)}) collective-permute-start(bf16[128,4096]{1,0:T(8,128)(2,1)S(1)} %shard_map.137), channel_id=1, source_target_pairs={{0,4},{2,10},{8,0},{10,18},{16,8},{18,26},{24,16},{26,30},{28,24},... | collective-permute-start | bytes 3145736 | tf_op jit(solution)/shard_map/ppermute | solution.py:425
  188.9 10.3 %collective-permute-start.20 = (bf16[96,4096]{1,0:T(8,128)(2,1)S(1)}, bf16[96,4096]{1,0:T(8,128)(2,1)S(1)}, u32[]{:S(2)}, u32[]{:S(2)}) collective-permute-start(bf16[96,4096]{1,0:T(8,128)(2,1)S(1)} %get-tuple-element.146), channel_id=1, source_target_pairs={{0,2},{2,0},{4,6},{6,4},{8,10},{10,8},{12,14},{14,12},{16,18},{18,... | collective-permute-start | bytes 2359304 | tf_op jit(solution)/shard_map/ppermute | solution.py:428
  191.0 8.3 %collective-permute-start.21 = (bf16[96,4096]{1,0:T(8,128)(2,1)S(1)}, bf16[96,4096]{1,0:T(8,128)(2,1)S(1)}, u32[]{:S(2)}, u32[]{:S(2)}) collective-permute-start(bf16[96,4096]{1,0:T(8,128)(2,1)S(1)} %get-tuple-element.147), channel_id=1, source_target_pairs={{0,2},{2,0},{4,6},{6,4},{8,10},{10,8},{12,14},{14,12},{16,18},{18,... | collective-permute-start | bytes 2359304 | tf_op jit(solution)/shard_map/ppermute | solution.py:428
  197.0 2.2 collective-permute-start.23
  200.5 25.2 %collective-permute-start.28 = (bf16[256,4096]{1,0:T(8,128)(2,1)S(1)}, bf16[256,4096]{1,0:T(8,128)(2,1)S(1)}, u32[]{:S(2)}, u32[]{:S(2)}) collective-permute-start(bf16[256,4096]{1,0:T(8,128)(2,1)S(1)} %shard_map.139), channel_id=1, source_target_pairs={{0,4},{2,10},{8,0},{10,18},{16,8},{18,26},{24,16},{26,30},{28,24},... | collective-permute-start | bytes 6291464 | tf_op jit(solution)/shard_map/ppermute | solution.py:425
  201.8 18.6 %collective-permute-start.26 = (bf16[768,512]{1,0:T(8,128)(2,1)}, bf16[768,512]{1,0:T(8,128)(2,1)S(1)}, u32[]{:S(2)}, u32[]{:S(2)}) collective-permute-start(bf16[768,512]{1,0:T(8,128)(2,1)} %bitcast.44), channel_id=1, source_target_pairs={{0,1},{1,0},{2,3},{3,2},{4,5},{5,4},{6,7},{7,6},{8,9},{9,8},{10,11... | collective-permute-start | bytes 2359304 | tf_op jit(solution)/shard_map/ppermute | solution.py:458
  218.6 4.9 %collective-permute-start.25 = (bf16[128,4096]{1,0:T(8,128)(2,1)S(1)}, bf16[128,4096]{1,0:T(8,128)(2,1)S(1)}, u32[]{:S(2)}, u32[]{:S(2)}) collective-permute-start(bf16[128,4096]{1,0:T(8,128)(2,1)S(1)} %get-tuple-element.160), channel_id=1, source_target_pairs={{0,2},{2,0},{4,6},{6,4},{8,10},{10,8},{12,14},{14,12},{16,18},{18,... | collective-permute-start | bytes 3145736 | tf_op jit(solution)/shard_map/ppermute | solution.py:428
  220.4 3.8 %collective-permute-start.27 = (bf16[128,4096]{1,0:T(8,128)(2,1)S(1)}, bf16[128,4096]{1,0:T(8,128)(2,1)S(1)}, u32[]{:S(2)}, u32[]{:S(2)}) collective-permute-start(bf16[128,4096]{1,0:T(8,128)(2,1)S(1)} %get-tuple-element.163), channel_id=1, source_target_pairs={{0,2},{2,0},{4,6},{6,4},{8,10},{10,8},{12,14},{14,12},{16,18},{18,... | collective-permute-start | bytes 3145736 | tf_op jit(solution)/shard_map/ppermute | solution.py:428
  227.1 25.2 %collective-permute-start.32 = (bf16[256,4096]{1,0:T(8,128)(2,1)S(1)}, bf16[256,4096]{1,0:T(8,128)(2,1)S(1)}, u32[]{:S(2)}, u32[]{:S(2)}) collective-permute-start(bf16[256,4096]{1,0:T(8,128)(2,1)S(1)} %shard_map.141), channel_id=1, source_target_pairs={{0,4},{2,10},{8,0},{10,18},{16,8},{18,26},{24,16},{26,30},{28,24},... | collective-permute-start | bytes 6291464 | tf_op jit(solution)/shard_map/ppermute | solution.py:425
  228.4 11.9 %collective-permute-start.30 = (bf16[768,256]{1,0:T(8,128)(2,1)S(1)}, bf16[768,256]{1,0:T(8,128)(2,1)S(1)}, u32[]{:S(2)}, u32[]{:S(2)}) collective-permute-start(bf16[768,256]{1,0:T(8,128)(2,1)S(1)} %bitcast.53), channel_id=1, source_target_pairs={{0,1},{1,0},{2,3},{3,2},{4,5},{5,4},{6,7},{7,6},{8,9},{9,8},{10,11... | collective-permute-start | bytes 1179656 | tf_op jit(solution)/shard_map/ppermute | solution.py:458
  238.4 4.2 %collective-permute-start.29 = (bf16[128,4096]{1,0:T(8,128)(2,1)S(1)}, bf16[128,4096]{1,0:T(8,128)(2,1)S(1)}, u32[]{:S(2)}, u32[]{:S(2)}) collective-permute-start(bf16[128,4096]{1,0:T(8,128)(2,1)S(1)} %get-tuple-element.172), channel_id=1, source_target_pairs={{0,2},{2,0},{4,6},{6,4},{8,10},{10,8},{12,14},{14,12},{16,18},{18,... | collective-permute-start | bytes 3145736 | tf_op jit(solution)/shard_map/ppermute | solution.py:428
  240.3 3.8 %collective-permute-start.31 = (bf16[128,4096]{1,0:T(8,128)(2,1)S(1)}, bf16[128,4096]{1,0:T(8,128)(2,1)S(1)}, u32[]{:S(2)}, u32[]{:S(2)}) collective-permute-start(bf16[128,4096]{1,0:T(8,128)(2,1)S(1)} %get-tuple-element.175), channel_id=1, source_target_pairs={{0,2},{2,0},{4,6},{6,4},{8,10},{10,8},{12,14},{14,12},{16,18},{18,... | collective-permute-start | bytes 3145736 | tf_op jit(solution)/shard_map/ppermute | solution.py:428
  253.7 14.0 %collective-permute-start.35 = (bf16[128,4096]{1,0:T(8,128)(2,1)S(1)}, bf16[128,4096]{1,0:T(8,128)(2,1)S(1)}, u32[]{:S(2)}, u32[]{:S(2)}) collective-permute-start(bf16[128,4096]{1,0:T(8,128)(2,1)S(1)} %get-tuple-element.188), channel_id=1, source_target_pairs={{0,4},{2,10},{8,0},{10,18},{16,8},{18,26},{24,16},{26,30},{28,24},... | collective-permute-start | bytes 3145736 | tf_op jit(solution)/shard_map/ppermute | solution.py:425
  255.0 26.2 %collective-permute-start.36 = (bf16[128,4096]{1,0:T(8,128)(2,1)S(1)}, bf16[128,4096]{1,0:T(8,128)(2,1)S(1)}, u32[]{:S(2)}, u32[]{:S(2)}) collective-permute-start(bf16[128,4096]{1,0:T(8,128)(2,1)S(1)} %get-tuple-element.189), channel_id=1, source_target_pairs={{0,6},{2,8},{8,2},{10,16},{16,10},{18,24},{24,18},{26,28},{28,26},... | collective-permute-start | bytes 3145736 | tf_op jit(solution)/shard_map/ppermute | solution.py:425
  262.7 2.0 collective-permute-start.33
  262.7 2.6 collective-permute-start.34
  (18 other events, 47.5 us)
